TPU v7x, 32 devices: a whole 2x2x4 slice. The times are simulated.
32 devices in a mesh: sims: 8 (over y, x, core), rows: 4 (over z).
Axes of the slice: x: 2, y: 2, z: 4, core: 2. Of those that a mesh axis runs over, the one named last changes fastest.
Arguments:
- maps: float32 [8, 256, 2048], P('sims', 'rows'), may hold values from -6 to 6
- weight: float32 [256, 2048], P('rows'), may hold values from 0.1 to 1.5
- beam: float32 [65], replicated, may hold values from 0.05 to 1
- pair_one: int32 [8], replicated, may hold values from 0 to 7, each once
- pair_two: int32 [8], replicated, may hold values from 0 to 7, each once
- owner: int32 [8], replicated, may hold values from 0 to 7
Outputs:
- estimate: float32 [8, 256, 2048], P('sims', 'rows')
- mean_field: float32 [8, 256, 2048], P(None, 'rows', 'sims')
Inputs may be any that keep to these rules, and one draw needn't show every extreme that they name: `pair_one`: each a permutation of the evolutions. `pair_two`: each a permutation of the evolutions.
All inputs are finite; a program needn't handle non-finite values.
Results may differ from a plain program's by a relative error of at most 0.00016.
Values sent between devices are 32-bit elements; how exact they have to be, the bound alone decides.
No kernel may reach another device: no remote copies, remote signals or barrier semaphores. Data moves between devices by JAX's collectives and lax.ppermute only.
A program may use at most 64 MiB of HBM per device.

v0:
```python
import functools

import jax
import jax.numpy as jnp
from jax import lax
from jax.experimental import pallas as pl
from jax.experimental.pallas import tpu as pltpu
from jax.sharding import PartitionSpec as P

ITERS = 3
OWNERS = 8

ridge_term = 0.5
step_size = 0.6
exact = lax.Precision.HIGHEST
lane = 128
wide = 256
rim = 4
vmem_bytes = 48 * 1024 * 1024


def split(value):
    high = value.astype(jnp.bfloat16)
    low = (value - high.astype(jnp.float32)).astype(jnp.bfloat16)
    return high, low


def dot(a, b):
    return jnp.dot(a, b, preferred_element_type=jnp.float32)


def dot3(a_high, a_low, b_high, b_low):
    return dot(a_high, b_high) + (dot(a_low, b_high) + dot(a_high, b_low))


class Plan:
    def __init__(self, row_devices, sim_devices, row_local, columns, taps):
        self.row_devices, self.sim_devices = row_devices, sim_devices
        self.row_local, self.columns = row_local, columns
        self.rows = row_devices * row_local
        self.margin = (taps - 1) // 2
        self.share = columns // row_devices
        self.halo = -(-self.margin * (2 * ITERS + 1) // lane) * lane
        self.width = self.share + 2 * self.halo
        self.slab = row_local + 2 * rim
        self.sharers = min(sim_devices, row_local // 8)
        self.share_rows = row_local // self.sharers
        self.length = max(2 * wide, -(-self.rows // lane) * lane)
        inner = range(lane, self.width - lane, wide)
        blocks = [(0, lane)] + [(a, min(a + wide, self.width - lane)) for a in inner]
        self.blocks = blocks + [(self.width - lane, self.width)]
        centre = range(self.halo, self.halo + self.share, wide)
        self.out_blocks = [(a, min(a + wide, self.halo + self.share)) for a in centre]

    def window(self, block):
        return max(0, block[0] - lane), min(self.width, block[1] + lane)

    def stage_blocks(self, iteration):
        low = self.halo - self.margin * (2 * (ITERS - 1 - iteration) + 1)
        return [i for i, (a, b) in enumerate(self.blocks) if b > low and a < self.width - low]


def weighted_kernel(plan, place, maps, weight, *refs):
    count = plan.row_devices
    pieces, parts, padded = refs[:count], refs[count : 2 * count], refs[2 * count]
    zeros = jnp.zeros((plan.row_local, plan.halo), jnp.float32)
    inner = slice(plan.halo, plan.halo + plan.columns)
    padded[:, : plan.halo] = zeros
    padded[:, plan.halo + plan.columns :] = zeros
    padded[:, inner] = weight[...]
    row = pl.multiple_of(lax.rem(place[1], plan.sharers) * plan.share_rows, plan.share_rows)
    for step in range(count):
        column = pl.multiple_of((place[0] ^ step) * plan.share, lane)
        parts[step][...] = padded[pl.ds(row, plan.share_rows), pl.ds(column, plan.width)]
    padded[:, inner] = weight[...] * maps[...]
    for step in range(count):
        column = pl.multiple_of((place[0] ^ step) * plan.share, lane)
        pieces[step][...] = padded[:, pl.ds(column, plan.width)]


def band(plan, taps, rows, columns, offset):
    spread = jnp.broadcast_to(taps[...], (rows, plan.length))
    if offset % plan.length:
        spread = pltpu.roll(spread, offset % plan.length, 1)
    rolled = pltpu.roll(spread, 0, 1, stride=1, stride_axis=0)[:, :columns]
    row = lax.broadcasted_iota(jnp.int32, (rows, columns), 0)
    column = lax.broadcasted_iota(jnp.int32, (rows, columns), 1)
    return jnp.where(jnp.abs(column - row - offset) <= plan.margin, rolled, 0.0)


def table_kernel(plan, place, taps, reverse, *refs):
    tables = list(refs)

    def put(value):
        high, low = split(value)
        tables.pop(0)[...] = high
        tables.pop(0)[...] = low

    rows = plan.rows
    put(jnp.dot(band(plan, taps, rows, rows, 0), band(plan, reverse, rows, rows, 0), precision=exact))
    slabs = []
    for device in range(plan.row_devices):
        first = device * plan.row_local - rim
        part = band(plan, reverse, plan.slab, rows, first)
        row = lax.broadcasted_iota(jnp.int32, part.shape, 0) + first
        slabs.append(jnp.where((row >= 0) & (row < rows), part, 0.0))
    put(jnp.concatenate(slabs, axis=0))
    size = 2 * wide
    forward = band(plan, taps, size, size, 0)
    backward = band(plan, reverse, size, size, 0)
    for block in plan.blocks:
        low, high = plan.window(block)
        extent = high - low
        column = lax.broadcasted_iota(jnp.int32, (extent, extent), 1) + (place[0] * plan.share - plan.halo + low)
        inside = (column >= 0) & (column < plan.columns)
        left = jnp.where(inside, forward[:extent, :extent], 0.0)
        right = backward[:extent, block[0] - low : block[1] - low]
        put(step_size * jnp.dot(left, right, precision=exact))
    for block in plan.out_blocks[:1]:
        low, high = plan.window(block)
        put(step_size * forward[: high - low, block[0] - low : block[1] - low])


def filter_kernel(plan, sharers, place, *refs):
    refs = list(refs)

    def take(number):
        taken = refs[:number]
        del refs[:number]
        return taken

    pieces = take(plan.row_devices)
    parts = take(len(sharers))
    square, final = take(2), take(2)
    bands = [take(2) for _ in plan.blocks]
    last = take(2)
    outs = take(plan.row_devices)
    seen, weight, image, total, field, high, low, mid_high, mid_low = refs
    for step, piece in enumerate(pieces):
        row = pl.multiple_of((place[0] ^ step) * plan.row_local, plan.row_local)
        value = piece[...]
        seen[pl.ds(row, plan.row_local), :] = value
        a, b = split(value)
        high[pl.ds(row, plan.row_local), :] = a
        low[pl.ds(row, plan.row_local), :] = b
    for part, owners in zip(parts, sharers):
        for slot, offset in enumerate(owners):
            for step in range(plan.row_devices):
                row = (place[0] ^ step) * plan.row_local
                row = row + (lax.rem(place[1], plan.sharers) ^ offset) * plan.share_rows
                row = pl.multiple_of(row, plan.share_rows)
                weight[pl.ds(row, plan.share_rows), :] = part[slot, step]

    def rows_pass(table, start, stop):
        count = table[0].shape[0]
        for a in range(start, stop, wide):
            b = min(a + wide, stop)
            value = dot3(table[0][...], table[1][...], high[:, a:b], low[:, a:b])
            mid_high[:count, a:b], mid_low[:count, a:b] = split(value)

    def columns_pass(table, count, window):
        a, b = window
        return dot3(mid_high[:count, a:b], mid_low[:count, a:b], table[0][...], table[1][...])

    keep = 1.0 - step_size * ridge_term
    for iteration in range(ITERS):
        chosen = plan.stage_blocks(iteration)
        windows = [plan.window(plan.blocks[i]) for i in chosen]
        rows_pass(square, windows[0][0], windows[-1][1])
        for i, window in zip(chosen, windows):
            a, b = plan.blocks[i]
            value = columns_pass(bands[i], plan.rows, window)
            if iteration > 0:
                value = value + keep * image[:, a:b]
            image[:, a:b] = value
            given = seen[:, a:b]
            residual = given - weight[:, a:b] * value
            total[:, a:b] = residual + keep * (total[:, a:b] if iteration > 0 else given)
            high[:, a:b], low[:, a:b] = split(residual)
    first, stop = plan.window(plan.out_blocks[0])[0], plan.window(plan.out_blocks[-1])[1]
    high[:, first:stop], low[:, first:stop] = split(total[:, first:stop])
    rows_pass(final, first, stop)
    count = plan.row_devices * plan.slab
    for block in plan.out_blocks:
        size = block[1] - block[0]
        field[:, block[0] - plan.halo : block[1] - plan.halo] = columns_pass(last, count, plan.window(block))
    for step, out in enumerate(outs):
        row = pl.multiple_of((place[0] ^ step) * plan.slab, 8)
        out[...] = field[pl.ds(row, plan.slab), :]


def divergence(own, partner):
    rows, columns = own.shape
    stop = rows - rim
    inner = slice(lane, columns - lane)
    here = partner[rim:stop]
    down, up = partner[rim + 2 : stop + 2, inner], partner[rim - 2 : stop - 2, inner]
    middle = here[:, inner]
    flow = own[rim + 1 : stop + 1, inner] * (down - middle) - own[rim - 1 : stop - 1, inner] * (middle - up)
    level = own[rim:stop]

    def shifted(value, amount):
        return pltpu.roll(value, amount % columns, 1)[:, inner]

    right = shifted(level, -1) * (shifted(here, -2) - middle)
    left = shifted(level, 1) * (middle - shifted(here, 2))
    return 0.25 * (flow + (right - left))


def estimate_kernel(plan, holders, field_width, place, pair_one, pair_two, owner, *refs):
    refs = list(refs)
    pieces = []
    for orders in holders:
        flat = []
        for order in orders:
            ref = refs.pop(0)
            flat += [(offset, ref.at[slot]) for slot, offset in enumerate(order)]
        pieces.append(sorted(flat, key=lambda entry: entry[0]))
    estimate = refs.pop(0)
    mean_field = refs.pop(0) if field_width else None
    own, first, second = refs[:3]
    sems = refs[3]
    rows_at, sim_at = place[0], place[1]
    edge = jnp.zeros((plan.slab, lane), jnp.float32)
    offset_one, offset_two = sim_at ^ pair_one[sim_at], sim_at ^ pair_two[sim_at]
    for step in range(plan.row_devices):
        column = pl.multiple_of(lane + (rows_at ^ step) * plan.share, lane)
        for offset, source in pieces[step]:
            def fetch(target, sem, source=source, column=column):
                pltpu.make_async_copy(source, target.at[:, pl.ds(column, plan.share)], sems.at[sem]).start()

            if offset == 0:
                fetch(own, 0)
            pl.when(offset == offset_one)(functools.partial(fetch, first, 1))
            pl.when(offset == offset_two)(functools.partial(fetch, second, 2))
    if field_width:
        every = refs[4]
        units = field_width // lane
        per = plan.share // lane
        for unit in range(units + 2):
            at = sim_at * units - 1 + unit
            inside = (at >= 0) & (at < plan.columns // lane)
            span = slice(unit * lane, (unit + 1) * lane)
            for step in range(plan.row_devices):
                def fetch_all(step=step, at=at, span=span, unit=unit):
                    column = pl.multiple_of(lax.rem(at, per) * lane, lane)
                    for offset, source in pieces[step]:
                        pltpu.make_async_copy(
                            source.at[:, pl.ds(column, lane)], every.at[sim_at ^ offset, :, span], sems.at[3 + unit]
                        ).start()

                pl.when(inside & (lax.div(at, per) == (rows_at ^ step)))(fetch_all)

            @pl.when(jnp.logical_not(inside))
            def _(span=span):
                every[:, :, span] = jnp.zeros((plan.sim_devices, plan.slab, lane), jnp.float32)

    for number, target in enumerate((own, first, second)):
        target[:, :lane] = edge
        target[:, lane + plan.columns :] = edge
        span = target.at[:, pl.ds(lane, plan.columns)]
        pltpu.make_async_copy(span, span, sems.at[number]).wait()
    for a in range(0, plan.columns, wide):
        span = slice(a, a + wide + 2 * lane)
        estimate[:, a : a + wide] = divergence(own[:, span], 2.0 * first[:, span] - second[:, span])
    if not field_width:
        return
    for unit in range(units + 2):
        at = sim_at * units - 1 + unit

        @pl.when((at >= 0) & (at < plan.columns // lane))
        def _(unit=unit):
            span = every.at[:, :, unit * lane : (unit + 1) * lane]
            pltpu.make_async_copy(span, span, sems.at[3 + unit]).wait()

    mean_field[...] = jnp.zeros(mean_field.shape, jnp.float32)
    for sim in range(plan.sim_devices):
        partner = 2.0 * every[pair_one[sim]] - every[pair_two[sim]]
        mean_field[owner[sim]] += divergence(every[sim], partner)
    for group in range(OWNERS):
        count = jnp.int32(0)
        for sim in range(plan.sim_devices):
            count = count + (owner[sim] == group).astype(jnp.int32)
        mean_field[group] = mean_field[group] / jnp.maximum(count, 1).astype(jnp.float32)


def exchange(value, axis, offset):
    count = lax.axis_size(axis)
    return lax.ppermute(value, axis, [(i, i ^ offset) for i in range(count)])


def gather(first, axis, bits):
    arrays, offsets = [first[None]], [[0]]
    for bit in bits:
        whole = jnp.concatenate(arrays, axis=0) if len(arrays) > 1 else arrays[0]
        arrays.append(exchange(whole, axis, bit))
        offsets.append([offset ^ bit for order in offsets for offset in order])
    return arrays, offsets


def call(kernel, out_shapes, in_specs, scratch, flops, moved, out_specs=None):
    vmem = pl.BlockSpec(memory_space=pltpu.VMEM)
    return pl.pallas_call(
        kernel,
        out_shape=out_shapes,
        in_specs=in_specs,
        out_specs=[vmem] * len(out_shapes) if out_specs is None else out_specs,
        scratch_shapes=scratch,
        compiler_params=pltpu.CompilerParams(vmem_limit_bytes=vmem_bytes),
        cost_estimate=pl.CostEstimate(flops=flops, bytes_accessed=moved, transcendentals=0),
    )


def body(maps, weight, beam, pair_one, pair_two, owner):
    sim_local, row_local, columns = maps.shape
    taps = beam.shape[0]
    row_devices, sim_devices = lax.axis_size("rows"), lax.axis_size("sims")
    plan = Plan(row_devices, sim_devices, row_local, columns, taps)
    place = jnp.stack([lax.axis_index("rows"), lax.axis_index("sims")]).astype(jnp.int32)
    vmem = pl.BlockSpec(memory_space=pltpu.VMEM)
    smem = pl.BlockSpec(memory_space=pltpu.SMEM)
    hbm = pl.BlockSpec(memory_space=pl.ANY)

    def f32(*shape):
        return jax.ShapeDtypeStruct(shape, jnp.float32)

    def b16(*shape):
        return jax.ShapeDtypeStruct(shape, jnp.bfloat16)

    cells = row_local * columns
    made = call(
        functools.partial(weighted_kernel, plan),
        [f32(row_local, plan.width)] * row_devices + [f32(plan.share_rows, plan.width)] * row_devices,
        [smem, vmem, vmem],
        [pltpu.VMEM((row_local, columns + 2 * plan.halo), jnp.float32)],
        cells,
        16 * cells,
    )(place, maps.reshape(row_local, columns), weight)
    pieces, parts = made[:row_devices], made[row_devices:]
    parts = [parts[0]] + [exchange(parts[d], "rows", d) for d in range(1, row_devices)]
    pieces = [pieces[0]] + [exchange(pieces[d], "rows", d) for d in range(1, row_devices)]
    bits = [1 << i for i in range(1, plan.sharers.bit_length() - 1)] + [1]
    parts, sharers = gather(jnp.stack(parts), "sims", bits)

    kernel = beam / jnp.sum(beam)
    blank = jnp.zeros((plan.length - taps,), jnp.float32)
    forward = jnp.roll(jnp.concatenate([kernel, blank]), -plan.margin)[None]
    backward = jnp.roll(jnp.concatenate([kernel[::-1], blank]), -plan.margin)[None]
    shapes = [(plan.rows, plan.rows), (row_devices * plan.slab, plan.rows)]
    for block in plan.blocks + plan.out_blocks[:1]:
        low, high = plan.window(block)
        shapes.append((high - low, block[1] - block[0]))
    tables = call(
        functools.partial(table_kernel, plan),
        [b16(*shape) for shape in shapes for _ in range(2)],
        [smem, vmem, vmem],
        [],
        1 << 32,
        1 << 23,
    )(place, forward, backward)

    full = (plan.rows, plan.width)
    tall = (max(plan.rows, row_devices * plan.slab), plan.width)
    filtered = call(
        functools.partial(filter_kernel, plan, sharers),
        [f32(plan.slab, plan.share)] * row_devices,
        [smem] + [vmem] * (len(pieces) + len(parts) + len(tables)),
        [pltpu.VMEM(full, jnp.float32)] * 4
        + [pltpu.VMEM((row_devices * plan.slab, plan.share), jnp.float32)]
        + [pltpu.VMEM(full, jnp.bfloat16)] * 2
        + [pltpu.VMEM(tall, jnp.bfloat16)] * 2,
        1 << 33,
        1 << 23,
    )(place, *pieces, *parts, *tables)

    held, holders = [], []
    for step in range(row_devices):
        piece = filtered[step] if step == 0 else exchange(filtered[step], "rows", step)
        bits = [1 << i for i in range(1, sim_devices.bit_length() - 1)]
        turn = step % max(len(bits), 1)
        arrays, offsets = gather(piece, "sims", bits[turn:] + bits[:turn] + [1])
        held += arrays
        holders.append(offsets)

    field_width = columns // sim_devices
    fused = field_width if field_width % lane == 0 else 0
    outs = [f32(row_local, columns)]
    extended = (plan.slab, columns + 2 * lane)
    scratch = [pltpu.VMEM(extended, jnp.float32)] * 3
    if fused:
        outs.append(f32(OWNERS, row_local, fused))
        scratch.append(pltpu.SemaphoreType.DMA((3 + fused // lane + 2,)))
        scratch.append(pltpu.VMEM((sim_devices, plan.slab, fused + 2 * lane), jnp.float32))
    else:
        scratch.append(pltpu.SemaphoreType.DMA((3,)))
    results = call(
        functools.partial(estimate_kernel, plan, holders, fused),
        outs,
        [smem] * 4 + [hbm] * len(held),
        scratch,
        1 << 24,
        1 << 23,
    )(place, pair_one, pair_two, owner, *held)
    estimate = results[0]
    if fused:
        mean_field = results[1]
    else:
        groups = jnp.arange(OWNERS, dtype=jnp.int32)
        local_owner = owner[place[1]]
        term = jnp.where((groups == local_owner)[:, None, None], estimate[None], 0.0)
        total = lax.psum_scatter(term, "sims", scatter_dimension=2, tiled=True)
        tally = jnp.sum((groups[:, None] == owner[None, :]).astype(jnp.float32), axis=1)
        mean_field = total / jnp.maximum(tally, 1.0)[:, None, None]
    return estimate.reshape(maps.shape), mean_field


def solution(mesh):
    in_specs = (P("sims", "rows", None), P("rows", None), P(), P(), P(), P())
    out_specs = (P("sims", "rows", None), P(None, "rows", "sims"))
    return jax.shard_map(body, mesh=mesh, in_specs=in_specs, out_specs=out_specs, check_vma=False)
```

profile of v0, /device:TPU:0, one launch (start us, length us, event | category | flops | bytes accessed | tf_op | source)
XLA Modules:
  0.0 83.4 jit_solution(3665269406367438058)
XLA Ops:
  0.6 0.1 pad_add_fusion.place
  0.7 1.0 %copy-done = f32[1,64,2048]{2,1,0:T(8,128)S(1)} copy-done((f32[1,64,2048]{2,1,0:T(8,128)S(1)}, f32[1,64,2048]{2,1,0:T(8,128)}, u32[]{:S(2)}) %copy-start) | copy-done | bytes 524312
  1.8 1.0 %copy-done.1 = f32[64,2048]{1,0:T(8,128)S(1)} copy-done((f32[64,2048]{1,0:T(8,128)S(1)}, f32[64,2048]{1,0:T(8,128)}, u32[]{:S(2)}) %copy-start.1) | copy-done | bytes 524312
  2.8 0.7 shard_map.77
  3.5 3.1 %collective-permute-start.3 = (f32[8,1024]{1,0:T(8,128)S(1)}, f32[8,1024]{1,0:T(8,128)S(1)}, u32[]{:S(2)}, u32[]{:S(2)}) collective-permute-start(f32[8,1024]{1,0:T(8,128)S(1)} %get-tuple-element.37), channel_id=1, source_target_pairs={{0,1},{1,0},{2,3},{3,2},{4,5},{5,4},{6,7},{7,6},{8,9},{9,8},{10,11... | collective-permute-start | bytes 98312 | tf_op jit(solution)/shard_map/ppermute | solution.py:289
  6.6 2.6 %collective-permute-start.4 = (f32[8,1024]{1,0:T(8,128)S(1)}, f32[8,1024]{1,0:T(8,128)S(1)}, u32[]{:S(2)}, u32[]{:S(2)}) collective-permute-start(f32[8,1024]{1,0:T(8,128)S(1)} %get-tuple-element.38), channel_id=1, source_target_pairs={{0,2},{1,3},{2,0},{3,1},{4,6},{5,7},{6,4},{7,5},{8,10},{9,11},{10,... | collective-permute-start | bytes 98312 | tf_op jit(solution)/shard_map/ppermute | solution.py:289
  9.2 0.0 collective-permute-start.5
  9.2 0.0 collective-permute-done.3
  9.2 2.8 %collective-permute-done.4 = f32[8,1024]{1,0:T(8,128)S(1)} collective-permute-done((f32[8,1024]{1,0:T(8,128)S(1)}, f32[8,1024]{1,0:T(8,128)S(1)}, u32[]{:S(2)}, u32[]{:S(2)}) %collective-permute-start.4) | collective-permute-done | bytes 32800 | tf_op jit(solution)/shard_map/ppermute | solution.py:289
  12.0 2.9 %collective-permute-done.5 = f32[8,1024]{1,0:T(8,128)S(1)} collective-permute-done((f32[8,1024]{1,0:T(8,128)S(1)}, f32[8,1024]{1,0:T(8,128)S(1)}, u32[]{:S(2)}, u32[]{:S(2)}) %collective-permute-start.5) | collective-permute-done | bytes 32800 | tf_op jit(solution)/shard_map/ppermute | solution.py:289
  14.9 1.6 %collective-permute-start.6 = (f32[1,4,8,1024]{3,2,1,0:T(8,128)S(1)}, f32[1,4,8,1024]{3,2,1,0:T(8,128)S(1)}, u32[]{:S(2)}, u32[]{:S(2)}) collective-permute-start(f32[1,4,8,1024]{3,2,1,0:T(8,128)S(1)} %maximum_bitcast_fusion.refs_4_), channel_id=1, source_target_pairs={{0,8},{4,12},{8,0},{12,4},{16,24},{20,28},{24,16},{28,20},{1,9},{5... | collective-permute-start | bytes 393224 | tf_op jit(solution)/shard_map/ppermute | solution.py:289
  16.5 0.0 collective-permute-start
  16.5 0.9 %collective-permute-start.1 = (f32[64,1024]{1,0:T(8,128)S(1)}, f32[64,1024]{1,0:T(8,128)S(1)}, u32[]{:S(2)}, u32[]{:S(2)}) collective-permute-start(f32[64,1024]{1,0:T(8,128)S(1)} %get-tuple-element.34), channel_id=1, source_target_pairs={{0,2},{1,3},{2,0},{3,1},{4,6},{5,7},{6,4},{7,5},{8,10},{9,11},{10,... | collective-permute-start | bytes 786440 | tf_op jit(solution)/shard_map/ppermute | solution.py:289
  17.4 3.5 %collective-permute-start.2 = (f32[64,1024]{1,0:T(8,128)S(1)}, f32[64,1024]{1,0:T(8,128)S(1)}, u32[]{:S(2)}, u32[]{:S(2)}) collective-permute-start(f32[64,1024]{1,0:T(8,128)S(1)} %get-tuple-element.35), channel_id=1, source_target_pairs={{0,3},{1,2},{2,1},{3,0},{4,7},{5,6},{6,5},{7,4},{8,11},{9,10},{10,... | collective-permute-start | bytes 786440 | tf_op jit(solution)/shard_map/ppermute | solution.py:289
  20.9 0.1 reverse.3
  21.0 0.6 reduce_sum.9
  21.6 0.0 collective-permute-done.6.refs_5_
  21.6 1.6 %collective-permute-start.7 = (f32[2,4,8,1024]{3,2,1,0:T(8,128)S(1)}, f32[2,4,8,1024]{3,2,1,0:T(8,128)S(1)}, u32[]{:S(2)}, u32[]{:S(2)}) collective-permute-start(f32[2,4,8,1024]{3,2,1,0:T(8,128)S(1)} %pad_maximum_fusion.9), channel_id=1, source_target_pairs={{0,16},{4,20},{8,24},{12,28},{16,0},{20,4},{24,8},{28,12},{1,17},{... | collective-permute-start | bytes 786440 | tf_op jit(solution)/shard_map/ppermute | solution.py:289
  23.2 0.6 broadcast_divide_fusion
  23.9 0.1 pad_slice_fusion
  24.0 0.1 pad_slice_fusion.1
  24.0 4.0 %collective-permute-done.7.refs_6_ = f32[2,4,8,1024]{3,2,1,0:T(8,128)S(1)} collective-permute-done((f32[2,4,8,1024]{3,2,1,0:T(8,128)S(1)}, f32[2,4,8,1024]{3,2,1,0:T(8,128)S(1)}, u32[]{:S(2)}, u32[]{:S(2)}) %collective-permute-start.7) | collective-permute-done | bytes 262176 | tf_op jit(solution)/shard_map/ppermute | solution.py:289
  28.1 0.1 collective-permute-start.8
  28.2 0.1 pad_maximum_fusion.11
  28.3 0.1 pad_maximum_fusion.10
  28.3 4.0 %shard_map.78 = (bf16[256,256]{1,0:T(8,128)(2,1)S(1)}, bf16[256,256]{1,0:T(8,128)(2,1)S(1)}, bf16[288,256]{1,0:T(8,128)(2,1)S(1)}, bf16[288,256]{1,0:T(8,128)(2,...) custom-call(s32[2]{0:T(128)S(1)} %pad_add_fusion.place, ...), custom_call_target="tpu_custom_call" | custom-call | flops 4294967296 | bytes 8388608 | tf_op jit(solution)/shard_map/pallas_call | solution.py:353
  32.4 0.0 collective-permute-done.refs_1_
  32.4 4.6 %collective-permute-done.1.refs_2_ = f32[64,1024]{1,0:T(8,128)S(1)} collective-permute-done((f32[64,1024]{1,0:T(8,128)S(1)}, f32[64,1024]{1,0:T(8,128)S(1)}, u32[]{:S(2)}, u32[]{:S(2)}) %collective-permute-start.1) | collective-permute-done | bytes 262176 | tf_op jit(solution)/shard_map/ppermute | solution.py:289
  36.9 0.0 collective-permute-done.2.refs_3_
  36.9 0.0 collective-permute-done.8.refs_7_
  36.9 6.0 %shard_map.79 = (f32[72,512]{1,0:T(8,128)S(1)}, f32[72,512]{1,0:T(8,128)S(1)}, f32[72,512]{1,0:T(8,128)S(1)}, f32[72,512]{1,0:T(8,128)S(1)}) custom-call(s32[2]{0:T(128)S(1)} %pad_add_fusion.place, f32[64,1024]{1,0:T(8,128)S(1)} %get-tuple-element.32.refs_0_, f32[64,1024]{1,0:T(8,128)S(1)} %collective-permute-done.refs_1_, ...), custom_call_target="tpu_custom_call" | custom-call | flops 8589934592 | bytes 8388608 | tf_op jit(solution)/shard_map/pallas_call | solution.py:364
  43.0 4.2 %collective-permute-start.12 = (f32[72,512]{1,0:T(8,128)S(1)}, f32[72,512]{1,0:T(8,128)S(1)}, u32[]{:S(2)}, u32[]{:S(2)}) collective-permute-start(f32[72,512]{1,0:T(8,128)S(1)} %get-tuple-element.57), channel_id=1, source_target_pairs={{0,1},{1,0},{2,3},{3,2},{4,5},{5,4},{6,7},{7,6},{8,9},{9,8},{10,11... | collective-permute-start | bytes 442376 | tf_op jit(solution)/shard_map/ppermute | solution.py:289
  47.1 0.1 collective-permute-start.16
  47.2 2.4 %collective-permute-start.20 = (f32[72,512]{1,0:T(8,128)S(1)}, f32[72,512]{1,0:T(8,128)S(1)}, u32[]{:S(2)}, u32[]{:S(2)}) collective-permute-start(f32[72,512]{1,0:T(8,128)S(1)} %get-tuple-element.59), channel_id=1, source_target_pairs={{0,3},{1,2},{2,1},{3,0},{4,7},{5,6},{6,5},{7,4},{8,11},{9,10},{10,... | collective-permute-start | bytes 442376 | tf_op jit(solution)/shard_map/ppermute | solution.py:289
  49.5 0.5 collective-permute-start.9
  50.1 3.3 %collective-permute-done.12 = f32[72,512]{1,0:T(8,128)S(1)} collective-permute-done((f32[72,512]{1,0:T(8,128)S(1)}, f32[72,512]{1,0:T(8,128)S(1)}, u32[]{:S(2)}, u32[]{:S(2)}) %collective-permute-start.12) | collective-permute-done | bytes 147488 | tf_op jit(solution)/shard_map/ppermute | solution.py:289
  53.4 1.5 %collective-permute-start.13 = (f32[1,72,512]{2,1,0:T(8,128)S(1)}, f32[1,72,512]{2,1,0:T(8,128)S(1)}, u32[]{:S(2)}, u32[]{:S(2)}) collective-permute-start(f32[1,72,512]{2,1,0:T(8,128)S(1)} %bitcast.22), channel_id=1, source_target_pairs={{0,16},{4,20},{8,24},{12,28},{16,0},{20,4},{24,8},{28,12},{1,17},{... | collective-permute-start | bytes 442376 | tf_op jit(solution)/shard_map/ppermute | solution.py:289
  54.9 3.5 %collective-permute-done.16 = f32[72,512]{1,0:T(8,128)S(1)} collective-permute-done((f32[72,512]{1,0:T(8,128)S(1)}, f32[72,512]{1,0:T(8,128)S(1)}, u32[]{:S(2)}, u32[]{:S(2)}) %collective-permute-start.16) | collective-permute-done | bytes 147488 | tf_op jit(solution)/shard_map/ppermute | solution.py:289
  58.4 0.6 collective-permute-start.17
  58.9 0.0 collective-permute-done.20
  59.0 1.5 %collective-permute-start.21 = (f32[1,72,512]{2,1,0:T(8,128)S(1)}, f32[1,72,512]{2,1,0:T(8,128)S(1)}, u32[]{:S(2)}, u32[]{:S(2)}) collective-permute-start(f32[1,72,512]{2,1,0:T(8,128)S(1)} %bitcast.30), channel_id=1, source_target_pairs={{0,16},{4,20},{8,24},{12,28},{16,0},{20,4},{24,8},{28,12},{1,17},{... | collective-permute-start | bytes 442376 | tf_op jit(solution)/shard_map/ppermute | solution.py:289
  60.5 0.0 collective-permute-done.9.refs_1_
  60.5 0.6 collective-permute-start.10
  61.1 0.0 collective-permute-done.13.refs_5_
  61.1 1.5 %collective-permute-start.14 = (f32[2,72,512]{2,1,0:T(8,128)S(1)}, f32[2,72,512]{2,1,0:T(8,128)S(1)}, u32[]{:S(2)}, u32[]{:S(2)}) collective-permute-start(f32[2,72,512]{2,1,0:T(8,128)S(1)} %pad_maximum_fusion.6), channel_id=1, source_target_pairs={{0,8},{4,12},{8,0},{12,4},{16,24},{20,28},{24,16},{28,20},{1,9},{5... | collective-permute-start | bytes 884744 | tf_op jit(solution)/shard_map/ppermute | solution.py:289
  62.6 2.4 %collective-permute-done.17.refs_9_ = f32[1,72,512]{2,1,0:T(8,128)S(1)} collective-permute-done((f32[1,72,512]{2,1,0:T(8,128)S(1)}, f32[1,72,512]{2,1,0:T(8,128)S(1)}, u32[]{:S(2)}, u32[]{:S(2)}) %collective-permute-start.17) | collective-permute-done | bytes 147488 | tf_op jit(solution)/shard_map/ppermute | solution.py:289
  65.1 1.6 %collective-permute-start.18 = (f32[2,72,512]{2,1,0:T(8,128)S(1)}, f32[2,72,512]{2,1,0:T(8,128)S(1)}, u32[]{:S(2)}, u32[]{:S(2)}) collective-permute-start(f32[2,72,512]{2,1,0:T(8,128)S(1)} %pad_maximum_fusion.7), channel_id=1, source_target_pairs={{0,16},{4,20},{8,24},{12,28},{16,0},{20,4},{24,8},{28,12},{1,17},{... | collective-permute-start | bytes 884744 | tf_op jit(solution)/shard_map/ppermute | solution.py:289
  66.6 0.0 collective-permute-done.21.refs_13_
  66.7 0.6 collective-permute-start.22
  67.3 4.8 %collective-permute-done.10.refs_2_ = f32[2,72,512]{2,1,0:T(8,128)S(1)} collective-permute-done((f32[2,72,512]{2,1,0:T(8,128)S(1)}, f32[2,72,512]{2,1,0:T(8,128)S(1)}, u32[]{:S(2)}, u32[]{:S(2)}) %collective-permute-start.10) | collective-permute-done | bytes 294944 | tf_op jit(solution)/shard_map/ppermute | solution.py:289
  72.1 0.1 collective-permute-start.11
  72.2 0.0 collective-permute-done.14.refs_6_
  72.2 0.6 collective-permute-start.15
  72.8 2.9 %collective-permute-done.18.refs_10_ = f32[2,72,512]{2,1,0:T(8,128)S(1)} collective-permute-done((f32[2,72,512]{2,1,0:T(8,128)S(1)}, f32[2,72,512]{2,1,0:T(8,128)S(1)}, u32[]{:S(2)}, u32[]{:S(2)}) %collective-permute-start.18) | collective-permute-done | bytes 294944 | tf_op jit(solution)/shard_map/ppermute | solution.py:289
  75.7 0.0 copy-start.2
  75.7 0.0 copy-start.3
  75.7 0.0 copy-start.4
  75.8 0.1 collective-permute-start.19
  75.8 0.0 collective-permute-done.22.refs_14_
  75.9 0.5 collective-permute-start.23
  76.4 0.0 collective-permute-done.11.refs_3_
  76.5 1.4 %collective-permute-done.19.refs_11_ = f32[4,72,512]{2,1,0:T(8,128)S(1)} collective-permute-done((f32[4,72,512]{2,1,0:T(8,128)S(1)}, f32[4,72,512]{2,1,0:T(8,128)S(1)}, u32[]{:S(2)}, u32[]{:S(2)}) %collective-permute-start.19) | collective-permute-done | bytes 589856 | tf_op jit(solution)/shard_map/ppermute | solution.py:289
  77.8 0.8 %collective-permute-done.23.refs_15_ = f32[4,72,512]{2,1,0:T(8,128)S(1)} collective-permute-done((f32[4,72,512]{2,1,0:T(8,128)S(1)}, f32[4,72,512]{2,1,0:T(8,128)S(1)}, u32[]{:S(2)}, u32[]{:S(2)}) %collective-permute-start.23) | collective-permute-done | bytes 589856 | tf_op jit(solution)/shard_map/ppermute | solution.py:289
  78.7 4.5 %shard_map.80 = (f32[64,2048]{1,0:T(8,128)}, f32[8,64,256]{2,1,0:T(8,128)}) custom-call(s32[2]{0:T(128)S(1)} %pad_add_fusion.place, s32[8]{0:T(128)S(1)} %copy-done.2, s32[8]{0:T(128)S(1)} %copy-done.3, s32[8]{0:T(128)S(1)} %copy-done.4, f32[1,72,512]{2,1,0:T(8,128)S(1)} %bitcast.21, f32[1,72,512]{2,1,0:T(8,128)S(1)} %collective-permute-done.9.refs_1_, ...), custom_call_target="tpu_custom_call" | custom-call | flops 16777216 | bytes 8388608 | tf_op jit(solution)/shard_map/pallas_call | solution.py:396
  (19 shorter events, 0.3 us)
Async XLA Ops:
  0.7 1.0 %copy-start = (f32[1,64,2048]{2,1,0:T(8,128)S(1)}, f32[1,64,2048]{2,1,0:T(8,128)}, u32[]{:S(2)}) copy-start(f32[1,64,2048]{2,1,0:T(8,128)} %param.6) | copy-start | bytes 1572868
  1.8 1.0 %copy-start.1 = (f32[64,2048]{1,0:T(8,128)S(1)}, f32[64,2048]{1,0:T(8,128)}, u32[]{:S(2)}) copy-start(f32[64,2048]{1,0:T(8,128)} %weight.1) | copy-start | bytes 1572868
  3.5 5.7 %collective-permute-start.3 = (f32[8,1024]{1,0:T(8,128)S(1)}, f32[8,1024]{1,0:T(8,128)S(1)}, u32[]{:S(2)}, u32[]{:S(2)}) collective-permute-start(f32[8,1024]{1,0:T(8,128)S(1)} %get-tuple-element.37), channel_id=1, source_target_pairs={{0,1},{1,0},{2,3},{3,2},{4,5},{5,4},{6,7},{7,6},{8,9},{9,8},{10,11... | collective-permute-start | bytes 98312 | tf_op jit(solution)/shard_map/ppermute | solution.py:289
  6.6 5.4 %collective-permute-start.4 = (f32[8,1024]{1,0:T(8,128)S(1)}, f32[8,1024]{1,0:T(8,128)S(1)}, u32[]{:S(2)}, u32[]{:S(2)}) collective-permute-start(f32[8,1024]{1,0:T(8,128)S(1)} %get-tuple-element.38), channel_id=1, source_target_pairs={{0,2},{1,3},{2,0},{3,1},{4,6},{5,7},{6,4},{7,5},{8,10},{9,11},{10,... | collective-permute-start | bytes 98312 | tf_op jit(solution)/shard_map/ppermute | solution.py:289
  9.2 5.7 %collective-permute-start.5 = (f32[8,1024]{1,0:T(8,128)S(1)}, f32[8,1024]{1,0:T(8,128)S(1)}, u32[]{:S(2)}, u32[]{:S(2)}) collective-permute-start(f32[8,1024]{1,0:T(8,128)S(1)} %get-tuple-element.39), channel_id=1, source_target_pairs={{0,3},{1,2},{2,1},{3,0},{4,7},{5,6},{6,5},{7,4},{8,11},{9,10},{10,... | collective-permute-start | bytes 98312 | tf_op jit(solution)/shard_map/ppermute | solution.py:289
  14.9 6.7 %collective-permute-start.6 = (f32[1,4,8,1024]{3,2,1,0:T(8,128)S(1)}, f32[1,4,8,1024]{3,2,1,0:T(8,128)S(1)}, u32[]{:S(2)}, u32[]{:S(2)}) collective-permute-start(f32[1,4,8,1024]{3,2,1,0:T(8,128)S(1)} %maximum_bitcast_fusion.refs_4_), channel_id=1, source_target_pairs={{0,8},{4,12},{8,0},{12,4},{16,24},{20,28},{24,16},{28,20},{1,9},{5... | collective-permute-start | bytes 393224 | tf_op jit(solution)/shard_map/ppermute | solution.py:289
  16.5 15.9 %collective-permute-start = (f32[64,1024]{1,0:T(8,128)S(1)}, f32[64,1024]{1,0:T(8,128)S(1)}, u32[]{:S(2)}, u32[]{:S(2)}) collective-permute-start(f32[64,1024]{1,0:T(8,128)S(1)} %get-tuple-element.33), channel_id=1, source_target_pairs={{0,1},{1,0},{2,3},{3,2},{4,5},{5,4},{6,7},{7,6},{8,9},{9,8},{10,11... | collective-permute-start | bytes 786440 | tf_op jit(solution)/shard_map/ppermute | solution.py:289
  16.5 4.4 %copy-start.5 = (f32[65]{0:T(128)S(1)}, f32[65]{0:T(128)}, u32[]{:S(2)}) copy-start(f32[65]{0:T(128)} %param.8) | copy-start | bytes 784
  16.5 20.4 %collective-permute-start.1 = (f32[64,1024]{1,0:T(8,128)S(1)}, f32[64,1024]{1,0:T(8,128)S(1)}, u32[]{:S(2)}, u32[]{:S(2)}) collective-permute-start(f32[64,1024]{1,0:T(8,128)S(1)} %get-tuple-element.34), channel_id=1, source_target_pairs={{0,2},{1,3},{2,0},{3,1},{4,6},{5,7},{6,4},{7,5},{8,10},{9,11},{10,... | collective-permute-start | bytes 786440 | tf_op jit(solution)/shard_map/ppermute | solution.py:289
  17.4 19.5 %collective-permute-start.2 = (f32[64,1024]{1,0:T(8,128)S(1)}, f32[64,1024]{1,0:T(8,128)S(1)}, u32[]{:S(2)}, u32[]{:S(2)}) collective-permute-start(f32[64,1024]{1,0:T(8,128)S(1)} %get-tuple-element.35), channel_id=1, source_target_pairs={{0,3},{1,2},{2,1},{3,0},{4,7},{5,6},{6,5},{7,4},{8,11},{9,10},{10,... | collective-permute-start | bytes 786440 | tf_op jit(solution)/shard_map/ppermute | solution.py:289
  21.6 6.4 %collective-permute-start.7 = (f32[2,4,8,1024]{3,2,1,0:T(8,128)S(1)}, f32[2,4,8,1024]{3,2,1,0:T(8,128)S(1)}, u32[]{:S(2)}, u32[]{:S(2)}) collective-permute-start(f32[2,4,8,1024]{3,2,1,0:T(8,128)S(1)} %pad_maximum_fusion.9), channel_id=1, source_target_pairs={{0,16},{4,20},{8,24},{12,28},{16,0},{20,4},{24,8},{28,12},{1,17},{... | collective-permute-start | bytes 786440 | tf_op jit(solution)/shard_map/ppermute | solution.py:289
  28.1 8.8 %collective-permute-start.8 = (f32[4,4,8,1024]{3,2,1,0:T(8,128)S(1)}, f32[4,4,8,1024]{3,2,1,0:T(8,128)S(1)}, u32[]{:S(2)}, u32[]{:S(2)}) collective-permute-start(f32[4,4,8,1024]{3,2,1,0:T(8,128)S(1)} %pad_maximum_fusion.4), channel_id=1, source_target_pairs={{0,4},{4,0},{8,12},{12,8},{16,20},{20,16},{24,28},{28,24},{1,5},{5... | collective-permute-start | bytes 1572872 | tf_op jit(solution)/shard_map/ppermute | solution.py:289
  43.0 10.4 %collective-permute-start.12 = (f32[72,512]{1,0:T(8,128)S(1)}, f32[72,512]{1,0:T(8,128)S(1)}, u32[]{:S(2)}, u32[]{:S(2)}) collective-permute-start(f32[72,512]{1,0:T(8,128)S(1)} %get-tuple-element.57), channel_id=1, source_target_pairs={{0,1},{1,0},{2,3},{3,2},{4,5},{5,4},{6,7},{7,6},{8,9},{9,8},{10,11... | collective-permute-start | bytes 442376 | tf_op jit(solution)/shard_map/ppermute | solution.py:289
  47.1 11.3 %collective-permute-start.16 = (f32[72,512]{1,0:T(8,128)S(1)}, f32[72,512]{1,0:T(8,128)S(1)}, u32[]{:S(2)}, u32[]{:S(2)}) collective-permute-start(f32[72,512]{1,0:T(8,128)S(1)} %get-tuple-element.58), channel_id=1, source_target_pairs={{0,2},{1,3},{2,0},{3,1},{4,6},{5,7},{6,4},{7,5},{8,10},{9,11},{10,... | collective-permute-start | bytes 442376 | tf_op jit(solution)/shard_map/ppermute | solution.py:289
  47.2 11.8 %collective-permute-start.20 = (f32[72,512]{1,0:T(8,128)S(1)}, f32[72,512]{1,0:T(8,128)S(1)}, u32[]{:S(2)}, u32[]{:S(2)}) collective-permute-start(f32[72,512]{1,0:T(8,128)S(1)} %get-tuple-element.59), channel_id=1, source_target_pairs={{0,3},{1,2},{2,1},{3,0},{4,7},{5,6},{6,5},{7,4},{8,11},{9,10},{10,... | collective-permute-start | bytes 442376 | tf_op jit(solution)/shard_map/ppermute | solution.py:289
  49.5 10.9 %collective-permute-start.9 = (f32[1,72,512]{2,1,0:T(8,128)S(1)}, f32[1,72,512]{2,1,0:T(8,128)S(1)}, u32[]{:S(2)}, u32[]{:S(2)}) collective-permute-start(f32[1,72,512]{2,1,0:T(8,128)S(1)} %bitcast.18), channel_id=1, source_target_pairs={{0,8},{4,12},{8,0},{12,4},{16,24},{20,28},{24,16},{28,20},{1,9},{5... | collective-permute-start | bytes 442376 | tf_op jit(solution)/shard_map/ppermute | solution.py:289
  53.4 7.7 %collective-permute-start.13 = (f32[1,72,512]{2,1,0:T(8,128)S(1)}, f32[1,72,512]{2,1,0:T(8,128)S(1)}, u32[]{:S(2)}, u32[]{:S(2)}) collective-permute-start(f32[1,72,512]{2,1,0:T(8,128)S(1)} %bitcast.22), channel_id=1, source_target_pairs={{0,16},{4,20},{8,24},{12,28},{16,0},{20,4},{24,8},{28,12},{1,17},{... | collective-permute-start | bytes 442376 | tf_op jit(solution)/shard_map/ppermute | solution.py:289
  58.4 6.6 %collective-permute-start.17 = (f32[1,72,512]{2,1,0:T(8,128)S(1)}, f32[1,72,512]{2,1,0:T(8,128)S(1)}, u32[]{:S(2)}, u32[]{:S(2)}) collective-permute-start(f32[1,72,512]{2,1,0:T(8,128)S(1)} %bitcast.26), channel_id=1, source_target_pairs={{0,8},{4,12},{8,0},{12,4},{16,24},{20,28},{24,16},{28,20},{1,9},{5... | collective-permute-start | bytes 442376 | tf_op jit(solution)/shard_map/ppermute | solution.py:289
  59.0 7.7 %collective-permute-start.21 = (f32[1,72,512]{2,1,0:T(8,128)S(1)}, f32[1,72,512]{2,1,0:T(8,128)S(1)}, u32[]{:S(2)}, u32[]{:S(2)}) collective-permute-start(f32[1,72,512]{2,1,0:T(8,128)S(1)} %bitcast.30), channel_id=1, source_target_pairs={{0,16},{4,20},{8,24},{12,28},{16,0},{20,4},{24,8},{28,12},{1,17},{... | collective-permute-start | bytes 442376 | tf_op jit(solution)/shard_map/ppermute | solution.py:289
  60.5 11.6 %collective-permute-start.10 = (f32[2,72,512]{2,1,0:T(8,128)S(1)}, f32[2,72,512]{2,1,0:T(8,128)S(1)}, u32[]{:S(2)}, u32[]{:S(2)}) collective-permute-start(f32[2,72,512]{2,1,0:T(8,128)S(1)} %pad_maximum_fusion.5), channel_id=1, source_target_pairs={{0,16},{4,20},{8,24},{12,28},{16,0},{20,4},{24,8},{28,12},{1,17},{... | collective-permute-start | bytes 884744 | tf_op jit(solution)/shard_map/ppermute | solution.py:289
  61.1 11.1 %collective-permute-start.14 = (f32[2,72,512]{2,1,0:T(8,128)S(1)}, f32[2,72,512]{2,1,0:T(8,128)S(1)}, u32[]{:S(2)}, u32[]{:S(2)}) collective-permute-start(f32[2,72,512]{2,1,0:T(8,128)S(1)} %pad_maximum_fusion.6), channel_id=1, source_target_pairs={{0,8},{4,12},{8,0},{12,4},{16,24},{20,28},{24,16},{28,20},{1,9},{5... | collective-permute-start | bytes 884744 | tf_op jit(solution)/shard_map/ppermute | solution.py:289
  65.1 10.6 %collective-permute-start.18 = (f32[2,72,512]{2,1,0:T(8,128)S(1)}, f32[2,72,512]{2,1,0:T(8,128)S(1)}, u32[]{:S(2)}, u32[]{:S(2)}) collective-permute-start(f32[2,72,512]{2,1,0:T(8,128)S(1)} %pad_maximum_fusion.7), channel_id=1, source_target_pairs={{0,16},{4,20},{8,24},{12,28},{16,0},{20,4},{24,8},{28,12},{1,17},{... | collective-permute-start | bytes 884744 | tf_op jit(solution)/shard_map/ppermute | solution.py:289
  66.7 9.2 %collective-permute-start.22 = (f32[2,72,512]{2,1,0:T(8,128)S(1)}, f32[2,72,512]{2,1,0:T(8,128)S(1)}, u32[]{:S(2)}, u32[]{:S(2)}) collective-permute-start(f32[2,72,512]{2,1,0:T(8,128)S(1)} %pad_maximum_fusion.8), channel_id=1, source_target_pairs={{0,8},{4,12},{8,0},{12,4},{16,24},{20,28},{24,16},{28,20},{1,9},{5... | collective-permute-start | bytes 884744 | tf_op jit(solution)/shard_map/ppermute | solution.py:289
  72.1 4.4 %collective-permute-start.11 = (f32[4,72,512]{2,1,0:T(8,128)S(1)}, f32[4,72,512]{2,1,0:T(8,128)S(1)}, u32[]{:S(2)}, u32[]{:S(2)}) collective-permute-start(f32[4,72,512]{2,1,0:T(8,128)S(1)} %pad_maximum_fusion), channel_id=1, source_target_pairs={{0,4},{4,0},{8,12},{12,8},{16,20},{20,16},{24,28},{28,24},{1,5},{5... | collective-permute-start | bytes 1769480 | tf_op jit(solution)/shard_map/ppermute | solution.py:289
  72.2 4.2 %collective-permute-start.15 = (f32[4,72,512]{2,1,0:T(8,128)S(1)}, f32[4,72,512]{2,1,0:T(8,128)S(1)}, u32[]{:S(2)}, u32[]{:S(2)}) collective-permute-start(f32[4,72,512]{2,1,0:T(8,128)S(1)} %pad_maximum_fusion.1), channel_id=1, source_target_pairs={{0,4},{4,0},{8,12},{12,8},{16,20},{20,16},{24,28},{28,24},{1,5},{5... | collective-permute-start | bytes 1769480 | tf_op jit(solution)/shard_map/ppermute | solution.py:289
  75.7 3.0 %copy-start.2 = (s32[8]{0:T(128)S(1)}, s32[8]{0:T(128)}, u32[]{:S(2)}) copy-start(s32[8]{0:T(128)} %pair_one.1) | copy-start | bytes 100
  75.7 2.9 %copy-start.3 = (s32[8]{0:T(128)S(1)}, s32[8]{0:T(128)}, u32[]{:S(2)}) copy-start(s32[8]{0:T(128)} %pair_two.1) | copy-start | bytes 100
  75.7 2.9 %copy-start.4 = (s32[8]{0:T(128)S(1)}, s32[8]{0:T(128)}, u32[]{:S(2)}) copy-start(s32[8]{0:T(128)} %owner.1) | copy-start | bytes 100
  75.8 2.1 %collective-permute-start.19 = (f32[4,72,512]{2,1,0:T(8,128)S(1)}, f32[4,72,512]{2,1,0:T(8,128)S(1)}, u32[]{:S(2)}, u32[]{:S(2)}) collective-permute-start(f32[4,72,512]{2,1,0:T(8,128)S(1)} %pad_maximum_fusion.2), channel_id=1, source_target_pairs={{0,4},{4,0},{8,12},{12,8},{16,20},{20,16},{24,28},{28,24},{1,5},{5... | collective-permute-start | bytes 1769480 | tf_op jit(solution)/shard_map/ppermute | solution.py:289
  75.9 2.8 %collective-permute-start.23 = (f32[4,72,512]{2,1,0:T(8,128)S(1)}, f32[4,72,512]{2,1,0:T(8,128)S(1)}, u32[]{:S(2)}, u32[]{:S(2)}) collective-permute-start(f32[4,72,512]{2,1,0:T(8,128)S(1)} %pad_maximum_fusion.3), channel_id=1, source_target_pairs={{0,4},{4,0},{8,12},{12,8},{16,20},{20,16},{24,28},{28,24},{1,5},{5... | collective-permute-start | bytes 1769480 | tf_op jit(solution)/shard_map/ppermute | solution.py:289
where the time goes:
time: 84.3 us; the launch traced here: 83.4 us
  waiting for transfers between devices  33.4 us (40%)
  starting transfers between devices  29.6 us (35%)
  Pallas kernels  15.3 us (18%)
  local copies, waits for them, and re-layouts  2.35 us (3%)
  other arithmetic  1.79 us (2%)
  between operations  0.97 us (1%)
    ppermute x24, waiting for transfers between devices, exchange(): return lax.ppermute(value, axis, [(i, i ^ offset) for i in range(count)])  33.4 us
    ppermute x24, starting transfers between devices, exchange(): return lax.ppermute(value, axis, [(i, i ^ offset) for i in range(count)])  29.6 us
    pallas_call x1, Pallas kernels, body(): call(functools.partial(filter_kernel, plan, sharers), [f32(plan.slab, pla...  6 us
    pallas_call x1, Pallas kernels, body(): call(functools.partial(estimate_kernel, plan, holders, fused), outs, [sme...  4.52 us
    pallas_call x1, Pallas kernels, body(): call(functools.partial(table_kernel, plan), [b16(*shape) for shape in sha...  4.02 us
    unnamed x12, local copies, waits for them, and re-layouts  2.11 us
  transfers between devices with their start and end apart: 24, of which 11 were waited for; matrix products, arithmetic and copies ran while one was open for 2% of the time, Pallas kernels for 5%

commit v1 on v0

--- a/solution.py
+++ b/solution.py
@@ -15,8 +15,9 @@
 exact = lax.Precision.HIGHEST
 lane = 128
 wide = 256
+stretch = 1024
 rim = 4
-vmem_bytes = 48 * 1024 * 1024
+loads = 4
 
 
 def split(value):
@@ -62,20 +63,35 @@
 
 def weighted_kernel(plan, place, maps, weight, *refs):
     count = plan.row_devices
-    pieces, parts, padded = refs[:count], refs[count : 2 * count], refs[2 * count]
+    pieces, parts = refs[:count], refs[count : 2 * count]
+    padded, weights, given, sems = refs[2 * count :]
+    chunk = plan.row_local // loads
+    copies = []
+    for number in range(loads):
+        rows = pl.ds(number * chunk, chunk)
+        inner = pl.ds(plan.halo, plan.columns)
+        copies.append((
+            pltpu.make_async_copy(weight.at[rows], weights.at[rows, inner], sems.at[0, number]),
+            pltpu.make_async_copy(maps.at[rows], given.at[rows], sems.at[1, number]),
+        ))
+        for copy in copies[-1]:
+            copy.start()
     zeros = jnp.zeros((plan.row_local, plan.halo), jnp.float32)
+    for target in (padded, weights):
+        target[:, : plan.halo] = zeros
+        target[:, plan.halo + plan.columns :] = zeros
     inner = slice(plan.halo, plan.halo + plan.columns)
-    padded[:, : plan.halo] = zeros
-    padded[:, plan.halo + plan.columns :] = zeros
-    padded[:, inner] = weight[...]
+    starts = [pl.multiple_of((place[0] ^ step) * plan.share, lane) for step in range(count)]
+    for number in range(loads):
+        for copy in copies[number]:
+            copy.wait()
+        rows = slice(number * chunk, (number + 1) * chunk)
+        padded[rows, inner] = weights[rows, inner] * given[rows]
+        for step, column in enumerate(starts):
+            pieces[step][rows] = padded[rows, pl.ds(column, plan.width)]
     row = pl.multiple_of(lax.rem(place[1], plan.sharers) * plan.share_rows, plan.share_rows)
-    for step in range(count):
-        column = pl.multiple_of((place[0] ^ step) * plan.share, lane)
-        parts[step][...] = padded[pl.ds(row, plan.share_rows), pl.ds(column, plan.width)]
-    padded[:, inner] = weight[...] * maps[...]
-    for step in range(count):
-        column = pl.multiple_of((place[0] ^ step) * plan.share, lane)
-        pieces[step][...] = padded[:, pl.ds(column, plan.width)]
+    for step, column in enumerate(starts):
+        parts[step][...] = weights[pl.ds(row, plan.share_rows), pl.ds(column, plan.width)]
 
 
 def band(plan, taps, rows, columns, offset):
@@ -131,11 +147,22 @@
 
     pieces = take(plan.row_devices)
     parts = take(len(sharers))
-    square, final = take(2), take(2)
-    bands = [take(2) for _ in plan.blocks]
-    last = take(2)
+    sources = take(2 * (len(plan.blocks) + 3))
     outs = take(plan.row_devices)
-    seen, weight, image, total, field, high, low, mid_high, mid_low = refs
+    seen, weight, image, total, field, high, low, mid_high, mid_low, sem, sems = refs[:11]
+    tables = refs[11:]
+    copies = [pltpu.make_async_copy(a, b, sems.at[i]) for i, (a, b) in enumerate(zip(sources, tables))]
+    for copy in copies:
+        copy.start()
+    groups = [(tables[i], tables[i + 1]) for i in range(0, len(tables), 2)]
+    square, final, bands, last = groups[0], groups[1], groups[2:-1], groups[-1]
+    for part, owners in zip(parts, sharers):
+        for slot, offset in enumerate(owners):
+            for step in range(plan.row_devices):
+                row = (place[0] ^ step) * plan.row_local
+                row = row + (lax.rem(place[1], plan.sharers) ^ offset) * plan.share_rows
+                rows = pl.ds(pl.multiple_of(row, plan.share_rows), plan.share_rows)
+                pltpu.make_async_copy(part.at[slot, step], weight.at[rows], sem).start()
     for step, piece in enumerate(pieces):
         row = pl.multiple_of((place[0] ^ step) * plan.row_local, plan.row_local)
         value = piece[...]
@@ -143,13 +170,6 @@
         a, b = split(value)
         high[pl.ds(row, plan.row_local), :] = a
         low[pl.ds(row, plan.row_local), :] = b
-    for part, owners in zip(parts, sharers):
-        for slot, offset in enumerate(owners):
-            for step in range(plan.row_devices):
-                row = (place[0] ^ step) * plan.row_local
-                row = row + (lax.rem(place[1], plan.sharers) ^ offset) * plan.share_rows
-                row = pl.multiple_of(row, plan.share_rows)
-                weight[pl.ds(row, plan.share_rows), :] = part[slot, step]
 
     def rows_pass(table, start, stop):
         count = table[0].shape[0]
@@ -166,7 +186,14 @@
     for iteration in range(ITERS):
         chosen = plan.stage_blocks(iteration)
         windows = [plan.window(plan.blocks[i]) for i in chosen]
+        if iteration == 0:
+            copies[0].wait()
+            copies[1].wait()
         rows_pass(square, windows[0][0], windows[-1][1])
+        if iteration == 0:
+            for copy in copies[2:]:
+                copy.wait()
+            pltpu.make_async_copy(weight, weight, sem).wait()
         for i, window in zip(chosen, windows):
             a, b = plan.blocks[i]
             value = columns_pass(bands[i], plan.rows, window)
@@ -218,23 +245,10 @@
         pieces.append(sorted(flat, key=lambda entry: entry[0]))
     estimate = refs.pop(0)
     mean_field = refs.pop(0) if field_width else None
-    own, first, second = refs[:3]
-    sems = refs[3]
+    own, partner, sems = refs[:3]
     rows_at, sim_at = place[0], place[1]
-    edge = jnp.zeros((plan.slab, lane), jnp.float32)
-    offset_one, offset_two = sim_at ^ pair_one[sim_at], sim_at ^ pair_two[sim_at]
-    for step in range(plan.row_devices):
-        column = pl.multiple_of(lane + (rows_at ^ step) * plan.share, lane)
-        for offset, source in pieces[step]:
-            def fetch(target, sem, source=source, column=column):
-                pltpu.make_async_copy(source, target.at[:, pl.ds(column, plan.share)], sems.at[sem]).start()
-
-            if offset == 0:
-                fetch(own, 0)
-            pl.when(offset == offset_one)(functools.partial(fetch, first, 1))
-            pl.when(offset == offset_two)(functools.partial(fetch, second, 2))
     if field_width:
-        every = refs[4]
+        every = refs[3]
         units = field_width // lane
         per = plan.share // lane
         for unit in range(units + 2):
@@ -246,7 +260,7 @@
                     column = pl.multiple_of(lax.rem(at, per) * lane, lane)
                     for offset, source in pieces[step]:
                         pltpu.make_async_copy(
-                            source.at[:, pl.ds(column, lane)], every.at[sim_at ^ offset, :, span], sems.at[3 + unit]
+                            source.at[:, pl.ds(column, lane)], every.at[sim_at ^ offset, :, span], sems.at[unit]
                         ).start()
 
                 pl.when(inside & (lax.div(at, per) == (rows_at ^ step)))(fetch_all)
@@ -255,14 +269,26 @@
             def _(span=span):
                 every[:, :, span] = jnp.zeros((plan.sim_devices, plan.slab, lane), jnp.float32)
 
-    for number, target in enumerate((own, first, second)):
+    edge = jnp.zeros((plan.slab, lane), jnp.float32)
+    for target in (own, partner):
         target[:, :lane] = edge
         target[:, lane + plan.columns :] = edge
-        span = target.at[:, pl.ds(lane, plan.columns)]
-        pltpu.make_async_copy(span, span, sems.at[number]).wait()
-    for a in range(0, plan.columns, wide):
-        span = slice(a, a + wide + 2 * lane)
-        estimate[:, a : a + wide] = divergence(own[:, span], 2.0 * first[:, span] - second[:, span])
+    one, two = sim_at ^ pair_one[sim_at], sim_at ^ pair_two[sim_at]
+
+    def factor(offset):
+        return jnp.where(one == offset, 2.0, 0.0) - jnp.where(two == offset, 1.0, 0.0)
+
+    for step in range(plan.row_devices):
+        column = pl.multiple_of(lane + (rows_at ^ step) * plan.share, lane)
+        own[:, pl.ds(column, plan.share)] = pieces[step][0][1][...]
+        mixed = factor(0) * pieces[step][0][1][...]
+        for offset, source in pieces[step][1:]:
+            mixed = mixed + factor(offset) * source[...]
+        partner[:, pl.ds(column, plan.share)] = mixed
+    for a in range(0, plan.columns, stretch):
+        b = min(a + stretch, plan.columns)
+        span = slice(a, b + 2 * lane)
+        estimate[:, a:b] = divergence(own[:, span], partner[:, span])
     if not field_width:
         return
     for unit in range(units + 2):
@@ -271,7 +297,7 @@
         @pl.when((at >= 0) & (at < plan.columns // lane))
         def _(unit=unit):
             span = every.at[:, :, unit * lane : (unit + 1) * lane]
-            pltpu.make_async_copy(span, span, sems.at[3 + unit]).wait()
+            pltpu.make_async_copy(span, span, sems.at[unit]).wait()
 
     mean_field[...] = jnp.zeros(mean_field.shape, jnp.float32)
     for sim in range(plan.sim_devices):
@@ -298,15 +324,15 @@
     return arrays, offsets
 
 
-def call(kernel, out_shapes, in_specs, scratch, flops, moved, out_specs=None):
+def call(kernel, out_shapes, in_specs, scratch, flops, moved, limit=48):
     vmem = pl.BlockSpec(memory_space=pltpu.VMEM)
     return pl.pallas_call(
         kernel,
         out_shape=out_shapes,
         in_specs=in_specs,
-        out_specs=[vmem] * len(out_shapes) if out_specs is None else out_specs,
+        out_specs=[vmem] * len(out_shapes),
         scratch_shapes=scratch,
-        compiler_params=pltpu.CompilerParams(vmem_limit_bytes=vmem_bytes),
+        compiler_params=pltpu.CompilerParams(vmem_limit_bytes=limit * 1024 * 1024),
         cost_estimate=pl.CostEstimate(flops=flops, bytes_accessed=moved, transcendentals=0),
     )
 
@@ -319,7 +345,7 @@
     place = jnp.stack([lax.axis_index("rows"), lax.axis_index("sims")]).astype(jnp.int32)
     vmem = pl.BlockSpec(memory_space=pltpu.VMEM)
     smem = pl.BlockSpec(memory_space=pltpu.SMEM)
-    hbm = pl.BlockSpec(memory_space=pl.ANY)
+    far = pl.BlockSpec(memory_space=pltpu.HBM)
 
     def f32(*shape):
         return jax.ShapeDtypeStruct(shape, jnp.float32)
@@ -331,44 +357,66 @@
     made = call(
         functools.partial(weighted_kernel, plan),
         [f32(row_local, plan.width)] * row_devices + [f32(plan.share_rows, plan.width)] * row_devices,
-        [smem, vmem, vmem],
-        [pltpu.VMEM((row_local, columns + 2 * plan.halo), jnp.float32)],
+        [smem, far, far],
+        [pltpu.VMEM((row_local, columns + 2 * plan.halo), jnp.float32)] * 2
+        + [pltpu.VMEM((row_local, columns), jnp.float32), pltpu.SemaphoreType.DMA((2, loads))],
         cells,
         16 * cells,
+        limit=60,
     )(place, maps.reshape(row_local, columns), weight)
     pieces, parts = made[:row_devices], made[row_devices:]
-    parts = [parts[0]] + [exchange(parts[d], "rows", d) for d in range(1, row_devices)]
     pieces = [pieces[0]] + [exchange(pieces[d], "rows", d) for d in range(1, row_devices)]
-    bits = [1 << i for i in range(1, plan.sharers.bit_length() - 1)] + [1]
-    parts, sharers = gather(jnp.stack(parts), "sims", bits)
-
-    kernel = beam / jnp.sum(beam)
-    blank = jnp.zeros((plan.length - taps,), jnp.float32)
-    forward = jnp.roll(jnp.concatenate([kernel, blank]), -plan.margin)[None]
-    backward = jnp.roll(jnp.concatenate([kernel[::-1], blank]), -plan.margin)[None]
+    sharers = []
     shapes = [(plan.rows, plan.rows), (row_devices * plan.slab, plan.rows)]
     for block in plan.blocks + plan.out_blocks[:1]:
         low, high = plan.window(block)
         shapes.append((high - low, block[1] - block[0]))
-    tables = call(
-        functools.partial(table_kernel, plan),
-        [b16(*shape) for shape in shapes for _ in range(2)],
-        [smem, vmem, vmem],
-        [],
-        1 << 32,
-        1 << 23,
-    )(place, forward, backward)
+
+    def prepare(parts, beam):
+        parts = list(parts)
+        for bit in [1 << i for i in reversed(range(row_devices.bit_length() - 1))]:
+            moved = [step for step in range(row_devices) if step & bit]
+            received = exchange(jnp.stack([parts[step] for step in moved]), "rows", bit)
+            for slot, step in enumerate(moved):
+                parts[step] = received[slot]
+        bits = [1 << i for i in range(1, plan.sharers.bit_length() - 1)] + [1]
+        arrays, offsets = gather(jnp.stack(parts), "sims", bits)
+        sharers[:] = offsets
+        kernel = beam / jnp.sum(beam)
+        blank = jnp.zeros((plan.length - taps,), jnp.float32)
+        forward = jnp.roll(jnp.concatenate([kernel, blank]), -plan.margin)[None]
+        backward = jnp.roll(jnp.concatenate([kernel[::-1], blank]), -plan.margin)[None]
+        tables = call(
+            functools.partial(table_kernel, plan),
+            [b16(*shape) for shape in shapes for _ in range(2)],
+            [smem, vmem, vmem],
+            [],
+            1 << 32,
+            1 << 23,
+        )(place, forward, backward)
+        return arrays, tables
+
+    made = jax.eval_shape(prepare, parts, beam)
+    parts, tables = lax.cond(
+        owner[0] >= 0,
+        prepare,
+        lambda parts, beam: jax.tree.map(lambda x: jnp.zeros(x.shape, x.dtype), made),
+        parts,
+        beam,
+    )
 
     full = (plan.rows, plan.width)
     tall = (max(plan.rows, row_devices * plan.slab), plan.width)
     filtered = call(
         functools.partial(filter_kernel, plan, sharers),
         [f32(plan.slab, plan.share)] * row_devices,
-        [smem] + [vmem] * (len(pieces) + len(parts) + len(tables)),
+        [smem] + [vmem] * len(pieces) + [far] * (len(parts) + len(tables)),
         [pltpu.VMEM(full, jnp.float32)] * 4
         + [pltpu.VMEM((row_devices * plan.slab, plan.share), jnp.float32)]
         + [pltpu.VMEM(full, jnp.bfloat16)] * 2
-        + [pltpu.VMEM(tall, jnp.bfloat16)] * 2,
+        + [pltpu.VMEM(tall, jnp.bfloat16)] * 2
+        + [pltpu.SemaphoreType.DMA, pltpu.SemaphoreType.DMA((2 * len(shapes),))]
+        + [pltpu.VMEM(shape, jnp.bfloat16) for shape in shapes for _ in range(2)],
         1 << 33,
         1 << 23,
     )(place, *pieces, *parts, *tables)
@@ -386,17 +434,17 @@
     fused = field_width if field_width % lane == 0 else 0
     outs = [f32(row_local, columns)]
     extended = (plan.slab, columns + 2 * lane)
-    scratch = [pltpu.VMEM(extended, jnp.float32)] * 3
+    scratch = [pltpu.VMEM(extended, jnp.float32)] * 2
     if fused:
         outs.append(f32(OWNERS, row_local, fused))
-        scratch.append(pltpu.SemaphoreType.DMA((3 + fused // lane + 2,)))
+        scratch.append(pltpu.SemaphoreType.DMA((fused // lane + 2,)))
         scratch.append(pltpu.VMEM((sim_devices, plan.slab, fused + 2 * lane), jnp.float32))
     else:
-        scratch.append(pltpu.SemaphoreType.DMA((3,)))
+        scratch.append(pltpu.SemaphoreType.DMA((1,)))
     results = call(
         functools.partial(estimate_kernel, plan, holders, fused),
         outs,
-        [smem] * 4 + [hbm] * len(held),
+        [smem] * 4 + [vmem] * len(held),
         scratch,
         1 << 24,
         1 << 23,

time: 84.3 us -> 105 us (1.25)
  waiting for transfers between devices: 33.4 us -> 51.6 us
  Pallas kernels: 15.3 us -> 19.7 us
  starting transfers between devices: 29.6 us -> 26.9 us
    ppermute x24 -> x23, waiting for transfers between devices: 33.4 us -> 51.6 us  [exchange(): return lax.ppermute(value, axis, [(i, i ^ offset) for i in range(count)])]
    ppermute x24 -> x23, starting transfers between devices: 29.6 us -> 26.9 us  [exchange(): return lax.ppermute(value, axis, [(i, i ^ offset) for i in range(count)])]
    pallas_call x1, Pallas kernels: 0.73 us -> 2.9 us  [body(): call(functools.partial(weighted_kernel, plan), [f32(row_local, plan.width...]
    pallas_call x1, Pallas kernels: 6 us -> 7.55 us  [body(): call(functools.partial(filter_kernel, plan, sharers), [f32(plan.slab, pla...]
    unnamed x12 -> x10, local copies, waits for them, and re-layouts: 2.11 us -> 1.32 us
  transfers between devices with their start and end apart: 24 -> 23, of which waited for: 11 -> 11; matrix products, arithmetic and copies ran while one was open for 2% -> 2% of each run, Pallas kernels for 5% -> 5%
where the time goes in v1:
time: 105 us; the launch traced here: 104 us
  waiting for transfers between devices  51.6 us (49%)
  starting transfers between devices  26.9 us (26%)
  Pallas kernels  19.7 us (19%)
  other arithmetic  2.31 us (2%)
  local copies, waits for them, and re-layouts  2.24 us (2%)
    ppermute x23, waiting for transfers between devices, exchange(): return lax.ppermute(value, axis, [(i, i ^ offset) for i in range(count)])  51.6 us
    ppermute x23, starting transfers between devices, exchange(): return lax.ppermute(value, axis, [(i, i ^ offset) for i in range(count)])  26.9 us
    pallas_call x1, Pallas kernels, body(): call(functools.partial(filter_kernel, plan, sharers), [f32(plan.slab, pla...  7.55 us
    pallas_call x1, Pallas kernels, prepare(): call(functools.partial(table_kernel, plan), [b16(*shape) for shape in sha...  4.8 us
    pallas_call x1, Pallas kernels, body(): call(functools.partial(estimate_kernel, plan, holders, fused), outs, [sme...  4.44 us
    pallas_call x1, Pallas kernels, body(): call(functools.partial(weighted_kernel, plan), [f32(row_local, plan.width...  2.9 us
  transfers between devices with their start and end apart: 23, of which 11 were waited for; matrix products, arithmetic and copies ran while one was open for 2% of the time, Pallas kernels for 5%

profile of v1, /device:TPU:0, one launch (start us, length us, event | category | flops | bytes accessed | tf_op | source)
XLA Modules:
  0.0 103.8 jit_solution(2955905351772658856)
XLA Ops:
  0.6 0.1 pad_add_fusion.place
  0.7 2.9 %shard_map.78 = (f32[64,1024]{1,0:T(8,128)}, f32[64,1024]{1,0:T(8,128)}, f32[64,1024]{1,0:T(8,128)}, f32[64,1024]{1,0:T(8,128)}, f32[8,1024]{1,0:T(8,128)}, /*in...) custom-call(s32[2]{0:T(128)S(1)} %pad_add_fusion.place, f32[64,2048]{1,0:T(8,128)} %bitcast.39, ...), custom_call_target="tpu_custom_call" | custom-call | flops 131072 | bytes 2097152 | tf_op jit(solution)/shard_map/pallas_call | solution.py:357
  3.6 3.1 %collective-permute-start.5 = (f32[64,1024]{1,0:T(8,128)}, f32[64,1024]{1,0:T(8,128)S(1)}, u32[]{:S(2)}, u32[]{:S(2)}) collective-permute-start(f32[64,1024]{1,0:T(8,128)} %get-tuple-element.71), channel_id=1, source_target_pairs={{0,1},{1,0},{2,3},{3,2},{4,5},{5,4},{6,7},{7,6},{8,9},{9,8},{10,11... | collective-permute-start | bytes 786440 | tf_op jit(solution)/shard_map/ppermute | solution.py:315
  6.7 2.6 %collective-permute-start.6 = (f32[64,1024]{1,0:T(8,128)}, f32[64,1024]{1,0:T(8,128)S(1)}, u32[]{:S(2)}, u32[]{:S(2)}) collective-permute-start(f32[64,1024]{1,0:T(8,128)} %get-tuple-element.72), channel_id=1, source_target_pairs={{0,2},{1,3},{2,0},{3,1},{4,6},{5,7},{6,4},{7,5},{8,10},{9,11},{10,... | collective-permute-start | bytes 786440 | tf_op jit(solution)/shard_map/ppermute | solution.py:315
  9.3 0.0 collective-permute-start.7
  9.3 0.7 copy-done.2
  10.0 0.0 copy-start.11
  10.0 0.6 copy-done.11
  10.7 46.2 %conditional.1 = (f32[1,4,8,1024]{3,2,1,0:T(8,128)S(1)}, f32[1,4,8,1024]{3,2,1,0:T(8,128)S(1)}, f32[2,4,8,1024]{3,2,1,0:T(8,128)S(1)}, f32[4,4,8,1024]{3,2,1,0:T...) conditional(s32[]{:T(128)} %bitcast.10, () %tuple.16, ...), branch_computations={%region_0.0_spmd, %region_1.3_spmd} | conditional | flops 4295427072 | bytes 19282528 | solution.py:400
  10.7 2.0 %collective-permute-start = (f32[2,8,1024]{2,1,0:T(8,128)S(1)}, f32[2,8,1024]{2,1,0:T(8,128)S(1)}, u32[]{:S(2)}, u32[]{:S(2)}) collective-permute-start(f32[2,8,1024]{2,1,0:T(8,128)S(1)} %pad_maximum_fusion.2), channel_id=1, source_target_pairs={{0,2},{1,3},{2,0},{3,1},{4,6},{5,7},{6,4},{7,5},{8,10},{9,11},{10,... | collective-permute-start | bytes 196616 | tf_op jit(solution)/shard_map/cond/branch_1_fun/ppermute | solution.py:315
  12.6 22.6 %collective-permute-done = f32[2,8,1024]{2,1,0:T(8,128)S(1)} collective-permute-done((f32[2,8,1024]{2,1,0:T(8,128)S(1)}, f32[2,8,1024]{2,1,0:T(8,128)S(1)}, u32[]{:S(2)}, u32[]{:S(2)}) %collective-permute-start) | collective-permute-done | bytes 65568 | tf_op jit(solution)/shard_map/cond/branch_1_fun/ppermute | solution.py:315
  35.3 0.1 collective-permute-start.1
  35.4 0.1 reverse.2
  35.5 0.6 reduce_sum.8
  36.1 3.5 %collective-permute-done.1 = f32[2,8,1024]{2,1,0:T(8,128)S(1)} collective-permute-done((f32[2,8,1024]{2,1,0:T(8,128)S(1)}, f32[2,8,1024]{2,1,0:T(8,128)S(1)}, u32[]{:S(2)}, u32[]{:S(2)}) %collective-permute-start.1) | collective-permute-done | bytes 65568 | tf_op jit(solution)/shard_map/cond/branch_1_fun/ppermute | solution.py:315
  39.7 1.6 %collective-permute-start.2 = (f32[1,4,8,1024]{3,2,1,0:T(8,128)S(1)}, f32[1,4,8,1024]{3,2,1,0:T(8,128)S(1)}, u32[]{:S(2)}, u32[]{:S(2)}) collective-permute-start(f32[1,4,8,1024]{3,2,1,0:T(8,128)S(1)} %maximum_bitcast_fusion), channel_id=1, source_target_pairs={{0,8},{4,12},{8,0},{12,4},{16,24},{20,28},{24,16},{28,20},{1,9},{5... | collective-permute-start | bytes 393224 | tf_op jit(solution)/shard_map/cond/branch_1_fun/ppermute | solution.py:315
  41.2 0.6 broadcast_divide_fusion.1
  41.8 2.9 %collective-permute-done.2 = f32[1,4,8,1024]{3,2,1,0:T(8,128)S(1)} collective-permute-done((f32[1,4,8,1024]{3,2,1,0:T(8,128)S(1)}, f32[1,4,8,1024]{3,2,1,0:T(8,128)S(1)}, u32[]{:S(2)}, u32[]{:S(2)}) %collective-permute-start.2) | collective-permute-done | bytes 131104 | tf_op jit(solution)/shard_map/cond/branch_1_fun/ppermute | solution.py:315
  44.7 1.6 %collective-permute-start.3 = (f32[2,4,8,1024]{3,2,1,0:T(8,128)S(1)}, f32[2,4,8,1024]{3,2,1,0:T(8,128)S(1)}, u32[]{:S(2)}, u32[]{:S(2)}) collective-permute-start(f32[2,4,8,1024]{3,2,1,0:T(8,128)S(1)} %pad_maximum_fusion.1), channel_id=1, source_target_pairs={{0,16},{4,20},{8,24},{12,28},{16,0},{20,4},{24,8},{28,12},{1,17},{... | collective-permute-start | bytes 786440 | tf_op jit(solution)/shard_map/cond/branch_1_fun/ppermute | solution.py:315
  46.3 0.6 broadcast_divide_fusion
  46.9 0.1 pad_slice_fusion
  47.0 0.1 pad_slice_fusion.1
  47.1 4.1 %collective-permute-done.3 = f32[2,4,8,1024]{3,2,1,0:T(8,128)S(1)} collective-permute-done((f32[2,4,8,1024]{3,2,1,0:T(8,128)S(1)}, f32[2,4,8,1024]{3,2,1,0:T(8,128)S(1)}, u32[]{:S(2)}, u32[]{:S(2)}) %collective-permute-start.3) | collective-permute-done | bytes 262176 | tf_op jit(solution)/shard_map/cond/branch_1_fun/ppermute | solution.py:315
  51.2 0.6 copy-done.8
  51.9 0.0 collective-permute-start.4
  51.9 0.1 pad_maximum_fusion.5
  52.0 0.1 pad_maximum_fusion.4
  52.0 4.8 %branch_1_fun.1 = (bf16[256,256]{1,0:T(8,128)(2,1)}, bf16[256,256]{1,0:T(8,128)(2,1)S(1)}, bf16[288,256]{1,0:T(8,128)(2,1)}, bf16[288,256]{1,0:T(8,128)(2,1)}, b...) custom-call(s32[2]{0:T(128)S(1)} %get-tuple-element.16.place, ...), custom_call_target="tpu_custom_call" | custom-call | flops 4294967296 | bytes 8388608 | tf_op jit(solution)/shard_map/cond/branch_1_fun/pallas_call | solution.py:389
  56.8 0.0 collective-permute-done.4
  56.9 0.0 collective-permute-done.5.refs_1_
  56.9 0.0 collective-permute-done.6.refs_2_
  56.9 0.0 collective-permute-done.7.refs_3_
  56.9 7.6 %shard_map.79 = (f32[72,512]{1,0:T(8,128)S(1)}, f32[72,512]{1,0:T(8,128)S(1)}, f32[72,512]{1,0:T(8,128)S(1)}, f32[72,512]{1,0:T(8,128)S(1)}) custom-call(s32[2]{0:T(128)S(1)} %pad_add_fusion.place, f32[64,1024]{1,0:T(8,128)S(1)} %copy-done.3, f32[64,1024]{1,0:T(8,128)S(1)} %collective-permute-done.5.refs_1_, f32[64,1024]{1,0:T(8,128)S(1)} %collective-permute-done.6.refs_2_, ...), custom_call_target="tpu_custom_call" | custom-call | flops 8589934592 | bytes 8388608 | tf_op jit(solution)/shard_map/pallas_call | solution.py:410
  64.5 0.1 collective-permute-start.11
  64.6 3.0 %collective-permute-start.15 = (f32[72,512]{1,0:T(8,128)S(1)}, f32[72,512]{1,0:T(8,128)S(1)}, u32[]{:S(2)}, u32[]{:S(2)}) collective-permute-start(f32[72,512]{1,0:T(8,128)S(1)} %get-tuple-element.100), channel_id=1, source_target_pairs={{0,2},{1,3},{2,0},{3,1},{4,6},{5,7},{6,4},{7,5},{8,10},{9,11},{10,... | collective-permute-start | bytes 442376 | tf_op jit(solution)/shard_map/ppermute | solution.py:315
  67.6 1.3 %collective-permute-start.19 = (f32[72,512]{1,0:T(8,128)S(1)}, f32[72,512]{1,0:T(8,128)S(1)}, u32[]{:S(2)}, u32[]{:S(2)}) collective-permute-start(f32[72,512]{1,0:T(8,128)S(1)} %get-tuple-element.101), channel_id=1, source_target_pairs={{0,3},{1,2},{2,1},{3,0},{4,7},{5,6},{6,5},{7,4},{8,11},{9,10},{10,... | collective-permute-start | bytes 442376 | tf_op jit(solution)/shard_map/ppermute | solution.py:315
  68.9 1.5 %collective-permute-start.8 = (f32[1,72,512]{2,1,0:T(8,128)S(1)}, f32[1,72,512]{2,1,0:T(8,128)S(1)}, u32[]{:S(2)}, u32[]{:S(2)}) collective-permute-start(f32[1,72,512]{2,1,0:T(8,128)S(1)} %bitcast.20), channel_id=1, source_target_pairs={{0,8},{4,12},{8,0},{12,4},{16,24},{20,28},{24,16},{28,20},{1,9},{5... | collective-permute-start | bytes 442376 | tf_op jit(solution)/shard_map/ppermute | solution.py:315
  70.4 3.2 %collective-permute-done.11 = f32[72,512]{1,0:T(8,128)S(1)} collective-permute-done((f32[72,512]{1,0:T(8,128)S(1)}, f32[72,512]{1,0:T(8,128)S(1)}, u32[]{:S(2)}, u32[]{:S(2)}) %collective-permute-start.11) | collective-permute-done | bytes 147488 | tf_op jit(solution)/shard_map/ppermute | solution.py:315
  73.7 1.5 %collective-permute-start.12 = (f32[1,72,512]{2,1,0:T(8,128)S(1)}, f32[1,72,512]{2,1,0:T(8,128)S(1)}, u32[]{:S(2)}, u32[]{:S(2)}) collective-permute-start(f32[1,72,512]{2,1,0:T(8,128)S(1)} %bitcast.24), channel_id=1, source_target_pairs={{0,16},{4,20},{8,24},{12,28},{16,0},{20,4},{24,8},{28,12},{1,17},{... | collective-permute-start | bytes 442376 | tf_op jit(solution)/shard_map/ppermute | solution.py:315
  75.2 3.4 %collective-permute-done.15 = f32[72,512]{1,0:T(8,128)S(1)} collective-permute-done((f32[72,512]{1,0:T(8,128)S(1)}, f32[72,512]{1,0:T(8,128)S(1)}, u32[]{:S(2)}, u32[]{:S(2)}) %collective-permute-start.15) | collective-permute-done | bytes 147488 | tf_op jit(solution)/shard_map/ppermute | solution.py:315
  78.6 1.5 %collective-permute-start.16 = (f32[1,72,512]{2,1,0:T(8,128)S(1)}, f32[1,72,512]{2,1,0:T(8,128)S(1)}, u32[]{:S(2)}, u32[]{:S(2)}) collective-permute-start(f32[1,72,512]{2,1,0:T(8,128)S(1)} %bitcast.28), channel_id=1, source_target_pairs={{0,8},{4,12},{8,0},{12,4},{16,24},{20,28},{24,16},{28,20},{1,9},{5... | collective-permute-start | bytes 442376 | tf_op jit(solution)/shard_map/ppermute | solution.py:315
  80.1 0.0 collective-permute-done.19
  80.1 1.5 %collective-permute-start.20 = (f32[1,72,512]{2,1,0:T(8,128)S(1)}, f32[1,72,512]{2,1,0:T(8,128)S(1)}, u32[]{:S(2)}, u32[]{:S(2)}) collective-permute-start(f32[1,72,512]{2,1,0:T(8,128)S(1)} %bitcast.32), channel_id=1, source_target_pairs={{0,16},{4,20},{8,24},{12,28},{16,0},{20,4},{24,8},{28,12},{1,17},{... | collective-permute-start | bytes 442376 | tf_op jit(solution)/shard_map/ppermute | solution.py:315
  81.6 0.0 collective-permute-done.8.refs_1_
  81.6 0.6 collective-permute-start.9
  82.2 0.0 collective-permute-done.12.refs_5_
  82.2 0.6 collective-permute-start.13
  82.8 2.5 %collective-permute-done.16.refs_9_ = f32[1,72,512]{2,1,0:T(8,128)S(1)} collective-permute-done((f32[1,72,512]{2,1,0:T(8,128)S(1)}, f32[1,72,512]{2,1,0:T(8,128)S(1)}, u32[]{:S(2)}, u32[]{:S(2)}) %collective-permute-start.16) | collective-permute-done | bytes 147488 | tf_op jit(solution)/shard_map/ppermute | solution.py:315
  85.3 1.6 %collective-permute-start.17 = (f32[2,72,512]{2,1,0:T(8,128)S(1)}, f32[2,72,512]{2,1,0:T(8,128)S(1)}, u32[]{:S(2)}, u32[]{:S(2)}) collective-permute-start(f32[2,72,512]{2,1,0:T(8,128)S(1)} %pad_maximum_fusion.12), channel_id=1, source_target_pairs={{0,16},{4,20},{8,24},{12,28},{16,0},{20,4},{24,8},{28,12},{1,17},{... | collective-permute-start | bytes 884744 | tf_op jit(solution)/shard_map/ppermute | solution.py:315
  86.9 0.0 collective-permute-done.20.refs_13_
  86.9 1.5 %collective-permute-start.21 = (f32[2,72,512]{2,1,0:T(8,128)S(1)}, f32[2,72,512]{2,1,0:T(8,128)S(1)}, u32[]{:S(2)}, u32[]{:S(2)}) collective-permute-start(f32[2,72,512]{2,1,0:T(8,128)S(1)} %pad_maximum_fusion.13), channel_id=1, source_target_pairs={{0,8},{4,12},{8,0},{12,4},{16,24},{20,28},{24,16},{28,20},{1,9},{5... | collective-permute-start | bytes 884744 | tf_op jit(solution)/shard_map/ppermute | solution.py:315
  88.5 4.6 %collective-permute-done.9.refs_2_ = f32[2,72,512]{2,1,0:T(8,128)S(1)} collective-permute-done((f32[2,72,512]{2,1,0:T(8,128)S(1)}, f32[2,72,512]{2,1,0:T(8,128)S(1)}, u32[]{:S(2)}, u32[]{:S(2)}) %collective-permute-start.9) | collective-permute-done | bytes 294944 | tf_op jit(solution)/shard_map/ppermute | solution.py:315
  93.1 0.1 collective-permute-start.10
  93.2 0.0 collective-permute-done.13.refs_6_
  93.2 0.6 collective-permute-start.14
  93.8 2.4 %collective-permute-done.17.refs_10_ = f32[2,72,512]{2,1,0:T(8,128)S(1)} collective-permute-done((f32[2,72,512]{2,1,0:T(8,128)S(1)}, f32[2,72,512]{2,1,0:T(8,128)S(1)}, u32[]{:S(2)}, u32[]{:S(2)}) %collective-permute-start.17) | collective-permute-done | bytes 294944 | tf_op jit(solution)/shard_map/ppermute | solution.py:315
  96.3 0.0 copy-start
  96.3 0.0 copy-start.1
  96.3 0.1 collective-permute-start.18
  96.4 0.0 collective-permute-done.21.refs_14_
  96.4 0.6 collective-permute-start.22
  97.0 1.4 %collective-permute-done.18.refs_11_ = f32[4,72,512]{2,1,0:T(8,128)S(1)} collective-permute-done((f32[4,72,512]{2,1,0:T(8,128)S(1)}, f32[4,72,512]{2,1,0:T(8,128)S(1)}, u32[]{:S(2)}, u32[]{:S(2)}) %collective-permute-start.18) | collective-permute-done | bytes 589856 | tf_op jit(solution)/shard_map/ppermute | solution.py:315
  98.4 0.8 collective-permute-done.22.refs_15_
  99.2 4.4 %shard_map.80 = (f32[64,2048]{1,0:T(8,128)}, f32[8,64,256]{2,1,0:T(8,128)}) custom-call(s32[2]{0:T(128)S(1)} %pad_add_fusion.place, s32[8]{0:T(128)S(1)} %copy-done, s32[8]{0:T(128)S(1)} %copy-done.1, s32[8]{0:T(128)S(1)} %copy-done.2, f32[1,72,512]{2,1,0:T(8,128)S(1)} %bitcast.23, f32[1,72,512]{2,1,0:T(8,128)S(1)} %collective-permute-done.8.refs_1_, ...), custom_call_target="tpu_custom_call" | custom-call | flops 16777216 | bytes 8388608 | tf_op jit(solution)/shard_map/pallas_call | solution.py:444
  (35 shorter events, 0.4 us)
Async XLA Ops:
  3.6 53.3 %collective-permute-start.5 = (f32[64,1024]{1,0:T(8,128)}, f32[64,1024]{1,0:T(8,128)S(1)}, u32[]{:S(2)}, u32[]{:S(2)}) collective-permute-start(f32[64,1024]{1,0:T(8,128)} %get-tuple-element.71), channel_id=1, source_target_pairs={{0,1},{1,0},{2,3},{3,2},{4,5},{5,4},{6,7},{7,6},{8,9},{9,8},{10,11... | collective-permute-start | bytes 786440 | tf_op jit(solution)/shard_map/ppermute | solution.py:315
  6.7 50.2 %collective-permute-start.6 = (f32[64,1024]{1,0:T(8,128)}, f32[64,1024]{1,0:T(8,128)S(1)}, u32[]{:S(2)}, u32[]{:S(2)}) collective-permute-start(f32[64,1024]{1,0:T(8,128)} %get-tuple-element.72), channel_id=1, source_target_pairs={{0,2},{1,3},{2,0},{3,1},{4,6},{5,7},{6,4},{7,5},{8,10},{9,11},{10,... | collective-permute-start | bytes 786440 | tf_op jit(solution)/shard_map/ppermute | solution.py:315
  9.3 47.6 %collective-permute-start.7 = (f32[64,1024]{1,0:T(8,128)}, f32[64,1024]{1,0:T(8,128)S(1)}, u32[]{:S(2)}, u32[]{:S(2)}) collective-permute-start(f32[64,1024]{1,0:T(8,128)} %get-tuple-element.73), channel_id=1, source_target_pairs={{0,3},{1,2},{2,1},{3,0},{4,7},{5,6},{6,5},{7,4},{8,11},{9,10},{10,... | collective-permute-start | bytes 786440 | tf_op jit(solution)/shard_map/ppermute | solution.py:315
  9.3 0.7 copy-start.2
  10.0 0.7 copy-start.11
  10.7 46.2 %copy-start.3 = (f32[64,1024]{1,0:T(8,128)S(1)}, f32[64,1024]{1,0:T(8,128)}, u32[]{:S(2)}) copy-start(f32[64,1024]{1,0:T(8,128)} %get-tuple-element.70.refs_0_) | copy-start | bytes 786436
  10.7 24.6 %collective-permute-start = (f32[2,8,1024]{2,1,0:T(8,128)S(1)}, f32[2,8,1024]{2,1,0:T(8,128)S(1)}, u32[]{:S(2)}, u32[]{:S(2)}) collective-permute-start(f32[2,8,1024]{2,1,0:T(8,128)S(1)} %pad_maximum_fusion.2), channel_id=1, source_target_pairs={{0,2},{1,3},{2,0},{3,1},{4,6},{5,7},{6,4},{7,5},{8,10},{9,11},{10,... | collective-permute-start | bytes 196616 | tf_op jit(solution)/shard_map/cond/branch_1_fun/ppermute | solution.py:315
  35.3 4.3 %collective-permute-start.1 = (f32[2,8,1024]{2,1,0:T(8,128)S(1)}, f32[2,8,1024]{2,1,0:T(8,128)S(1)}, u32[]{:S(2)}, u32[]{:S(2)}) collective-permute-start(f32[2,8,1024]{2,1,0:T(8,128)S(1)} %pad_maximum_fusion.3), channel_id=1, source_target_pairs={{0,1},{1,0},{2,3},{3,2},{4,5},{5,4},{6,7},{7,6},{8,9},{9,8},{10,11... | collective-permute-start | bytes 196616 | tf_op jit(solution)/shard_map/cond/branch_1_fun/ppermute | solution.py:315
  36.1 3.6 %copy-start.10 = (f32[8,1024]{1,0:T(8,128)S(1)}, f32[8,1024]{1,0:T(8,128)}, u32[]{:S(2)}) copy-start(f32[8,1024]{1,0:T(8,128)} %get-tuple-element.12) | copy-start | bytes 98308 | tf_op jit(solution)/shard_map/cond
  39.7 11.5 %copy-start.6 = (f32[1,4,8,1024]{3,2,1,0:T(8,128)}, f32[1,4,8,1024]{3,2,1,0:T(8,128)S(1)}, u32[]{:S(2)}) copy-start(f32[1,4,8,1024]{3,2,1,0:T(8,128)S(1)} %maximum_bitcast_fusion) | copy-start | bytes 393220 | tf_op jit(solution)/shard_map/cond
  39.7 5.0 %collective-permute-start.2 = (f32[1,4,8,1024]{3,2,1,0:T(8,128)S(1)}, f32[1,4,8,1024]{3,2,1,0:T(8,128)S(1)}, u32[]{:S(2)}, u32[]{:S(2)}) collective-permute-start(f32[1,4,8,1024]{3,2,1,0:T(8,128)S(1)} %maximum_bitcast_fusion), channel_id=1, source_target_pairs={{0,8},{4,12},{8,0},{12,4},{16,24},{20,28},{24,16},{28,20},{1,9},{5... | collective-permute-start | bytes 393224 | tf_op jit(solution)/shard_map/cond/branch_1_fun/ppermute | solution.py:315
  44.7 6.5 %copy-start.4 = (f32[1,4,8,1024]{3,2,1,0:T(8,128)}, f32[1,4,8,1024]{3,2,1,0:T(8,128)S(1)}, u32[]{:S(2)}) copy-start(f32[1,4,8,1024]{3,2,1,0:T(8,128)S(1)} %collective-permute-done.2) | copy-start | bytes 393220 | tf_op jit(solution)/shard_map/cond
  44.7 6.4 %collective-permute-start.3 = (f32[2,4,8,1024]{3,2,1,0:T(8,128)S(1)}, f32[2,4,8,1024]{3,2,1,0:T(8,128)S(1)}, u32[]{:S(2)}, u32[]{:S(2)}) collective-permute-start(f32[2,4,8,1024]{3,2,1,0:T(8,128)S(1)} %pad_maximum_fusion.1), channel_id=1, source_target_pairs={{0,16},{4,20},{8,24},{12,28},{16,0},{20,4},{24,8},{28,12},{1,17},{... | collective-permute-start | bytes 786440 | tf_op jit(solution)/shard_map/cond/branch_1_fun/ppermute | solution.py:315
  51.2 0.7 copy-start.8
  51.9 5.0 %collective-permute-start.4 = (f32[4,4,8,1024]{3,2,1,0:T(8,128)S(1)}, f32[4,4,8,1024]{3,2,1,0:T(8,128)}, u32[]{:S(2)}, u32[]{:S(2)}) collective-permute-start(f32[4,4,8,1024]{3,2,1,0:T(8,128)S(1)} %pad_maximum_fusion), channel_id=1, source_target_pairs={{0,4},{4,0},{8,12},{12,8},{16,20},{20,16},{24,28},{28,24},{1,5},{5... | collective-permute-start | bytes 1572872 | tf_op jit(solution)/shard_map/cond/branch_1_fun/ppermute | solution.py:315
  52.0 4.8 %copy-start.5 = (f32[1,4,8,1024]{3,2,1,0:T(8,128)S(1)}, f32[1,4,8,1024]{3,2,1,0:T(8,128)}, u32[]{:S(2)}) copy-start(f32[1,4,8,1024]{3,2,1,0:T(8,128)} %copy-done.4) | copy-start | bytes 393220 | tf_op jit(solution)/shard_map/cond
  52.0 4.8 %copy-start.7 = (f32[1,4,8,1024]{3,2,1,0:T(8,128)S(1)}, f32[1,4,8,1024]{3,2,1,0:T(8,128)}, u32[]{:S(2)}) copy-start(f32[1,4,8,1024]{3,2,1,0:T(8,128)} %copy-done.6) | copy-start | bytes 393220 | tf_op jit(solution)/shard_map/cond
  52.0 4.8 %copy-start.9 = (f32[2,4,8,1024]{3,2,1,0:T(8,128)S(1)}, f32[2,4,8,1024]{3,2,1,0:T(8,128)}, u32[]{:S(2)}) copy-start(f32[2,4,8,1024]{3,2,1,0:T(8,128)} %copy-done.8) | copy-start | bytes 786436 | tf_op jit(solution)/shard_map/cond
  64.5 9.2 %collective-permute-start.11 = (f32[72,512]{1,0:T(8,128)S(1)}, f32[72,512]{1,0:T(8,128)S(1)}, u32[]{:S(2)}, u32[]{:S(2)}) collective-permute-start(f32[72,512]{1,0:T(8,128)S(1)} %get-tuple-element.99), channel_id=1, source_target_pairs={{0,1},{1,0},{2,3},{3,2},{4,5},{5,4},{6,7},{7,6},{8,9},{9,8},{10,11... | collective-permute-start | bytes 442376 | tf_op jit(solution)/shard_map/ppermute | solution.py:315
  64.6 14.0 %collective-permute-start.15 = (f32[72,512]{1,0:T(8,128)S(1)}, f32[72,512]{1,0:T(8,128)S(1)}, u32[]{:S(2)}, u32[]{:S(2)}) collective-permute-start(f32[72,512]{1,0:T(8,128)S(1)} %get-tuple-element.100), channel_id=1, source_target_pairs={{0,2},{1,3},{2,0},{3,1},{4,6},{5,7},{6,4},{7,5},{8,10},{9,11},{10,... | collective-permute-start | bytes 442376 | tf_op jit(solution)/shard_map/ppermute | solution.py:315
  67.6 12.5 %collective-permute-start.19 = (f32[72,512]{1,0:T(8,128)S(1)}, f32[72,512]{1,0:T(8,128)S(1)}, u32[]{:S(2)}, u32[]{:S(2)}) collective-permute-start(f32[72,512]{1,0:T(8,128)S(1)} %get-tuple-element.101), channel_id=1, source_target_pairs={{0,3},{1,2},{2,1},{3,0},{4,7},{5,6},{6,5},{7,4},{8,11},{9,10},{10,... | collective-permute-start | bytes 442376 | tf_op jit(solution)/shard_map/ppermute | solution.py:315
  68.9 12.7 %collective-permute-start.8 = (f32[1,72,512]{2,1,0:T(8,128)S(1)}, f32[1,72,512]{2,1,0:T(8,128)S(1)}, u32[]{:S(2)}, u32[]{:S(2)}) collective-permute-start(f32[1,72,512]{2,1,0:T(8,128)S(1)} %bitcast.20), channel_id=1, source_target_pairs={{0,8},{4,12},{8,0},{12,4},{16,24},{20,28},{24,16},{28,20},{1,9},{5... | collective-permute-start | bytes 442376 | tf_op jit(solution)/shard_map/ppermute | solution.py:315
  73.7 8.5 %collective-permute-start.12 = (f32[1,72,512]{2,1,0:T(8,128)S(1)}, f32[1,72,512]{2,1,0:T(8,128)S(1)}, u32[]{:S(2)}, u32[]{:S(2)}) collective-permute-start(f32[1,72,512]{2,1,0:T(8,128)S(1)} %bitcast.24), channel_id=1, source_target_pairs={{0,16},{4,20},{8,24},{12,28},{16,0},{20,4},{24,8},{28,12},{1,17},{... | collective-permute-start | bytes 442376 | tf_op jit(solution)/shard_map/ppermute | solution.py:315
  78.6 6.7 %collective-permute-start.16 = (f32[1,72,512]{2,1,0:T(8,128)S(1)}, f32[1,72,512]{2,1,0:T(8,128)S(1)}, u32[]{:S(2)}, u32[]{:S(2)}) collective-permute-start(f32[1,72,512]{2,1,0:T(8,128)S(1)} %bitcast.28), channel_id=1, source_target_pairs={{0,8},{4,12},{8,0},{12,4},{16,24},{20,28},{24,16},{28,20},{1,9},{5... | collective-permute-start | bytes 442376 | tf_op jit(solution)/shard_map/ppermute | solution.py:315
  80.1 6.8 %collective-permute-start.20 = (f32[1,72,512]{2,1,0:T(8,128)S(1)}, f32[1,72,512]{2,1,0:T(8,128)S(1)}, u32[]{:S(2)}, u32[]{:S(2)}) collective-permute-start(f32[1,72,512]{2,1,0:T(8,128)S(1)} %bitcast.32), channel_id=1, source_target_pairs={{0,16},{4,20},{8,24},{12,28},{16,0},{20,4},{24,8},{28,12},{1,17},{... | collective-permute-start | bytes 442376 | tf_op jit(solution)/shard_map/ppermute | solution.py:315
  81.6 11.4 %collective-permute-start.9 = (f32[2,72,512]{2,1,0:T(8,128)S(1)}, f32[2,72,512]{2,1,0:T(8,128)S(1)}, u32[]{:S(2)}, u32[]{:S(2)}) collective-permute-start(f32[2,72,512]{2,1,0:T(8,128)S(1)} %pad_maximum_fusion.10), channel_id=1, source_target_pairs={{0,16},{4,20},{8,24},{12,28},{16,0},{20,4},{24,8},{28,12},{1,17},{... | collective-permute-start | bytes 884744 | tf_op jit(solution)/shard_map/ppermute | solution.py:315
  82.2 11.0 %collective-permute-start.13 = (f32[2,72,512]{2,1,0:T(8,128)S(1)}, f32[2,72,512]{2,1,0:T(8,128)S(1)}, u32[]{:S(2)}, u32[]{:S(2)}) collective-permute-start(f32[2,72,512]{2,1,0:T(8,128)S(1)} %pad_maximum_fusion.11), channel_id=1, source_target_pairs={{0,8},{4,12},{8,0},{12,4},{16,24},{20,28},{24,16},{28,20},{1,9},{5... | collective-permute-start | bytes 884744 | tf_op jit(solution)/shard_map/ppermute | solution.py:315
  85.3 10.9 %collective-permute-start.17 = (f32[2,72,512]{2,1,0:T(8,128)S(1)}, f32[2,72,512]{2,1,0:T(8,128)S(1)}, u32[]{:S(2)}, u32[]{:S(2)}) collective-permute-start(f32[2,72,512]{2,1,0:T(8,128)S(1)} %pad_maximum_fusion.12), channel_id=1, source_target_pairs={{0,16},{4,20},{8,24},{12,28},{16,0},{20,4},{24,8},{28,12},{1,17},{... | collective-permute-start | bytes 884744 | tf_op jit(solution)/shard_map/ppermute | solution.py:315
  86.9 9.4 %collective-permute-start.21 = (f32[2,72,512]{2,1,0:T(8,128)S(1)}, f32[2,72,512]{2,1,0:T(8,128)S(1)}, u32[]{:S(2)}, u32[]{:S(2)}) collective-permute-start(f32[2,72,512]{2,1,0:T(8,128)S(1)} %pad_maximum_fusion.13), channel_id=1, source_target_pairs={{0,8},{4,12},{8,0},{12,4},{16,24},{20,28},{24,16},{28,20},{1,9},{5... | collective-permute-start | bytes 884744 | tf_op jit(solution)/shard_map/ppermute | solution.py:315
  93.1 3.9 %collective-permute-start.10 = (f32[4,72,512]{2,1,0:T(8,128)S(1)}, f32[4,72,512]{2,1,0:T(8,128)S(1)}, u32[]{:S(2)}, u32[]{:S(2)}) collective-permute-start(f32[4,72,512]{2,1,0:T(8,128)S(1)} %pad_maximum_fusion.6), channel_id=1, source_target_pairs={{0,4},{4,0},{8,12},{12,8},{16,20},{20,16},{24,28},{28,24},{1,5},{5... | collective-permute-start | bytes 1769480 | tf_op jit(solution)/shard_map/ppermute | solution.py:315
  93.2 3.7 %collective-permute-start.14 = (f32[4,72,512]{2,1,0:T(8,128)S(1)}, f32[4,72,512]{2,1,0:T(8,128)S(1)}, u32[]{:S(2)}, u32[]{:S(2)}) collective-permute-start(f32[4,72,512]{2,1,0:T(8,128)S(1)} %pad_maximum_fusion.7), channel_id=1, source_target_pairs={{0,4},{4,0},{8,12},{12,8},{16,20},{20,16},{24,28},{28,24},{1,5},{5... | collective-permute-start | bytes 1769480 | tf_op jit(solution)/shard_map/ppermute | solution.py:315
  96.3 2.9 %copy-start = (s32[8]{0:T(128)S(1)}, s32[8]{0:T(128)}, u32[]{:S(2)}) copy-start(s32[8]{0:T(128)} %pair_one.1) | copy-start | bytes 100
  96.3 2.9 %copy-start.1 = (s32[8]{0:T(128)S(1)}, s32[8]{0:T(128)}, u32[]{:S(2)}) copy-start(s32[8]{0:T(128)} %pair_two.1) | copy-start | bytes 100
  96.3 2.1 %collective-permute-start.18 = (f32[4,72,512]{2,1,0:T(8,128)S(1)}, f32[4,72,512]{2,1,0:T(8,128)S(1)}, u32[]{:S(2)}, u32[]{:S(2)}) collective-permute-start(f32[4,72,512]{2,1,0:T(8,128)S(1)} %pad_maximum_fusion.8), channel_id=1, source_target_pairs={{0,4},{4,0},{8,12},{12,8},{16,20},{20,16},{24,28},{28,24},{1,5},{5... | collective-permute-start | bytes 1769480 | tf_op jit(solution)/shard_map/ppermute | solution.py:315
  96.4 2.8 %collective-permute-start.22 = (f32[4,72,512]{2,1,0:T(8,128)S(1)}, f32[4,72,512]{2,1,0:T(8,128)S(1)}, u32[]{:S(2)}, u32[]{:S(2)}) collective-permute-start(f32[4,72,512]{2,1,0:T(8,128)S(1)} %pad_maximum_fusion.9), channel_id=1, source_target_pairs={{0,4},{4,0},{8,12},{12,8},{16,20},{20,16},{24,28},{28,24},{1,5},{5... | collective-permute-start | bytes 1769480 | tf_op jit(solution)/shard_map/ppermute | solution.py:315

commit v2 on v1

--- a/solution.py
+++ b/solution.py
@@ -61,37 +61,45 @@
         return [i for i, (a, b) in enumerate(self.blocks) if b > low and a < self.width - low]
 
 
+def share_kernel(plan, place, weight, *refs):
+    parts, padded, sem = refs[: plan.row_devices], refs[-2], refs[-1]
+    row = pl.multiple_of(lax.rem(place[1], plan.sharers) * plan.share_rows, plan.share_rows)
+    source = weight.at[pl.ds(row, plan.share_rows)]
+    copy = pltpu.make_async_copy(source, padded.at[:, pl.ds(plan.halo, plan.columns)], sem)
+    copy.start()
+    zeros = jnp.zeros((plan.share_rows, plan.halo), jnp.float32)
+    padded[:, : plan.halo] = zeros
+    padded[:, plan.halo + plan.columns :] = zeros
+    copy.wait()
+    for step, part in enumerate(parts):
+        column = pl.multiple_of((place[0] ^ step) * plan.share, lane)
+        part[...] = padded[:, pl.ds(column, plan.width)]
+
+
 def weighted_kernel(plan, place, maps, weight, *refs):
-    count = plan.row_devices
-    pieces, parts = refs[:count], refs[count : 2 * count]
-    padded, weights, given, sems = refs[2 * count :]
+    pieces = refs[: plan.row_devices]
+    padded, weights, given, sems = refs[plan.row_devices :]
     chunk = plan.row_local // loads
     copies = []
     for number in range(loads):
         rows = pl.ds(number * chunk, chunk)
-        inner = pl.ds(plan.halo, plan.columns)
         copies.append((
-            pltpu.make_async_copy(weight.at[rows], weights.at[rows, inner], sems.at[0, number]),
+            pltpu.make_async_copy(weight.at[rows], weights.at[rows], sems.at[0, number]),
             pltpu.make_async_copy(maps.at[rows], given.at[rows], sems.at[1, number]),
         ))
         for copy in copies[-1]:
             copy.start()
     zeros = jnp.zeros((plan.row_local, plan.halo), jnp.float32)
-    for target in (padded, weights):
-        target[:, : plan.halo] = zeros
-        target[:, plan.halo + plan.columns :] = zeros
-    inner = slice(plan.halo, plan.halo + plan.columns)
-    starts = [pl.multiple_of((place[0] ^ step) * plan.share, lane) for step in range(count)]
+    padded[:, : plan.halo] = zeros
+    padded[:, plan.halo + plan.columns :] = zeros
     for number in range(loads):
         for copy in copies[number]:
             copy.wait()
         rows = slice(number * chunk, (number + 1) * chunk)
-        padded[rows, inner] = weights[rows, inner] * given[rows]
-        for step, column in enumerate(starts):
-            pieces[step][rows] = padded[rows, pl.ds(column, plan.width)]
-    row = pl.multiple_of(lax.rem(place[1], plan.sharers) * plan.share_rows, plan.share_rows)
-    for step, column in enumerate(starts):
-        parts[step][...] = weights[pl.ds(row, plan.share_rows), pl.ds(column, plan.width)]
+        padded[rows, plan.halo : plan.halo + plan.columns] = weights[rows] * given[rows]
+        for step, piece in enumerate(pieces):
+            column = pl.multiple_of((place[0] ^ step) * plan.share, lane)
+            piece[rows] = padded[rows, pl.ds(column, plan.width)]
 
 
 def band(plan, taps, rows, columns, offset):
@@ -147,22 +155,11 @@
 
     pieces = take(plan.row_devices)
     parts = take(len(sharers))
-    sources = take(2 * (len(plan.blocks) + 3))
+    square, final = take(2), take(2)
+    bands = [take(2) for _ in plan.blocks]
+    last = take(2)
     outs = take(plan.row_devices)
-    seen, weight, image, total, field, high, low, mid_high, mid_low, sem, sems = refs[:11]
-    tables = refs[11:]
-    copies = [pltpu.make_async_copy(a, b, sems.at[i]) for i, (a, b) in enumerate(zip(sources, tables))]
-    for copy in copies:
-        copy.start()
-    groups = [(tables[i], tables[i + 1]) for i in range(0, len(tables), 2)]
-    square, final, bands, last = groups[0], groups[1], groups[2:-1], groups[-1]
-    for part, owners in zip(parts, sharers):
-        for slot, offset in enumerate(owners):
-            for step in range(plan.row_devices):
-                row = (place[0] ^ step) * plan.row_local
-                row = row + (lax.rem(place[1], plan.sharers) ^ offset) * plan.share_rows
-                rows = pl.ds(pl.multiple_of(row, plan.share_rows), plan.share_rows)
-                pltpu.make_async_copy(part.at[slot, step], weight.at[rows], sem).start()
+    seen, weight, image, total, field, high, low, mid_high, mid_low = refs
     for step, piece in enumerate(pieces):
         row = pl.multiple_of((place[0] ^ step) * plan.row_local, plan.row_local)
         value = piece[...]
@@ -170,6 +167,13 @@
         a, b = split(value)
         high[pl.ds(row, plan.row_local), :] = a
         low[pl.ds(row, plan.row_local), :] = b
+    for part, owners in zip(parts, sharers):
+        for slot, offset in enumerate(owners):
+            for step in range(plan.row_devices):
+                row = (place[0] ^ step) * plan.row_local
+                row = row + (lax.rem(place[1], plan.sharers) ^ offset) * plan.share_rows
+                row = pl.multiple_of(row, plan.share_rows)
+                weight[pl.ds(row, plan.share_rows), :] = part[slot, step]
 
     def rows_pass(table, start, stop):
         count = table[0].shape[0]
@@ -186,14 +190,7 @@
     for iteration in range(ITERS):
         chosen = plan.stage_blocks(iteration)
         windows = [plan.window(plan.blocks[i]) for i in chosen]
-        if iteration == 0:
-            copies[0].wait()
-            copies[1].wait()
         rows_pass(square, windows[0][0], windows[-1][1])
-        if iteration == 0:
-            for copy in copies[2:]:
-                copy.wait()
-            pltpu.make_async_copy(weight, weight, sem).wait()
         for i, window in zip(chosen, windows):
             a, b = plan.blocks[i]
             value = columns_pass(bands[i], plan.rows, window)
@@ -354,17 +351,28 @@
         return jax.ShapeDtypeStruct(shape, jnp.bfloat16)
 
     cells = row_local * columns
-    made = call(
+    parts = call(
+        functools.partial(share_kernel, plan),
+        [f32(plan.share_rows, plan.width)] * row_devices,
+        [smem, far],
+        [pltpu.VMEM((plan.share_rows, columns + 2 * plan.halo), jnp.float32), pltpu.SemaphoreType.DMA],
+        0,
+        1 << 18,
+        limit=60,
+    )(place, weight)
+    pieces = call(
         functools.partial(weighted_kernel, plan),
-        [f32(row_local, plan.width)] * row_devices + [f32(plan.share_rows, plan.width)] * row_devices,
+        [f32(row_local, plan.width)] * row_devices,
         [smem, far, far],
-        [pltpu.VMEM((row_local, columns + 2 * plan.halo), jnp.float32)] * 2
-        + [pltpu.VMEM((row_local, columns), jnp.float32), pltpu.SemaphoreType.DMA((2, loads))],
+        [pltpu.VMEM((row_local, columns + 2 * plan.halo), jnp.float32)]
+        + [pltpu.VMEM((row_local, columns), jnp.float32)] * 2
+        + [pltpu.SemaphoreType.DMA((2, loads))],
         cells,
         16 * cells,
         limit=60,
     )(place, maps.reshape(row_local, columns), weight)
-    pieces, parts = made[:row_devices], made[row_devices:]
+    parts = [parts[0]] + [exchange(parts[d], "rows", d) for d in range(1, row_devices)]
+    pieces, parts = lax.optimization_barrier((pieces, parts))
     pieces = [pieces[0]] + [exchange(pieces[d], "rows", d) for d in range(1, row_devices)]
     sharers = []
     shapes = [(plan.rows, plan.rows), (row_devices * plan.slab, plan.rows)]
@@ -373,12 +381,6 @@
         shapes.append((high - low, block[1] - block[0]))
 
     def prepare(parts, beam):
-        parts = list(parts)
-        for bit in [1 << i for i in reversed(range(row_devices.bit_length() - 1))]:
-            moved = [step for step in range(row_devices) if step & bit]
-            received = exchange(jnp.stack([parts[step] for step in moved]), "rows", bit)
-            for slot, step in enumerate(moved):
-                parts[step] = received[slot]
         bits = [1 << i for i in range(1, plan.sharers.bit_length() - 1)] + [1]
         arrays, offsets = gather(jnp.stack(parts), "sims", bits)
         sharers[:] = offsets
@@ -398,7 +400,7 @@
 
     made = jax.eval_shape(prepare, parts, beam)
     parts, tables = lax.cond(
-        owner[0] >= 0,
+        lax.axis_index("rows") < row_devices,
         prepare,
         lambda parts, beam: jax.tree.map(lambda x: jnp.zeros(x.shape, x.dtype), made),
         parts,
@@ -410,25 +412,27 @@
     filtered = call(
         functools.partial(filter_kernel, plan, sharers),
         [f32(plan.slab, plan.share)] * row_devices,
-        [smem] + [vmem] * len(pieces) + [far] * (len(parts) + len(tables)),
+        [smem] + [vmem] * len(pieces) + [vmem] * (len(parts) + len(tables)),
         [pltpu.VMEM(full, jnp.float32)] * 4
         + [pltpu.VMEM((row_devices * plan.slab, plan.share), jnp.float32)]
         + [pltpu.VMEM(full, jnp.bfloat16)] * 2
-        + [pltpu.VMEM(tall, jnp.bfloat16)] * 2
-        + [pltpu.SemaphoreType.DMA, pltpu.SemaphoreType.DMA((2 * len(shapes),))]
-        + [pltpu.VMEM(shape, jnp.bfloat16) for shape in shapes for _ in range(2)],
+        + [pltpu.VMEM(tall, jnp.bfloat16)] * 2,
         1 << 33,
         1 << 23,
     )(place, *pieces, *parts, *tables)
 
-    held, holders = [], []
+    moved = [filtered[0]] + [exchange(filtered[step], "rows", step) for step in range(1, row_devices)]
+    bits = [1 << i for i in range(1, sim_devices.bit_length() - 1)]
+    arrays, holders = [], []
     for step in range(row_devices):
-        piece = filtered[step] if step == 0 else exchange(filtered[step], "rows", step)
-        bits = [1 << i for i in range(1, sim_devices.bit_length() - 1)]
         turn = step % max(len(bits), 1)
-        arrays, offsets = gather(piece, "sims", bits[turn:] + bits[:turn] + [1])
-        held += arrays
+        found, offsets = gather(moved[step], "sims", bits[turn:] + bits[:turn])
+        arrays.append(found)
         holders.append(offsets)
+    held = []
+    for found, offsets in zip(arrays, holders):
+        held += found + [exchange(jnp.concatenate(found), "sims", 1)]
+        offsets.append([offset ^ 1 for order in offsets for offset in order])
 
     field_width = columns // sim_devices
     fused = field_width if field_width % lane == 0 else 0

time: 105 us -> 84.2 us (0.80)
  the two profiles are of different devices: /device:TPU:0 before, /device:TPU:9 now
where the time goes in v2:
time: 84.2 us; the launch traced here: 84 us
  starting transfers between devices  34.8 us (41%)
  waiting for transfers between devices  21.7 us (26%)
  Pallas kernels  20.7 us (25%)
  other arithmetic  3.39 us (4%)
  local copies, waits for them, and re-layouts  2.27 us (3%)
  between operations  1.01 us (1%)
    ppermute x24, starting transfers between devices, exchange(): return lax.ppermute(value, axis, [(i, i ^ offset) for i in range(count)])  34.8 us
    ppermute x24, waiting for transfers between devices, exchange(): return lax.ppermute(value, axis, [(i, i ^ offset) for i in range(count)])  21.7 us
    pallas_call x1, Pallas kernels, body(): call(functools.partial(filter_kernel, plan, sharers), [f32(plan.slab, pla...  6.68 us
    pallas_call x1, Pallas kernels, prepare(): call(functools.partial(table_kernel, plan), [b16(*shape) for shape in sha...  4.78 us
    pallas_call x1, Pallas kernels, body(): call(functools.partial(estimate_kernel, plan, holders, fused), outs, [sme...  4.36 us
    pallas_call x1, Pallas kernels, body(): call(functools.partial(weighted_kernel, plan), [f32(row_local, plan.width...  2.87 us
    pallas_call x1, Pallas kernels, body(): call(functools.partial(share_kernel, plan), [f32(plan.share_rows, plan.wi...  2.04 us
  transfers between devices with their start and end apart: 24, of which 10 were waited for; matrix products, arithmetic and copies ran while one was open for 4% of the time, Pallas kernels for 9%

profile of v2, /device:TPU:9, one launch (start us, length us, event | category | flops | bytes accessed | tf_op | source)
XLA Modules:
  0.0 84.0 jit_solution(4399379126520683764)
XLA Ops:
  0.6 0.1 pad_add_fusion.place
  0.7 2.0 %shard_map.79 = (f32[8,1024]{1,0:T(8,128)}, f32[8,1024]{1,0:T(8,128)}, f32[8,1024]{1,0:T(8,128)}, f32[8,1024]{1,0:T(8,128)}) custom-call(s32[2]{0:T(128)S(1)} %pad_add_fusion.place, f32[64,2048]{1,0:T(8,128)} %weight.3), custom_call_target="tpu_custom_call" | custom-call | bytes 262144 | tf_op jit(solution)/shard_map/pallas_call | solution.py:354
  2.8 0.1 collective-permute-start.3
  2.8 2.5 %collective-permute-start.4 = (f32[8,1024]{1,0:T(8,128)}, f32[8,1024]{1,0:T(8,128)S(1)}, u32[]{:S(2)}, u32[]{:S(2)}) collective-permute-start(f32[8,1024]{1,0:T(8,128)} %get-tuple-element.84), channel_id=1, source_target_pairs={{0,2},{1,3},{2,0},{3,1},{4,6},{5,7},{6,4},{7,5},{8,10},{9,11},{10,... | collective-permute-start | bytes 98312 | tf_op jit(solution)/shard_map/ppermute | solution.py:312
  5.3 0.2 collective-permute-start.5
  5.5 2.9 %shard_map.78 = (f32[64,1024]{1,0:T(8,128)}, f32[64,1024]{1,0:T(8,128)}, f32[64,1024]{1,0:T(8,128)}, f32[64,1024]{1,0:T(8,128)}) custom-call(s32[2]{0:T(128)S(1)} %pad_add_fusion.place, f32[64,2048]{1,0:T(8,128)} %bitcast.36, f32[64,2048]{1,0:T(8,128)} %weight.3), custom_call_target="tpu_custom_call" | custom-call | flops 131072 | bytes 2097152 | tf_op jit(solution)/shard_map/pallas_call | solution.py:363
  8.4 0.0 collective-permute-done.3
  8.4 0.0 collective-permute-done.4
  8.4 0.5 collective-permute-done.5
  8.9 2.6 %collective-permute-start.6 = (f32[64,1024]{1,0:T(8,128)}, f32[64,1024]{1,0:T(8,128)S(1)}, u32[]{:S(2)}, u32[]{:S(2)}) collective-permute-start(f32[64,1024]{1,0:T(8,128)} %get-tuple-element.87), channel_id=1, source_target_pairs={{0,1},{1,0},{2,3},{3,2},{4,5},{5,4},{6,7},{7,6},{8,9},{9,8},{10,11... | collective-permute-start | bytes 786440 | tf_op jit(solution)/shard_map/ppermute | solution.py:312
  11.5 0.7 collective-permute-start.7
  12.2 0.6 collective-permute-start.8
  12.7 21.6 %conditional.1 = (f32[1,4,8,1024]{3,2,1,0:T(8,128)S(1)}, f32[1,4,8,1024]{3,2,1,0:T(8,128)S(1)}, f32[2,4,8,1024]{3,2,1,0:T(8,128)S(1)}, f32[4,4,8,1024]{3,2,1,0:T...) conditional(s32[]{:T(128)} %convert_element_type.3, () %tuple.18, ...), branch_computations={%region_0.0_spmd, %region_1.3_spmd} | conditional | flops 4295394304 | bytes 18103900 | solution.py:402
  12.7 0.9 %maximum_bitcast_fusion = f32[1,4,8,1024]{3,2,1,0:T(8,128)S(1)} fusion(f32[1,8,1024]{2,1,0:T(8,128)} %bitcast.40, f32[1,8,1024]{2,1,0:T(8,128)} %bitcast.39, f32[1,8,1024]{2,1,0:T(8,128)} %bitcast.38, f32[1,8,1024]{2,1,0:T(8,128)} %bitcast.37), kind=kLoop, calls=%fused_computation.2 | loop fusion | flops 98304 | bytes 262144 | tf_op jit(solution)/shard_map/cond/branch_1_fun/broadcast_in_dim | solution.py:316
  13.6 0.0 copy-start.16
  13.6 1.3 %collective-permute-start = (f32[1,4,8,1024]{3,2,1,0:T(8,128)S(1)}, f32[1,4,8,1024]{3,2,1,0:T(8,128)S(1)}, u32[]{:S(2)}, u32[]{:S(2)}) collective-permute-start(f32[1,4,8,1024]{3,2,1,0:T(8,128)S(1)} %maximum_bitcast_fusion), channel_id=1, source_target_pairs={{0,8},{4,12},{8,0},{12,4},{16,24},{20,28},{24,16},{28,20},{1,9},{5... | collective-permute-start | bytes 393224 | tf_op jit(solution)/shard_map/cond/branch_1_fun/ppermute | solution.py:312
  14.9 0.1 reverse.2
  15.0 0.7 reduce_sum.8
  15.7 0.7 broadcast_divide_fusion.1
  16.4 1.5 %collective-permute-done = f32[1,4,8,1024]{3,2,1,0:T(8,128)S(1)} collective-permute-done((f32[1,4,8,1024]{3,2,1,0:T(8,128)S(1)}, f32[1,4,8,1024]{3,2,1,0:T(8,128)S(1)}, u32[]{:S(2)}, u32[]{:S(2)}) %collective-permute-start) | collective-permute-done | bytes 131104 | tf_op jit(solution)/shard_map/cond/branch_1_fun/ppermute | solution.py:312
  17.8 1.3 %collective-permute-start.1 = (f32[2,4,8,1024]{3,2,1,0:T(8,128)S(1)}, f32[2,4,8,1024]{3,2,1,0:T(8,128)S(1)}, u32[]{:S(2)}, u32[]{:S(2)}) collective-permute-start(f32[2,4,8,1024]{3,2,1,0:T(8,128)S(1)} %pad_maximum_fusion.1), channel_id=1, source_target_pairs={{0,16},{4,20},{8,24},{12,28},{16,0},{20,4},{24,8},{28,12},{1,17},{... | collective-permute-start | bytes 786440 | tf_op jit(solution)/shard_map/cond/branch_1_fun/ppermute | solution.py:312
  19.1 0.7 broadcast_divide_fusion
  19.8 0.1 pad_slice_fusion
  19.9 0.1 pad_slice_fusion.1
  20.0 3.4 %collective-permute-done.1 = f32[2,4,8,1024]{3,2,1,0:T(8,128)S(1)} collective-permute-done((f32[2,4,8,1024]{3,2,1,0:T(8,128)S(1)}, f32[2,4,8,1024]{3,2,1,0:T(8,128)S(1)}, u32[]{:S(2)}, u32[]{:S(2)}) %collective-permute-start.1) | collective-permute-done | bytes 262176 | tf_op jit(solution)/shard_map/cond/branch_1_fun/ppermute | solution.py:312
  23.5 0.7 copy-done.8
  24.1 4.5 %collective-permute-start.2 = (f32[4,4,8,1024]{3,2,1,0:T(8,128)S(1)}, f32[4,4,8,1024]{3,2,1,0:T(8,128)}, u32[]{:S(2)}, u32[]{:S(2)}) collective-permute-start(f32[4,4,8,1024]{3,2,1,0:T(8,128)S(1)} %pad_maximum_fusion), channel_id=1, source_target_pairs={{0,4},{4,0},{8,12},{12,8},{16,20},{20,16},{24,28},{28,24},{1,5},{5... | collective-permute-start | bytes 1572872 | tf_op jit(solution)/shard_map/cond/branch_1_fun/ppermute | solution.py:312
  28.7 0.1 pad_maximum_fusion.3
  28.8 0.1 pad_maximum_fusion.2
  28.8 0.7 copy-done.15
  29.5 4.8 %branch_1_fun.1 = (bf16[256,256]{1,0:T(8,128)(2,1)}, bf16[256,256]{1,0:T(8,128)(2,1)}, bf16[288,256]{1,0:T(8,128)(2,1)}, bf16[288,256]{1,0:T(8,128)(2,1)S(1)}, b...) custom-call(s32[2]{0:T(128)S(1)} %copy-done.15, ...), custom_call_target="tpu_custom_call" | custom-call | flops 4294967296 | bytes 8388608 | tf_op jit(solution)/shard_map/cond/branch_1_fun/pallas_call | solution.py:391
  34.3 0.0 collective-permute-done.2
  34.3 0.0 collective-permute-done.6.refs_1_
  34.3 0.0 collective-permute-done.7.refs_2_
  34.4 0.6 copy-done.14
  35.0 6.7 %shard_map.80 = (f32[72,512]{1,0:T(8,128)S(1)}, f32[72,512]{1,0:T(8,128)S(1)}, f32[72,512]{1,0:T(8,128)S(1)}, f32[72,512]{1,0:T(8,128)S(1)}) custom-call(s32[2]{0:T(128)S(1)} %copy-done.14, f32[64,1024]{1,0:T(8,128)S(1)} %copy-done.3, f32[64,1024]{1,0:T(8,128)S(1)} %collective-permute-done.6.refs_1_, f32[64,1024]{1,0:T(8,128)S(1)} %collective-permute-done.7.refs_2_, ...), custom_call_target="tpu_custom_call" | custom-call | flops 8589934592 | bytes 8388608 | tf_op jit(solution)/shard_map/pallas_call | solution.py:412
  41.7 2.6 %collective-permute-start.12 = (f32[72,512]{1,0:T(8,128)S(1)}, f32[72,512]{1,0:T(8,128)S(1)}, u32[]{:S(2)}, u32[]{:S(2)}) collective-permute-start(f32[72,512]{1,0:T(8,128)S(1)} %get-tuple-element.115), channel_id=1, source_target_pairs={{0,1},{1,0},{2,3},{3,2},{4,5},{5,4},{6,7},{7,6},{8,9},{9,8},{10,11... | collective-permute-start | bytes 442376 | tf_op jit(solution)/shard_map/ppermute | solution.py:312
  44.3 1.3 %collective-permute-start.20 = (f32[72,512]{1,0:T(8,128)S(1)}, f32[72,512]{1,0:T(8,128)S(1)}, u32[]{:S(2)}, u32[]{:S(2)}) collective-permute-start(f32[72,512]{1,0:T(8,128)S(1)} %get-tuple-element.117), channel_id=1, source_target_pairs={{0,3},{1,2},{2,1},{3,0},{4,7},{5,6},{6,5},{7,4},{8,11},{9,10},{10,... | collective-permute-start | bytes 442376 | tf_op jit(solution)/shard_map/ppermute | solution.py:312
  45.6 1.2 %collective-permute-start.9 = (f32[1,72,512]{2,1,0:T(8,128)S(1)}, f32[1,72,512]{2,1,0:T(8,128)S(1)}, u32[]{:S(2)}, u32[]{:S(2)}) collective-permute-start(f32[1,72,512]{2,1,0:T(8,128)S(1)} %bitcast.18), channel_id=1, source_target_pairs={{0,8},{4,12},{8,0},{12,4},{16,24},{20,28},{24,16},{28,20},{1,9},{5... | collective-permute-start | bytes 442376 | tf_op jit(solution)/shard_map/ppermute | solution.py:312
  46.8 2.4 %collective-permute-done.12 = f32[72,512]{1,0:T(8,128)S(1)} collective-permute-done((f32[72,512]{1,0:T(8,128)S(1)}, f32[72,512]{1,0:T(8,128)S(1)}, u32[]{:S(2)}, u32[]{:S(2)}) %collective-permute-start.12) | collective-permute-done | bytes 147488 | tf_op jit(solution)/shard_map/ppermute | solution.py:312
  49.1 1.3 %collective-permute-start.13 = (f32[1,72,512]{2,1,0:T(8,128)S(1)}, f32[1,72,512]{2,1,0:T(8,128)S(1)}, u32[]{:S(2)}, u32[]{:S(2)}) collective-permute-start(f32[1,72,512]{2,1,0:T(8,128)S(1)} %bitcast.22), channel_id=1, source_target_pairs={{0,16},{4,20},{8,24},{12,28},{16,0},{20,4},{24,8},{28,12},{1,17},{... | collective-permute-start | bytes 442376 | tf_op jit(solution)/shard_map/ppermute | solution.py:312
  50.5 0.0 collective-permute-done.16
  50.5 1.3 %collective-permute-start.17 = (f32[1,72,512]{2,1,0:T(8,128)S(1)}, f32[1,72,512]{2,1,0:T(8,128)S(1)}, u32[]{:S(2)}, u32[]{:S(2)}) collective-permute-start(f32[1,72,512]{2,1,0:T(8,128)S(1)} %bitcast.26), channel_id=1, source_target_pairs={{0,8},{4,12},{8,0},{12,4},{16,24},{20,28},{24,16},{28,20},{1,9},{5... | collective-permute-start | bytes 442376 | tf_op jit(solution)/shard_map/ppermute | solution.py:312
  51.7 6.2 %collective-permute-done.20 = f32[72,512]{1,0:T(8,128)S(1)} collective-permute-done((f32[72,512]{1,0:T(8,128)S(1)}, f32[72,512]{1,0:T(8,128)S(1)}, u32[]{:S(2)}, u32[]{:S(2)}) %collective-permute-start.20) | collective-permute-done | bytes 147488 | tf_op jit(solution)/shard_map/ppermute | solution.py:312
  57.9 1.0 %collective-permute-start.21 = (f32[1,72,512]{2,1,0:T(8,128)S(1)}, f32[1,72,512]{2,1,0:T(8,128)S(1)}, u32[]{:S(2)}, u32[]{:S(2)}) collective-permute-start(f32[1,72,512]{2,1,0:T(8,128)S(1)} %bitcast.30), channel_id=1, source_target_pairs={{0,16},{4,20},{8,24},{12,28},{16,0},{20,4},{24,8},{28,12},{1,17},{... | collective-permute-start | bytes 442376 | tf_op jit(solution)/shard_map/ppermute | solution.py:312
  58.9 0.6 collective-permute-start.10
  59.5 0.0 collective-permute-done.13.refs_5_
  59.5 1.0 %collective-permute-start.14 = (f32[2,72,512]{2,1,0:T(8,128)S(1)}, f32[2,72,512]{2,1,0:T(8,128)S(1)}, u32[]{:S(2)}, u32[]{:S(2)}) collective-permute-start(f32[2,72,512]{2,1,0:T(8,128)S(1)} %pad_maximum_fusion.9), channel_id=1, source_target_pairs={{0,8},{4,12},{8,0},{12,4},{16,24},{20,28},{24,16},{28,20},{1,9},{5... | collective-permute-start | bytes 884744 | tf_op jit(solution)/shard_map/ppermute | solution.py:312
  60.5 1.3 %collective-permute-start.18 = (f32[2,72,512]{2,1,0:T(8,128)S(1)}, f32[2,72,512]{2,1,0:T(8,128)S(1)}, u32[]{:S(2)}, u32[]{:S(2)}) collective-permute-start(f32[2,72,512]{2,1,0:T(8,128)S(1)} %pad_maximum_fusion.10), channel_id=1, source_target_pairs={{0,16},{4,20},{8,24},{12,28},{16,0},{20,4},{24,8},{28,12},{1,17},{... | collective-permute-start | bytes 884744 | tf_op jit(solution)/shard_map/ppermute | solution.py:312
  61.8 0.1 collective-permute-done.21.refs_13_
  61.9 1.0 %collective-permute-start.22 = (f32[2,72,512]{2,1,0:T(8,128)S(1)}, f32[2,72,512]{2,1,0:T(8,128)S(1)}, u32[]{:S(2)}, u32[]{:S(2)}) collective-permute-start(f32[2,72,512]{2,1,0:T(8,128)S(1)} %pad_maximum_fusion.11), channel_id=1, source_target_pairs={{0,8},{4,12},{8,0},{12,4},{16,24},{20,28},{24,16},{28,20},{1,9},{5... | collective-permute-start | bytes 884744 | tf_op jit(solution)/shard_map/ppermute | solution.py:312
  62.9 4.7 %collective-permute-done.10.refs_2_ = f32[2,72,512]{2,1,0:T(8,128)S(1)} collective-permute-done((f32[2,72,512]{2,1,0:T(8,128)S(1)}, f32[2,72,512]{2,1,0:T(8,128)S(1)}, u32[]{:S(2)}, u32[]{:S(2)}) %collective-permute-start.10) | collective-permute-done | bytes 294944 | tf_op jit(solution)/shard_map/ppermute | solution.py:312
  67.7 5.4 %collective-permute-start.11 = (f32[4,72,512]{2,1,0:T(8,128)S(1)}, f32[4,72,512]{2,1,0:T(8,128)S(1)}, u32[]{:S(2)}, u32[]{:S(2)}) collective-permute-start(f32[4,72,512]{2,1,0:T(8,128)S(1)} %pad_maximum_fusion.4), channel_id=1, source_target_pairs={{0,4},{4,0},{8,12},{12,8},{16,20},{20,16},{24,28},{28,24},{1,5},{5... | collective-permute-start | bytes 1769480 | tf_op jit(solution)/shard_map/ppermute | solution.py:312
  73.2 0.1 collective-permute-start.15
  73.2 0.7 collective-permute-done.18.refs_10_
  74.0 0.0 copy-start
  74.0 0.0 copy-start.1
  74.0 0.0 copy-start.2
  74.0 3.0 %collective-permute-start.19 = (f32[4,72,512]{2,1,0:T(8,128)S(1)}, f32[4,72,512]{2,1,0:T(8,128)S(1)}, u32[]{:S(2)}, u32[]{:S(2)}) collective-permute-start(f32[4,72,512]{2,1,0:T(8,128)S(1)} %pad_maximum_fusion.6), channel_id=1, source_target_pairs={{0,4},{4,0},{8,12},{12,8},{16,20},{20,16},{24,28},{28,24},{1,5},{5... | collective-permute-start | bytes 1769480 | tf_op jit(solution)/shard_map/ppermute | solution.py:312
  77.0 0.0 collective-permute-done.22.refs_14_
  77.0 0.1 collective-permute-start.23
  77.1 1.5 %collective-permute-done.19.refs_11_ = f32[4,72,512]{2,1,0:T(8,128)S(1)} collective-permute-done((f32[4,72,512]{2,1,0:T(8,128)S(1)}, f32[4,72,512]{2,1,0:T(8,128)S(1)}, u32[]{:S(2)}, u32[]{:S(2)}) %collective-permute-start.19) | collective-permute-done | bytes 589856 | tf_op jit(solution)/shard_map/ppermute | solution.py:312
  78.6 0.8 %collective-permute-done.23.refs_15_ = f32[4,72,512]{2,1,0:T(8,128)S(1)} collective-permute-done((f32[4,72,512]{2,1,0:T(8,128)S(1)}, f32[4,72,512]{2,1,0:T(8,128)S(1)}, u32[]{:S(2)}, u32[]{:S(2)}) %collective-permute-start.23) | collective-permute-done | bytes 589856 | tf_op jit(solution)/shard_map/ppermute | solution.py:312
  79.5 4.4 %shard_map.81 = (f32[64,2048]{1,0:T(8,128)}, f32[8,64,256]{2,1,0:T(8,128)}) custom-call(s32[2]{0:T(128)S(1)} %copy-done.14, s32[8]{0:T(128)S(1)} %copy-done, s32[8]{0:T(128)S(1)} %copy-done.1, s32[8]{0:T(128)S(1)} %copy-done.2, f32[1,72,512]{2,1,0:T(8,128)S(1)} %bitcast.21, f32[1,72,512]{2,1,0:T(8,128)S(1)} %collective-permute-done.9.refs_1_, ...), custom_call_target="tpu_custom_call" | custom-call | flops 16777216 | bytes 8388608 | tf_op jit(solution)/shard_map/pallas_call | solution.py:448
  (44 shorter events, 0.4 us)
Async XLA Ops:
  0.7 4.8 %copy-start.13 = (s32[2]{0:T(128)}, s32[2]{0:T(128)S(1)}, u32[]{:S(2)}) copy-start(s32[2]{0:T(128)S(1)} %pad_add_fusion.place) | copy-start | bytes 28
  2.8 5.6 %collective-permute-start.3 = (f32[8,1024]{1,0:T(8,128)}, f32[8,1024]{1,0:T(8,128)S(1)}, u32[]{:S(2)}, u32[]{:S(2)}) collective-permute-start(f32[8,1024]{1,0:T(8,128)} %get-tuple-element.83), channel_id=1, source_target_pairs={{0,1},{1,0},{2,3},{3,2},{4,5},{5,4},{6,7},{7,6},{8,9},{9,8},{10,11... | collective-permute-start | bytes 98312 | tf_op jit(solution)/shard_map/ppermute | solution.py:312
  2.8 5.5 %collective-permute-start.4 = (f32[8,1024]{1,0:T(8,128)}, f32[8,1024]{1,0:T(8,128)S(1)}, u32[]{:S(2)}, u32[]{:S(2)}) collective-permute-start(f32[8,1024]{1,0:T(8,128)} %get-tuple-element.84), channel_id=1, source_target_pairs={{0,2},{1,3},{2,0},{3,1},{4,6},{5,7},{6,4},{7,5},{8,10},{9,11},{10,... | collective-permute-start | bytes 98312 | tf_op jit(solution)/shard_map/ppermute | solution.py:312
  5.3 3.6 %collective-permute-start.5 = (f32[8,1024]{1,0:T(8,128)}, f32[8,1024]{1,0:T(8,128)S(1)}, u32[]{:S(2)}, u32[]{:S(2)}) collective-permute-start(f32[8,1024]{1,0:T(8,128)} %get-tuple-element.85), channel_id=1, source_target_pairs={{0,3},{1,2},{2,1},{3,0},{4,7},{5,6},{6,5},{7,4},{8,11},{9,10},{10,... | collective-permute-start | bytes 98312 | tf_op jit(solution)/shard_map/ppermute | solution.py:312
  8.4 3.1 %copy-start.10 = (f32[8,1024]{1,0:T(8,128)}, f32[8,1024]{1,0:T(8,128)S(1)}, u32[]{:S(2)}) copy-start(f32[8,1024]{1,0:T(8,128)S(1)} %collective-permute-done.3) | copy-start | bytes 98308
  8.4 3.8 %copy-start.11 = (f32[8,1024]{1,0:T(8,128)}, f32[8,1024]{1,0:T(8,128)S(1)}, u32[]{:S(2)}) copy-start(f32[8,1024]{1,0:T(8,128)S(1)} %collective-permute-done.4) | copy-start | bytes 98308
  8.9 3.9 %copy-start.12 = (f32[8,1024]{1,0:T(8,128)}, f32[8,1024]{1,0:T(8,128)S(1)}, u32[]{:S(2)}) copy-start(f32[8,1024]{1,0:T(8,128)S(1)} %collective-permute-done.5) | copy-start | bytes 98308
  8.9 25.4 %collective-permute-start.6 = (f32[64,1024]{1,0:T(8,128)}, f32[64,1024]{1,0:T(8,128)S(1)}, u32[]{:S(2)}, u32[]{:S(2)}) collective-permute-start(f32[64,1024]{1,0:T(8,128)} %get-tuple-element.87), channel_id=1, source_target_pairs={{0,1},{1,0},{2,3},{3,2},{4,5},{5,4},{6,7},{7,6},{8,9},{9,8},{10,11... | collective-permute-start | bytes 786440 | tf_op jit(solution)/shard_map/ppermute | solution.py:312
  11.5 22.8 %collective-permute-start.7 = (f32[64,1024]{1,0:T(8,128)}, f32[64,1024]{1,0:T(8,128)S(1)}, u32[]{:S(2)}, u32[]{:S(2)}) collective-permute-start(f32[64,1024]{1,0:T(8,128)} %get-tuple-element.88), channel_id=1, source_target_pairs={{0,2},{1,3},{2,0},{3,1},{4,6},{5,7},{6,4},{7,5},{8,10},{9,11},{10,... | collective-permute-start | bytes 786440 | tf_op jit(solution)/shard_map/ppermute | solution.py:312
  12.2 22.1 %collective-permute-start.8 = (f32[64,1024]{1,0:T(8,128)}, f32[64,1024]{1,0:T(8,128)S(1)}, u32[]{:S(2)}, u32[]{:S(2)}) collective-permute-start(f32[64,1024]{1,0:T(8,128)} %get-tuple-element.89), channel_id=1, source_target_pairs={{0,3},{1,2},{2,1},{3,0},{4,7},{5,6},{6,5},{7,4},{8,11},{9,10},{10,... | collective-permute-start | bytes 786440 | tf_op jit(solution)/shard_map/ppermute | solution.py:312
  12.7 21.6 %copy-start.3 = (f32[64,1024]{1,0:T(8,128)S(1)}, f32[64,1024]{1,0:T(8,128)}, u32[]{:S(2)}) copy-start(f32[64,1024]{1,0:T(8,128)} %get-tuple-element.86.refs_0_) | copy-start | bytes 786436
  13.6 9.8 %copy-start.6 = (f32[1,4,8,1024]{3,2,1,0:T(8,128)}, f32[1,4,8,1024]{3,2,1,0:T(8,128)S(1)}, u32[]{:S(2)}) copy-start(f32[1,4,8,1024]{3,2,1,0:T(8,128)S(1)} %maximum_bitcast_fusion) | copy-start | bytes 393220 | tf_op jit(solution)/shard_map/cond
  13.6 1.3 %copy-start.16 = (f32[65]{0:T(128)S(1)}, f32[65]{0:T(128)}, u32[]{:S(2)}) copy-start(f32[65]{0:T(128)} %get-tuple-element.121) | copy-start | bytes 784 | tf_op jit(solution)/shard_map/cond
  13.6 4.2 %collective-permute-start = (f32[1,4,8,1024]{3,2,1,0:T(8,128)S(1)}, f32[1,4,8,1024]{3,2,1,0:T(8,128)S(1)}, u32[]{:S(2)}, u32[]{:S(2)}) collective-permute-start(f32[1,4,8,1024]{3,2,1,0:T(8,128)S(1)} %maximum_bitcast_fusion), channel_id=1, source_target_pairs={{0,8},{4,12},{8,0},{12,4},{16,24},{20,28},{24,16},{28,20},{1,9},{5... | collective-permute-start | bytes 393224 | tf_op jit(solution)/shard_map/cond/branch_1_fun/ppermute | solution.py:312
  17.8 5.6 %copy-start.4 = (f32[1,4,8,1024]{3,2,1,0:T(8,128)}, f32[1,4,8,1024]{3,2,1,0:T(8,128)S(1)}, u32[]{:S(2)}) copy-start(f32[1,4,8,1024]{3,2,1,0:T(8,128)S(1)} %collective-permute-done) | copy-start | bytes 393220 | tf_op jit(solution)/shard_map/cond
  17.8 5.6 %collective-permute-start.1 = (f32[2,4,8,1024]{3,2,1,0:T(8,128)S(1)}, f32[2,4,8,1024]{3,2,1,0:T(8,128)S(1)}, u32[]{:S(2)}, u32[]{:S(2)}) collective-permute-start(f32[2,4,8,1024]{3,2,1,0:T(8,128)S(1)} %pad_maximum_fusion.1), channel_id=1, source_target_pairs={{0,16},{4,20},{8,24},{12,28},{16,0},{20,4},{24,8},{28,12},{1,17},{... | collective-permute-start | bytes 786440 | tf_op jit(solution)/shard_map/cond/branch_1_fun/ppermute | solution.py:312
  23.4 0.7 copy-start.8
  24.1 10.2 %collective-permute-start.2 = (f32[4,4,8,1024]{3,2,1,0:T(8,128)S(1)}, f32[4,4,8,1024]{3,2,1,0:T(8,128)}, u32[]{:S(2)}, u32[]{:S(2)}) collective-permute-start(f32[4,4,8,1024]{3,2,1,0:T(8,128)S(1)} %pad_maximum_fusion), channel_id=1, source_target_pairs={{0,4},{4,0},{8,12},{12,8},{16,20},{20,16},{24,28},{28,24},{1,5},{5... | collective-permute-start | bytes 1572872 | tf_op jit(solution)/shard_map/cond/branch_1_fun/ppermute | solution.py:312
  28.8 0.7 copy-start.15
  29.5 4.8 %copy-start.5 = (f32[1,4,8,1024]{3,2,1,0:T(8,128)S(1)}, f32[1,4,8,1024]{3,2,1,0:T(8,128)}, u32[]{:S(2)}) copy-start(f32[1,4,8,1024]{3,2,1,0:T(8,128)} %copy-done.4) | copy-start | bytes 393220 | tf_op jit(solution)/shard_map/cond
  29.5 4.8 %copy-start.7 = (f32[1,4,8,1024]{3,2,1,0:T(8,128)S(1)}, f32[1,4,8,1024]{3,2,1,0:T(8,128)}, u32[]{:S(2)}) copy-start(f32[1,4,8,1024]{3,2,1,0:T(8,128)} %copy-done.6) | copy-start | bytes 393220 | tf_op jit(solution)/shard_map/cond
  29.5 4.8 %copy-start.9 = (f32[2,4,8,1024]{3,2,1,0:T(8,128)S(1)}, f32[2,4,8,1024]{3,2,1,0:T(8,128)}, u32[]{:S(2)}) copy-start(f32[2,4,8,1024]{3,2,1,0:T(8,128)} %copy-done.8) | copy-start | bytes 786436 | tf_op jit(solution)/shard_map/cond
  34.3 0.7 copy-start.14
  41.7 7.5 %collective-permute-start.12 = (f32[72,512]{1,0:T(8,128)S(1)}, f32[72,512]{1,0:T(8,128)S(1)}, u32[]{:S(2)}, u32[]{:S(2)}) collective-permute-start(f32[72,512]{1,0:T(8,128)S(1)} %get-tuple-element.115), channel_id=1, source_target_pairs={{0,1},{1,0},{2,3},{3,2},{4,5},{5,4},{6,7},{7,6},{8,9},{9,8},{10,11... | collective-permute-start | bytes 442376 | tf_op jit(solution)/shard_map/ppermute | solution.py:312
  44.3 6.2 %collective-permute-start.16 = (f32[72,512]{1,0:T(8,128)S(1)}, f32[72,512]{1,0:T(8,128)S(1)}, u32[]{:S(2)}, u32[]{:S(2)}) collective-permute-start(f32[72,512]{1,0:T(8,128)S(1)} %get-tuple-element.116), channel_id=1, source_target_pairs={{0,2},{1,3},{2,0},{3,1},{4,6},{5,7},{6,4},{7,5},{8,10},{9,11},{10,... | collective-permute-start | bytes 442376 | tf_op jit(solution)/shard_map/ppermute | solution.py:312
  44.3 13.6 %collective-permute-start.20 = (f32[72,512]{1,0:T(8,128)S(1)}, f32[72,512]{1,0:T(8,128)S(1)}, u32[]{:S(2)}, u32[]{:S(2)}) collective-permute-start(f32[72,512]{1,0:T(8,128)S(1)} %get-tuple-element.117), channel_id=1, source_target_pairs={{0,3},{1,2},{2,1},{3,0},{4,7},{5,6},{6,5},{7,4},{8,11},{9,10},{10,... | collective-permute-start | bytes 442376 | tf_op jit(solution)/shard_map/ppermute | solution.py:312
  45.6 13.3 %collective-permute-start.9 = (f32[1,72,512]{2,1,0:T(8,128)S(1)}, f32[1,72,512]{2,1,0:T(8,128)S(1)}, u32[]{:S(2)}, u32[]{:S(2)}) collective-permute-start(f32[1,72,512]{2,1,0:T(8,128)S(1)} %bitcast.18), channel_id=1, source_target_pairs={{0,8},{4,12},{8,0},{12,4},{16,24},{20,28},{24,16},{28,20},{1,9},{5... | collective-permute-start | bytes 442376 | tf_op jit(solution)/shard_map/ppermute | solution.py:312
  49.1 10.3 %collective-permute-start.13 = (f32[1,72,512]{2,1,0:T(8,128)S(1)}, f32[1,72,512]{2,1,0:T(8,128)S(1)}, u32[]{:S(2)}, u32[]{:S(2)}) collective-permute-start(f32[1,72,512]{2,1,0:T(8,128)S(1)} %bitcast.22), channel_id=1, source_target_pairs={{0,16},{4,20},{8,24},{12,28},{16,0},{20,4},{24,8},{28,12},{1,17},{... | collective-permute-start | bytes 442376 | tf_op jit(solution)/shard_map/ppermute | solution.py:312
  50.5 10.0 %collective-permute-start.17 = (f32[1,72,512]{2,1,0:T(8,128)S(1)}, f32[1,72,512]{2,1,0:T(8,128)S(1)}, u32[]{:S(2)}, u32[]{:S(2)}) collective-permute-start(f32[1,72,512]{2,1,0:T(8,128)S(1)} %bitcast.26), channel_id=1, source_target_pairs={{0,8},{4,12},{8,0},{12,4},{16,24},{20,28},{24,16},{28,20},{1,9},{5... | collective-permute-start | bytes 442376 | tf_op jit(solution)/shard_map/ppermute | solution.py:312
  57.9 4.0 %collective-permute-start.21 = (f32[1,72,512]{2,1,0:T(8,128)S(1)}, f32[1,72,512]{2,1,0:T(8,128)S(1)}, u32[]{:S(2)}, u32[]{:S(2)}) collective-permute-start(f32[1,72,512]{2,1,0:T(8,128)S(1)} %bitcast.30), channel_id=1, source_target_pairs={{0,16},{4,20},{8,24},{12,28},{16,0},{20,4},{24,8},{28,12},{1,17},{... | collective-permute-start | bytes 442376 | tf_op jit(solution)/shard_map/ppermute | solution.py:312
  58.9 8.7 %collective-permute-start.10 = (f32[2,72,512]{2,1,0:T(8,128)S(1)}, f32[2,72,512]{2,1,0:T(8,128)S(1)}, u32[]{:S(2)}, u32[]{:S(2)}) collective-permute-start(f32[2,72,512]{2,1,0:T(8,128)S(1)} %pad_maximum_fusion.8), channel_id=1, source_target_pairs={{0,16},{4,20},{8,24},{12,28},{16,0},{20,4},{24,8},{28,12},{1,17},{... | collective-permute-start | bytes 884744 | tf_op jit(solution)/shard_map/ppermute | solution.py:312
  59.5 13.6 %collective-permute-start.14 = (f32[2,72,512]{2,1,0:T(8,128)S(1)}, f32[2,72,512]{2,1,0:T(8,128)S(1)}, u32[]{:S(2)}, u32[]{:S(2)}) collective-permute-start(f32[2,72,512]{2,1,0:T(8,128)S(1)} %pad_maximum_fusion.9), channel_id=1, source_target_pairs={{0,8},{4,12},{8,0},{12,4},{16,24},{20,28},{24,16},{28,20},{1,9},{5... | collective-permute-start | bytes 884744 | tf_op jit(solution)/shard_map/ppermute | solution.py:312
  60.5 13.4 %collective-permute-start.18 = (f32[2,72,512]{2,1,0:T(8,128)S(1)}, f32[2,72,512]{2,1,0:T(8,128)S(1)}, u32[]{:S(2)}, u32[]{:S(2)}) collective-permute-start(f32[2,72,512]{2,1,0:T(8,128)S(1)} %pad_maximum_fusion.10), channel_id=1, source_target_pairs={{0,16},{4,20},{8,24},{12,28},{16,0},{20,4},{24,8},{28,12},{1,17},{... | collective-permute-start | bytes 884744 | tf_op jit(solution)/shard_map/ppermute | solution.py:312
  61.9 15.0 %collective-permute-start.22 = (f32[2,72,512]{2,1,0:T(8,128)S(1)}, f32[2,72,512]{2,1,0:T(8,128)S(1)}, u32[]{:S(2)}, u32[]{:S(2)}) collective-permute-start(f32[2,72,512]{2,1,0:T(8,128)S(1)} %pad_maximum_fusion.11), channel_id=1, source_target_pairs={{0,8},{4,12},{8,0},{12,4},{16,24},{20,28},{24,16},{28,20},{1,9},{5... | collective-permute-start | bytes 884744 | tf_op jit(solution)/shard_map/ppermute | solution.py:312
  67.7 9.5 %collective-permute-start.11 = (f32[4,72,512]{2,1,0:T(8,128)S(1)}, f32[4,72,512]{2,1,0:T(8,128)S(1)}, u32[]{:S(2)}, u32[]{:S(2)}) collective-permute-start(f32[4,72,512]{2,1,0:T(8,128)S(1)} %pad_maximum_fusion.4), channel_id=1, source_target_pairs={{0,4},{4,0},{8,12},{12,8},{16,20},{20,16},{24,28},{28,24},{1,5},{5... | collective-permute-start | bytes 1769480 | tf_op jit(solution)/shard_map/ppermute | solution.py:312
  73.2 4.0 %collective-permute-start.15 = (f32[4,72,512]{2,1,0:T(8,128)S(1)}, f32[4,72,512]{2,1,0:T(8,128)S(1)}, u32[]{:S(2)}, u32[]{:S(2)}) collective-permute-start(f32[4,72,512]{2,1,0:T(8,128)S(1)} %pad_maximum_fusion.5), channel_id=1, source_target_pairs={{0,4},{4,0},{8,12},{12,8},{16,20},{20,16},{24,28},{28,24},{1,5},{5... | collective-permute-start | bytes 1769480 | tf_op jit(solution)/shard_map/ppermute | solution.py:312
  74.0 5.5 %copy-start = (s32[8]{0:T(128)S(1)}, s32[8]{0:T(128)}, u32[]{:S(2)}) copy-start(s32[8]{0:T(128)} %pair_one.1) | copy-start | bytes 100
  74.0 5.5 %copy-start.1 = (s32[8]{0:T(128)S(1)}, s32[8]{0:T(128)}, u32[]{:S(2)}) copy-start(s32[8]{0:T(128)} %pair_two.1) | copy-start | bytes 100
  74.0 5.5 %copy-start.2 = (s32[8]{0:T(128)S(1)}, s32[8]{0:T(128)}, u32[]{:S(2)}) copy-start(s32[8]{0:T(128)} %owner.1) | copy-start | bytes 100
  74.0 4.6 %collective-permute-start.19 = (f32[4,72,512]{2,1,0:T(8,128)S(1)}, f32[4,72,512]{2,1,0:T(8,128)S(1)}, u32[]{:S(2)}, u32[]{:S(2)}) collective-permute-start(f32[4,72,512]{2,1,0:T(8,128)S(1)} %pad_maximum_fusion.6), channel_id=1, source_target_pairs={{0,4},{4,0},{8,12},{12,8},{16,20},{20,16},{24,28},{28,24},{1,5},{5... | collective-permute-start | bytes 1769480 | tf_op jit(solution)/shard_map/ppermute | solution.py:312
  77.0 2.4 %collective-permute-start.23 = (f32[4,72,512]{2,1,0:T(8,128)S(1)}, f32[4,72,512]{2,1,0:T(8,128)S(1)}, u32[]{:S(2)}, u32[]{:S(2)}) collective-permute-start(f32[4,72,512]{2,1,0:T(8,128)S(1)} %pad_maximum_fusion.7), channel_id=1, source_target_pairs={{0,4},{4,0},{8,12},{12,8},{16,20},{20,16},{24,28},{28,24},{1,5},{5... | collective-permute-start | bytes 1769480 | tf_op jit(solution)/shard_map/ppermute | solution.py:312

commit v3 on v2

--- a/solution.py
+++ b/solution.py
@@ -46,6 +46,7 @@
         self.slab = row_local + 2 * rim
         self.sharers = min(sim_devices, row_local // 8)
         self.share_rows = row_local // self.sharers
+        self.head = row_local // 2
         self.length = max(2 * wide, -(-self.rows // lane) * lane)
         inner = range(lane, self.width - lane, wide)
         blocks = [(0, lane)] + [(a, min(a + wide, self.width - lane)) for a in inner]
@@ -61,58 +62,65 @@
         return [i for i, (a, b) in enumerate(self.blocks) if b > low and a < self.width - low]
 
 
-def share_kernel(plan, place, weight, *refs):
-    parts, padded, sem = refs[: plan.row_devices], refs[-2], refs[-1]
-    row = pl.multiple_of(lax.rem(place[1], plan.sharers) * plan.share_rows, plan.share_rows)
-    source = weight.at[pl.ds(row, plan.share_rows)]
-    copy = pltpu.make_async_copy(source, padded.at[:, pl.ds(plan.halo, plan.columns)], sem)
-    copy.start()
-    zeros = jnp.zeros((plan.share_rows, plan.halo), jnp.float32)
-    padded[:, : plan.halo] = zeros
-    padded[:, plan.halo + plan.columns :] = zeros
-    copy.wait()
-    for step, part in enumerate(parts):
-        column = pl.multiple_of((place[0] ^ step) * plan.share, lane)
-        part[...] = padded[:, pl.ds(column, plan.width)]
-
-
-def weighted_kernel(plan, place, maps, weight, *refs):
-    pieces = refs[: plan.row_devices]
-    padded, weights, given, sems = refs[plan.row_devices :]
+def piece_kernel(plan, place, maps, weight, *refs):
+    count = plan.row_devices
+    heads, tails = refs[:count], refs[count : 2 * count]
+    product, weights, given, sems = refs[2 * count :]
     chunk = plan.row_local // loads
+    inner = slice(plan.halo, plan.halo + plan.columns)
     copies = []
     for number in range(loads):
         rows = pl.ds(number * chunk, chunk)
         copies.append((
-            pltpu.make_async_copy(weight.at[rows], weights.at[rows], sems.at[0, number]),
+            pltpu.make_async_copy(weight.at[rows], weights.at[rows, inner], sems.at[0, number]),
             pltpu.make_async_copy(maps.at[rows], given.at[rows], sems.at[1, number]),
         ))
         for copy in copies[-1]:
             copy.start()
     zeros = jnp.zeros((plan.row_local, plan.halo), jnp.float32)
-    padded[:, : plan.halo] = zeros
-    padded[:, plan.halo + plan.columns :] = zeros
+    for target in (product, weights):
+        target[:, : plan.halo] = zeros
+        target[:, plan.halo + plan.columns :] = zeros
     for number in range(loads):
         for copy in copies[number]:
             copy.wait()
         rows = slice(number * chunk, (number + 1) * chunk)
-        padded[rows, plan.halo : plan.halo + plan.columns] = weights[rows] * given[rows]
-        for step, piece in enumerate(pieces):
-            column = pl.multiple_of((place[0] ^ step) * plan.share, lane)
-            piece[rows] = padded[rows, pl.ds(column, plan.width)]
+        product[rows, inner] = weights[rows, inner] * given[rows]
+    row = pl.multiple_of(lax.rem(place[1], plan.sharers) * plan.share_rows, plan.share_rows)
+    for step in range(count):
+        span = pl.ds(pl.multiple_of((place[0] ^ step) * plan.share, lane), plan.width)
+        heads[step][: plan.share_rows] = weights[pl.ds(row, plan.share_rows), span]
+        heads[step][plan.share_rows :] = product[: plan.head, span]
+        tails[step][...] = product[plan.head :, span]
 
 
 def band(plan, taps, rows, columns, offset):
-    spread = jnp.broadcast_to(taps[...], (rows, plan.length))
     if offset % plan.length:
-        spread = pltpu.roll(spread, offset % plan.length, 1)
+        taps = pltpu.roll(taps, offset % plan.length, 1)
+    spread = jnp.broadcast_to(taps[:1], (rows, plan.length))
     rolled = pltpu.roll(spread, 0, 1, stride=1, stride_axis=0)[:, :columns]
     row = lax.broadcasted_iota(jnp.int32, (rows, columns), 0)
     column = lax.broadcasted_iota(jnp.int32, (rows, columns), 1)
     return jnp.where(jnp.abs(column - row - offset) <= plan.margin, rolled, 0.0)
 
 
-def table_kernel(plan, place, taps, reverse, *refs):
+def table_kernel(plan, place, beam, *refs):
+    refs, line = refs[:-1], refs[-1]
+    count = beam.shape[1]
+    line[...] = jnp.zeros(line.shape, jnp.float32)
+    line[:1, :count] = beam[...]
+    kernel = line[...]
+    kernel = kernel / jnp.sum(kernel[:1], axis=1, keepdims=True)
+    size = kernel.shape[1]
+    row = lax.broadcasted_iota(jnp.int32, (size, size), 0)
+    column = lax.broadcasted_iota(jnp.int32, (size, size), 1)
+    mirror = (row + column == count - 1).astype(jnp.float32)
+    blank = jnp.zeros((kernel.shape[0], plan.length - size), jnp.float32)
+
+    def centred(values):
+        return pltpu.roll(jnp.concatenate([values, blank], axis=1), plan.length - plan.margin, 1)
+
+    taps, reverse = centred(kernel), centred(jnp.dot(kernel, mirror, precision=exact))
     tables = list(refs)
 
     def put(value):
@@ -153,20 +161,19 @@
         del refs[:number]
         return taken
 
-    pieces = take(plan.row_devices)
+    heads, tails = take(plan.row_devices), take(plan.row_devices)
     parts = take(len(sharers))
     square, final = take(2), take(2)
     bands = [take(2) for _ in plan.blocks]
     last = take(2)
     outs = take(plan.row_devices)
     seen, weight, image, total, field, high, low, mid_high, mid_low = refs
-    for step, piece in enumerate(pieces):
+    for step in range(plan.row_devices):
         row = pl.multiple_of((place[0] ^ step) * plan.row_local, plan.row_local)
-        value = piece[...]
-        seen[pl.ds(row, plan.row_local), :] = value
-        a, b = split(value)
-        high[pl.ds(row, plan.row_local), :] = a
-        low[pl.ds(row, plan.row_local), :] = b
+        for first, value in ((0, heads[step][plan.share_rows :]), (plan.head, tails[step][...])):
+            rows = pl.ds(row + first, value.shape[0])
+            seen[rows, :] = value
+            high[rows, :], low[rows, :] = split(value)
     for part, owners in zip(parts, sharers):
         for slot, offset in enumerate(owners):
             for step in range(plan.row_devices):
@@ -344,6 +351,9 @@
     smem = pl.BlockSpec(memory_space=pltpu.SMEM)
     far = pl.BlockSpec(memory_space=pltpu.HBM)
 
+    def pinned(value):
+        return pltpu.with_memory_space_constraint(value, pltpu.HBM)
+
     def f32(*shape):
         return jax.ShapeDtypeStruct(shape, jnp.float32)
 
@@ -351,59 +361,49 @@
         return jax.ShapeDtypeStruct(shape, jnp.bfloat16)
 
     cells = row_local * columns
-    parts = call(
-        functools.partial(share_kernel, plan),
-        [f32(plan.share_rows, plan.width)] * row_devices,
-        [smem, far],
-        [pltpu.VMEM((plan.share_rows, columns + 2 * plan.halo), jnp.float32), pltpu.SemaphoreType.DMA],
-        0,
-        1 << 18,
-        limit=60,
-    )(place, weight)
-    pieces = call(
-        functools.partial(weighted_kernel, plan),
-        [f32(row_local, plan.width)] * row_devices,
+    near = plan.share_rows + plan.head
+    made = call(
+        functools.partial(piece_kernel, plan),
+        [f32(near, plan.width)] * row_devices + [f32(row_local - plan.head, plan.width)] * row_devices,
         [smem, far, far],
-        [pltpu.VMEM((row_local, columns + 2 * plan.halo), jnp.float32)]
-        + [pltpu.VMEM((row_local, columns), jnp.float32)] * 2
-        + [pltpu.SemaphoreType.DMA((2, loads))],
+        [pltpu.VMEM((row_local, columns + 2 * plan.halo), jnp.float32)] * 2
+        + [pltpu.VMEM((row_local, columns), jnp.float32), pltpu.SemaphoreType.DMA((2, loads))],
         cells,
         16 * cells,
-        limit=60,
-    )(place, maps.reshape(row_local, columns), weight)
-    parts = [parts[0]] + [exchange(parts[d], "rows", d) for d in range(1, row_devices)]
-    pieces, parts = lax.optimization_barrier((pieces, parts))
-    pieces = [pieces[0]] + [exchange(pieces[d], "rows", d) for d in range(1, row_devices)]
+    )(place, pinned(maps.reshape(row_local, columns)), pinned(weight))
+    heads, tails = made[:row_devices], made[row_devices:]
+    heads = [heads[0]] + [exchange(heads[d], "rows", d) for d in range(1, row_devices)]
+    tails = [tails[0]] + [exchange(tails[d], "rows", d) for d in range(1, row_devices)]
     sharers = []
     shapes = [(plan.rows, plan.rows), (row_devices * plan.slab, plan.rows)]
     for block in plan.blocks + plan.out_blocks[:1]:
         low, high = plan.window(block)
         shapes.append((high - low, block[1] - block[0]))
 
-    def prepare(parts, beam):
-        bits = [1 << i for i in range(1, plan.sharers.bit_length() - 1)] + [1]
-        arrays, offsets = gather(jnp.stack(parts), "sims", bits)
-        sharers[:] = offsets
-        kernel = beam / jnp.sum(beam)
-        blank = jnp.zeros((plan.length - taps,), jnp.float32)
-        forward = jnp.roll(jnp.concatenate([kernel, blank]), -plan.margin)[None]
-        backward = jnp.roll(jnp.concatenate([kernel[::-1], blank]), -plan.margin)[None]
+    def prepare(heads, beam):
+        first = jnp.stack([head[: plan.share_rows] for head in heads])[None]
+        found = {0: first}
+        for bit in [1 << i for i in range(1, plan.sharers.bit_length() - 1)]:
+            found |= {offset | bit: exchange(value, "sims", bit) for offset, value in found.items()}
+        across = list(found)
         tables = call(
             functools.partial(table_kernel, plan),
             [b16(*shape) for shape in shapes for _ in range(2)],
-            [smem, vmem, vmem],
-            [],
+            [smem, vmem],
+            [pltpu.VMEM((8, lane), jnp.float32)],
             1 << 32,
             1 << 23,
-        )(place, forward, backward)
-        return arrays, tables
-
-    made = jax.eval_shape(prepare, parts, beam)
+        )(place, beam[None])
+        sharers[:] = [[offset] for offset in across] + [[offset ^ 1 for offset in across]]
+        whole, tables = lax.optimization_barrier((jnp.concatenate(list(found.values())), tables))
+        return [*found.values(), exchange(whole, "sims", 1)], tables
+
+    made = jax.eval_shape(prepare, heads, beam)
     parts, tables = lax.cond(
         lax.axis_index("rows") < row_devices,
         prepare,
-        lambda parts, beam: jax.tree.map(lambda x: jnp.zeros(x.shape, x.dtype), made),
-        parts,
+        lambda heads, beam: jax.tree.map(lambda x: jnp.zeros(x.shape, x.dtype), made),
+        heads,
         beam,
     )
 
@@ -412,14 +412,14 @@
     filtered = call(
         functools.partial(filter_kernel, plan, sharers),
         [f32(plan.slab, plan.share)] * row_devices,
-        [smem] + [vmem] * len(pieces) + [vmem] * (len(parts) + len(tables)),
+        [smem] + [vmem] * (2 * row_devices + len(parts) + len(tables)),
         [pltpu.VMEM(full, jnp.float32)] * 4
         + [pltpu.VMEM((row_devices * plan.slab, plan.share), jnp.float32)]
         + [pltpu.VMEM(full, jnp.bfloat16)] * 2
         + [pltpu.VMEM(tall, jnp.bfloat16)] * 2,
         1 << 33,
         1 << 23,
-    )(place, *pieces, *parts, *tables)
+    )(place, *heads, *tails, *parts, *tables)
 
     moved = [filtered[0]] + [exchange(filtered[step], "rows", step) for step in range(1, row_devices)]
     bits = [1 << i for i in range(1, sim_devices.bit_length() - 1)]

time: 84.2 us -> 93.7 us (1.11)
  the two profiles are of different devices: /device:TPU:9 before, /device:TPU:0 now
where the time goes in v3:
time: 93.7 us; the launch traced here: 92.4 us
  starting transfers between devices  41.5 us (44%)
  waiting for transfers between devices  28.1 us (30%)
  Pallas kernels  18.1 us (19%)
  other arithmetic  2.1 us (2%)
  local copies, waits for them, and re-layouts  1.53 us (2%)
  between operations  0.94 us (1%)
    ppermute x25, starting transfers between devices, exchange(): return lax.ppermute(value, axis, [(i, i ^ offset) for i in range(count)])  41.5 us
    ppermute x25, waiting for transfers between devices, exchange(): return lax.ppermute(value, axis, [(i, i ^ offset) for i in range(count)])  28.1 us
    pallas_call x1, Pallas kernels, body(): call(functools.partial(filter_kernel, plan, sharers), [f32(plan.slab, pla...  6.81 us
    pallas_call x1, Pallas kernels, body(): call(functools.partial(estimate_kernel, plan, holders, fused), outs, [sme...  4.38 us
    pallas_call x1, Pallas kernels, prepare(): call(functools.partial(table_kernel, plan), [b16(*shape) for shape in sha...  4.29 us
    pallas_call x1, Pallas kernels, body(): call(functools.partial(piece_kernel, plan), [f32(near, plan.width)] * row...  2.65 us
  transfers between devices with their start and end apart: 25, of which 12 were waited for; matrix products, arithmetic and copies ran while one was open for 3% of the time, Pallas kernels for 5%

profile of v3, /device:TPU:0, one launch (start us, length us, event | category | flops | bytes accessed | tf_op | source)
XLA Modules:
  0.0 92.4 jit_solution(5452180671424317692)
XLA Ops:
  0.6 0.1 pad_add_fusion.place
  0.7 2.6 %shard_map.78 = (f32[40,1024]{1,0:T(8,128)}, f32[40,1024]{1,0:T(8,128)S(1)}, f32[40,1024]{1,0:T(8,128)S(1)}, f32[40,1024]{1,0:T(8,128)S(1)}, f32[32,1024]{1,0:T(...) custom-call(s32[2]{0:T(128)S(1)} %pad_add_fusion.place, f32[64,2048]{1,0:T(8,128)} %bitcast.35, ...), custom_call_target="tpu_custom_call" | custom-call | flops 131072 | bytes 2097152 | tf_op jit(solution)/shard_map/pallas_call | solution.py:365
  3.4 3.1 %collective-permute-start.4 = (f32[40,1024]{1,0:T(8,128)S(1)}, f32[40,1024]{1,0:T(8,128)}, u32[]{:S(2)}, u32[]{:S(2)}) collective-permute-start(f32[40,1024]{1,0:T(8,128)S(1)} %get-tuple-element.89), channel_id=1, source_target_pairs={{0,1},{1,0},{2,3},{3,2},{4,5},{5,4},{6,7},{7,6},{8,9},{9,8},{10,11... | collective-permute-start | bytes 491528 | tf_op jit(solution)/shard_map/ppermute | solution.py:319
  6.5 2.6 %collective-permute-start.5 = (f32[40,1024]{1,0:T(8,128)S(1)}, f32[40,1024]{1,0:T(8,128)S(1)}, u32[]{:S(2)}, u32[]{:S(2)}) collective-permute-start(f32[40,1024]{1,0:T(8,128)S(1)} %get-tuple-element.90), channel_id=1, source_target_pairs={{0,2},{1,3},{2,0},{3,1},{4,6},{5,7},{6,4},{7,5},{8,10},{9,11},{10,... | collective-permute-start | bytes 491528 | tf_op jit(solution)/shard_map/ppermute | solution.py:319
  9.0 0.0 collective-permute-start.6
  9.0 0.9 collective-permute-start.7
  9.9 3.5 %collective-permute-start.8 = (f32[32,1024]{1,0:T(8,128)S(1)}, f32[32,1024]{1,0:T(8,128)S(1)}, u32[]{:S(2)}, u32[]{:S(2)}) collective-permute-start(f32[32,1024]{1,0:T(8,128)S(1)} %get-tuple-element.94), channel_id=1, source_target_pairs={{0,2},{1,3},{2,0},{3,1},{4,6},{5,7},{6,4},{7,5},{8,10},{9,11},{10,... | collective-permute-start | bytes 393224 | tf_op jit(solution)/shard_map/ppermute | solution.py:319
  13.4 0.9 collective-permute-done.4.refs_1_
  14.3 4.8 %collective-permute-start.9 = (f32[32,1024]{1,0:T(8,128)S(1)}, f32[32,1024]{1,0:T(8,128)S(1)}, u32[]{:S(2)}, u32[]{:S(2)}) collective-permute-start(f32[32,1024]{1,0:T(8,128)S(1)} %get-tuple-element.95), channel_id=1, source_target_pairs={{0,3},{1,2},{2,1},{3,0},{4,7},{5,6},{6,5},{7,4},{8,11},{9,10},{10,... | collective-permute-start | bytes 393224 | tf_op jit(solution)/shard_map/ppermute | solution.py:319
  19.1 2.4 %collective-permute-done.5.refs_2_ = f32[40,1024]{1,0:T(8,128)S(1)} collective-permute-done((f32[40,1024]{1,0:T(8,128)S(1)}, f32[40,1024]{1,0:T(8,128)S(1)}, u32[]{:S(2)}, u32[]{:S(2)}) %collective-permute-start.5) | collective-permute-done | bytes 163872 | tf_op jit(solution)/shard_map/ppermute | solution.py:319
  21.5 0.0 collective-permute-done.6.refs_3_
  21.5 0.7 copy-done.3
  22.2 0.1 copy-done.4
  22.2 15.8 %conditional.1 = (f32[1,4,8,1024]{3,2,1,0:T(8,128)}, f32[1,4,8,1024]{3,2,1,0:T(8,128)}, f32[1,4,8,1024]{3,2,1,0:T(8,128)}, f32[1,4,8,1024]{3,2,1,0:T(8,128)}, f3...) conditional(s32[]{:T(128)} %convert_element_type.3, () %tuple.17, ...), branch_computations={%region_0.0_spmd, %region_1.0_spmd} | conditional | flops 4295458816 | bytes 13631816 | solution.py:402
  22.2 0.8 slice_bitcast_fusion.2
  23.0 0.6 maximum_bitcast_fusion
  23.7 1.5 %collective-permute-start = (f32[1,4,8,1024]{3,2,1,0:T(8,128)}, f32[1,4,8,1024]{3,2,1,0:T(8,128)}, u32[]{:S(2)}, u32[]{:S(2)}) collective-permute-start(f32[1,4,8,1024]{3,2,1,0:T(8,128)} %maximum_bitcast_fusion), channel_id=1, source_target_pairs={{0,8},{4,12},{8,0},{12,4},{16,24},{20,28},{24,16},{28,20},{1,9},{5... | collective-permute-start | bytes 393224 | tf_op jit(solution)/shard_map/cond/branch_1_fun/ppermute | solution.py:319
  25.2 1.5 %collective-permute-start.1 = (f32[1,4,8,1024]{3,2,1,0:T(8,128)}, f32[1,4,8,1024]{3,2,1,0:T(8,128)}, u32[]{:S(2)}, u32[]{:S(2)}) collective-permute-start(f32[1,4,8,1024]{3,2,1,0:T(8,128)} %maximum_bitcast_fusion), channel_id=1, source_target_pairs={{0,16},{4,20},{8,24},{12,28},{16,0},{20,4},{24,8},{28,12},{1,17},{... | collective-permute-start | bytes 393224 | tf_op jit(solution)/shard_map/cond/branch_1_fun/ppermute | solution.py:319
  26.7 2.3 %collective-permute-done = f32[1,4,8,1024]{3,2,1,0:T(8,128)} collective-permute-done((f32[1,4,8,1024]{3,2,1,0:T(8,128)}, f32[1,4,8,1024]{3,2,1,0:T(8,128)}, u32[]{:S(2)}, u32[]{:S(2)}) %collective-permute-start) | collective-permute-done | bytes 131104 | tf_op jit(solution)/shard_map/cond/branch_1_fun/ppermute | solution.py:319
  29.0 1.5 %collective-permute-start.2 = (f32[1,4,8,1024]{3,2,1,0:T(8,128)}, f32[1,4,8,1024]{3,2,1,0:T(8,128)}, u32[]{:S(2)}, u32[]{:S(2)}) collective-permute-start(f32[1,4,8,1024]{3,2,1,0:T(8,128)} %collective-permute-done), channel_id=1, source_target_pairs={{0,16},{4,20},{8,24},{12,28},{16,0},{20,4},{24,8},{28,12},{1,17},{... | collective-permute-start | bytes 393224 | tf_op jit(solution)/shard_map/cond/branch_1_fun/ppermute | solution.py:319
  30.5 4.3 %branch_1_fun.1 = (bf16[256,256]{1,0:T(8,128)(2,1)S(1)}, bf16[256,256]{1,0:T(8,128)(2,1)S(1)}, bf16[288,256]{1,0:T(8,128)(2,1)S(1)}, bf16[288,256]{1,0:T(8,128)(...) custom-call(s32[2]{0:T(128)S(1)} %get-tuple-element.16.place, ...), custom_call_target="tpu_custom_call" | custom-call | flops 4294967296 | bytes 8388608 | tf_op jit(solution)/shard_map/cond/branch_1_fun/pallas_call | solution.py:389
  34.8 0.0 collective-permute-done.1
  34.8 0.0 collective-permute-done.2
  34.8 1.1 %pad_maximum_fusion = f32[4,4,8,1024]{3,2,1,0:T(8,128)S(1)} fusion(f32[1,4,8,1024]{3,2,1,0:T(8,128)} %collective-permute-done.2, f32[1,4,8,1024]{3,2,1,0:T(8,128)} %collective-permute-done.1, f32[1,4,8,1024]{3,2,1,0:T(8,128)} %collective-permute-done, f32[1,4,8,1024]{3,2,1,0:T(8,128)} %maximum_bitcast_fusion), kind=kLoop, calls=%fused_computation | loop fusion | flops 393216 | bytes 1048576 | tf_op jit(solution)/shard_map/cond/branch_1_fun/concatenate | solution.py:398
  35.9 0.1 collective-permute-start.3
  36.0 2.0 %collective-permute-done.3 = f32[4,4,8,1024]{3,2,1,0:T(8,128)} collective-permute-done((f32[4,4,8,1024]{3,2,1,0:T(8,128)S(1)}, f32[4,4,8,1024]{3,2,1,0:T(8,128)}, u32[]{:S(2)}, u32[]{:S(2)}) %collective-permute-start.3) | collective-permute-done | bytes 524320 | tf_op jit(solution)/shard_map/cond/branch_1_fun/ppermute | solution.py:319
  38.0 0.0 collective-permute-done.7.refs_5_
  38.0 0.0 collective-permute-done.8.refs_6_
  38.0 0.0 collective-permute-done.9.refs_7_
  38.1 6.8 %shard_map.79 = (f32[72,512]{1,0:T(8,128)S(1)}, f32[72,512]{1,0:T(8,128)S(1)}, f32[72,512]{1,0:T(8,128)S(1)}, f32[72,512]{1,0:T(8,128)S(1)}) custom-call(s32[2]{0:T(128)S(1)} %pad_add_fusion.place, f32[40,1024]{1,0:T(8,128)} %get-tuple-element.88.refs_0_, f32[40,1024]{1,0:T(8,128)} %collective-permute-done.4.refs_1_, f32[40,1024]{1,0:T(8,128)} %copy-done.3, ...), custom_call_target="tpu_custom_call" | custom-call | flops 8589934592 | bytes 8388608 | tf_op jit(solution)/shard_map/pallas_call | solution.py:412
  44.9 9.7 %collective-permute-start.13 = (f32[72,512]{1,0:T(8,128)S(1)}, f32[72,512]{1,0:T(8,128)S(1)}, u32[]{:S(2)}, u32[]{:S(2)}) collective-permute-start(f32[72,512]{1,0:T(8,128)S(1)} %get-tuple-element.118), channel_id=1, source_target_pairs={{0,1},{1,0},{2,3},{3,2},{4,5},{5,4},{6,7},{7,6},{8,9},{9,8},{10,11... | collective-permute-start | bytes 442376 | tf_op jit(solution)/shard_map/ppermute | solution.py:319
  54.6 1.0 %collective-permute-start.17 = (f32[72,512]{1,0:T(8,128)S(1)}, f32[72,512]{1,0:T(8,128)S(1)}, u32[]{:S(2)}, u32[]{:S(2)}) collective-permute-start(f32[72,512]{1,0:T(8,128)S(1)} %get-tuple-element.119), channel_id=1, source_target_pairs={{0,2},{1,3},{2,0},{3,1},{4,6},{5,7},{6,4},{7,5},{8,10},{9,11},{10,... | collective-permute-start | bytes 442376 | tf_op jit(solution)/shard_map/ppermute | solution.py:319
  55.5 1.5 %collective-permute-start.21 = (f32[72,512]{1,0:T(8,128)S(1)}, f32[72,512]{1,0:T(8,128)S(1)}, u32[]{:S(2)}, u32[]{:S(2)}) collective-permute-start(f32[72,512]{1,0:T(8,128)S(1)} %get-tuple-element.120), channel_id=1, source_target_pairs={{0,3},{1,2},{2,1},{3,0},{4,7},{5,6},{6,5},{7,4},{8,11},{9,10},{10,... | collective-permute-start | bytes 442376 | tf_op jit(solution)/shard_map/ppermute | solution.py:319
  57.0 1.5 %collective-permute-start.10 = (f32[1,72,512]{2,1,0:T(8,128)S(1)}, f32[1,72,512]{2,1,0:T(8,128)S(1)}, u32[]{:S(2)}, u32[]{:S(2)}) collective-permute-start(f32[1,72,512]{2,1,0:T(8,128)S(1)} %bitcast.19), channel_id=1, source_target_pairs={{0,8},{4,12},{8,0},{12,4},{16,24},{20,28},{24,16},{28,20},{1,9},{5... | collective-permute-start | bytes 442376 | tf_op jit(solution)/shard_map/ppermute | solution.py:319
  58.5 2.5 %collective-permute-done.13 = f32[72,512]{1,0:T(8,128)S(1)} collective-permute-done((f32[72,512]{1,0:T(8,128)S(1)}, f32[72,512]{1,0:T(8,128)S(1)}, u32[]{:S(2)}, u32[]{:S(2)}) %collective-permute-start.13) | collective-permute-done | bytes 147488 | tf_op jit(solution)/shard_map/ppermute | solution.py:319
  61.0 1.0 %collective-permute-start.14 = (f32[1,72,512]{2,1,0:T(8,128)S(1)}, f32[1,72,512]{2,1,0:T(8,128)S(1)}, u32[]{:S(2)}, u32[]{:S(2)}) collective-permute-start(f32[1,72,512]{2,1,0:T(8,128)S(1)} %bitcast.23), channel_id=1, source_target_pairs={{0,16},{4,20},{8,24},{12,28},{16,0},{20,4},{24,8},{28,12},{1,17},{... | collective-permute-start | bytes 442376 | tf_op jit(solution)/shard_map/ppermute | solution.py:319
  62.0 6.5 %collective-permute-done.17 = f32[72,512]{1,0:T(8,128)S(1)} collective-permute-done((f32[72,512]{1,0:T(8,128)S(1)}, f32[72,512]{1,0:T(8,128)S(1)}, u32[]{:S(2)}, u32[]{:S(2)}) %collective-permute-start.17) | collective-permute-done | bytes 147488 | tf_op jit(solution)/shard_map/ppermute | solution.py:319
  68.5 1.5 %collective-permute-start.18 = (f32[1,72,512]{2,1,0:T(8,128)S(1)}, f32[1,72,512]{2,1,0:T(8,128)S(1)}, u32[]{:S(2)}, u32[]{:S(2)}) collective-permute-start(f32[1,72,512]{2,1,0:T(8,128)S(1)} %bitcast.27), channel_id=1, source_target_pairs={{0,8},{4,12},{8,0},{12,4},{16,24},{20,28},{24,16},{28,20},{1,9},{5... | collective-permute-start | bytes 442376 | tf_op jit(solution)/shard_map/ppermute | solution.py:319
  70.0 0.0 collective-permute-done.21
  70.0 1.0 %collective-permute-start.22 = (f32[1,72,512]{2,1,0:T(8,128)S(1)}, f32[1,72,512]{2,1,0:T(8,128)S(1)}, u32[]{:S(2)}, u32[]{:S(2)}) collective-permute-start(f32[1,72,512]{2,1,0:T(8,128)S(1)} %bitcast.31), channel_id=1, source_target_pairs={{0,16},{4,20},{8,24},{12,28},{16,0},{20,4},{24,8},{28,12},{1,17},{... | collective-permute-start | bytes 442376 | tf_op jit(solution)/shard_map/ppermute | solution.py:319
  71.0 0.0 collective-permute-done.10.refs_1_
  71.0 1.1 %collective-permute-start.11 = (f32[2,72,512]{2,1,0:T(8,128)S(1)}, f32[2,72,512]{2,1,0:T(8,128)S(1)}, u32[]{:S(2)}, u32[]{:S(2)}) collective-permute-start(f32[2,72,512]{2,1,0:T(8,128)S(1)} %pad_maximum_fusion.5), channel_id=1, source_target_pairs={{0,16},{4,20},{8,24},{12,28},{16,0},{20,4},{24,8},{28,12},{1,17},{... | collective-permute-start | bytes 884744 | tf_op jit(solution)/shard_map/ppermute | solution.py:319
  72.1 0.0 collective-permute-done.14.refs_5_
  72.2 0.6 collective-permute-start.15
  72.8 2.5 %collective-permute-done.18.refs_9_ = f32[1,72,512]{2,1,0:T(8,128)S(1)} collective-permute-done((f32[1,72,512]{2,1,0:T(8,128)S(1)}, f32[1,72,512]{2,1,0:T(8,128)S(1)}, u32[]{:S(2)}, u32[]{:S(2)}) %collective-permute-start.18) | collective-permute-done | bytes 147488 | tf_op jit(solution)/shard_map/ppermute | solution.py:319
  75.3 1.0 %collective-permute-start.19 = (f32[2,72,512]{2,1,0:T(8,128)S(1)}, f32[2,72,512]{2,1,0:T(8,128)S(1)}, u32[]{:S(2)}, u32[]{:S(2)}) collective-permute-start(f32[2,72,512]{2,1,0:T(8,128)S(1)} %pad_maximum_fusion.7), channel_id=1, source_target_pairs={{0,16},{4,20},{8,24},{12,28},{16,0},{20,4},{24,8},{28,12},{1,17},{... | collective-permute-start | bytes 884744 | tf_op jit(solution)/shard_map/ppermute | solution.py:319
  76.4 0.5 collective-permute-done.22.refs_13_
  76.8 1.1 %collective-permute-start.23 = (f32[2,72,512]{2,1,0:T(8,128)S(1)}, f32[2,72,512]{2,1,0:T(8,128)S(1)}, u32[]{:S(2)}, u32[]{:S(2)}) collective-permute-start(f32[2,72,512]{2,1,0:T(8,128)S(1)} %pad_maximum_fusion.8), channel_id=1, source_target_pairs={{0,8},{4,12},{8,0},{12,4},{16,24},{20,28},{24,16},{28,20},{1,9},{5... | collective-permute-start | bytes 884744 | tf_op jit(solution)/shard_map/ppermute | solution.py:319
  77.9 3.7 %collective-permute-done.11.refs_2_ = f32[2,72,512]{2,1,0:T(8,128)S(1)} collective-permute-done((f32[2,72,512]{2,1,0:T(8,128)S(1)}, f32[2,72,512]{2,1,0:T(8,128)S(1)}, u32[]{:S(2)}, u32[]{:S(2)}) %collective-permute-start.11) | collective-permute-done | bytes 294944 | tf_op jit(solution)/shard_map/ppermute | solution.py:319
  81.7 0.1 collective-permute-start.12
  81.8 0.0 collective-permute-done.15.refs_6_
  81.8 0.5 collective-permute-start.16
  82.4 2.4 %collective-permute-done.19.refs_10_ = f32[2,72,512]{2,1,0:T(8,128)S(1)} collective-permute-done((f32[2,72,512]{2,1,0:T(8,128)S(1)}, f32[2,72,512]{2,1,0:T(8,128)S(1)}, u32[]{:S(2)}, u32[]{:S(2)}) %collective-permute-start.19) | collective-permute-done | bytes 294944 | tf_op jit(solution)/shard_map/ppermute | solution.py:319
  84.9 0.0 copy-start
  84.9 0.0 copy-start.1
  84.9 0.0 copy-start.2
  84.9 0.1 collective-permute-start.20
  85.0 0.0 collective-permute-done.23.refs_14_
  85.0 0.5 collective-permute-start.24
  85.6 0.0 collective-permute-done.12.refs_3_
  85.6 0.0 collective-permute-done.16.refs_7_
  85.6 1.4 %collective-permute-done.20.refs_11_ = f32[4,72,512]{2,1,0:T(8,128)S(1)} collective-permute-done((f32[4,72,512]{2,1,0:T(8,128)S(1)}, f32[4,72,512]{2,1,0:T(8,128)S(1)}, u32[]{:S(2)}, u32[]{:S(2)}) %collective-permute-start.20) | collective-permute-done | bytes 589856 | tf_op jit(solution)/shard_map/ppermute | solution.py:319
  87.0 0.8 collective-permute-done.24.refs_15_
  87.8 4.4 %shard_map.80 = (f32[64,2048]{1,0:T(8,128)}, f32[8,64,256]{2,1,0:T(8,128)}) custom-call(s32[2]{0:T(128)S(1)} %pad_add_fusion.place, s32[8]{0:T(128)S(1)} %copy-done, s32[8]{0:T(128)S(1)} %copy-done.1, s32[8]{0:T(128)S(1)} %copy-done.2, f32[1,72,512]{2,1,0:T(8,128)S(1)} %bitcast.22, f32[1,72,512]{2,1,0:T(8,128)S(1)} %collective-permute-done.10.refs_1_, ...), custom_call_target="tpu_custom_call" | custom-call | flops 16777216 | bytes 8388608 | tf_op jit(solution)/shard_map/pallas_call | solution.py:448
  (16 shorter events, 0.3 us)
Async XLA Ops:
  3.4 11.0 %collective-permute-start.4 = (f32[40,1024]{1,0:T(8,128)S(1)}, f32[40,1024]{1,0:T(8,128)}, u32[]{:S(2)}, u32[]{:S(2)}) collective-permute-start(f32[40,1024]{1,0:T(8,128)S(1)} %get-tuple-element.89), channel_id=1, source_target_pairs={{0,1},{1,0},{2,3},{3,2},{4,5},{5,4},{6,7},{7,6},{8,9},{9,8},{10,11... | collective-permute-start | bytes 491528 | tf_op jit(solution)/shard_map/ppermute | solution.py:319
  6.5 15.1 %collective-permute-start.5 = (f32[40,1024]{1,0:T(8,128)S(1)}, f32[40,1024]{1,0:T(8,128)S(1)}, u32[]{:S(2)}, u32[]{:S(2)}) collective-permute-start(f32[40,1024]{1,0:T(8,128)S(1)} %get-tuple-element.90), channel_id=1, source_target_pairs={{0,2},{1,3},{2,0},{3,1},{4,6},{5,7},{6,4},{7,5},{8,10},{9,11},{10,... | collective-permute-start | bytes 491528 | tf_op jit(solution)/shard_map/ppermute | solution.py:319
  9.0 12.5 %collective-permute-start.6 = (f32[40,1024]{1,0:T(8,128)S(1)}, f32[40,1024]{1,0:T(8,128)S(1)}, u32[]{:S(2)}, u32[]{:S(2)}) collective-permute-start(f32[40,1024]{1,0:T(8,128)S(1)} %get-tuple-element.91), channel_id=1, source_target_pairs={{0,3},{1,2},{2,1},{3,0},{4,7},{5,6},{6,5},{7,4},{8,11},{9,10},{10,... | collective-permute-start | bytes 491528 | tf_op jit(solution)/shard_map/ppermute | solution.py:319
  9.0 29.0 %collective-permute-start.7 = (f32[32,1024]{1,0:T(8,128)S(1)}, f32[32,1024]{1,0:T(8,128)S(1)}, u32[]{:S(2)}, u32[]{:S(2)}) collective-permute-start(f32[32,1024]{1,0:T(8,128)S(1)} %get-tuple-element.93), channel_id=1, source_target_pairs={{0,1},{1,0},{2,3},{3,2},{4,5},{5,4},{6,7},{7,6},{8,9},{9,8},{10,11... | collective-permute-start | bytes 393224 | tf_op jit(solution)/shard_map/ppermute | solution.py:319
  9.9 28.1 %collective-permute-start.8 = (f32[32,1024]{1,0:T(8,128)S(1)}, f32[32,1024]{1,0:T(8,128)S(1)}, u32[]{:S(2)}, u32[]{:S(2)}) collective-permute-start(f32[32,1024]{1,0:T(8,128)S(1)} %get-tuple-element.94), channel_id=1, source_target_pairs={{0,2},{1,3},{2,0},{3,1},{4,6},{5,7},{6,4},{7,5},{8,10},{9,11},{10,... | collective-permute-start | bytes 393224 | tf_op jit(solution)/shard_map/ppermute | solution.py:319
  14.3 23.7 %collective-permute-start.9 = (f32[32,1024]{1,0:T(8,128)S(1)}, f32[32,1024]{1,0:T(8,128)S(1)}, u32[]{:S(2)}, u32[]{:S(2)}) collective-permute-start(f32[32,1024]{1,0:T(8,128)S(1)} %get-tuple-element.95), channel_id=1, source_target_pairs={{0,3},{1,2},{2,1},{3,0},{4,7},{5,6},{6,5},{7,4},{8,11},{9,10},{10,... | collective-permute-start | bytes 393224 | tf_op jit(solution)/shard_map/ppermute | solution.py:319
  19.1 2.4 %copy-start.5 = (f32[65]{0:T(128)S(1)}, f32[65]{0:T(128)}, u32[]{:S(2)}) copy-start(f32[65]{0:T(128)} %param.10) | copy-start | bytes 784
  21.5 0.7 copy-start.3
  21.5 0.7 copy-start.4
  23.7 5.3 %collective-permute-start = (f32[1,4,8,1024]{3,2,1,0:T(8,128)}, f32[1,4,8,1024]{3,2,1,0:T(8,128)}, u32[]{:S(2)}, u32[]{:S(2)}) collective-permute-start(f32[1,4,8,1024]{3,2,1,0:T(8,128)} %maximum_bitcast_fusion), channel_id=1, source_target_pairs={{0,8},{4,12},{8,0},{12,4},{16,24},{20,28},{24,16},{28,20},{1,9},{5... | collective-permute-start | bytes 393224 | tf_op jit(solution)/shard_map/cond/branch_1_fun/ppermute | solution.py:319
  25.2 9.6 %collective-permute-start.1 = (f32[1,4,8,1024]{3,2,1,0:T(8,128)}, f32[1,4,8,1024]{3,2,1,0:T(8,128)}, u32[]{:S(2)}, u32[]{:S(2)}) collective-permute-start(f32[1,4,8,1024]{3,2,1,0:T(8,128)} %maximum_bitcast_fusion), channel_id=1, source_target_pairs={{0,16},{4,20},{8,24},{12,28},{16,0},{20,4},{24,8},{28,12},{1,17},{... | collective-permute-start | bytes 393224 | tf_op jit(solution)/shard_map/cond/branch_1_fun/ppermute | solution.py:319
  29.0 5.8 %collective-permute-start.2 = (f32[1,4,8,1024]{3,2,1,0:T(8,128)}, f32[1,4,8,1024]{3,2,1,0:T(8,128)}, u32[]{:S(2)}, u32[]{:S(2)}) collective-permute-start(f32[1,4,8,1024]{3,2,1,0:T(8,128)} %collective-permute-done), channel_id=1, source_target_pairs={{0,16},{4,20},{8,24},{12,28},{16,0},{20,4},{24,8},{28,12},{1,17},{... | collective-permute-start | bytes 393224 | tf_op jit(solution)/shard_map/cond/branch_1_fun/ppermute | solution.py:319
  35.9 2.1 %collective-permute-start.3 = (f32[4,4,8,1024]{3,2,1,0:T(8,128)S(1)}, f32[4,4,8,1024]{3,2,1,0:T(8,128)}, u32[]{:S(2)}, u32[]{:S(2)}) collective-permute-start(f32[4,4,8,1024]{3,2,1,0:T(8,128)S(1)} %pad_maximum_fusion), channel_id=1, source_target_pairs={{0,4},{4,0},{8,12},{12,8},{16,20},{20,16},{24,28},{28,24},{1,5},{5... | collective-permute-start | bytes 1572872 | tf_op jit(solution)/shard_map/cond/branch_1_fun/ppermute | solution.py:319
  44.9 16.2 %collective-permute-start.13 = (f32[72,512]{1,0:T(8,128)S(1)}, f32[72,512]{1,0:T(8,128)S(1)}, u32[]{:S(2)}, u32[]{:S(2)}) collective-permute-start(f32[72,512]{1,0:T(8,128)S(1)} %get-tuple-element.118), channel_id=1, source_target_pairs={{0,1},{1,0},{2,3},{3,2},{4,5},{5,4},{6,7},{7,6},{8,9},{9,8},{10,11... | collective-permute-start | bytes 442376 | tf_op jit(solution)/shard_map/ppermute | solution.py:319
  54.6 13.9 %collective-permute-start.17 = (f32[72,512]{1,0:T(8,128)S(1)}, f32[72,512]{1,0:T(8,128)S(1)}, u32[]{:S(2)}, u32[]{:S(2)}) collective-permute-start(f32[72,512]{1,0:T(8,128)S(1)} %get-tuple-element.119), channel_id=1, source_target_pairs={{0,2},{1,3},{2,0},{3,1},{4,6},{5,7},{6,4},{7,5},{8,10},{9,11},{10,... | collective-permute-start | bytes 442376 | tf_op jit(solution)/shard_map/ppermute | solution.py:319
  55.5 14.5 %collective-permute-start.21 = (f32[72,512]{1,0:T(8,128)S(1)}, f32[72,512]{1,0:T(8,128)S(1)}, u32[]{:S(2)}, u32[]{:S(2)}) collective-permute-start(f32[72,512]{1,0:T(8,128)S(1)} %get-tuple-element.120), channel_id=1, source_target_pairs={{0,3},{1,2},{2,1},{3,0},{4,7},{5,6},{6,5},{7,4},{8,11},{9,10},{10,... | collective-permute-start | bytes 442376 | tf_op jit(solution)/shard_map/ppermute | solution.py:319
  57.0 14.0 %collective-permute-start.10 = (f32[1,72,512]{2,1,0:T(8,128)S(1)}, f32[1,72,512]{2,1,0:T(8,128)S(1)}, u32[]{:S(2)}, u32[]{:S(2)}) collective-permute-start(f32[1,72,512]{2,1,0:T(8,128)S(1)} %bitcast.19), channel_id=1, source_target_pairs={{0,8},{4,12},{8,0},{12,4},{16,24},{20,28},{24,16},{28,20},{1,9},{5... | collective-permute-start | bytes 442376 | tf_op jit(solution)/shard_map/ppermute | solution.py:319
  61.0 11.1 %collective-permute-start.14 = (f32[1,72,512]{2,1,0:T(8,128)S(1)}, f32[1,72,512]{2,1,0:T(8,128)S(1)}, u32[]{:S(2)}, u32[]{:S(2)}) collective-permute-start(f32[1,72,512]{2,1,0:T(8,128)S(1)} %bitcast.23), channel_id=1, source_target_pairs={{0,16},{4,20},{8,24},{12,28},{16,0},{20,4},{24,8},{28,12},{1,17},{... | collective-permute-start | bytes 442376 | tf_op jit(solution)/shard_map/ppermute | solution.py:319
  68.5 6.8 %collective-permute-start.18 = (f32[1,72,512]{2,1,0:T(8,128)S(1)}, f32[1,72,512]{2,1,0:T(8,128)S(1)}, u32[]{:S(2)}, u32[]{:S(2)}) collective-permute-start(f32[1,72,512]{2,1,0:T(8,128)S(1)} %bitcast.27), channel_id=1, source_target_pairs={{0,8},{4,12},{8,0},{12,4},{16,24},{20,28},{24,16},{28,20},{1,9},{5... | collective-permute-start | bytes 442376 | tf_op jit(solution)/shard_map/ppermute | solution.py:319
  70.0 6.8 %collective-permute-start.22 = (f32[1,72,512]{2,1,0:T(8,128)S(1)}, f32[1,72,512]{2,1,0:T(8,128)S(1)}, u32[]{:S(2)}, u32[]{:S(2)}) collective-permute-start(f32[1,72,512]{2,1,0:T(8,128)S(1)} %bitcast.31), channel_id=1, source_target_pairs={{0,16},{4,20},{8,24},{12,28},{16,0},{20,4},{24,8},{28,12},{1,17},{... | collective-permute-start | bytes 442376 | tf_op jit(solution)/shard_map/ppermute | solution.py:319
  71.0 10.7 %collective-permute-start.11 = (f32[2,72,512]{2,1,0:T(8,128)S(1)}, f32[2,72,512]{2,1,0:T(8,128)S(1)}, u32[]{:S(2)}, u32[]{:S(2)}) collective-permute-start(f32[2,72,512]{2,1,0:T(8,128)S(1)} %pad_maximum_fusion.5), channel_id=1, source_target_pairs={{0,16},{4,20},{8,24},{12,28},{16,0},{20,4},{24,8},{28,12},{1,17},{... | collective-permute-start | bytes 884744 | tf_op jit(solution)/shard_map/ppermute | solution.py:319
  72.2 9.6 %collective-permute-start.15 = (f32[2,72,512]{2,1,0:T(8,128)S(1)}, f32[2,72,512]{2,1,0:T(8,128)S(1)}, u32[]{:S(2)}, u32[]{:S(2)}) collective-permute-start(f32[2,72,512]{2,1,0:T(8,128)S(1)} %pad_maximum_fusion.6), channel_id=1, source_target_pairs={{0,8},{4,12},{8,0},{12,4},{16,24},{20,28},{24,16},{28,20},{1,9},{5... | collective-permute-start | bytes 884744 | tf_op jit(solution)/shard_map/ppermute | solution.py:319
  75.3 9.5 %collective-permute-start.19 = (f32[2,72,512]{2,1,0:T(8,128)S(1)}, f32[2,72,512]{2,1,0:T(8,128)S(1)}, u32[]{:S(2)}, u32[]{:S(2)}) collective-permute-start(f32[2,72,512]{2,1,0:T(8,128)S(1)} %pad_maximum_fusion.7), channel_id=1, source_target_pairs={{0,16},{4,20},{8,24},{12,28},{16,0},{20,4},{24,8},{28,12},{1,17},{... | collective-permute-start | bytes 884744 | tf_op jit(solution)/shard_map/ppermute | solution.py:319
  76.8 8.1 %collective-permute-start.23 = (f32[2,72,512]{2,1,0:T(8,128)S(1)}, f32[2,72,512]{2,1,0:T(8,128)S(1)}, u32[]{:S(2)}, u32[]{:S(2)}) collective-permute-start(f32[2,72,512]{2,1,0:T(8,128)S(1)} %pad_maximum_fusion.8), channel_id=1, source_target_pairs={{0,8},{4,12},{8,0},{12,4},{16,24},{20,28},{24,16},{28,20},{1,9},{5... | collective-permute-start | bytes 884744 | tf_op jit(solution)/shard_map/ppermute | solution.py:319
  81.7 3.9 %collective-permute-start.12 = (f32[4,72,512]{2,1,0:T(8,128)S(1)}, f32[4,72,512]{2,1,0:T(8,128)S(1)}, u32[]{:S(2)}, u32[]{:S(2)}) collective-permute-start(f32[4,72,512]{2,1,0:T(8,128)S(1)} %pad_maximum_fusion.1), channel_id=1, source_target_pairs={{0,4},{4,0},{8,12},{12,8},{16,20},{20,16},{24,28},{28,24},{1,5},{5... | collective-permute-start | bytes 1769480 | tf_op jit(solution)/shard_map/ppermute | solution.py:319
  81.8 3.8 %collective-permute-start.16 = (f32[4,72,512]{2,1,0:T(8,128)S(1)}, f32[4,72,512]{2,1,0:T(8,128)S(1)}, u32[]{:S(2)}, u32[]{:S(2)}) collective-permute-start(f32[4,72,512]{2,1,0:T(8,128)S(1)} %pad_maximum_fusion.2), channel_id=1, source_target_pairs={{0,4},{4,0},{8,12},{12,8},{16,20},{20,16},{24,28},{28,24},{1,5},{5... | collective-permute-start | bytes 1769480 | tf_op jit(solution)/shard_map/ppermute | solution.py:319
  84.9 3.0 %copy-start = (s32[8]{0:T(128)S(1)}, s32[8]{0:T(128)}, u32[]{:S(2)}) copy-start(s32[8]{0:T(128)} %pair_one.1) | copy-start | bytes 100
  84.9 2.9 %copy-start.1 = (s32[8]{0:T(128)S(1)}, s32[8]{0:T(128)}, u32[]{:S(2)}) copy-start(s32[8]{0:T(128)} %pair_two.1) | copy-start | bytes 100
  84.9 2.9 %copy-start.2 = (s32[8]{0:T(128)S(1)}, s32[8]{0:T(128)}, u32[]{:S(2)}) copy-start(s32[8]{0:T(128)} %owner.1) | copy-start | bytes 100
  84.9 2.1 %collective-permute-start.20 = (f32[4,72,512]{2,1,0:T(8,128)S(1)}, f32[4,72,512]{2,1,0:T(8,128)S(1)}, u32[]{:S(2)}, u32[]{:S(2)}) collective-permute-start(f32[4,72,512]{2,1,0:T(8,128)S(1)} %pad_maximum_fusion.3), channel_id=1, source_target_pairs={{0,4},{4,0},{8,12},{12,8},{16,20},{20,16},{24,28},{28,24},{1,5},{5... | collective-permute-start | bytes 1769480 | tf_op jit(solution)/shard_map/ppermute | solution.py:319
  85.0 2.8 %collective-permute-start.24 = (f32[4,72,512]{2,1,0:T(8,128)S(1)}, f32[4,72,512]{2,1,0:T(8,128)S(1)}, u32[]{:S(2)}, u32[]{:S(2)}) collective-permute-start(f32[4,72,512]{2,1,0:T(8,128)S(1)} %pad_maximum_fusion.4), channel_id=1, source_target_pairs={{0,4},{4,0},{8,12},{12,8},{16,20},{20,16},{24,28},{28,24},{1,5},{5... | collective-permute-start | bytes 1769480 | tf_op jit(solution)/shard_map/ppermute | solution.py:319

commit v4 on v2

--- a/solution.py
+++ b/solution.py
@@ -18,6 +18,7 @@
 stretch = 1024
 rim = 4
 loads = 4
+vmem_bytes = 48 * 1024 * 1024
 
 
 def split(value):
@@ -28,10 +29,6 @@
 
 def dot(a, b):
     return jnp.dot(a, b, preferred_element_type=jnp.float32)
-
-
-def dot3(a_high, a_low, b_high, b_low):
-    return dot(a_high, b_high) + (dot(a_low, b_high) + dot(a_high, b_low))
 
 
 class Plan:
@@ -103,16 +100,32 @@
 
 
 def band(plan, taps, rows, columns, offset):
-    spread = jnp.broadcast_to(taps[...], (rows, plan.length))
     if offset % plan.length:
-        spread = pltpu.roll(spread, offset % plan.length, 1)
+        taps = pltpu.roll(taps, offset % plan.length, 1)
+    spread = jnp.broadcast_to(taps[:1], (rows, plan.length))
     rolled = pltpu.roll(spread, 0, 1, stride=1, stride_axis=0)[:, :columns]
     row = lax.broadcasted_iota(jnp.int32, (rows, columns), 0)
     column = lax.broadcasted_iota(jnp.int32, (rows, columns), 1)
     return jnp.where(jnp.abs(column - row - offset) <= plan.margin, rolled, 0.0)
 
 
-def table_kernel(plan, place, taps, reverse, *refs):
+def table_kernel(plan, place, beam, *refs):
+    refs, line = refs[:-1], refs[-1]
+    count = beam.shape[1]
+    line[...] = jnp.zeros(line.shape, jnp.float32)
+    line[:1, :count] = beam[...]
+    kernel = line[...]
+    kernel = kernel / jnp.sum(kernel[:1], axis=1, keepdims=True)
+    size = kernel.shape[1]
+    row = lax.broadcasted_iota(jnp.int32, (size, size), 0)
+    column = lax.broadcasted_iota(jnp.int32, (size, size), 1)
+    mirror = (row + column == count - 1).astype(jnp.float32)
+    blank = jnp.zeros((kernel.shape[0], plan.length - size), jnp.float32)
+
+    def centred(values):
+        return pltpu.roll(jnp.concatenate([values, blank], axis=1), plan.length - plan.margin, 1)
+
+    taps, reverse = centred(kernel), centred(jnp.dot(kernel, mirror, precision=exact))
     tables = list(refs)
 
     def put(value):
@@ -159,48 +172,54 @@
     bands = [take(2) for _ in plan.blocks]
     last = take(2)
     outs = take(plan.row_devices)
-    seen, weight, image, total, field, high, low, mid_high, mid_low = refs
-    for step, piece in enumerate(pieces):
-        row = pl.multiple_of((place[0] ^ step) * plan.row_local, plan.row_local)
-        value = piece[...]
-        seen[pl.ds(row, plan.row_local), :] = value
-        a, b = split(value)
-        high[pl.ds(row, plan.row_local), :] = a
-        low[pl.ds(row, plan.row_local), :] = b
+    seen, weight, image, base, total, field, high, low, mid_high, mid_low, sem = refs
     for part, owners in zip(parts, sharers):
         for slot, offset in enumerate(owners):
             for step in range(plan.row_devices):
                 row = (place[0] ^ step) * plan.row_local
                 row = row + (lax.rem(place[1], plan.sharers) ^ offset) * plan.share_rows
-                row = pl.multiple_of(row, plan.share_rows)
-                weight[pl.ds(row, plan.share_rows), :] = part[slot, step]
-
-    def rows_pass(table, start, stop):
+                rows = pl.ds(pl.multiple_of(row, plan.share_rows), plan.share_rows)
+                pltpu.make_async_copy(part.at[slot, step], weight.at[rows], sem).start()
+    for step, piece in enumerate(pieces):
+        rows = pl.ds(pl.multiple_of((place[0] ^ step) * plan.row_local, plan.row_local), plan.row_local)
+        value = piece[...]
+        seen[rows, :] = value
+        high[rows, :], low[rows, :] = split(value)
+    def rows_pass(table, start, stop, full=True):
         count = table[0].shape[0]
         for a in range(start, stop, wide):
             b = min(a + wide, stop)
-            value = dot3(table[0][...], table[1][...], high[:, a:b], low[:, a:b])
-            mid_high[:count, a:b], mid_low[:count, a:b] = split(value)
-
-    def columns_pass(table, count, window):
+            value = dot(table[0][...], high[:, a:b]) + dot(table[1][...], high[:, a:b])
+            if full:
+                value = value + dot(table[0][...], low[:, a:b])
+                mid_high[:count, a:b], mid_low[:count, a:b] = split(value)
+            else:
+                mid_high[:count, a:b] = value.astype(jnp.bfloat16)
+
+    def columns_pass(table, count, window, full=True):
         a, b = window
-        return dot3(mid_high[:count, a:b], mid_low[:count, a:b], table[0][...], table[1][...])
+        value = dot(mid_high[:count, a:b], table[0][...]) + dot(mid_high[:count, a:b], table[1][...])
+        return value + dot(mid_low[:count, a:b], table[0][...]) if full else value
 
     keep = 1.0 - step_size * ridge_term
     for iteration in range(ITERS):
         chosen = plan.stage_blocks(iteration)
         windows = [plan.window(plan.blocks[i]) for i in chosen]
-        rows_pass(square, windows[0][0], windows[-1][1])
+        rows_pass(square, windows[0][0], windows[-1][1], iteration == 0)
+        if iteration == 0:
+            pltpu.make_async_copy(weight, weight, sem).wait()
         for i, window in zip(chosen, windows):
             a, b = plan.blocks[i]
-            value = columns_pass(bands[i], plan.rows, window)
-            if iteration > 0:
-                value = value + keep * image[:, a:b]
+            value = columns_pass(bands[i], plan.rows, window, iteration == 0)
+            if iteration == 0:
+                base[:, a:b] = value
+            else:
+                value = keep * image[:, a:b] + base[:, a:b] - value
             image[:, a:b] = value
+            product = weight[:, a:b] * value
             given = seen[:, a:b]
-            residual = given - weight[:, a:b] * value
-            total[:, a:b] = residual + keep * (total[:, a:b] if iteration > 0 else given)
-            high[:, a:b], low[:, a:b] = split(residual)
+            total[:, a:b] = given - product + keep * (total[:, a:b] if iteration > 0 else given)
+            high[:, a:b] = product.astype(jnp.bfloat16)
     first, stop = plan.window(plan.out_blocks[0])[0], plan.window(plan.out_blocks[-1])[1]
     high[:, first:stop], low[:, first:stop] = split(total[:, first:stop])
     rows_pass(final, first, stop)
@@ -242,10 +261,10 @@
         pieces.append(sorted(flat, key=lambda entry: entry[0]))
     estimate = refs.pop(0)
     mean_field = refs.pop(0) if field_width else None
-    own, partner, sems = refs[:3]
+    own, partner, result, done, sems = refs[:5]
     rows_at, sim_at = place[0], place[1]
     if field_width:
-        every = refs[3]
+        every, means, sent = refs[5:]
         units = field_width // lane
         per = plan.share // lane
         for unit in range(units + 2):
@@ -285,8 +304,11 @@
     for a in range(0, plan.columns, stretch):
         b = min(a + stretch, plan.columns)
         span = slice(a, b + 2 * lane)
-        estimate[:, a:b] = divergence(own[:, span], partner[:, span])
+        result[:, a:b] = divergence(own[:, span], partner[:, span])
+    copies = [pltpu.make_async_copy(result, estimate, done)]
+    copies[0].start()
     if not field_width:
+        copies[0].wait()
         return
     for unit in range(units + 2):
         at = sim_at * units - 1 + unit
@@ -296,15 +318,18 @@
             span = every.at[:, :, unit * lane : (unit + 1) * lane]
             pltpu.make_async_copy(span, span, sems.at[unit]).wait()
 
-    mean_field[...] = jnp.zeros(mean_field.shape, jnp.float32)
+    means[...] = jnp.zeros(means.shape, jnp.float32)
     for sim in range(plan.sim_devices):
-        partner = 2.0 * every[pair_one[sim]] - every[pair_two[sim]]
-        mean_field[owner[sim]] += divergence(every[sim], partner)
+        means[owner[sim]] += divergence(every[sim], 2.0 * every[pair_one[sim]] - every[pair_two[sim]])
     for group in range(OWNERS):
         count = jnp.int32(0)
         for sim in range(plan.sim_devices):
             count = count + (owner[sim] == group).astype(jnp.int32)
-        mean_field[group] = mean_field[group] / jnp.maximum(count, 1).astype(jnp.float32)
+        means[group] = means[group] / jnp.maximum(count, 1).astype(jnp.float32)
+        copies.append(pltpu.make_async_copy(means.at[group], mean_field.at[group], sent.at[group]))
+        copies[-1].start()
+    for copy in copies:
+        copy.wait()
 
 
 def exchange(value, axis, offset):
@@ -321,15 +346,14 @@
     return arrays, offsets
 
 
-def call(kernel, out_shapes, in_specs, scratch, flops, moved, limit=48):
-    vmem = pl.BlockSpec(memory_space=pltpu.VMEM)
+def call(kernel, out_shapes, in_specs, scratch, flops, moved, outs_in=pltpu.VMEM):
     return pl.pallas_call(
         kernel,
         out_shape=out_shapes,
         in_specs=in_specs,
-        out_specs=[vmem] * len(out_shapes),
+        out_specs=[pl.BlockSpec(memory_space=outs_in)] * len(out_shapes),
         scratch_shapes=scratch,
-        compiler_params=pltpu.CompilerParams(vmem_limit_bytes=limit * 1024 * 1024),
+        compiler_params=pltpu.CompilerParams(vmem_limit_bytes=vmem_bytes),
         cost_estimate=pl.CostEstimate(flops=flops, bytes_accessed=moved, transcendentals=0),
     )
 
@@ -344,6 +368,9 @@
     smem = pl.BlockSpec(memory_space=pltpu.SMEM)
     far = pl.BlockSpec(memory_space=pltpu.HBM)
 
+    def pinned(value):
+        return pltpu.with_memory_space_constraint(value, pltpu.HBM)
+
     def f32(*shape):
         return jax.ShapeDtypeStruct(shape, jnp.float32)
 
@@ -358,8 +385,7 @@
         [pltpu.VMEM((plan.share_rows, columns + 2 * plan.halo), jnp.float32), pltpu.SemaphoreType.DMA],
         0,
         1 << 18,
-        limit=60,
-    )(place, weight)
+    )(place, pinned(weight))
     pieces = call(
         functools.partial(weighted_kernel, plan),
         [f32(row_local, plan.width)] * row_devices,
@@ -369,8 +395,7 @@
         + [pltpu.SemaphoreType.DMA((2, loads))],
         cells,
         16 * cells,
-        limit=60,
-    )(place, maps.reshape(row_local, columns), weight)
+    )(place, pinned(maps.reshape(row_local, columns)), pinned(weight))
     parts = [parts[0]] + [exchange(parts[d], "rows", d) for d in range(1, row_devices)]
     pieces, parts = lax.optimization_barrier((pieces, parts))
     pieces = [pieces[0]] + [exchange(pieces[d], "rows", d) for d in range(1, row_devices)]
@@ -380,31 +405,29 @@
         low, high = plan.window(block)
         shapes.append((high - low, block[1] - block[0]))
 
-    def prepare(parts, beam):
-        bits = [1 << i for i in range(1, plan.sharers.bit_length() - 1)] + [1]
-        arrays, offsets = gather(jnp.stack(parts), "sims", bits)
-        sharers[:] = offsets
-        kernel = beam / jnp.sum(beam)
-        blank = jnp.zeros((plan.length - taps,), jnp.float32)
-        forward = jnp.roll(jnp.concatenate([kernel, blank]), -plan.margin)[None]
-        backward = jnp.roll(jnp.concatenate([kernel[::-1], blank]), -plan.margin)[None]
-        tables = call(
-            functools.partial(table_kernel, plan),
-            [b16(*shape) for shape in shapes for _ in range(2)],
-            [smem, vmem, vmem],
-            [],
-            1 << 32,
-            1 << 23,
-        )(place, forward, backward)
-        return arrays, tables
-
-    made = jax.eval_shape(prepare, parts, beam)
-    parts, tables = lax.cond(
+    tables = call(
+        functools.partial(table_kernel, plan),
+        [b16(*shape) for shape in shapes for _ in range(2)],
+        [smem, vmem],
+        [pltpu.VMEM((8, lane), jnp.float32)],
+        1 << 32,
+        1 << 23,
+    )(place, beam[None])
+    parts, tables = lax.optimization_barrier((parts, tables))
+
+    def spread(parts):
+        found = {0: jnp.stack(parts)[None]}
+        for bit in [1 << i for i in range(1, plan.sharers.bit_length() - 1)]:
+            found |= {offset | bit: exchange(value, "sims", bit) for offset, value in found.items()}
+        sharers[:] = [[offset] for offset in found] + [[offset ^ 1 for offset in found]]
+        return [*found.values(), exchange(jnp.concatenate(list(found.values())), "sims", 1)]
+
+    made = jax.eval_shape(spread, parts)
+    parts = lax.cond(
         lax.axis_index("rows") < row_devices,
-        prepare,
-        lambda parts, beam: jax.tree.map(lambda x: jnp.zeros(x.shape, x.dtype), made),
+        spread,
+        lambda parts: jax.tree.map(lambda x: jnp.zeros(x.shape, x.dtype), made),
         parts,
-        beam,
     )
 
     full = (plan.rows, plan.width)
@@ -412,11 +435,12 @@
     filtered = call(
         functools.partial(filter_kernel, plan, sharers),
         [f32(plan.slab, plan.share)] * row_devices,
-        [smem] + [vmem] * len(pieces) + [vmem] * (len(parts) + len(tables)),
-        [pltpu.VMEM(full, jnp.float32)] * 4
+        [smem] + [vmem] * row_devices + [far] * len(parts) + [vmem] * len(tables),
+        [pltpu.VMEM(full, jnp.float32)] * 5
         + [pltpu.VMEM((row_devices * plan.slab, plan.share), jnp.float32)]
         + [pltpu.VMEM(full, jnp.bfloat16)] * 2
-        + [pltpu.VMEM(tall, jnp.bfloat16)] * 2,
+        + [pltpu.VMEM(tall, jnp.bfloat16)] * 2
+        + [pltpu.SemaphoreType.DMA],
         1 << 33,
         1 << 23,
     )(place, *pieces, *parts, *tables)
@@ -439,10 +463,13 @@
     outs = [f32(row_local, columns)]
     extended = (plan.slab, columns + 2 * lane)
     scratch = [pltpu.VMEM(extended, jnp.float32)] * 2
+    scratch += [pltpu.VMEM((row_local, columns), jnp.float32), pltpu.SemaphoreType.DMA]
     if fused:
         outs.append(f32(OWNERS, row_local, fused))
         scratch.append(pltpu.SemaphoreType.DMA((fused // lane + 2,)))
         scratch.append(pltpu.VMEM((sim_devices, plan.slab, fused + 2 * lane), jnp.float32))
+        scratch.append(pltpu.VMEM((OWNERS, row_local, fused), jnp.float32))
+        scratch.append(pltpu.SemaphoreType.DMA((OWNERS,)))
     else:
         scratch.append(pltpu.SemaphoreType.DMA((1,)))
     results = call(
@@ -452,6 +479,7 @@
         scratch,
         1 << 24,
         1 << 23,
+        outs_in=pltpu.HBM,
     )(place, pair_one, pair_two, owner, *held)
     estimate = results[0]
     if fused:

time: 84.2 us -> 97.6 us (1.16)
  the two profiles are of different devices: /device:TPU:9 before, /device:TPU:0 now
where the time goes in v4:
time: 97.6 us; the launch traced here: 97 us
  starting transfers between devices  30.7 us (31%)
  waiting for transfers between devices  30.6 us (31%)
  Pallas kernels  18.6 us (19%)
  local copies, waits for them, and re-layouts  13.8 us (14%)
  other arithmetic  2.12 us (2%)
  between operations  1.04 us (1%)
    ppermute x25, starting transfers between devices, exchange(): return lax.ppermute(value, axis, [(i, i ^ offset) for i in range(count)])  30.7 us
    ppermute x25, waiting for transfers between devices, exchange(): return lax.ppermute(value, axis, [(i, i ^ offset) for i in range(count)])  30.6 us
    unnamed x58, local copies, waits for them, and re-layouts  13.8 us
    pallas_call x1, Pallas kernels, body(): call(functools.partial(filter_kernel, plan, sharers), [f32(plan.slab, pla...  6.03 us
    pallas_call x1, Pallas kernels, body(): call(functools.partial(estimate_kernel, plan, holders, fused), outs, [sme...  4.35 us
    pallas_call x1, Pallas kernels, body(): call(functools.partial(table_kernel, plan), [b16(*shape) for shape in sha...  4.3 us
    pallas_call x1, Pallas kernels, body(): call(functools.partial(share_kernel, plan), [f32(plan.share_rows, plan.wi...  2.01 us
  transfers between devices with their start and end apart: 25, of which 14 were waited for; matrix products, arithmetic and copies ran while one was open for 2% of the time, Pallas kernels for 6%

profile of v4, /device:TPU:0, one launch (start us, length us, event | category | flops | bytes accessed | tf_op | source)
XLA Modules:
  0.0 97.0 jit_solution(8332931701509254249)
XLA Ops:
  0.6 0.1 pad_add_fusion.place
  0.7 2.0 %shard_map.78 = (f32[8,1024]{1,0:T(8,128)}, f32[8,1024]{1,0:T(8,128)S(1)}, f32[8,1024]{1,0:T(8,128)S(1)}, f32[8,1024]{1,0:T(8,128)S(1)}) custom-call(s32[2]{0:T(128)S(1)} %pad_add_fusion.place, f32[64,2048]{1,0:T(8,128)} %weight.3), custom_call_target="tpu_custom_call" | custom-call | bytes 262144 | tf_op jit(solution)/shard_map/pallas_call | solution.py:381
  2.7 3.1 %collective-permute-start.4 = (f32[8,1024]{1,0:T(8,128)S(1)}, f32[8,1024]{1,0:T(8,128)S(1)}, u32[]{:S(2)}, u32[]{:S(2)}) collective-permute-start(f32[8,1024]{1,0:T(8,128)S(1)} %get-tuple-element.82), channel_id=1, source_target_pairs={{0,1},{1,0},{2,3},{3,2},{4,5},{5,4},{6,7},{7,6},{8,9},{9,8},{10,11... | collective-permute-start | bytes 98312 | tf_op jit(solution)/shard_map/ppermute | solution.py:337
  5.8 2.6 %collective-permute-start.5 = (f32[8,1024]{1,0:T(8,128)S(1)}, f32[8,1024]{1,0:T(8,128)S(1)}, u32[]{:S(2)}, u32[]{:S(2)}) collective-permute-start(f32[8,1024]{1,0:T(8,128)S(1)} %get-tuple-element.83), channel_id=1, source_target_pairs={{0,2},{1,3},{2,0},{3,1},{4,6},{5,7},{6,4},{7,5},{8,10},{9,11},{10,... | collective-permute-start | bytes 98312 | tf_op jit(solution)/shard_map/ppermute | solution.py:337
  8.4 1.9 %shard_map.77 = (f32[64,1024]{1,0:T(8,128)S(1)}, f32[64,1024]{1,0:T(8,128)S(1)}, f32[64,1024]{1,0:T(8,128)S(1)}, f32[64,1024]{1,0:T(8,128)S(1)}) custom-call(s32[2]{0:T(128)S(1)} %pad_add_fusion.place, f32[64,2048]{1,0:T(8,128)} %bitcast.32, f32[64,2048]{1,0:T(8,128)} %weight.3), custom_call_target="tpu_custom_call" | custom-call | flops 131072 | bytes 2097152 | tf_op jit(solution)/shard_map/pallas_call | solution.py:389
  10.4 0.9 collective-permute-done.5
  11.2 2.9 %collective-permute-done.6 = f32[8,1024]{1,0:T(8,128)S(1)} collective-permute-done((f32[8,1024]{1,0:T(8,128)S(1)}, f32[8,1024]{1,0:T(8,128)S(1)}, u32[]{:S(2)}, u32[]{:S(2)}) %collective-permute-start.6) | collective-permute-done | bytes 32800 | tf_op jit(solution)/shard_map/ppermute | solution.py:337
  14.1 0.6 copy-done.27
  14.7 0.9 collective-permute-start.8
  15.7 3.5 %collective-permute-start.9 = (f32[64,1024]{1,0:T(8,128)S(1)}, f32[64,1024]{1,0:T(8,128)S(1)}, u32[]{:S(2)}, u32[]{:S(2)}) collective-permute-start(f32[64,1024]{1,0:T(8,128)S(1)} %get-tuple-element.88), channel_id=1, source_target_pairs={{0,3},{1,2},{2,1},{3,0},{4,7},{5,6},{6,5},{7,4},{8,11},{9,10},{10,... | collective-permute-start | bytes 786440 | tf_op jit(solution)/shard_map/ppermute | solution.py:337
  19.2 4.3 %shard_map.79 = (bf16[256,256]{1,0:T(8,128)(2,1)S(1)}, bf16[256,256]{1,0:T(8,128)(2,1)S(1)}, bf16[288,256]{1,0:T(8,128)(2,1)S(1)}, bf16[288,256]{1,0:T(8,128)(2,...) custom-call(s32[2]{0:T(128)S(1)} %pad_add_fusion.place, ...), custom_call_target="tpu_custom_call" | custom-call | flops 4294967296 | bytes 8388608 | tf_op jit(solution)/shard_map/pallas_call | solution.py:408
  23.5 0.6 copy-done.8
  24.1 0.7 copy-done.10
  24.8 0.6 copy-done.12
  25.4 0.6 copy-done.14
  26.0 0.6 copy-done.16
  26.7 0.6 copy-done.18
  27.3 0.6 copy-done.20
  27.9 0.7 copy-done.4
  28.6 0.1 copy-done.6
  28.7 14.5 %conditional.1 = (f32[1,4,8,1024]{3,2,1,0:T(8,128)}, f32[1,4,8,1024]{3,2,1,0:T(8,128)}, f32[1,4,8,1024]{3,2,1,0:T(8,128)}, f32[1,4,8,1024]{3,2,1,0:T(8,128)}, f32[4,4,8,1024]{3,2,1,0:T(8,128)}) conditional(s32[]{:T(128)} %convert_element_type.3, () %tuple.19, (f32[8,1024]{1,0:T(8,128)S(1)}, f32[8,1024]{1,0:T(8,128)S(1)}, f32[8,1024]{1,0:T(8,128)S(1)}, ...), branch_computations={%region_0.0_spmd, %region_1.0_spmd} | conditional | flops 491520 | bytes 4980936 | solution.py:426
  28.7 0.7 maximum_bitcast_fusion
  29.4 1.5 %collective-permute-start = (f32[1,4,8,1024]{3,2,1,0:T(8,128)}, f32[1,4,8,1024]{3,2,1,0:T(8,128)}, u32[]{:S(2)}, u32[]{:S(2)}) collective-permute-start(f32[1,4,8,1024]{3,2,1,0:T(8,128)} %maximum_bitcast_fusion), channel_id=1, source_target_pairs={{0,8},{4,12},{8,0},{12,4},{16,24},{20,28},{24,16},{28,20},{1,9},{5... | collective-permute-start | bytes 393224 | tf_op jit(solution)/shard_map/cond/branch_1_fun/ppermute | solution.py:337
  30.9 1.5 %collective-permute-start.1 = (f32[1,4,8,1024]{3,2,1,0:T(8,128)}, f32[1,4,8,1024]{3,2,1,0:T(8,128)}, u32[]{:S(2)}, u32[]{:S(2)}) collective-permute-start(f32[1,4,8,1024]{3,2,1,0:T(8,128)} %maximum_bitcast_fusion), channel_id=1, source_target_pairs={{0,16},{4,20},{8,24},{12,28},{16,0},{20,4},{24,8},{28,12},{1,17},{... | collective-permute-start | bytes 393224 | tf_op jit(solution)/shard_map/cond/branch_1_fun/ppermute | solution.py:337
  32.4 2.3 %collective-permute-done = f32[1,4,8,1024]{3,2,1,0:T(8,128)} collective-permute-done((f32[1,4,8,1024]{3,2,1,0:T(8,128)}, f32[1,4,8,1024]{3,2,1,0:T(8,128)}, u32[]{:S(2)}, u32[]{:S(2)}) %collective-permute-start) | collective-permute-done | bytes 131104 | tf_op jit(solution)/shard_map/cond/branch_1_fun/ppermute | solution.py:337
  34.7 1.5 %collective-permute-start.2 = (f32[1,4,8,1024]{3,2,1,0:T(8,128)}, f32[1,4,8,1024]{3,2,1,0:T(8,128)}, u32[]{:S(2)}, u32[]{:S(2)}) collective-permute-start(f32[1,4,8,1024]{3,2,1,0:T(8,128)} %collective-permute-done), channel_id=1, source_target_pairs={{0,16},{4,20},{8,24},{12,28},{16,0},{20,4},{24,8},{28,12},{1,17},{... | collective-permute-start | bytes 393224 | tf_op jit(solution)/shard_map/cond/branch_1_fun/ppermute | solution.py:337
  36.2 0.6 collective-permute-done.1
  36.8 3.1 %collective-permute-done.2 = f32[1,4,8,1024]{3,2,1,0:T(8,128)} collective-permute-done((f32[1,4,8,1024]{3,2,1,0:T(8,128)}, f32[1,4,8,1024]{3,2,1,0:T(8,128)}, u32[]{:S(2)}, u32[]{:S(2)}) %collective-permute-start.2) | collective-permute-done | bytes 131104 | tf_op jit(solution)/shard_map/cond/branch_1_fun/ppermute | solution.py:337
  39.9 1.1 %pad_maximum_fusion = f32[4,4,8,1024]{3,2,1,0:T(8,128)S(1)} fusion(f32[1,4,8,1024]{3,2,1,0:T(8,128)} %collective-permute-done.2, f32[1,4,8,1024]{3,2,1,0:T(8,128)} %collective-permute-done.1, f32[1,4,8,1024]{3,2,1,0:T(8,128)} %collective-permute-done, f32[1,4,8,1024]{3,2,1,0:T(8,128)} %maximum_bitcast_fusion), kind=kLoop, calls=%fused_computation | loop fusion | flops 393216 | bytes 1048576 | tf_op jit(solution)/shard_map/cond/branch_1_fun/concatenate | solution.py:423
  41.1 0.1 collective-permute-start.3
  41.2 2.0 %collective-permute-done.3 = f32[4,4,8,1024]{3,2,1,0:T(8,128)} collective-permute-done((f32[4,4,8,1024]{3,2,1,0:T(8,128)S(1)}, f32[4,4,8,1024]{3,2,1,0:T(8,128)}, u32[]{:S(2)}, u32[]{:S(2)}) %collective-permute-start.3) | collective-permute-done | bytes 524320 | tf_op jit(solution)/shard_map/cond/branch_1_fun/ppermute | solution.py:337
  43.2 0.9 copy-done.5
  44.1 0.9 copy-done.7
  45.1 0.9 copy-done.9
  46.0 0.9 copy-done.11
  46.9 0.9 copy-done.13
  47.8 0.8 copy-done.15
  48.7 0.8 copy-done.17
  49.5 0.8 copy-done.19
  50.3 0.8 copy-done.21
  51.2 6.0 %shard_map.80 = (f32[72,512]{1,0:T(8,128)S(1)}, f32[72,512]{1,0:T(8,128)S(1)}, f32[72,512]{1,0:T(8,128)S(1)}, f32[72,512]{1,0:T(8,128)S(1)}) custom-call(s32[2]{0:T(128)S(1)} %pad_add_fusion.place, f32[64,1024]{1,0:T(8,128)S(1)} %get-tuple-element.85.refs_0_, f32[64,1024]{1,0:T(8,128)S(1)} %collective-permute-done.7.refs_1_, ...), custom_call_target="tpu_custom_call" | custom-call | flops 8589934592 | bytes 8388608 | tf_op jit(solution)/shard_map/pallas_call | solution.py:435
  57.2 0.1 collective-permute-start.13
  57.3 0.9 collective-permute-start.17
  58.2 3.5 %collective-permute-start.21 = (f32[72,512]{1,0:T(8,128)S(1)}, f32[72,512]{1,0:T(8,128)S(1)}, u32[]{:S(2)}, u32[]{:S(2)}) collective-permute-start(f32[72,512]{1,0:T(8,128)S(1)} %get-tuple-element.137), channel_id=1, source_target_pairs={{0,3},{1,2},{2,1},{3,0},{4,7},{5,6},{6,5},{7,4},{8,11},{9,10},{10,... | collective-permute-start | bytes 442376 | tf_op jit(solution)/shard_map/ppermute | solution.py:337
  61.7 1.5 %collective-permute-start.10 = (f32[1,72,512]{2,1,0:T(8,128)S(1)}, f32[1,72,512]{2,1,0:T(8,128)S(1)}, u32[]{:S(2)}, u32[]{:S(2)}) collective-permute-start(f32[1,72,512]{2,1,0:T(8,128)S(1)} %bitcast.15), channel_id=1, source_target_pairs={{0,8},{4,12},{8,0},{12,4},{16,24},{20,28},{24,16},{28,20},{1,9},{5... | collective-permute-start | bytes 442376 | tf_op jit(solution)/shard_map/ppermute | solution.py:337
  63.2 1.2 %collective-permute-done.13 = f32[72,512]{1,0:T(8,128)S(1)} collective-permute-done((f32[72,512]{1,0:T(8,128)S(1)}, f32[72,512]{1,0:T(8,128)S(1)}, u32[]{:S(2)}, u32[]{:S(2)}) %collective-permute-start.13) | collective-permute-done | bytes 147488 | tf_op jit(solution)/shard_map/ppermute | solution.py:337
  64.4 1.5 %collective-permute-start.14 = (f32[1,72,512]{2,1,0:T(8,128)S(1)}, f32[1,72,512]{2,1,0:T(8,128)S(1)}, u32[]{:S(2)}, u32[]{:S(2)}) collective-permute-start(f32[1,72,512]{2,1,0:T(8,128)S(1)} %bitcast.19), channel_id=1, source_target_pairs={{0,16},{4,20},{8,24},{12,28},{16,0},{20,4},{24,8},{28,12},{1,17},{... | collective-permute-start | bytes 442376 | tf_op jit(solution)/shard_map/ppermute | solution.py:337
  65.9 5.4 %collective-permute-done.17 = f32[72,512]{1,0:T(8,128)S(1)} collective-permute-done((f32[72,512]{1,0:T(8,128)S(1)}, f32[72,512]{1,0:T(8,128)S(1)}, u32[]{:S(2)}, u32[]{:S(2)}) %collective-permute-start.17) | collective-permute-done | bytes 147488 | tf_op jit(solution)/shard_map/ppermute | solution.py:337
  71.3 1.5 %collective-permute-start.18 = (f32[1,72,512]{2,1,0:T(8,128)S(1)}, f32[1,72,512]{2,1,0:T(8,128)S(1)}, u32[]{:S(2)}, u32[]{:S(2)}) collective-permute-start(f32[1,72,512]{2,1,0:T(8,128)S(1)} %bitcast.23), channel_id=1, source_target_pairs={{0,8},{4,12},{8,0},{12,4},{16,24},{20,28},{24,16},{28,20},{1,9},{5... | collective-permute-start | bytes 442376 | tf_op jit(solution)/shard_map/ppermute | solution.py:337
  72.8 1.5 %collective-permute-start.22 = (f32[1,72,512]{2,1,0:T(8,128)S(1)}, f32[1,72,512]{2,1,0:T(8,128)S(1)}, u32[]{:S(2)}, u32[]{:S(2)}) collective-permute-start(f32[1,72,512]{2,1,0:T(8,128)S(1)} %bitcast.27), channel_id=1, source_target_pairs={{0,16},{4,20},{8,24},{12,28},{16,0},{20,4},{24,8},{28,12},{1,17},{... | collective-permute-start | bytes 442376 | tf_op jit(solution)/shard_map/ppermute | solution.py:337
  74.4 0.5 collective-permute-start.11
  75.0 0.6 collective-permute-start.15
  75.6 2.2 %collective-permute-done.18.refs_9_ = f32[1,72,512]{2,1,0:T(8,128)S(1)} collective-permute-done((f32[1,72,512]{2,1,0:T(8,128)S(1)}, f32[1,72,512]{2,1,0:T(8,128)S(1)}, u32[]{:S(2)}, u32[]{:S(2)}) %collective-permute-start.18) | collective-permute-done | bytes 147488 | tf_op jit(solution)/shard_map/ppermute | solution.py:337
  77.8 1.6 %collective-permute-start.19 = (f32[2,72,512]{2,1,0:T(8,128)S(1)}, f32[2,72,512]{2,1,0:T(8,128)S(1)}, u32[]{:S(2)}, u32[]{:S(2)}) collective-permute-start(f32[2,72,512]{2,1,0:T(8,128)S(1)} %pad_maximum_fusion.7), channel_id=1, source_target_pairs={{0,16},{4,20},{8,24},{12,28},{16,0},{20,4},{24,8},{28,12},{1,17},{... | collective-permute-start | bytes 884744 | tf_op jit(solution)/shard_map/ppermute | solution.py:337
  79.4 0.2 collective-permute-done.22.refs_13_
  79.6 1.6 %collective-permute-start.23 = (f32[2,72,512]{2,1,0:T(8,128)S(1)}, f32[2,72,512]{2,1,0:T(8,128)S(1)}, u32[]{:S(2)}, u32[]{:S(2)}) collective-permute-start(f32[2,72,512]{2,1,0:T(8,128)S(1)} %pad_maximum_fusion.8), channel_id=1, source_target_pairs={{0,8},{4,12},{8,0},{12,4},{16,24},{20,28},{24,16},{28,20},{1,9},{5... | collective-permute-start | bytes 884744 | tf_op jit(solution)/shard_map/ppermute | solution.py:337
  81.2 4.7 %collective-permute-done.11.refs_2_ = f32[2,72,512]{2,1,0:T(8,128)S(1)} collective-permute-done((f32[2,72,512]{2,1,0:T(8,128)S(1)}, f32[2,72,512]{2,1,0:T(8,128)S(1)}, u32[]{:S(2)}, u32[]{:S(2)}) %collective-permute-start.11) | collective-permute-done | bytes 294944 | tf_op jit(solution)/shard_map/ppermute | solution.py:337
  86.1 0.6 collective-permute-start.16
  86.7 2.8 %collective-permute-done.19.refs_10_ = f32[2,72,512]{2,1,0:T(8,128)S(1)} collective-permute-done((f32[2,72,512]{2,1,0:T(8,128)S(1)}, f32[2,72,512]{2,1,0:T(8,128)S(1)}, u32[]{:S(2)}, u32[]{:S(2)}) %collective-permute-start.19) | collective-permute-done | bytes 294944 | tf_op jit(solution)/shard_map/ppermute | solution.py:337
  89.5 0.1 collective-permute-start.20
  89.7 0.5 collective-permute-start.24
  90.2 1.4 %collective-permute-done.20.refs_11_ = f32[4,72,512]{2,1,0:T(8,128)S(1)} collective-permute-done((f32[4,72,512]{2,1,0:T(8,128)S(1)}, f32[4,72,512]{2,1,0:T(8,128)S(1)}, u32[]{:S(2)}, u32[]{:S(2)}) %collective-permute-start.20) | collective-permute-done | bytes 589856 | tf_op jit(solution)/shard_map/ppermute | solution.py:337
  91.6 0.8 collective-permute-done.24.refs_15_
  92.4 4.4 %shard_map.81 = (f32[64,2048]{1,0:T(8,128)}, f32[8,64,256]{2,1,0:T(8,128)}) custom-call(s32[2]{0:T(128)S(1)} %pad_add_fusion.place, s32[8]{0:T(128)S(1)} %copy-done, s32[8]{0:T(128)S(1)} %copy-done.1, s32[8]{0:T(128)S(1)} %copy-done.2, f32[1,72,512]{2,1,0:T(8,128)S(1)} %bitcast.18, f32[1,72,512]{2,1,0:T(8,128)S(1)} %collective-permute-done.10.refs_1_, ...), custom_call_target="tpu_custom_call" | custom-call | flops 16777216 | bytes 8388608 | tf_op jit(solution)/shard_map/pallas_call | solution.py:475
  (61 shorter events, 0.4 us)
Async XLA Ops:
  2.7 7.6 %collective-permute-start.4 = (f32[8,1024]{1,0:T(8,128)S(1)}, f32[8,1024]{1,0:T(8,128)S(1)}, u32[]{:S(2)}, u32[]{:S(2)}) collective-permute-start(f32[8,1024]{1,0:T(8,128)S(1)} %get-tuple-element.82), channel_id=1, source_target_pairs={{0,1},{1,0},{2,3},{3,2},{4,5},{5,4},{6,7},{7,6},{8,9},{9,8},{10,11... | collective-permute-start | bytes 98312 | tf_op jit(solution)/shard_map/ppermute | solution.py:337
  5.8 5.4 %collective-permute-start.5 = (f32[8,1024]{1,0:T(8,128)S(1)}, f32[8,1024]{1,0:T(8,128)S(1)}, u32[]{:S(2)}, u32[]{:S(2)}) collective-permute-start(f32[8,1024]{1,0:T(8,128)S(1)} %get-tuple-element.83), channel_id=1, source_target_pairs={{0,2},{1,3},{2,0},{3,1},{4,6},{5,7},{6,4},{7,5},{8,10},{9,11},{10,... | collective-permute-start | bytes 98312 | tf_op jit(solution)/shard_map/ppermute | solution.py:337
  8.4 5.7 %collective-permute-start.6 = (f32[8,1024]{1,0:T(8,128)S(1)}, f32[8,1024]{1,0:T(8,128)S(1)}, u32[]{:S(2)}, u32[]{:S(2)}) collective-permute-start(f32[8,1024]{1,0:T(8,128)S(1)} %get-tuple-element.84), channel_id=1, source_target_pairs={{0,3},{1,2},{2,1},{3,0},{4,7},{5,6},{6,5},{7,4},{8,11},{9,10},{10,... | collective-permute-start | bytes 98312 | tf_op jit(solution)/shard_map/ppermute | solution.py:337
  10.4 3.8 %copy-start.23 = (f32[8,1024]{1,0:T(8,128)}, f32[8,1024]{1,0:T(8,128)S(1)}, u32[]{:S(2)}) copy-start(f32[8,1024]{1,0:T(8,128)S(1)} %collective-permute-done.4) | copy-start | bytes 98308
  11.2 2.9 %copy-start.25 = (f32[8,1024]{1,0:T(8,128)}, f32[8,1024]{1,0:T(8,128)S(1)}, u32[]{:S(2)}) copy-start(f32[8,1024]{1,0:T(8,128)S(1)} %collective-permute-done.5) | copy-start | bytes 98308
  14.1 0.6 copy-start.27
  14.7 4.4 %copy-start.3 = (f32[65]{0:T(128)S(1)}, f32[65]{0:T(128)}, u32[]{:S(2)}) copy-start(f32[65]{0:T(128)} %param.10) | copy-start | bytes 784
  14.7 28.4 %collective-permute-start.7 = (f32[64,1024]{1,0:T(8,128)S(1)}, f32[64,1024]{1,0:T(8,128)S(1)}, u32[]{:S(2)}, u32[]{:S(2)}) collective-permute-start(f32[64,1024]{1,0:T(8,128)S(1)} %get-tuple-element.86), channel_id=1, source_target_pairs={{0,1},{1,0},{2,3},{3,2},{4,5},{5,4},{6,7},{7,6},{8,9},{9,8},{10,11... | collective-permute-start | bytes 786440 | tf_op jit(solution)/shard_map/ppermute | solution.py:337
  14.7 28.4 %collective-permute-start.8 = (f32[64,1024]{1,0:T(8,128)S(1)}, f32[64,1024]{1,0:T(8,128)S(1)}, u32[]{:S(2)}, u32[]{:S(2)}) collective-permute-start(f32[64,1024]{1,0:T(8,128)S(1)} %get-tuple-element.87), channel_id=1, source_target_pairs={{0,2},{1,3},{2,0},{3,1},{4,6},{5,7},{6,4},{7,5},{8,10},{9,11},{10,... | collective-permute-start | bytes 786440 | tf_op jit(solution)/shard_map/ppermute | solution.py:337
  15.7 27.5 %collective-permute-start.9 = (f32[64,1024]{1,0:T(8,128)S(1)}, f32[64,1024]{1,0:T(8,128)S(1)}, u32[]{:S(2)}, u32[]{:S(2)}) collective-permute-start(f32[64,1024]{1,0:T(8,128)S(1)} %get-tuple-element.88), channel_id=1, source_target_pairs={{0,3},{1,2},{2,1},{3,0},{4,7},{5,6},{6,5},{7,4},{8,11},{9,10},{10,... | collective-permute-start | bytes 786440 | tf_op jit(solution)/shard_map/ppermute | solution.py:337
  19.1 8.8 %copy-start.22 = (f32[8,1024]{1,0:T(8,128)S(1)}, f32[8,1024]{1,0:T(8,128)}, u32[]{:S(2)}) copy-start(f32[8,1024]{1,0:T(8,128)} %get-tuple-element.109) | copy-start | bytes 98308
  19.1 8.8 %copy-start.24 = (f32[8,1024]{1,0:T(8,128)S(1)}, f32[8,1024]{1,0:T(8,128)}, u32[]{:S(2)}) copy-start(f32[8,1024]{1,0:T(8,128)} %copy-done.23) | copy-start | bytes 98308
  19.1 8.8 %copy-start.26 = (f32[8,1024]{1,0:T(8,128)S(1)}, f32[8,1024]{1,0:T(8,128)}, u32[]{:S(2)}) copy-start(f32[8,1024]{1,0:T(8,128)} %copy-done.25) | copy-start | bytes 98308
  19.1 8.8 %copy-start.28 = (f32[8,1024]{1,0:T(8,128)S(1)}, f32[8,1024]{1,0:T(8,128)}, u32[]{:S(2)}) copy-start(f32[8,1024]{1,0:T(8,128)} %copy-done.27) | copy-start | bytes 98308
  23.5 0.6 copy-start.8
  24.1 0.7 copy-start.10
  24.8 0.6 copy-start.12
  25.4 0.6 copy-start.14
  26.0 0.6 copy-start.16
  26.7 0.6 copy-start.18
  27.3 0.6 copy-start.20
  27.9 0.7 copy-start.4
  27.9 0.8 copy-start.6
  29.4 5.3 %collective-permute-start = (f32[1,4,8,1024]{3,2,1,0:T(8,128)}, f32[1,4,8,1024]{3,2,1,0:T(8,128)}, u32[]{:S(2)}, u32[]{:S(2)}) collective-permute-start(f32[1,4,8,1024]{3,2,1,0:T(8,128)} %maximum_bitcast_fusion), channel_id=1, source_target_pairs={{0,8},{4,12},{8,0},{12,4},{16,24},{20,28},{24,16},{28,20},{1,9},{5... | collective-permute-start | bytes 393224 | tf_op jit(solution)/shard_map/cond/branch_1_fun/ppermute | solution.py:337
  30.9 5.9 %collective-permute-start.1 = (f32[1,4,8,1024]{3,2,1,0:T(8,128)}, f32[1,4,8,1024]{3,2,1,0:T(8,128)}, u32[]{:S(2)}, u32[]{:S(2)}) collective-permute-start(f32[1,4,8,1024]{3,2,1,0:T(8,128)} %maximum_bitcast_fusion), channel_id=1, source_target_pairs={{0,16},{4,20},{8,24},{12,28},{16,0},{20,4},{24,8},{28,12},{1,17},{... | collective-permute-start | bytes 393224 | tf_op jit(solution)/shard_map/cond/branch_1_fun/ppermute | solution.py:337
  34.7 5.3 %collective-permute-start.2 = (f32[1,4,8,1024]{3,2,1,0:T(8,128)}, f32[1,4,8,1024]{3,2,1,0:T(8,128)}, u32[]{:S(2)}, u32[]{:S(2)}) collective-permute-start(f32[1,4,8,1024]{3,2,1,0:T(8,128)} %collective-permute-done), channel_id=1, source_target_pairs={{0,16},{4,20},{8,24},{12,28},{16,0},{20,4},{24,8},{28,12},{1,17},{... | collective-permute-start | bytes 393224 | tf_op jit(solution)/shard_map/cond/branch_1_fun/ppermute | solution.py:337
  41.1 2.1 %collective-permute-start.3 = (f32[4,4,8,1024]{3,2,1,0:T(8,128)S(1)}, f32[4,4,8,1024]{3,2,1,0:T(8,128)}, u32[]{:S(2)}, u32[]{:S(2)}) collective-permute-start(f32[4,4,8,1024]{3,2,1,0:T(8,128)S(1)} %pad_maximum_fusion), channel_id=1, source_target_pairs={{0,4},{4,0},{8,12},{12,8},{16,20},{20,16},{24,28},{28,24},{1,5},{5... | collective-permute-start | bytes 1572872 | tf_op jit(solution)/shard_map/cond/branch_1_fun/ppermute | solution.py:337
  43.2 1.0 copy-start.5
  44.1 0.9 copy-start.7
  45.1 0.9 copy-start.9
  46.0 0.9 copy-start.11
  46.9 0.9 copy-start.13
  47.8 0.8 copy-start.15
  48.7 0.8 copy-start.17
  49.5 0.8 copy-start.19
  50.3 0.8 copy-start.21
  57.2 7.2 %collective-permute-start.13 = (f32[72,512]{1,0:T(8,128)S(1)}, f32[72,512]{1,0:T(8,128)S(1)}, u32[]{:S(2)}, u32[]{:S(2)}) collective-permute-start(f32[72,512]{1,0:T(8,128)S(1)} %get-tuple-element.135), channel_id=1, source_target_pairs={{0,1},{1,0},{2,3},{3,2},{4,5},{5,4},{6,7},{7,6},{8,9},{9,8},{10,11... | collective-permute-start | bytes 442376 | tf_op jit(solution)/shard_map/ppermute | solution.py:337
  57.3 14.0 %collective-permute-start.17 = (f32[72,512]{1,0:T(8,128)S(1)}, f32[72,512]{1,0:T(8,128)S(1)}, u32[]{:S(2)}, u32[]{:S(2)}) collective-permute-start(f32[72,512]{1,0:T(8,128)S(1)} %get-tuple-element.136), channel_id=1, source_target_pairs={{0,2},{1,3},{2,0},{3,1},{4,6},{5,7},{6,4},{7,5},{8,10},{9,11},{10,... | collective-permute-start | bytes 442376 | tf_op jit(solution)/shard_map/ppermute | solution.py:337
  58.2 14.6 %collective-permute-start.21 = (f32[72,512]{1,0:T(8,128)S(1)}, f32[72,512]{1,0:T(8,128)S(1)}, u32[]{:S(2)}, u32[]{:S(2)}) collective-permute-start(f32[72,512]{1,0:T(8,128)S(1)} %get-tuple-element.137), channel_id=1, source_target_pairs={{0,3},{1,2},{2,1},{3,0},{4,7},{5,6},{6,5},{7,4},{8,11},{9,10},{10,... | collective-permute-start | bytes 442376 | tf_op jit(solution)/shard_map/ppermute | solution.py:337
  61.7 12.7 %collective-permute-start.10 = (f32[1,72,512]{2,1,0:T(8,128)S(1)}, f32[1,72,512]{2,1,0:T(8,128)S(1)}, u32[]{:S(2)}, u32[]{:S(2)}) collective-permute-start(f32[1,72,512]{2,1,0:T(8,128)S(1)} %bitcast.15), channel_id=1, source_target_pairs={{0,8},{4,12},{8,0},{12,4},{16,24},{20,28},{24,16},{28,20},{1,9},{5... | collective-permute-start | bytes 442376 | tf_op jit(solution)/shard_map/ppermute | solution.py:337
  64.4 10.6 %collective-permute-start.14 = (f32[1,72,512]{2,1,0:T(8,128)S(1)}, f32[1,72,512]{2,1,0:T(8,128)S(1)}, u32[]{:S(2)}, u32[]{:S(2)}) collective-permute-start(f32[1,72,512]{2,1,0:T(8,128)S(1)} %bitcast.19), channel_id=1, source_target_pairs={{0,16},{4,20},{8,24},{12,28},{16,0},{20,4},{24,8},{28,12},{1,17},{... | collective-permute-start | bytes 442376 | tf_op jit(solution)/shard_map/ppermute | solution.py:337
  71.3 6.4 %collective-permute-start.18 = (f32[1,72,512]{2,1,0:T(8,128)S(1)}, f32[1,72,512]{2,1,0:T(8,128)S(1)}, u32[]{:S(2)}, u32[]{:S(2)}) collective-permute-start(f32[1,72,512]{2,1,0:T(8,128)S(1)} %bitcast.23), channel_id=1, source_target_pairs={{0,8},{4,12},{8,0},{12,4},{16,24},{20,28},{24,16},{28,20},{1,9},{5... | collective-permute-start | bytes 442376 | tf_op jit(solution)/shard_map/ppermute | solution.py:337
  72.8 6.8 %collective-permute-start.22 = (f32[1,72,512]{2,1,0:T(8,128)S(1)}, f32[1,72,512]{2,1,0:T(8,128)S(1)}, u32[]{:S(2)}, u32[]{:S(2)}) collective-permute-start(f32[1,72,512]{2,1,0:T(8,128)S(1)} %bitcast.27), channel_id=1, source_target_pairs={{0,16},{4,20},{8,24},{12,28},{16,0},{20,4},{24,8},{28,12},{1,17},{... | collective-permute-start | bytes 442376 | tf_op jit(solution)/shard_map/ppermute | solution.py:337
  74.4 11.5 %collective-permute-start.11 = (f32[2,72,512]{2,1,0:T(8,128)S(1)}, f32[2,72,512]{2,1,0:T(8,128)S(1)}, u32[]{:S(2)}, u32[]{:S(2)}) collective-permute-start(f32[2,72,512]{2,1,0:T(8,128)S(1)} %pad_maximum_fusion.5), channel_id=1, source_target_pairs={{0,16},{4,20},{8,24},{12,28},{16,0},{20,4},{24,8},{28,12},{1,17},{... | collective-permute-start | bytes 884744 | tf_op jit(solution)/shard_map/ppermute | solution.py:337
  75.0 11.1 %collective-permute-start.15 = (f32[2,72,512]{2,1,0:T(8,128)S(1)}, f32[2,72,512]{2,1,0:T(8,128)S(1)}, u32[]{:S(2)}, u32[]{:S(2)}) collective-permute-start(f32[2,72,512]{2,1,0:T(8,128)S(1)} %pad_maximum_fusion.6), channel_id=1, source_target_pairs={{0,8},{4,12},{8,0},{12,4},{16,24},{20,28},{24,16},{28,20},{1,9},{5... | collective-permute-start | bytes 884744 | tf_op jit(solution)/shard_map/ppermute | solution.py:337
  77.8 11.7 %collective-permute-start.19 = (f32[2,72,512]{2,1,0:T(8,128)S(1)}, f32[2,72,512]{2,1,0:T(8,128)S(1)}, u32[]{:S(2)}, u32[]{:S(2)}) collective-permute-start(f32[2,72,512]{2,1,0:T(8,128)S(1)} %pad_maximum_fusion.7), channel_id=1, source_target_pairs={{0,16},{4,20},{8,24},{12,28},{16,0},{20,4},{24,8},{28,12},{1,17},{... | collective-permute-start | bytes 884744 | tf_op jit(solution)/shard_map/ppermute | solution.py:337
  79.6 10.0 %collective-permute-start.23 = (f32[2,72,512]{2,1,0:T(8,128)S(1)}, f32[2,72,512]{2,1,0:T(8,128)S(1)}, u32[]{:S(2)}, u32[]{:S(2)}) collective-permute-start(f32[2,72,512]{2,1,0:T(8,128)S(1)} %pad_maximum_fusion.8), channel_id=1, source_target_pairs={{0,8},{4,12},{8,0},{12,4},{16,24},{20,28},{24,16},{28,20},{1,9},{5... | collective-permute-start | bytes 884744 | tf_op jit(solution)/shard_map/ppermute | solution.py:337
  86.0 4.2 %collective-permute-start.12 = (f32[4,72,512]{2,1,0:T(8,128)S(1)}, f32[4,72,512]{2,1,0:T(8,128)S(1)}, u32[]{:S(2)}, u32[]{:S(2)}) collective-permute-start(f32[4,72,512]{2,1,0:T(8,128)S(1)} %pad_maximum_fusion.1), channel_id=1, source_target_pairs={{0,4},{4,0},{8,12},{12,8},{16,20},{20,16},{24,28},{28,24},{1,5},{5... | collective-permute-start | bytes 1769480 | tf_op jit(solution)/shard_map/ppermute | solution.py:337
  86.1 4.1 %collective-permute-start.16 = (f32[4,72,512]{2,1,0:T(8,128)S(1)}, f32[4,72,512]{2,1,0:T(8,128)S(1)}, u32[]{:S(2)}, u32[]{:S(2)}) collective-permute-start(f32[4,72,512]{2,1,0:T(8,128)S(1)} %pad_maximum_fusion.2), channel_id=1, source_target_pairs={{0,4},{4,0},{8,12},{12,8},{16,20},{20,16},{24,28},{28,24},{1,5},{5... | collective-permute-start | bytes 1769480 | tf_op jit(solution)/shard_map/ppermute | solution.py:337
  89.5 3.0 %copy-start = (s32[8]{0:T(128)S(1)}, s32[8]{0:T(128)}, u32[]{:S(2)}) copy-start(s32[8]{0:T(128)} %pair_one.1) | copy-start | bytes 100
  89.5 2.9 %copy-start.1 = (s32[8]{0:T(128)S(1)}, s32[8]{0:T(128)}, u32[]{:S(2)}) copy-start(s32[8]{0:T(128)} %pair_two.1) | copy-start | bytes 100
  89.5 2.9 %copy-start.2 = (s32[8]{0:T(128)S(1)}, s32[8]{0:T(128)}, u32[]{:S(2)}) copy-start(s32[8]{0:T(128)} %owner.1) | copy-start | bytes 100
  89.5 2.1 %collective-permute-start.20 = (f32[4,72,512]{2,1,0:T(8,128)S(1)}, f32[4,72,512]{2,1,0:T(8,128)S(1)}, u32[]{:S(2)}, u32[]{:S(2)}) collective-permute-start(f32[4,72,512]{2,1,0:T(8,128)S(1)} %pad_maximum_fusion.3), channel_id=1, source_target_pairs={{0,4},{4,0},{8,12},{12,8},{16,20},{20,16},{24,28},{28,24},{1,5},{5... | collective-permute-start | bytes 1769480 | tf_op jit(solution)/shard_map/ppermute | solution.py:337
  89.7 2.8 %collective-permute-start.24 = (f32[4,72,512]{2,1,0:T(8,128)S(1)}, f32[4,72,512]{2,1,0:T(8,128)S(1)}, u32[]{:S(2)}, u32[]{:S(2)}) collective-permute-start(f32[4,72,512]{2,1,0:T(8,128)S(1)} %pad_maximum_fusion.4), channel_id=1, source_target_pairs={{0,4},{4,0},{8,12},{12,8},{16,20},{20,16},{24,28},{28,24},{1,5},{5... | collective-permute-start | bytes 1769480 | tf_op jit(solution)/shard_map/ppermute | solution.py:337

commit v5 on v4

--- a/solution.py
+++ b/solution.py
@@ -36,6 +36,7 @@
         self.row_devices, self.sim_devices = row_devices, sim_devices
         self.row_local, self.columns = row_local, columns
         self.rows = row_devices * row_local
+        self.steps = [0, *range(row_devices - 1, 0, -1)]
         self.margin = (taps - 1) // 2
         self.share = columns // row_devices
         self.halo = -(-self.margin * (2 * ITERS + 1) // lane) * lane
@@ -58,45 +59,37 @@
         return [i for i, (a, b) in enumerate(self.blocks) if b > low and a < self.width - low]
 
 
-def share_kernel(plan, place, weight, *refs):
-    parts, padded, sem = refs[: plan.row_devices], refs[-2], refs[-1]
-    row = pl.multiple_of(lax.rem(place[1], plan.sharers) * plan.share_rows, plan.share_rows)
-    source = weight.at[pl.ds(row, plan.share_rows)]
-    copy = pltpu.make_async_copy(source, padded.at[:, pl.ds(plan.halo, plan.columns)], sem)
-    copy.start()
-    zeros = jnp.zeros((plan.share_rows, plan.halo), jnp.float32)
-    padded[:, : plan.halo] = zeros
-    padded[:, plan.halo + plan.columns :] = zeros
-    copy.wait()
-    for step, part in enumerate(parts):
-        column = pl.multiple_of((place[0] ^ step) * plan.share, lane)
-        part[...] = padded[:, pl.ds(column, plan.width)]
-
-
-def weighted_kernel(plan, place, maps, weight, *refs):
-    pieces = refs[: plan.row_devices]
-    padded, weights, given, sems = refs[plan.row_devices :]
+def piece_kernel(plan, maps, weight, *refs):
+    count = plan.row_devices
+    pieces, parts = refs[:count], refs[count : 2 * count]
+    padded, weights, given, sems = refs[2 * count :]
+    rows_at, sims_at = lax.axis_index("rows"), lax.axis_index("sims")
     chunk = plan.row_local // loads
+    inner = slice(plan.halo, plan.halo + plan.columns)
     copies = []
     for number in range(loads):
         rows = pl.ds(number * chunk, chunk)
         copies.append((
-            pltpu.make_async_copy(weight.at[rows], weights.at[rows], sems.at[0, number]),
+            pltpu.make_async_copy(weight.at[rows], weights.at[rows, inner], sems.at[0, number]),
             pltpu.make_async_copy(maps.at[rows], given.at[rows], sems.at[1, number]),
         ))
         for copy in copies[-1]:
             copy.start()
     zeros = jnp.zeros((plan.row_local, plan.halo), jnp.float32)
-    padded[:, : plan.halo] = zeros
-    padded[:, plan.halo + plan.columns :] = zeros
+    for target in (padded, weights):
+        target[:, : plan.halo] = zeros
+        target[:, plan.halo + plan.columns :] = zeros
+    starts = [pl.multiple_of((rows_at ^ step) * plan.share, lane) for step in plan.steps]
     for number in range(loads):
         for copy in copies[number]:
             copy.wait()
         rows = slice(number * chunk, (number + 1) * chunk)
-        padded[rows, plan.halo : plan.halo + plan.columns] = weights[rows] * given[rows]
-        for step, piece in enumerate(pieces):
-            column = pl.multiple_of((place[0] ^ step) * plan.share, lane)
+        padded[rows, inner] = weights[rows, inner] * given[rows]
+        for piece, column in zip(pieces, starts):
             piece[rows] = padded[rows, pl.ds(column, plan.width)]
+    row = pl.multiple_of(lax.rem(sims_at, plan.sharers) * plan.share_rows, plan.share_rows)
+    for part, column in zip(parts, starts):
+        part[...] = weights[pl.ds(row, plan.share_rows), pl.ds(column, plan.width)]
 
 
 def band(plan, taps, rows, columns, offset):
@@ -109,7 +102,7 @@
     return jnp.where(jnp.abs(column - row - offset) <= plan.margin, rolled, 0.0)
 
 
-def table_kernel(plan, place, beam, *refs):
+def table_kernel(plan, beam, *refs):
     refs, line = refs[:-1], refs[-1]
     count = beam.shape[1]
     line[...] = jnp.zeros(line.shape, jnp.float32)
@@ -144,21 +137,33 @@
     put(jnp.concatenate(slabs, axis=0))
     size = 2 * wide
     forward = band(plan, taps, size, size, 0)
-    backward = band(plan, reverse, size, size, 0)
+    backward = band(plan, reverse, size, size, 0)[:, lane : lane + wide]
+    square = step_size * jnp.dot(forward, backward, precision=exact)
     for block in plan.blocks:
         low, high = plan.window(block)
-        extent = high - low
-        column = lax.broadcasted_iota(jnp.int32, (extent, extent), 1) + (place[0] * plan.share - plan.halo + low)
-        inside = (column >= 0) & (column < plan.columns)
-        left = jnp.where(inside, forward[:extent, :extent], 0.0)
-        right = backward[:extent, block[0] - low : block[1] - low]
-        put(step_size * jnp.dot(left, right, precision=exact))
+        first = low - block[0] + lane
+        wanted = square[first : first + high - low, : block[1] - block[0]]
+        high_term, low_term = tables[0], tables[1]
+        put(wanted)
+        origin = lax.axis_index("rows") * plan.share - plan.halo + low
+        reach = origin + high - low
+        cut = ((origin < 0) & (reach > 0)) | ((origin < plan.columns) & (reach > plan.columns))
+
+        @pl.when(cut)
+        def _(origin=origin, extent=high - low, first=first, span=block[1] - block[0], terms=(high_term, low_term)):
+            column = lax.broadcasted_iota(jnp.int32, (size, size), 1) + (origin - first)
+            inside = (column >= 0) & (column < plan.columns)
+            value = step_size * jnp.dot(jnp.where(inside, forward, 0.0), backward, precision=exact)
+            high_part, low_part = split(value[first : first + extent, :span])
+            terms[0][...] = high_part
+            terms[1][...] = low_part
+
     for block in plan.out_blocks[:1]:
         low, high = plan.window(block)
         put(step_size * forward[: high - low, block[0] - low : block[1] - low])
 
 
-def filter_kernel(plan, sharers, place, *refs):
+def filter_kernel(plan, sharers, *refs):
     refs = list(refs)
 
     def take(number):
@@ -175,13 +180,13 @@
     seen, weight, image, base, total, field, high, low, mid_high, mid_low, sem = refs
     for part, owners in zip(parts, sharers):
         for slot, offset in enumerate(owners):
-            for step in range(plan.row_devices):
-                row = (place[0] ^ step) * plan.row_local
-                row = row + (lax.rem(place[1], plan.sharers) ^ offset) * plan.share_rows
+            for index, step in enumerate(plan.steps):
+                row = (lax.axis_index("rows") ^ step) * plan.row_local
+                row = row + (lax.rem(lax.axis_index("sims"), plan.sharers) ^ offset) * plan.share_rows
                 rows = pl.ds(pl.multiple_of(row, plan.share_rows), plan.share_rows)
-                pltpu.make_async_copy(part.at[slot, step], weight.at[rows], sem).start()
-    for step, piece in enumerate(pieces):
-        rows = pl.ds(pl.multiple_of((place[0] ^ step) * plan.row_local, plan.row_local), plan.row_local)
+                pltpu.make_async_copy(part.at[slot, index], weight.at[rows], sem).start()
+    for step, piece in zip(plan.steps, pieces):
+        rows = pl.ds(pl.multiple_of((lax.axis_index("rows") ^ step) * plan.row_local, plan.row_local), plan.row_local)
         value = piece[...]
         seen[rows, :] = value
         high[rows, :], low[rows, :] = split(value)
@@ -207,14 +212,14 @@
         windows = [plan.window(plan.blocks[i]) for i in chosen]
         rows_pass(square, windows[0][0], windows[-1][1], iteration == 0)
         if iteration == 0:
+            for i, window in zip(chosen, windows):
+                base[:, slice(*plan.blocks[i])] = columns_pass(bands[i], plan.rows, window)
             pltpu.make_async_copy(weight, weight, sem).wait()
         for i, window in zip(chosen, windows):
             a, b = plan.blocks[i]
-            value = columns_pass(bands[i], plan.rows, window, iteration == 0)
-            if iteration == 0:
-                base[:, a:b] = value
-            else:
-                value = keep * image[:, a:b] + base[:, a:b] - value
+            value = base[:, a:b]
+            if iteration > 0:
+                value = keep * image[:, a:b] + value - columns_pass(bands[i], plan.rows, window, False)
             image[:, a:b] = value
             product = weight[:, a:b] * value
             given = seen[:, a:b]
@@ -227,8 +232,8 @@
     for block in plan.out_blocks:
         size = block[1] - block[0]
         field[:, block[0] - plan.halo : block[1] - plan.halo] = columns_pass(last, count, plan.window(block))
-    for step, out in enumerate(outs):
-        row = pl.multiple_of((place[0] ^ step) * plan.slab, 8)
+    for step, out in zip(plan.steps, outs):
+        row = pl.multiple_of((lax.axis_index("rows") ^ step) * plan.slab, 8)
         out[...] = field[pl.ds(row, plan.slab), :]
 
 
@@ -250,7 +255,7 @@
     return 0.25 * (flow + (right - left))
 
 
-def estimate_kernel(plan, holders, field_width, place, pair_one, pair_two, owner, *refs):
+def estimate_kernel(plan, holders, field_width, pair_one, pair_two, owner, *refs):
     refs = list(refs)
     pieces = []
     for orders in holders:
@@ -262,7 +267,7 @@
     estimate = refs.pop(0)
     mean_field = refs.pop(0) if field_width else None
     own, partner, result, done, sems = refs[:5]
-    rows_at, sim_at = place[0], place[1]
+    rows_at, sim_at = lax.axis_index("rows"), lax.axis_index("sims")
     if field_width:
         every, means, sent = refs[5:]
         units = field_width // lane
@@ -271,10 +276,10 @@
             at = sim_at * units - 1 + unit
             inside = (at >= 0) & (at < plan.columns // lane)
             span = slice(unit * lane, (unit + 1) * lane)
-            for step in range(plan.row_devices):
-                def fetch_all(step=step, at=at, span=span, unit=unit):
+            for step, sources in zip(plan.steps, pieces):
+                def fetch_all(sources=sources, at=at, span=span, unit=unit):
                     column = pl.multiple_of(lax.rem(at, per) * lane, lane)
-                    for offset, source in pieces[step]:
+                    for offset, source in sources:
                         pltpu.make_async_copy(
                             source.at[:, pl.ds(column, lane)], every.at[sim_at ^ offset, :, span], sems.at[unit]
                         ).start()
@@ -294,11 +299,11 @@
     def factor(offset):
         return jnp.where(one == offset, 2.0, 0.0) - jnp.where(two == offset, 1.0, 0.0)
 
-    for step in range(plan.row_devices):
+    for step, sources in zip(plan.steps, pieces):
         column = pl.multiple_of(lane + (rows_at ^ step) * plan.share, lane)
-        own[:, pl.ds(column, plan.share)] = pieces[step][0][1][...]
-        mixed = factor(0) * pieces[step][0][1][...]
-        for offset, source in pieces[step][1:]:
+        own[:, pl.ds(column, plan.share)] = sources[0][1][...]
+        mixed = factor(0) * sources[0][1][...]
+        for offset, source in sources[1:]:
             mixed = mixed + factor(offset) * source[...]
         partner[:, pl.ds(column, plan.share)] = mixed
     for a in range(0, plan.columns, stretch):
@@ -337,6 +342,10 @@
     return lax.ppermute(value, axis, [(i, i ^ offset) for i in range(count)])
 
 
+def exchange_all(plan, values):
+    return [exchange(value, "rows", step) if step else value for step, value in zip(plan.steps, values)]
+
+
 def gather(first, axis, bits):
     arrays, offsets = [first[None]], [[0]]
     for bit in bits:
@@ -358,12 +367,63 @@
     )
 
 
+def run_filter(plan, sharers, pieces, parts, tables):
+    vmem = pl.BlockSpec(memory_space=pltpu.VMEM)
+    far = pl.BlockSpec(memory_space=pltpu.HBM)
+    full = (plan.rows, plan.width)
+    tall = (max(plan.rows, plan.row_devices * plan.slab), plan.width)
+    return call(
+        functools.partial(filter_kernel, plan, sharers),
+        [jax.ShapeDtypeStruct((plan.slab, plan.share), jnp.float32)] * plan.row_devices,
+        [vmem] * plan.row_devices + [far] * len(parts) + [vmem] * len(tables),
+        [pltpu.VMEM(full, jnp.float32)] * 5
+        + [pltpu.VMEM((plan.row_devices * plan.slab, plan.share), jnp.float32)]
+        + [pltpu.VMEM(full, jnp.bfloat16)] * 2
+        + [pltpu.VMEM(tall, jnp.bfloat16)] * 2
+        + [pltpu.SemaphoreType.DMA],
+        1 << 33,
+        1 << 23,
+    )(*pieces, *parts, *tables)
+
+
+def run_estimate(plan, holders, pair_one, pair_two, owner, held):
+    vmem = pl.BlockSpec(memory_space=pltpu.VMEM)
+    smem = pl.BlockSpec(memory_space=pltpu.SMEM)
+
+    def f32(*shape):
+        return jax.ShapeDtypeStruct(shape, jnp.float32)
+
+    field_width = plan.columns // plan.sim_devices
+    fused = field_width if field_width % lane == 0 else 0
+    outs = [f32(plan.row_local, plan.columns)]
+    extended = (plan.slab, plan.columns + 2 * lane)
+    scratch = [pltpu.VMEM(extended, jnp.float32)] * 2
+    scratch += [pltpu.VMEM((plan.row_local, plan.columns), jnp.float32), pltpu.SemaphoreType.DMA]
+    if fused:
+        outs.append(f32(OWNERS, plan.row_local, fused))
+        scratch.append(pltpu.SemaphoreType.DMA((fused // lane + 2,)))
+        scratch.append(pltpu.VMEM((plan.sim_devices, plan.slab, fused + 2 * lane), jnp.float32))
+        scratch.append(pltpu.VMEM((OWNERS, plan.row_local, fused), jnp.float32))
+        scratch.append(pltpu.SemaphoreType.DMA((OWNERS,)))
+    else:
+        scratch.append(pltpu.SemaphoreType.DMA((1,)))
+    results = call(
+        functools.partial(estimate_kernel, plan, holders, fused),
+        outs,
+        [smem] * 3 + [vmem] * len(held),
+        scratch,
+        1 << 24,
+        1 << 23,
+        outs_in=pltpu.HBM,
+    )(pair_one, pair_two, owner, *held)
+    return results, fused
+
+
 def body(maps, weight, beam, pair_one, pair_two, owner):
     sim_local, row_local, columns = maps.shape
     taps = beam.shape[0]
     row_devices, sim_devices = lax.axis_size("rows"), lax.axis_size("sims")
     plan = Plan(row_devices, sim_devices, row_local, columns, taps)
-    place = jnp.stack([lax.axis_index("rows"), lax.axis_index("sims")]).astype(jnp.int32)
     vmem = pl.BlockSpec(memory_space=pltpu.VMEM)
     smem = pl.BlockSpec(memory_space=pltpu.SMEM)
     far = pl.BlockSpec(memory_space=pltpu.HBM)
@@ -378,42 +438,24 @@
         return jax.ShapeDtypeStruct(shape, jnp.bfloat16)
 
     cells = row_local * columns
-    parts = call(
-        functools.partial(share_kernel, plan),
-        [f32(plan.share_rows, plan.width)] * row_devices,
-        [smem, far],
-        [pltpu.VMEM((plan.share_rows, columns + 2 * plan.halo), jnp.float32), pltpu.SemaphoreType.DMA],
-        0,
-        1 << 18,
-    )(place, pinned(weight))
-    pieces = call(
-        functools.partial(weighted_kernel, plan),
-        [f32(row_local, plan.width)] * row_devices,
-        [smem, far, far],
-        [pltpu.VMEM((row_local, columns + 2 * plan.halo), jnp.float32)]
-        + [pltpu.VMEM((row_local, columns), jnp.float32)] * 2
-        + [pltpu.SemaphoreType.DMA((2, loads))],
+    made = call(
+        functools.partial(piece_kernel, plan),
+        [f32(row_local, plan.width)] * row_devices + [f32(plan.share_rows, plan.width)] * row_devices,
+        [far, far],
+        [pltpu.VMEM((row_local, columns + 2 * plan.halo), jnp.float32)] * 2
+        + [pltpu.VMEM((row_local, columns), jnp.float32), pltpu.SemaphoreType.DMA((2, loads))],
         cells,
         16 * cells,
-    )(place, pinned(maps.reshape(row_local, columns)), pinned(weight))
-    parts = [parts[0]] + [exchange(parts[d], "rows", d) for d in range(1, row_devices)]
+    )(pinned(maps.reshape(row_local, columns)), pinned(weight))
+    pieces, parts = made[:row_devices], made[row_devices:]
+    parts = exchange_all(plan, parts)
     pieces, parts = lax.optimization_barrier((pieces, parts))
-    pieces = [pieces[0]] + [exchange(pieces[d], "rows", d) for d in range(1, row_devices)]
-    sharers = []
+    pieces = exchange_all(plan, pieces)
     shapes = [(plan.rows, plan.rows), (row_devices * plan.slab, plan.rows)]
     for block in plan.blocks + plan.out_blocks[:1]:
         low, high = plan.window(block)
         shapes.append((high - low, block[1] - block[0]))
 
-    tables = call(
-        functools.partial(table_kernel, plan),
-        [b16(*shape) for shape in shapes for _ in range(2)],
-        [smem, vmem],
-        [pltpu.VMEM((8, lane), jnp.float32)],
-        1 << 32,
-        1 << 23,
-    )(place, beam[None])
-    parts, tables = lax.optimization_barrier((parts, tables))
 
     def spread(parts):
         found = {0: jnp.stack(parts)[None]}
@@ -422,6 +464,7 @@
         sharers[:] = [[offset] for offset in found] + [[offset ^ 1 for offset in found]]
         return [*found.values(), exchange(jnp.concatenate(list(found.values())), "sims", 1)]
 
+    sharers = []
     made = jax.eval_shape(spread, parts)
     parts = lax.cond(
         lax.axis_index("rows") < row_devices,
@@ -429,28 +472,22 @@
         lambda parts: jax.tree.map(lambda x: jnp.zeros(x.shape, x.dtype), made),
         parts,
     )
-
-    full = (plan.rows, plan.width)
-    tall = (max(plan.rows, row_devices * plan.slab), plan.width)
-    filtered = call(
-        functools.partial(filter_kernel, plan, sharers),
-        [f32(plan.slab, plan.share)] * row_devices,
-        [smem] + [vmem] * row_devices + [far] * len(parts) + [vmem] * len(tables),
-        [pltpu.VMEM(full, jnp.float32)] * 5
-        + [pltpu.VMEM((row_devices * plan.slab, plan.share), jnp.float32)]
-        + [pltpu.VMEM(full, jnp.bfloat16)] * 2
-        + [pltpu.VMEM(tall, jnp.bfloat16)] * 2
-        + [pltpu.SemaphoreType.DMA],
-        1 << 33,
-        1 << 23,
-    )(place, *pieces, *parts, *tables)
-
-    moved = [filtered[0]] + [exchange(filtered[step], "rows", step) for step in range(1, row_devices)]
+    beam, parts = lax.optimization_barrier((beam, parts))
+    tables = call(
+        functools.partial(table_kernel, plan),
+        [b16(*shape) for shape in shapes for _ in range(2)],
+        [vmem],
+        [pltpu.VMEM((8, lane), jnp.float32)],
+        0,
+        0,
+    )(beam[None])
+    filtered = run_filter(plan, sharers, pieces, parts, tables)
+    moved = exchange_all(plan, filtered)
     bits = [1 << i for i in range(1, sim_devices.bit_length() - 1)]
     arrays, holders = [], []
-    for step in range(row_devices):
+    for step, piece in enumerate(moved):
         turn = step % max(len(bits), 1)
-        found, offsets = gather(moved[step], "sims", bits[turn:] + bits[:turn])
+        found, offsets = gather(piece, "sims", bits[turn:] + bits[:turn])
         arrays.append(found)
         holders.append(offsets)
     held = []
@@ -458,35 +495,13 @@
         held += found + [exchange(jnp.concatenate(found), "sims", 1)]
         offsets.append([offset ^ 1 for order in offsets for offset in order])
 
-    field_width = columns // sim_devices
-    fused = field_width if field_width % lane == 0 else 0
-    outs = [f32(row_local, columns)]
-    extended = (plan.slab, columns + 2 * lane)
-    scratch = [pltpu.VMEM(extended, jnp.float32)] * 2
-    scratch += [pltpu.VMEM((row_local, columns), jnp.float32), pltpu.SemaphoreType.DMA]
-    if fused:
-        outs.append(f32(OWNERS, row_local, fused))
-        scratch.append(pltpu.SemaphoreType.DMA((fused // lane + 2,)))
-        scratch.append(pltpu.VMEM((sim_devices, plan.slab, fused + 2 * lane), jnp.float32))
-        scratch.append(pltpu.VMEM((OWNERS, row_local, fused), jnp.float32))
-        scratch.append(pltpu.SemaphoreType.DMA((OWNERS,)))
-    else:
-        scratch.append(pltpu.SemaphoreType.DMA((1,)))
-    results = call(
-        functools.partial(estimate_kernel, plan, holders, fused),
-        outs,
-        [smem] * 4 + [vmem] * len(held),
-        scratch,
-        1 << 24,
-        1 << 23,
-        outs_in=pltpu.HBM,
-    )(place, pair_one, pair_two, owner, *held)
+    results, fused = run_estimate(plan, holders, pair_one, pair_two, owner, held)
     estimate = results[0]
     if fused:
         mean_field = results[1]
     else:
         groups = jnp.arange(OWNERS, dtype=jnp.int32)
-        local_owner = owner[place[1]]
+        local_owner = owner[lax.axis_index("sims")]
         term = jnp.where((groups == local_owner)[:, None, None], estimate[None], 0.0)
         total = lax.psum_scatter(term, "sims", scatter_dimension=2, tiled=True)
         tally = jnp.sum((groups[:, None] == owner[None, :]).astype(jnp.float32), axis=1)

time: 97.6 us -> 81.7 us (0.84)
  local copies, waits for them, and re-layouts: 13.8 us -> 0.67 us
  Pallas kernels: 18.6 us -> 14.2 us
  waiting for transfers between devices: 30.6 us -> 33 us
    unnamed x58 -> x8, local copies, waits for them, and re-layouts: 13.8 us -> 0.67 us
    pallas_call x4 -> x3, Pallas kernels: 14.3 us -> 11.1 us  [the longest x1 5.47 us: run_filter(): call(functools.partial(filter_kernel, plan, sharers), [jax.ShapeDtypeStru...]
    ppermute x25, waiting for transfers between devices: 30.6 us -> 33 us  [exchange(): return lax.ppermute(value, axis, [(i, i ^ offset) for i in range(count)])]
    pallas_call x1, Pallas kernels: 4.3 us -> 3.09 us  [body(): call(functools.partial(table_kernel, plan), [b16(*shape) for shape in sha...]
  transfers between devices with their start and end apart: 25 -> 25, of which waited for: 14 -> 15; matrix products, arithmetic and copies ran while one was open for 2% -> 2% of each run, Pallas kernels for 6% -> 4%
where the time goes in v5:
time: 81.7 us; the launch traced here: 81.5 us
  waiting for transfers between devices  33 us (40%)
  starting transfers between devices  30.6 us (37%)
  Pallas kernels  14.2 us (17%)
  other arithmetic  2.04 us (2%)
  between operations  0.94 us (1%)
    ppermute x25, waiting for transfers between devices, exchange(): return lax.ppermute(value, axis, [(i, i ^ offset) for i in range(count)])  33 us
    ppermute x25, starting transfers between devices, exchange(): return lax.ppermute(value, axis, [(i, i ^ offset) for i in range(count)])  30.6 us
    pallas_call x1, Pallas kernels, run_filter(): call(functools.partial(filter_kernel, plan, sharers), [jax.ShapeDtypeStru...  5.47 us
    pallas_call x1, Pallas kernels, run_estimate(): call(functools.partial(estimate_kernel, plan, holders, fused), outs, [sme...  4.22 us
    pallas_call x1, Pallas kernels, body(): call(functools.partial(table_kernel, plan), [b16(*shape) for shape in sha...  3.09 us
  transfers between devices with their start and end apart: 25, of which 15 were waited for; matrix products, arithmetic and copies ran while one was open for 2% of the time, Pallas kernels for 4%

profile of v5, /device:TPU:0, one launch (start us, length us, event | category | flops | bytes accessed | tf_op | source)
XLA Modules:
  0.0 81.5 jit_solution(17760319335904343573)
XLA Ops:
  0.6 1.4 %shard_map.77 = (f32[64,1024]{1,0:T(8,128)S(1)}, f32[64,1024]{1,0:T(8,128)S(1)}, f32[64,1024]{1,0:T(8,128)S(1)}, f32[64,1024]{1,0:T(8,128)S(1)}, f32[8,1024]{1,0...) custom-call(f32[64,2048]{1,0:T(8,128)} %bitcast.30, f32[64,2048]{1,0:T(8,128)} %weight.1), custom_call_target="tpu_custom_call" | custom-call | flops 131072 | bytes 2097152 | tf_op jit(solution)/shard_map/pallas_call | solution.py:441
  2.0 5.1 %collective-permute-start.4 = (f32[8,1024]{1,0:T(8,128)S(1)}, f32[8,1024]{1,0:T(8,128)S(1)}, u32[]{:S(2)}, u32[]{:S(2)}) collective-permute-start(f32[8,1024]{1,0:T(8,128)S(1)} %get-tuple-element.68), channel_id=1, source_target_pairs={{0,3},{1,2},{2,1},{3,0},{4,7},{5,6},{6,5},{7,4},{8,11},{9,10},{10,... | collective-permute-start | bytes 98312 | tf_op jit(solution)/shard_map/ppermute | solution.py:342
  7.1 0.0 collective-permute-start.5
  7.2 0.6 collective-permute-start.6
  7.8 1.3 %collective-permute-done.4 = f32[8,1024]{1,0:T(8,128)S(1)} collective-permute-done((f32[8,1024]{1,0:T(8,128)S(1)}, f32[8,1024]{1,0:T(8,128)S(1)}, u32[]{:S(2)}, u32[]{:S(2)}) %collective-permute-start.4) | collective-permute-done | bytes 32800 | tf_op jit(solution)/shard_map/ppermute | solution.py:342
  9.0 2.9 %collective-permute-done.5 = f32[8,1024]{1,0:T(8,128)S(1)} collective-permute-done((f32[8,1024]{1,0:T(8,128)S(1)}, f32[8,1024]{1,0:T(8,128)S(1)}, u32[]{:S(2)}, u32[]{:S(2)}) %collective-permute-start.5) | collective-permute-done | bytes 32800 | tf_op jit(solution)/shard_map/ppermute | solution.py:342
  12.0 0.0 collective-permute-done.6
  12.0 1.5 %collective-permute-start.7 = (f32[64,1024]{1,0:T(8,128)S(1)}, f32[64,1024]{1,0:T(8,128)S(1)}, u32[]{:S(2)}, u32[]{:S(2)}) collective-permute-start(f32[64,1024]{1,0:T(8,128)S(1)} %get-tuple-element.72), channel_id=1, source_target_pairs={{0,3},{1,2},{2,1},{3,0},{4,7},{5,6},{6,5},{7,4},{8,11},{9,10},{10,... | collective-permute-start | bytes 786440 | tf_op jit(solution)/shard_map/ppermute | solution.py:342
  13.4 0.6 collective-permute-start.8
  14.0 2.4 %collective-permute-start.9 = (f32[64,1024]{1,0:T(8,128)S(1)}, f32[64,1024]{1,0:T(8,128)S(1)}, u32[]{:S(2)}, u32[]{:S(2)}) collective-permute-start(f32[64,1024]{1,0:T(8,128)S(1)} %get-tuple-element.74), channel_id=1, source_target_pairs={{0,1},{1,0},{2,3},{3,2},{4,5},{5,4},{6,7},{7,6},{8,9},{9,8},{10,11... | collective-permute-start | bytes 786440 | tf_op jit(solution)/shard_map/ppermute | solution.py:342
  16.4 14.5 %conditional.1 = (f32[1,4,8,1024]{3,2,1,0:T(8,128)}, f32[1,4,8,1024]{3,2,1,0:T(8,128)}, f32[1,4,8,1024]{3,2,1,0:T(8,128)}, f32[1,4,8,1024]{3,2,1,0:T(8,128)}, f32[4,4,8,1024]{3,2,1,0:T(8,128)}) conditional(s32[]{:T(128)} %convert_element_type.3, () %tuple.19, (f32[8,1024]{1,0:T(8,128)S(1)}, f32[8,1024]{1,0:T(8,128)S(1)}, f32[8,1024]{1,0:T(8,128)S(1)}, ...), branch_computations={%region_0.0_spmd, %region_1.0_spmd} | conditional | flops 491520 | bytes 4980936 | solution.py:469
  16.4 0.7 maximum_bitcast_fusion
  17.0 1.5 %collective-permute-start = (f32[1,4,8,1024]{3,2,1,0:T(8,128)}, f32[1,4,8,1024]{3,2,1,0:T(8,128)}, u32[]{:S(2)}, u32[]{:S(2)}) collective-permute-start(f32[1,4,8,1024]{3,2,1,0:T(8,128)} %maximum_bitcast_fusion), channel_id=1, source_target_pairs={{0,8},{4,12},{8,0},{12,4},{16,24},{20,28},{24,16},{28,20},{1,9},{5... | collective-permute-start | bytes 393224 | tf_op jit(solution)/shard_map/cond/branch_1_fun/ppermute | solution.py:342
  18.5 1.5 %collective-permute-start.1 = (f32[1,4,8,1024]{3,2,1,0:T(8,128)}, f32[1,4,8,1024]{3,2,1,0:T(8,128)}, u32[]{:S(2)}, u32[]{:S(2)}) collective-permute-start(f32[1,4,8,1024]{3,2,1,0:T(8,128)} %maximum_bitcast_fusion), channel_id=1, source_target_pairs={{0,16},{4,20},{8,24},{12,28},{16,0},{20,4},{24,8},{28,12},{1,17},{... | collective-permute-start | bytes 393224 | tf_op jit(solution)/shard_map/cond/branch_1_fun/ppermute | solution.py:342
  20.0 2.3 %collective-permute-done = f32[1,4,8,1024]{3,2,1,0:T(8,128)} collective-permute-done((f32[1,4,8,1024]{3,2,1,0:T(8,128)}, f32[1,4,8,1024]{3,2,1,0:T(8,128)}, u32[]{:S(2)}, u32[]{:S(2)}) %collective-permute-start) | collective-permute-done | bytes 131104 | tf_op jit(solution)/shard_map/cond/branch_1_fun/ppermute | solution.py:342
  22.3 1.5 %collective-permute-start.2 = (f32[1,4,8,1024]{3,2,1,0:T(8,128)}, f32[1,4,8,1024]{3,2,1,0:T(8,128)}, u32[]{:S(2)}, u32[]{:S(2)}) collective-permute-start(f32[1,4,8,1024]{3,2,1,0:T(8,128)} %collective-permute-done), channel_id=1, source_target_pairs={{0,16},{4,20},{8,24},{12,28},{16,0},{20,4},{24,8},{28,12},{1,17},{... | collective-permute-start | bytes 393224 | tf_op jit(solution)/shard_map/cond/branch_1_fun/ppermute | solution.py:342
  23.8 0.8 %collective-permute-done.1 = f32[1,4,8,1024]{3,2,1,0:T(8,128)} collective-permute-done((f32[1,4,8,1024]{3,2,1,0:T(8,128)}, f32[1,4,8,1024]{3,2,1,0:T(8,128)}, u32[]{:S(2)}, u32[]{:S(2)}) %collective-permute-start.1) | collective-permute-done | bytes 131104 | tf_op jit(solution)/shard_map/cond/branch_1_fun/ppermute | solution.py:342
  24.7 2.9 %collective-permute-done.2 = f32[1,4,8,1024]{3,2,1,0:T(8,128)} collective-permute-done((f32[1,4,8,1024]{3,2,1,0:T(8,128)}, f32[1,4,8,1024]{3,2,1,0:T(8,128)}, u32[]{:S(2)}, u32[]{:S(2)}) %collective-permute-start.2) | collective-permute-done | bytes 131104 | tf_op jit(solution)/shard_map/cond/branch_1_fun/ppermute | solution.py:342
  27.6 1.1 %pad_maximum_fusion = f32[4,4,8,1024]{3,2,1,0:T(8,128)S(1)} fusion(f32[1,4,8,1024]{3,2,1,0:T(8,128)} %collective-permute-done.2, f32[1,4,8,1024]{3,2,1,0:T(8,128)} %collective-permute-done.1, f32[1,4,8,1024]{3,2,1,0:T(8,128)} %collective-permute-done, f32[1,4,8,1024]{3,2,1,0:T(8,128)} %maximum_bitcast_fusion), kind=kLoop, calls=%fused_computation | loop fusion | flops 393216 | bytes 1048576 | tf_op jit(solution)/shard_map/cond/branch_1_fun/concatenate | solution.py:465
  28.7 0.1 collective-permute-start.3
  28.8 2.0 %collective-permute-done.3 = f32[4,4,8,1024]{3,2,1,0:T(8,128)} collective-permute-done((f32[4,4,8,1024]{3,2,1,0:T(8,128)S(1)}, f32[4,4,8,1024]{3,2,1,0:T(8,128)}, u32[]{:S(2)}, u32[]{:S(2)}) %collective-permute-start.3) | collective-permute-done | bytes 524320 | tf_op jit(solution)/shard_map/cond/branch_1_fun/ppermute | solution.py:342
  30.8 0.7 copy-done.3
  31.5 3.1 %shard_map.78 = (bf16[256,256]{1,0:T(8,128)(2,1)S(1)}, bf16[256,256]{1,0:T(8,128)(2,1)S(1)}, bf16[288,256]{1,0:T(8,128)(2,1)S(1)}, bf16[288,256]{1,0:T(8,128)(2,...) custom-call(f32[1,65]{1,0:T(1,128)S(1)} %bitcast.29), custom_call_target="tpu_custom_call" | custom-call | tf_op jit(solution)/shard_map/pallas_call | solution.py:476
  34.6 0.0 collective-permute-done.7.refs_1_
  34.6 1.1 %collective-permute-done.8.refs_2_ = f32[64,1024]{1,0:T(8,128)S(1)} collective-permute-done((f32[64,1024]{1,0:T(8,128)S(1)}, f32[64,1024]{1,0:T(8,128)S(1)}, u32[]{:S(2)}, u32[]{:S(2)}) %collective-permute-start.8) | collective-permute-done | bytes 262176 | tf_op jit(solution)/shard_map/ppermute | solution.py:342
  35.7 0.0 collective-permute-done.9.refs_3_
  35.7 5.5 %shard_map.79 = (f32[72,512]{1,0:T(8,128)S(1)}, f32[72,512]{1,0:T(8,128)S(1)}, f32[72,512]{1,0:T(8,128)S(1)}, f32[72,512]{1,0:T(8,128)S(1)}) custom-call(f32[64,1024]{1,0:T(8,128)S(1)} %get-tuple-element.71.refs_0_, f32[64,1024]{1,0:T(8,128)S(1)} %collective-permute-done.7.refs_1_, f32[64,1024]{1,0:T(8,128)S(1)} %collective-permute-done.8.refs_2_, ...), custom_call_target="tpu_custom_call" | custom-call | flops 8589934592 | bytes 8388608 | tf_op jit(solution)/shard_map/pallas_call | solution.py:375
  41.2 2.7 %collective-permute-start.13 = (f32[72,512]{1,0:T(8,128)S(1)}, f32[72,512]{1,0:T(8,128)S(1)}, u32[]{:S(2)}, u32[]{:S(2)}) collective-permute-start(f32[72,512]{1,0:T(8,128)S(1)} %get-tuple-element.107), channel_id=1, source_target_pairs={{0,3},{1,2},{2,1},{3,0},{4,7},{5,6},{6,5},{7,4},{8,11},{9,10},{10,... | collective-permute-start | bytes 442376 | tf_op jit(solution)/shard_map/ppermute | solution.py:342
  43.9 0.0 collective-permute-start.17
  43.9 1.7 %collective-permute-start.21 = (f32[72,512]{1,0:T(8,128)S(1)}, f32[72,512]{1,0:T(8,128)S(1)}, u32[]{:S(2)}, u32[]{:S(2)}) collective-permute-start(f32[72,512]{1,0:T(8,128)S(1)} %get-tuple-element.109), channel_id=1, source_target_pairs={{0,1},{1,0},{2,3},{3,2},{4,5},{5,4},{6,7},{7,6},{8,9},{9,8},{10,11... | collective-permute-start | bytes 442376 | tf_op jit(solution)/shard_map/ppermute | solution.py:342
  45.7 1.5 %collective-permute-start.10 = (f32[1,72,512]{2,1,0:T(8,128)S(1)}, f32[1,72,512]{2,1,0:T(8,128)S(1)}, u32[]{:S(2)}, u32[]{:S(2)}) collective-permute-start(f32[1,72,512]{2,1,0:T(8,128)S(1)} %bitcast.13), channel_id=1, source_target_pairs={{0,8},{4,12},{8,0},{12,4},{16,24},{20,28},{24,16},{28,20},{1,9},{5... | collective-permute-start | bytes 442376 | tf_op jit(solution)/shard_map/ppermute | solution.py:342
  47.2 2.7 %collective-permute-done.13 = f32[72,512]{1,0:T(8,128)S(1)} collective-permute-done((f32[72,512]{1,0:T(8,128)S(1)}, f32[72,512]{1,0:T(8,128)S(1)}, u32[]{:S(2)}, u32[]{:S(2)}) %collective-permute-start.13) | collective-permute-done | bytes 147488 | tf_op jit(solution)/shard_map/ppermute | solution.py:342
  49.9 1.5 %collective-permute-start.14 = (f32[1,72,512]{2,1,0:T(8,128)S(1)}, f32[1,72,512]{2,1,0:T(8,128)S(1)}, u32[]{:S(2)}, u32[]{:S(2)}) collective-permute-start(f32[1,72,512]{2,1,0:T(8,128)S(1)} %bitcast.17), channel_id=1, source_target_pairs={{0,16},{4,20},{8,24},{12,28},{16,0},{20,4},{24,8},{28,12},{1,17},{... | collective-permute-start | bytes 442376 | tf_op jit(solution)/shard_map/ppermute | solution.py:342
  51.4 3.8 %collective-permute-done.17 = f32[72,512]{1,0:T(8,128)S(1)} collective-permute-done((f32[72,512]{1,0:T(8,128)S(1)}, f32[72,512]{1,0:T(8,128)S(1)}, u32[]{:S(2)}, u32[]{:S(2)}) %collective-permute-start.17) | collective-permute-done | bytes 147488 | tf_op jit(solution)/shard_map/ppermute | solution.py:342
  55.2 1.5 %collective-permute-start.18 = (f32[1,72,512]{2,1,0:T(8,128)S(1)}, f32[1,72,512]{2,1,0:T(8,128)S(1)}, u32[]{:S(2)}, u32[]{:S(2)}) collective-permute-start(f32[1,72,512]{2,1,0:T(8,128)S(1)} %bitcast.21), channel_id=1, source_target_pairs={{0,8},{4,12},{8,0},{12,4},{16,24},{20,28},{24,16},{28,20},{1,9},{5... | collective-permute-start | bytes 442376 | tf_op jit(solution)/shard_map/ppermute | solution.py:342
  56.7 0.0 collective-permute-done.21
  56.7 1.5 %collective-permute-start.22 = (f32[1,72,512]{2,1,0:T(8,128)S(1)}, f32[1,72,512]{2,1,0:T(8,128)S(1)}, u32[]{:S(2)}, u32[]{:S(2)}) collective-permute-start(f32[1,72,512]{2,1,0:T(8,128)S(1)} %bitcast.25), channel_id=1, source_target_pairs={{0,16},{4,20},{8,24},{12,28},{16,0},{20,4},{24,8},{28,12},{1,17},{... | collective-permute-start | bytes 442376 | tf_op jit(solution)/shard_map/ppermute | solution.py:342
  58.2 0.0 collective-permute-done.10.refs_1_
  58.2 0.6 collective-permute-start.11
  58.8 0.0 collective-permute-done.14.refs_5_
  58.8 0.6 collective-permute-start.15
  59.4 1.3 %collective-permute-done.18.refs_9_ = f32[1,72,512]{2,1,0:T(8,128)S(1)} collective-permute-done((f32[1,72,512]{2,1,0:T(8,128)S(1)}, f32[1,72,512]{2,1,0:T(8,128)S(1)}, u32[]{:S(2)}, u32[]{:S(2)}) %collective-permute-start.18) | collective-permute-done | bytes 147488 | tf_op jit(solution)/shard_map/ppermute | solution.py:342
  60.7 1.6 %collective-permute-start.19 = (f32[2,72,512]{2,1,0:T(8,128)S(1)}, f32[2,72,512]{2,1,0:T(8,128)S(1)}, u32[]{:S(2)}, u32[]{:S(2)}) collective-permute-start(f32[2,72,512]{2,1,0:T(8,128)S(1)} %pad_maximum_fusion.7), channel_id=1, source_target_pairs={{0,16},{4,20},{8,24},{12,28},{16,0},{20,4},{24,8},{28,12},{1,17},{... | collective-permute-start | bytes 884744 | tf_op jit(solution)/shard_map/ppermute | solution.py:342
  62.3 1.2 %collective-permute-done.22.refs_13_ = f32[1,72,512]{2,1,0:T(8,128)S(1)} collective-permute-done((f32[1,72,512]{2,1,0:T(8,128)S(1)}, f32[1,72,512]{2,1,0:T(8,128)S(1)}, u32[]{:S(2)}, u32[]{:S(2)}) %collective-permute-start.22) | collective-permute-done | bytes 147488 | tf_op jit(solution)/shard_map/ppermute | solution.py:342
  63.5 1.4 %collective-permute-start.23 = (f32[2,72,512]{2,1,0:T(8,128)S(1)}, f32[2,72,512]{2,1,0:T(8,128)S(1)}, u32[]{:S(2)}, u32[]{:S(2)}) collective-permute-start(f32[2,72,512]{2,1,0:T(8,128)S(1)} %pad_maximum_fusion.8), channel_id=1, source_target_pairs={{0,8},{4,12},{8,0},{12,4},{16,24},{20,28},{24,16},{28,20},{1,9},{5... | collective-permute-start | bytes 884744 | tf_op jit(solution)/shard_map/ppermute | solution.py:342
  64.8 4.9 %collective-permute-done.11.refs_2_ = f32[2,72,512]{2,1,0:T(8,128)S(1)} collective-permute-done((f32[2,72,512]{2,1,0:T(8,128)S(1)}, f32[2,72,512]{2,1,0:T(8,128)S(1)}, u32[]{:S(2)}, u32[]{:S(2)}) %collective-permute-start.11) | collective-permute-done | bytes 294944 | tf_op jit(solution)/shard_map/ppermute | solution.py:342
  69.8 0.1 collective-permute-start.12
  69.9 0.0 collective-permute-done.15.refs_6_
  69.9 0.5 collective-permute-start.16
  70.5 3.6 %collective-permute-done.19.refs_10_ = f32[2,72,512]{2,1,0:T(8,128)S(1)} collective-permute-done((f32[2,72,512]{2,1,0:T(8,128)S(1)}, f32[2,72,512]{2,1,0:T(8,128)S(1)}, u32[]{:S(2)}, u32[]{:S(2)}) %collective-permute-start.19) | collective-permute-done | bytes 294944 | tf_op jit(solution)/shard_map/ppermute | solution.py:342
  74.1 0.0 copy-start
  74.1 0.0 copy-start.1
  74.1 0.0 copy-start.2
  74.1 0.1 collective-permute-start.20
  74.2 0.0 collective-permute-done.23.refs_14_
  74.3 0.5 collective-permute-start.24
  74.8 0.0 collective-permute-done.12.refs_3_
  74.8 0.0 collective-permute-done.16.refs_7_
  74.8 1.4 %collective-permute-done.20.refs_11_ = f32[4,72,512]{2,1,0:T(8,128)S(1)} collective-permute-done((f32[4,72,512]{2,1,0:T(8,128)S(1)}, f32[4,72,512]{2,1,0:T(8,128)S(1)}, u32[]{:S(2)}, u32[]{:S(2)}) %collective-permute-start.20) | collective-permute-done | bytes 589856 | tf_op jit(solution)/shard_map/ppermute | solution.py:342
  76.2 0.8 %collective-permute-done.24.refs_15_ = f32[4,72,512]{2,1,0:T(8,128)S(1)} collective-permute-done((f32[4,72,512]{2,1,0:T(8,128)S(1)}, f32[4,72,512]{2,1,0:T(8,128)S(1)}, u32[]{:S(2)}, u32[]{:S(2)}) %collective-permute-start.24) | collective-permute-done | bytes 589856 | tf_op jit(solution)/shard_map/ppermute | solution.py:342
  77.1 0.0 copy-done
  77.1 0.0 copy-done.1
  77.1 0.0 copy-done.2
  77.1 4.2 %shard_map.80 = (f32[64,2048]{1,0:T(8,128)}, f32[8,64,256]{2,1,0:T(8,128)}) custom-call(s32[8]{0:T(128)S(1)} %copy-done, s32[8]{0:T(128)S(1)} %copy-done.1, s32[8]{0:T(128)S(1)} %copy-done.2, f32[1,72,512]{2,1,0:T(8,128)S(1)} %bitcast.16, f32[1,72,512]{2,1,0:T(8,128)S(1)} %collective-permute-done.10.refs_1_, ...), custom_call_target="tpu_custom_call" | custom-call | flops 16777216 | bytes 8388608 | tf_op jit(solution)/shard_map/pallas_call | solution.py:410
  (9 shorter events, 0.2 us)
Async XLA Ops:
  2.0 7.0 %collective-permute-start.4 = (f32[8,1024]{1,0:T(8,128)S(1)}, f32[8,1024]{1,0:T(8,128)S(1)}, u32[]{:S(2)}, u32[]{:S(2)}) collective-permute-start(f32[8,1024]{1,0:T(8,128)S(1)} %get-tuple-element.68), channel_id=1, source_target_pairs={{0,3},{1,2},{2,1},{3,0},{4,7},{5,6},{6,5},{7,4},{8,11},{9,10},{10,... | collective-permute-start | bytes 98312 | tf_op jit(solution)/shard_map/ppermute | solution.py:342
  7.1 4.8 %collective-permute-start.5 = (f32[8,1024]{1,0:T(8,128)S(1)}, f32[8,1024]{1,0:T(8,128)S(1)}, u32[]{:S(2)}, u32[]{:S(2)}) collective-permute-start(f32[8,1024]{1,0:T(8,128)S(1)} %get-tuple-element.69), channel_id=1, source_target_pairs={{0,2},{1,3},{2,0},{3,1},{4,6},{5,7},{6,4},{7,5},{8,10},{9,11},{10,... | collective-permute-start | bytes 98312 | tf_op jit(solution)/shard_map/ppermute | solution.py:342
  7.2 4.8 %collective-permute-start.6 = (f32[8,1024]{1,0:T(8,128)S(1)}, f32[8,1024]{1,0:T(8,128)S(1)}, u32[]{:S(2)}, u32[]{:S(2)}) collective-permute-start(f32[8,1024]{1,0:T(8,128)S(1)} %get-tuple-element.70), channel_id=1, source_target_pairs={{0,1},{1,0},{2,3},{3,2},{4,5},{5,4},{6,7},{7,6},{8,9},{9,8},{10,11... | collective-permute-start | bytes 98312 | tf_op jit(solution)/shard_map/ppermute | solution.py:342
  12.0 22.6 %collective-permute-start.7 = (f32[64,1024]{1,0:T(8,128)S(1)}, f32[64,1024]{1,0:T(8,128)S(1)}, u32[]{:S(2)}, u32[]{:S(2)}) collective-permute-start(f32[64,1024]{1,0:T(8,128)S(1)} %get-tuple-element.72), channel_id=1, source_target_pairs={{0,3},{1,2},{2,1},{3,0},{4,7},{5,6},{6,5},{7,4},{8,11},{9,10},{10,... | collective-permute-start | bytes 786440 | tf_op jit(solution)/shard_map/ppermute | solution.py:342
  13.4 22.3 %collective-permute-start.8 = (f32[64,1024]{1,0:T(8,128)S(1)}, f32[64,1024]{1,0:T(8,128)S(1)}, u32[]{:S(2)}, u32[]{:S(2)}) collective-permute-start(f32[64,1024]{1,0:T(8,128)S(1)} %get-tuple-element.73), channel_id=1, source_target_pairs={{0,2},{1,3},{2,0},{3,1},{4,6},{5,7},{6,4},{7,5},{8,10},{9,11},{10,... | collective-permute-start | bytes 786440 | tf_op jit(solution)/shard_map/ppermute | solution.py:342
  14.0 21.7 %collective-permute-start.9 = (f32[64,1024]{1,0:T(8,128)S(1)}, f32[64,1024]{1,0:T(8,128)S(1)}, u32[]{:S(2)}, u32[]{:S(2)}) collective-permute-start(f32[64,1024]{1,0:T(8,128)S(1)} %get-tuple-element.74), channel_id=1, source_target_pairs={{0,1},{1,0},{2,3},{3,2},{4,5},{5,4},{6,7},{7,6},{8,9},{9,8},{10,11... | collective-permute-start | bytes 786440 | tf_op jit(solution)/shard_map/ppermute | solution.py:342
  17.0 5.3 %collective-permute-start = (f32[1,4,8,1024]{3,2,1,0:T(8,128)}, f32[1,4,8,1024]{3,2,1,0:T(8,128)}, u32[]{:S(2)}, u32[]{:S(2)}) collective-permute-start(f32[1,4,8,1024]{3,2,1,0:T(8,128)} %maximum_bitcast_fusion), channel_id=1, source_target_pairs={{0,8},{4,12},{8,0},{12,4},{16,24},{20,28},{24,16},{28,20},{1,9},{5... | collective-permute-start | bytes 393224 | tf_op jit(solution)/shard_map/cond/branch_1_fun/ppermute | solution.py:342
  18.5 6.1 %collective-permute-start.1 = (f32[1,4,8,1024]{3,2,1,0:T(8,128)}, f32[1,4,8,1024]{3,2,1,0:T(8,128)}, u32[]{:S(2)}, u32[]{:S(2)}) collective-permute-start(f32[1,4,8,1024]{3,2,1,0:T(8,128)} %maximum_bitcast_fusion), channel_id=1, source_target_pairs={{0,16},{4,20},{8,24},{12,28},{16,0},{20,4},{24,8},{28,12},{1,17},{... | collective-permute-start | bytes 393224 | tf_op jit(solution)/shard_map/cond/branch_1_fun/ppermute | solution.py:342
  22.3 5.3 %collective-permute-start.2 = (f32[1,4,8,1024]{3,2,1,0:T(8,128)}, f32[1,4,8,1024]{3,2,1,0:T(8,128)}, u32[]{:S(2)}, u32[]{:S(2)}) collective-permute-start(f32[1,4,8,1024]{3,2,1,0:T(8,128)} %collective-permute-done), channel_id=1, source_target_pairs={{0,16},{4,20},{8,24},{12,28},{16,0},{20,4},{24,8},{28,12},{1,17},{... | collective-permute-start | bytes 393224 | tf_op jit(solution)/shard_map/cond/branch_1_fun/ppermute | solution.py:342
  28.7 2.1 %collective-permute-start.3 = (f32[4,4,8,1024]{3,2,1,0:T(8,128)S(1)}, f32[4,4,8,1024]{3,2,1,0:T(8,128)}, u32[]{:S(2)}, u32[]{:S(2)}) collective-permute-start(f32[4,4,8,1024]{3,2,1,0:T(8,128)S(1)} %pad_maximum_fusion), channel_id=1, source_target_pairs={{0,4},{4,0},{8,12},{12,8},{16,20},{20,16},{24,28},{28,24},{1,5},{5... | collective-permute-start | bytes 1572872 | tf_op jit(solution)/shard_map/cond/branch_1_fun/ppermute | solution.py:342
  30.8 0.7 copy-start.3
  41.2 8.7 %collective-permute-start.13 = (f32[72,512]{1,0:T(8,128)S(1)}, f32[72,512]{1,0:T(8,128)S(1)}, u32[]{:S(2)}, u32[]{:S(2)}) collective-permute-start(f32[72,512]{1,0:T(8,128)S(1)} %get-tuple-element.107), channel_id=1, source_target_pairs={{0,3},{1,2},{2,1},{3,0},{4,7},{5,6},{6,5},{7,4},{8,11},{9,10},{10,... | collective-permute-start | bytes 442376 | tf_op jit(solution)/shard_map/ppermute | solution.py:342
  43.9 11.2 %collective-permute-start.17 = (f32[72,512]{1,0:T(8,128)S(1)}, f32[72,512]{1,0:T(8,128)S(1)}, u32[]{:S(2)}, u32[]{:S(2)}) collective-permute-start(f32[72,512]{1,0:T(8,128)S(1)} %get-tuple-element.108), channel_id=1, source_target_pairs={{0,2},{1,3},{2,0},{3,1},{4,6},{5,7},{6,4},{7,5},{8,10},{9,11},{10,... | collective-permute-start | bytes 442376 | tf_op jit(solution)/shard_map/ppermute | solution.py:342
  43.9 12.7 %collective-permute-start.21 = (f32[72,512]{1,0:T(8,128)S(1)}, f32[72,512]{1,0:T(8,128)S(1)}, u32[]{:S(2)}, u32[]{:S(2)}) collective-permute-start(f32[72,512]{1,0:T(8,128)S(1)} %get-tuple-element.109), channel_id=1, source_target_pairs={{0,1},{1,0},{2,3},{3,2},{4,5},{5,4},{6,7},{7,6},{8,9},{9,8},{10,11... | collective-permute-start | bytes 442376 | tf_op jit(solution)/shard_map/ppermute | solution.py:342
  45.7 12.5 %collective-permute-start.10 = (f32[1,72,512]{2,1,0:T(8,128)S(1)}, f32[1,72,512]{2,1,0:T(8,128)S(1)}, u32[]{:S(2)}, u32[]{:S(2)}) collective-permute-start(f32[1,72,512]{2,1,0:T(8,128)S(1)} %bitcast.13), channel_id=1, source_target_pairs={{0,8},{4,12},{8,0},{12,4},{16,24},{20,28},{24,16},{28,20},{1,9},{5... | collective-permute-start | bytes 442376 | tf_op jit(solution)/shard_map/ppermute | solution.py:342
  49.9 8.9 %collective-permute-start.14 = (f32[1,72,512]{2,1,0:T(8,128)S(1)}, f32[1,72,512]{2,1,0:T(8,128)S(1)}, u32[]{:S(2)}, u32[]{:S(2)}) collective-permute-start(f32[1,72,512]{2,1,0:T(8,128)S(1)} %bitcast.17), channel_id=1, source_target_pairs={{0,16},{4,20},{8,24},{12,28},{16,0},{20,4},{24,8},{28,12},{1,17},{... | collective-permute-start | bytes 442376 | tf_op jit(solution)/shard_map/ppermute | solution.py:342
  55.2 5.5 %collective-permute-start.18 = (f32[1,72,512]{2,1,0:T(8,128)S(1)}, f32[1,72,512]{2,1,0:T(8,128)S(1)}, u32[]{:S(2)}, u32[]{:S(2)}) collective-permute-start(f32[1,72,512]{2,1,0:T(8,128)S(1)} %bitcast.21), channel_id=1, source_target_pairs={{0,8},{4,12},{8,0},{12,4},{16,24},{20,28},{24,16},{28,20},{1,9},{5... | collective-permute-start | bytes 442376 | tf_op jit(solution)/shard_map/ppermute | solution.py:342
  56.7 6.8 %collective-permute-start.22 = (f32[1,72,512]{2,1,0:T(8,128)S(1)}, f32[1,72,512]{2,1,0:T(8,128)S(1)}, u32[]{:S(2)}, u32[]{:S(2)}) collective-permute-start(f32[1,72,512]{2,1,0:T(8,128)S(1)} %bitcast.25), channel_id=1, source_target_pairs={{0,16},{4,20},{8,24},{12,28},{16,0},{20,4},{24,8},{28,12},{1,17},{... | collective-permute-start | bytes 442376 | tf_op jit(solution)/shard_map/ppermute | solution.py:342
  58.2 11.6 %collective-permute-start.11 = (f32[2,72,512]{2,1,0:T(8,128)S(1)}, f32[2,72,512]{2,1,0:T(8,128)S(1)}, u32[]{:S(2)}, u32[]{:S(2)}) collective-permute-start(f32[2,72,512]{2,1,0:T(8,128)S(1)} %pad_maximum_fusion.5), channel_id=1, source_target_pairs={{0,16},{4,20},{8,24},{12,28},{16,0},{20,4},{24,8},{28,12},{1,17},{... | collective-permute-start | bytes 884744 | tf_op jit(solution)/shard_map/ppermute | solution.py:342
  58.8 11.1 %collective-permute-start.15 = (f32[2,72,512]{2,1,0:T(8,128)S(1)}, f32[2,72,512]{2,1,0:T(8,128)S(1)}, u32[]{:S(2)}, u32[]{:S(2)}) collective-permute-start(f32[2,72,512]{2,1,0:T(8,128)S(1)} %pad_maximum_fusion.6), channel_id=1, source_target_pairs={{0,8},{4,12},{8,0},{12,4},{16,24},{20,28},{24,16},{28,20},{1,9},{5... | collective-permute-start | bytes 884744 | tf_op jit(solution)/shard_map/ppermute | solution.py:342
  60.7 13.4 %collective-permute-start.19 = (f32[2,72,512]{2,1,0:T(8,128)S(1)}, f32[2,72,512]{2,1,0:T(8,128)S(1)}, u32[]{:S(2)}, u32[]{:S(2)}) collective-permute-start(f32[2,72,512]{2,1,0:T(8,128)S(1)} %pad_maximum_fusion.7), channel_id=1, source_target_pairs={{0,16},{4,20},{8,24},{12,28},{16,0},{20,4},{24,8},{28,12},{1,17},{... | collective-permute-start | bytes 884744 | tf_op jit(solution)/shard_map/ppermute | solution.py:342
  63.5 10.8 %collective-permute-start.23 = (f32[2,72,512]{2,1,0:T(8,128)S(1)}, f32[2,72,512]{2,1,0:T(8,128)S(1)}, u32[]{:S(2)}, u32[]{:S(2)}) collective-permute-start(f32[2,72,512]{2,1,0:T(8,128)S(1)} %pad_maximum_fusion.8), channel_id=1, source_target_pairs={{0,8},{4,12},{8,0},{12,4},{16,24},{20,28},{24,16},{28,20},{1,9},{5... | collective-permute-start | bytes 884744 | tf_op jit(solution)/shard_map/ppermute | solution.py:342
  69.8 5.0 %collective-permute-start.12 = (f32[4,72,512]{2,1,0:T(8,128)S(1)}, f32[4,72,512]{2,1,0:T(8,128)S(1)}, u32[]{:S(2)}, u32[]{:S(2)}) collective-permute-start(f32[4,72,512]{2,1,0:T(8,128)S(1)} %pad_maximum_fusion.1), channel_id=1, source_target_pairs={{0,4},{4,0},{8,12},{12,8},{16,20},{20,16},{24,28},{28,24},{1,5},{5... | collective-permute-start | bytes 1769480 | tf_op jit(solution)/shard_map/ppermute | solution.py:342
  69.9 4.9 %collective-permute-start.16 = (f32[4,72,512]{2,1,0:T(8,128)S(1)}, f32[4,72,512]{2,1,0:T(8,128)S(1)}, u32[]{:S(2)}, u32[]{:S(2)}) collective-permute-start(f32[4,72,512]{2,1,0:T(8,128)S(1)} %pad_maximum_fusion.2), channel_id=1, source_target_pairs={{0,4},{4,0},{8,12},{12,8},{16,20},{20,16},{24,28},{28,24},{1,5},{5... | collective-permute-start | bytes 1769480 | tf_op jit(solution)/shard_map/ppermute | solution.py:342
  74.1 3.0 %copy-start = (s32[8]{0:T(128)S(1)}, s32[8]{0:T(128)}, u32[]{:S(2)}) copy-start(s32[8]{0:T(128)} %pair_one.1) | copy-start | bytes 100
  74.1 2.9 %copy-start.1 = (s32[8]{0:T(128)S(1)}, s32[8]{0:T(128)}, u32[]{:S(2)}) copy-start(s32[8]{0:T(128)} %pair_two.1) | copy-start | bytes 100
  74.1 2.9 %copy-start.2 = (s32[8]{0:T(128)S(1)}, s32[8]{0:T(128)}, u32[]{:S(2)}) copy-start(s32[8]{0:T(128)} %owner.1) | copy-start | bytes 100
  74.1 2.1 %collective-permute-start.20 = (f32[4,72,512]{2,1,0:T(8,128)S(1)}, f32[4,72,512]{2,1,0:T(8,128)S(1)}, u32[]{:S(2)}, u32[]{:S(2)}) collective-permute-start(f32[4,72,512]{2,1,0:T(8,128)S(1)} %pad_maximum_fusion.3), channel_id=1, source_target_pairs={{0,4},{4,0},{8,12},{12,8},{16,20},{20,16},{24,28},{28,24},{1,5},{5... | collective-permute-start | bytes 1769480 | tf_op jit(solution)/shard_map/ppermute | solution.py:342
  74.3 2.8 %collective-permute-start.24 = (f32[4,72,512]{2,1,0:T(8,128)S(1)}, f32[4,72,512]{2,1,0:T(8,128)S(1)}, u32[]{:S(2)}, u32[]{:S(2)}) collective-permute-start(f32[4,72,512]{2,1,0:T(8,128)S(1)} %pad_maximum_fusion.4), channel_id=1, source_target_pairs={{0,4},{4,0},{8,12},{12,8},{16,20},{20,16},{24,28},{28,24},{1,5},{5... | collective-permute-start | bytes 1769480 | tf_op jit(solution)/shard_map/ppermute | solution.py:342

commit v6 on v5

--- a/solution.py
+++ b/solution.py
@@ -16,7 +16,7 @@
 lane = 128
 wide = 256
 stretch = 1024
-rim = 4
+rim = 2
 loads = 4
 vmem_bytes = 48 * 1024 * 1024
 
@@ -41,7 +41,8 @@
         self.share = columns // row_devices
         self.halo = -(-self.margin * (2 * ITERS + 1) // lane) * lane
         self.width = self.share + 2 * self.halo
-        self.slab = row_local + 2 * rim
+        self.slab = row_local + 4 * rim
+        self.chips = sim_devices // 2
         self.sharers = min(sim_devices, row_local // 8)
         self.share_rows = row_local // self.sharers
         self.length = max(2 * wide, -(-self.rows // lane) * lane)
@@ -50,6 +51,10 @@
         self.blocks = blocks + [(self.width - lane, self.width)]
         centre = range(self.halo, self.halo + self.share, wide)
         self.out_blocks = [(a, min(a + wide, self.halo + self.share)) for a in centre]
+
+    def sides(self):
+        left = (self.halo - rim - self.margin) // lane * lane
+        return left, (self.halo + self.share - self.margin) // lane * lane
 
     def window(self, block):
         return max(0, block[0] - lane), min(self.width, block[1] + lane)
@@ -132,8 +137,9 @@
     for device in range(plan.row_devices):
         first = device * plan.row_local - rim
         part = band(plan, reverse, plan.slab, rows, first)
-        row = lax.broadcasted_iota(jnp.int32, part.shape, 0) + first
-        slabs.append(jnp.where((row >= 0) & (row < rows), part, 0.0))
+        row = lax.broadcasted_iota(jnp.int32, part.shape, 0)
+        inside = (row + first >= 0) & (row + first < rows) & (row < plan.row_local + 2 * rim)
+        slabs.append(jnp.where(inside, part, 0.0))
     put(jnp.concatenate(slabs, axis=0))
     size = 2 * wide
     forward = band(plan, taps, size, size, 0)
@@ -161,6 +167,14 @@
     for block in plan.out_blocks[:1]:
         low, high = plan.window(block)
         put(step_size * forward[: high - low, block[0] - low : block[1] - low])
+    left, right = plan.sides()
+    column = lax.broadcasted_iota(jnp.int32, (wide, lane), 1)
+    before = band(plan, taps, wide, lane, left - (plan.halo - lane))
+    behind = band(plan, taps, wide, lane, right - (plan.halo + plan.share))
+    rows_at = lax.axis_index("rows")
+    before = jnp.where((column >= lane - rim) & (rows_at > 0), before, 0.0)
+    behind = jnp.where((column < rim) & (rows_at < plan.row_devices - 1), behind, 0.0)
+    put(step_size * jnp.concatenate([before, behind], axis=0))
 
 
 def filter_kernel(plan, sharers, *refs):
@@ -175,9 +189,9 @@
     parts = take(len(sharers))
     square, final = take(2), take(2)
     bands = [take(2) for _ in plan.blocks]
-    last = take(2)
+    last, edges = take(2), take(2)
     outs = take(plan.row_devices)
-    seen, weight, image, base, total, field, high, low, mid_high, mid_low, sem = refs
+    seen, weight, image, base, total, field, side, high, low, mid_high, mid_low, sem = refs
     for part, owners in zip(parts, sharers):
         for slot, offset in enumerate(owners):
             for index, step in enumerate(plan.steps):
@@ -232,6 +246,18 @@
     for block in plan.out_blocks:
         size = block[1] - block[0]
         field[:, block[0] - plan.halo : block[1] - plan.halo] = columns_pass(last, count, plan.window(block))
+    value = jnp.zeros((count, lane), jnp.float32)
+    for number, start in enumerate(plan.sides()):
+        part = slice(number * wide, (number + 1) * wide)
+        a, b = mid_high[:count, start : start + wide], mid_low[:count, start : start + wide]
+        value = value + dot(a, edges[0][part]) + dot(a, edges[1][part]) + dot(b, edges[0][part])
+    side[:count] = value
+    turned = side[...].T
+    turned = jnp.concatenate([turned[lane - rim :], turned[:rim]], axis=0)
+    for device in range(plan.row_devices):
+        shift = (side.shape[0] - device * plan.slab - rim) % side.shape[0]
+        row = (device + 1) * plan.slab - 2 * rim
+        field[row : row + 2 * rim, :lane] = pltpu.roll(turned, shift, 1)[:, :lane]
     for step, out in zip(plan.steps, outs):
         row = pl.multiple_of((lax.axis_index("rows") ^ step) * plan.slab, 8)
         out[...] = field[pl.ds(row, plan.slab), :]
@@ -239,10 +265,9 @@
 
 def divergence(own, partner):
     rows, columns = own.shape
-    stop = rows - rim
-    inner = slice(lane, columns - lane)
+    stop, inner = rows - rim, slice(0, columns - lane)
     here = partner[rim:stop]
-    down, up = partner[rim + 2 : stop + 2, inner], partner[rim - 2 : stop - 2, inner]
+    down, up = partner[2 * rim :, inner], partner[: stop - rim, inner]
     middle = here[:, inner]
     flow = own[rim + 1 : stop + 1, inner] * (down - middle) - own[rim - 1 : stop - 1, inner] * (middle - up)
     level = own[rim:stop]
@@ -255,83 +280,57 @@
     return 0.25 * (flow + (right - left))
 
 
-def estimate_kernel(plan, holders, field_width, pair_one, pair_two, owner, *refs):
-    refs = list(refs)
-    pieces = []
-    for orders in holders:
-        flat = []
-        for order in orders:
-            ref = refs.pop(0)
-            flat += [(offset, ref.at[slot]) for slot, offset in enumerate(order)]
-        pieces.append(sorted(flat, key=lambda entry: entry[0]))
-    estimate = refs.pop(0)
-    mean_field = refs.pop(0) if field_width else None
-    own, partner, result, done, sems = refs[:5]
-    rows_at, sim_at = lax.axis_index("rows"), lax.axis_index("sims")
-    if field_width:
-        every, means, sent = refs[5:]
-        units = field_width // lane
-        per = plan.share // lane
-        for unit in range(units + 2):
-            at = sim_at * units - 1 + unit
-            inside = (at >= 0) & (at < plan.columns // lane)
-            span = slice(unit * lane, (unit + 1) * lane)
-            for step, sources in zip(plan.steps, pieces):
-                def fetch_all(sources=sources, at=at, span=span, unit=unit):
-                    column = pl.multiple_of(lax.rem(at, per) * lane, lane)
-                    for offset, source in sources:
-                        pltpu.make_async_copy(
-                            source.at[:, pl.ds(column, lane)], every.at[sim_at ^ offset, :, span], sems.at[unit]
-                        ).start()
-
-                pl.when(inside & (lax.div(at, per) == (rows_at ^ step)))(fetch_all)
-
-            @pl.when(jnp.logical_not(inside))
-            def _(span=span):
-                every[:, :, span] = jnp.zeros((plan.sim_devices, plan.slab, lane), jnp.float32)
-
-    edge = jnp.zeros((plan.slab, lane), jnp.float32)
-    for target in (own, partner):
-        target[:, :lane] = edge
-        target[:, lane + plan.columns :] = edge
-    one, two = sim_at ^ pair_one[sim_at], sim_at ^ pair_two[sim_at]
-
-    def factor(offset):
-        return jnp.where(one == offset, 2.0, 0.0) - jnp.where(two == offset, 1.0, 0.0)
-
-    for step, sources in zip(plan.steps, pieces):
-        column = pl.multiple_of(lane + (rows_at ^ step) * plan.share, lane)
-        own[:, pl.ds(column, plan.share)] = sources[0][1][...]
-        mixed = factor(0) * sources[0][1][...]
-        for offset, source in sources[1:]:
-            mixed = mixed + factor(offset) * source[...]
-        partner[:, pl.ds(column, plan.share)] = mixed
-    for a in range(0, plan.columns, stretch):
-        b = min(a + stretch, plan.columns)
-        span = slice(a, b + 2 * lane)
-        result[:, a:b] = divergence(own[:, span], partner[:, span])
-    copies = [pltpu.make_async_copy(result, estimate, done)]
-    copies[0].start()
-    if not field_width:
-        copies[0].wait()
-        return
-    for unit in range(units + 2):
-        at = sim_at * units - 1 + unit
-
-        @pl.when((at >= 0) & (at < plan.columns // lane))
-        def _(unit=unit):
-            span = every.at[:, :, unit * lane : (unit + 1) * lane]
-            pltpu.make_async_copy(span, span, sems.at[unit]).wait()
-
-    means[...] = jnp.zeros(means.shape, jnp.float32)
-    for sim in range(plan.sim_devices):
-        means[owner[sim]] += divergence(every[sim], 2.0 * every[pair_one[sim]] - every[pair_two[sim]])
+def collect(plan, near, far, every, corner):
+    core = lax.axis_index("sims") % 2
+    here = lax.axis_index("sims") // 2
+    corner[...] = jnp.zeros(corner.shape, jnp.float32)
+    kept = plan.row_local + 2 * rim
+    for step in range(plan.chips):
+        for source, parity in ((near[step], core), (far[step], 1 - core)):
+            at = 2 * (here ^ step) + parity
+            every[at, :, : plan.share] = source[:kept]
+            corner[lane - rim :] = source[kept : kept + rim, :lane]
+            corner[:rim] = source[kept + rim : kept + 2 * rim, :lane]
+            every[at, rim : kept - rim, plan.share :] = corner[...].T[: plan.row_local]
+
+
+def mixed(every, pair_one, pair_two, sim):
+    return divergence(every[sim], 2.0 * every[pair_one[sim]] - every[pair_two[sim]])
+
+
+def estimate_kernel(plan, pair_one, pair_two, *refs):
+    near, far, outs = refs[: plan.chips], refs[plan.chips : 2 * plan.chips], refs[2 * plan.chips : -2]
+    every, corner = refs[-2:]
+    collect(plan, near, far, every, corner)
+    chip, core = lax.axis_index("sims") // 2, lax.axis_index("sims") % 2
+    for step, out in enumerate(outs):
+        out[...] = mixed(every, pair_one, pair_two, 2 * (chip ^ step) + core)
+
+
+def mean_kernel(plan, field_width, pair_one, pair_two, owner, *refs):
+    near, far, done = [refs[first * plan.chips : (first + 1) * plan.chips] for first in range(3)]
+    mean_field, every, corner, whole = refs[3 * plan.chips :]
+    collect(plan, near, far, every, corner)
+    chip, core = lax.axis_index("sims") // 2, lax.axis_index("sims") % 2
+    whole[...] = jnp.zeros(whole.shape, jnp.float32)
+    for step, estimate in enumerate(done):
+        sim = 2 * (chip ^ step)
+        whole[owner[sim + core]] += estimate[...]
+        whole[owner[sim + 1 - core]] += mixed(every, pair_one, pair_two, sim + 1 - core)
+    span = pl.ds(pl.multiple_of(core * field_width, lane), field_width) if field_width < plan.share else slice(None)
     for group in range(OWNERS):
         count = jnp.int32(0)
         for sim in range(plan.sim_devices):
             count = count + (owner[sim] == group).astype(jnp.int32)
-        means[group] = means[group] / jnp.maximum(count, 1).astype(jnp.float32)
-        copies.append(pltpu.make_async_copy(means.at[group], mean_field.at[group], sent.at[group]))
+        mean_field[group] = whole[group, :, span] / jnp.maximum(count, 1).astype(jnp.float32)
+
+
+def join_kernel(plan, *refs):
+    pieces, estimate, sems = refs[: plan.chips], refs[plan.chips], refs[plan.chips + 1]
+    copies = []
+    for step, piece in enumerate(pieces):
+        column = pl.multiple_of(((lax.axis_index("sims") // 2) ^ step) * plan.share, lane)
+        copies.append(pltpu.make_async_copy(piece, estimate.at[:, pl.ds(column, plan.share)], sems.at[step]))
         copies[-1].start()
     for copy in copies:
         copy.wait()
@@ -344,15 +343,6 @@
 
 def exchange_all(plan, values):
     return [exchange(value, "rows", step) if step else value for step, value in zip(plan.steps, values)]
-
-
-def gather(first, axis, bits):
-    arrays, offsets = [first[None]], [[0]]
-    for bit in bits:
-        whole = jnp.concatenate(arrays, axis=0) if len(arrays) > 1 else arrays[0]
-        arrays.append(exchange(whole, axis, bit))
-        offsets.append([offset ^ bit for order in offsets for offset in order])
-    return arrays, offsets
 
 
 def call(kernel, out_shapes, in_specs, scratch, flops, moved, outs_in=pltpu.VMEM):
@@ -378,6 +368,7 @@
         [vmem] * plan.row_devices + [far] * len(parts) + [vmem] * len(tables),
         [pltpu.VMEM(full, jnp.float32)] * 5
         + [pltpu.VMEM((plan.row_devices * plan.slab, plan.share), jnp.float32)]
+        + [pltpu.VMEM((-(-plan.row_devices * plan.slab // lane) * lane, lane), jnp.float32)]
         + [pltpu.VMEM(full, jnp.bfloat16)] * 2
         + [pltpu.VMEM(tall, jnp.bfloat16)] * 2
         + [pltpu.SemaphoreType.DMA],
@@ -386,37 +377,67 @@
     )(*pieces, *parts, *tables)
 
 
-def run_estimate(plan, holders, pair_one, pair_two, owner, held):
+def order_of(plan, offset):
+    return jnp.where(offset == 0, 0, plan.row_devices - offset)
+
+
+def run_estimates(plan, pieces, pair_one, pair_two, owner):
     vmem = pl.BlockSpec(memory_space=pltpu.VMEM)
     smem = pl.BlockSpec(memory_space=pltpu.SMEM)
+    axes = ("sims", "rows")
+    places = [(sim, row) for sim in range(plan.sim_devices) for row in range(plan.row_devices)]
 
     def f32(*shape):
         return jax.ShapeDtypeStruct(shape, jnp.float32)
 
-    field_width = plan.columns // plan.sim_devices
-    fused = field_width if field_width % lane == 0 else 0
-    outs = [f32(plan.row_local, plan.columns)]
-    extended = (plan.slab, plan.columns + 2 * lane)
-    scratch = [pltpu.VMEM(extended, jnp.float32)] * 2
-    scratch += [pltpu.VMEM((plan.row_local, plan.columns), jnp.float32), pltpu.SemaphoreType.DMA]
-    if fused:
-        outs.append(f32(OWNERS, plan.row_local, fused))
-        scratch.append(pltpu.SemaphoreType.DMA((fused // lane + 2,)))
-        scratch.append(pltpu.VMEM((plan.sim_devices, plan.slab, fused + 2 * lane), jnp.float32))
-        scratch.append(pltpu.VMEM((OWNERS, plan.row_local, fused), jnp.float32))
-        scratch.append(pltpu.SemaphoreType.DMA((OWNERS,)))
-    else:
-        scratch.append(pltpu.SemaphoreType.DMA((1,)))
-    results = call(
-        functools.partial(estimate_kernel, plan, holders, fused),
-        outs,
-        [smem] * 3 + [vmem] * len(held),
+    def hop(value, target):
+        count = plan.row_devices
+        pairs = [(sim * count + row, target(sim, row)[0] * count + target(sim, row)[1]) for sim, row in places]
+        return lax.ppermute(value, axes, pairs)
+
+    moved = jnp.stack(exchange_all(plan, pieces))
+    here = (lax.axis_index("sims") // 2) ^ lax.axis_index("rows")
+    near = []
+    for step in range(plan.chips):
+        value = lax.dynamic_index_in_dim(moved, order_of(plan, here ^ step), keepdims=False)
+        near.append(exchange(value, "sims", 2 * step) if step else value)
+    far = [exchange(value, "sims", 1) for value in near]
+    scratch = [
+        pltpu.VMEM((plan.sim_devices, plan.row_local + 2 * rim, plan.share + lane), jnp.float32),
+        pltpu.VMEM((lane, lane), jnp.float32),
+    ]
+    found = call(
+        functools.partial(estimate_kernel, plan),
+        [f32(plan.row_local, plan.share)] * plan.chips,
+        [smem] * 2 + [vmem] * (2 * plan.chips),
         scratch,
         1 << 24,
         1 << 23,
+    )(pair_one, pair_two, *near, *far)
+    field_width = plan.columns // plan.sim_devices
+    kept = field_width if field_width % lane == 0 else plan.share
+    [mean_field] = call(
+        functools.partial(mean_kernel, plan, kept),
+        [f32(OWNERS, plan.row_local, kept)],
+        [smem] * 3 + [vmem] * (3 * plan.chips),
+        scratch + [pltpu.VMEM((OWNERS, plan.row_local, plan.share), jnp.float32)],
+        1 << 24,
+        1 << 23,
+    )(pair_one, pair_two, owner, *near, *far, *found)
+    if kept != field_width:
+        start = (lax.axis_index("sims") % 2) * field_width
+        mean_field = lax.dynamic_slice_in_dim(mean_field, start, field_width, axis=2)
+    moved = [value if step == 0 else exchange(value, "sims", 2 * step) for step, value in enumerate(found)]
+    [estimate] = call(
+        functools.partial(join_kernel, plan),
+        [f32(plan.row_local, plan.columns)],
+        [vmem] * plan.chips,
+        [pltpu.SemaphoreType.DMA((plan.chips,))],
+        0,
+        1 << 20,
         outs_in=pltpu.HBM,
-    )(pair_one, pair_two, owner, *held)
-    return results, fused
+    )(*moved)
+    return estimate, mean_field
 
 
 def body(maps, weight, beam, pair_one, pair_two, owner):
@@ -455,6 +476,7 @@
     for block in plan.blocks + plan.out_blocks[:1]:
         low, high = plan.window(block)
         shapes.append((high - low, block[1] - block[0]))
+    shapes.append((2 * wide, lane))
 
 
     def spread(parts):
@@ -482,30 +504,7 @@
         0,
     )(beam[None])
     filtered = run_filter(plan, sharers, pieces, parts, tables)
-    moved = exchange_all(plan, filtered)
-    bits = [1 << i for i in range(1, sim_devices.bit_length() - 1)]
-    arrays, holders = [], []
-    for step, piece in enumerate(moved):
-        turn = step % max(len(bits), 1)
-        found, offsets = gather(piece, "sims", bits[turn:] + bits[:turn])
-        arrays.append(found)
-        holders.append(offsets)
-    held = []
-    for found, offsets in zip(arrays, holders):
-        held += found + [exchange(jnp.concatenate(found), "sims", 1)]
-        offsets.append([offset ^ 1 for order in offsets for offset in order])
-
-    results, fused = run_estimate(plan, holders, pair_one, pair_two, owner, held)
-    estimate = results[0]
-    if fused:
-        mean_field = results[1]
-    else:
-        groups = jnp.arange(OWNERS, dtype=jnp.int32)
-        local_owner = owner[lax.axis_index("sims")]
-        term = jnp.where((groups == local_owner)[:, None, None], estimate[None], 0.0)
-        total = lax.psum_scatter(term, "sims", scatter_dimension=2, tiled=True)
-        tally = jnp.sum((groups[:, None] == owner[None, :]).astype(jnp.float32), axis=1)
-        mean_field = total / jnp.maximum(tally, 1.0)[:, None, None]
+    estimate, mean_field = run_estimates(plan, filtered, pair_one, pair_two, owner)
     return estimate.reshape(maps.shape), mean_field
 
 

time: 81.7 us -> 80.7 us (0.988)
  starting transfers between devices: 30.6 us -> 25.9 us
  waiting for transfers between devices: 33 us -> 35.6 us
  Pallas kernels: 14.2 us -> 15.5 us
    ppermute x25 -> x23, starting transfers between devices: 30.6 us -> 25.9 us  [exchange(): return lax.ppermute(value, axis, [(i, i ^ offset) for i in range(count)])]
    ppermute x25 -> x23, waiting for transfers between devices: 33 us -> 35.6 us  [exchange(): return lax.ppermute(value, axis, [(i, i ^ offset) for i in range(count)])]
    pallas_call x1 -> x3, Pallas kernels: 4.22 us -> 5.05 us  [the longest x1 2.6 us: run_estimates(): call(functools.partial(mean_kernel, plan, kept), [f32(OWNERS, plan.row_lo...]
  transfers between devices with their start and end apart: 25 -> 23, of which waited for: 15 -> 16; matrix products, arithmetic and copies ran while one was open for 2% -> 2% of each run, Pallas kernels for 4% -> 7%
where the time goes in v6:
time: 80.7 us; the launch traced here: 80.5 us
  waiting for transfers between devices  35.6 us (44%)
  starting transfers between devices  25.9 us (32%)
  Pallas kernels  15.5 us (19%)
  other arithmetic  1.83 us (2%)
  between operations  0.88 us (1%)
    ppermute x23, waiting for transfers between devices, exchange(): return lax.ppermute(value, axis, [(i, i ^ offset) for i in range(count)])  35.6 us
    ppermute x23, starting transfers between devices, exchange(): return lax.ppermute(value, axis, [(i, i ^ offset) for i in range(count)])  25.9 us
    pallas_call x1, Pallas kernels, run_filter(): call(functools.partial(filter_kernel, plan, sharers), [jax.ShapeDtypeStru...  5.92 us
    pallas_call x1, Pallas kernels, body(): call(functools.partial(table_kernel, plan), [b16(*shape) for shape in sha...  3.14 us
    pallas_call x1, Pallas kernels, run_estimates(): call(functools.partial(mean_kernel, plan, kept), [f32(OWNERS, plan.row_lo...  2.6 us
    pallas_call x1, Pallas kernels, run_estimates(): call(functools.partial(estimate_kernel, plan), [f32(plan.row_local, plan....  1.64 us
  transfers between devices with their start and end apart: 23, of which 16 were waited for; matrix products, arithmetic and copies ran while one was open for 2% of the time, Pallas kernels for 7%

profile of v6, /device:TPU:0, one launch (start us, length us, event | category | flops | bytes accessed | tf_op | source)
XLA Modules:
  0.0 80.5 jit_solution(7024412882885975534)
XLA Ops:
  0.6 1.4 %shard_map.77 = (f32[64,1024]{1,0:T(8,128)S(1)}, f32[64,1024]{1,0:T(8,128)S(1)}, f32[64,1024]{1,0:T(8,128)S(1)}, f32[64,1024]{1,0:T(8,128)S(1)}, f32[8,1024]{1,0...) custom-call(f32[64,2048]{1,0:T(8,128)} %bitcast.23, f32[64,2048]{1,0:T(8,128)} %weight.1), custom_call_target="tpu_custom_call" | custom-call | flops 131072 | bytes 2097152 | tf_op jit(solution)/shard_map/pallas_call | solution.py:462
  2.0 5.1 %collective-permute-start.4 = (f32[8,1024]{1,0:T(8,128)S(1)}, f32[8,1024]{1,0:T(8,128)S(1)}, u32[]{:S(2)}, u32[]{:S(2)}) collective-permute-start(f32[8,1024]{1,0:T(8,128)S(1)} %get-tuple-element.72), channel_id=1, source_target_pairs={{0,3},{1,2},{2,1},{3,0},{4,7},{5,6},{6,5},{7,4},{8,11},{9,10},{10,... | collective-permute-start | bytes 98312 | tf_op jit(solution)/shard_map/ppermute | solution.py:341
  7.1 0.0 collective-permute-start.5
  7.2 0.6 collective-permute-start.6
  7.8 1.3 %collective-permute-done.4 = f32[8,1024]{1,0:T(8,128)S(1)} collective-permute-done((f32[8,1024]{1,0:T(8,128)S(1)}, f32[8,1024]{1,0:T(8,128)S(1)}, u32[]{:S(2)}, u32[]{:S(2)}) %collective-permute-start.4) | collective-permute-done | bytes 32800 | tf_op jit(solution)/shard_map/ppermute | solution.py:341
  9.0 2.9 %collective-permute-done.5 = f32[8,1024]{1,0:T(8,128)S(1)} collective-permute-done((f32[8,1024]{1,0:T(8,128)S(1)}, f32[8,1024]{1,0:T(8,128)S(1)}, u32[]{:S(2)}, u32[]{:S(2)}) %collective-permute-start.5) | collective-permute-done | bytes 32800 | tf_op jit(solution)/shard_map/ppermute | solution.py:341
  12.0 0.0 collective-permute-done.6
  12.0 1.5 %collective-permute-start.7 = (f32[64,1024]{1,0:T(8,128)S(1)}, f32[64,1024]{1,0:T(8,128)S(1)}, u32[]{:S(2)}, u32[]{:S(2)}) collective-permute-start(f32[64,1024]{1,0:T(8,128)S(1)} %get-tuple-element.76), channel_id=1, source_target_pairs={{0,3},{1,2},{2,1},{3,0},{4,7},{5,6},{6,5},{7,4},{8,11},{9,10},{10,... | collective-permute-start | bytes 786440 | tf_op jit(solution)/shard_map/ppermute | solution.py:341
  13.4 0.6 collective-permute-start.8
  14.0 2.4 %collective-permute-start.9 = (f32[64,1024]{1,0:T(8,128)S(1)}, f32[64,1024]{1,0:T(8,128)S(1)}, u32[]{:S(2)}, u32[]{:S(2)}) collective-permute-start(f32[64,1024]{1,0:T(8,128)S(1)} %get-tuple-element.78), channel_id=1, source_target_pairs={{0,1},{1,0},{2,3},{3,2},{4,5},{5,4},{6,7},{7,6},{8,9},{9,8},{10,11... | collective-permute-start | bytes 786440 | tf_op jit(solution)/shard_map/ppermute | solution.py:341
  16.4 14.5 %conditional.1 = (f32[1,4,8,1024]{3,2,1,0:T(8,128)}, f32[1,4,8,1024]{3,2,1,0:T(8,128)}, f32[1,4,8,1024]{3,2,1,0:T(8,128)}, f32[1,4,8,1024]{3,2,1,0:T(8,128)}, f32[4,4,8,1024]{3,2,1,0:T(8,128)}) conditional(s32[]{:T(128)} %convert_element_type.3, () %tuple.19, (f32[8,1024]{1,0:T(8,128)S(1)}, f32[8,1024]{1,0:T(8,128)S(1)}, f32[8,1024]{1,0:T(8,128)S(1)}, ...), branch_computations={%region_0.0_spmd, %region_1.0_spmd} | conditional | flops 491520 | bytes 4980936 | solution.py:491
  16.4 0.7 maximum_bitcast_fusion
  17.0 1.5 %collective-permute-start = (f32[1,4,8,1024]{3,2,1,0:T(8,128)}, f32[1,4,8,1024]{3,2,1,0:T(8,128)}, u32[]{:S(2)}, u32[]{:S(2)}) collective-permute-start(f32[1,4,8,1024]{3,2,1,0:T(8,128)} %maximum_bitcast_fusion), channel_id=1, source_target_pairs={{0,8},{4,12},{8,0},{12,4},{16,24},{20,28},{24,16},{28,20},{1,9},{5... | collective-permute-start | bytes 393224 | tf_op jit(solution)/shard_map/cond/branch_1_fun/ppermute | solution.py:341
  18.5 1.5 %collective-permute-start.1 = (f32[1,4,8,1024]{3,2,1,0:T(8,128)}, f32[1,4,8,1024]{3,2,1,0:T(8,128)}, u32[]{:S(2)}, u32[]{:S(2)}) collective-permute-start(f32[1,4,8,1024]{3,2,1,0:T(8,128)} %maximum_bitcast_fusion), channel_id=1, source_target_pairs={{0,16},{4,20},{8,24},{12,28},{16,0},{20,4},{24,8},{28,12},{1,17},{... | collective-permute-start | bytes 393224 | tf_op jit(solution)/shard_map/cond/branch_1_fun/ppermute | solution.py:341
  20.0 2.3 %collective-permute-done = f32[1,4,8,1024]{3,2,1,0:T(8,128)} collective-permute-done((f32[1,4,8,1024]{3,2,1,0:T(8,128)}, f32[1,4,8,1024]{3,2,1,0:T(8,128)}, u32[]{:S(2)}, u32[]{:S(2)}) %collective-permute-start) | collective-permute-done | bytes 131104 | tf_op jit(solution)/shard_map/cond/branch_1_fun/ppermute | solution.py:341
  22.3 1.5 %collective-permute-start.2 = (f32[1,4,8,1024]{3,2,1,0:T(8,128)}, f32[1,4,8,1024]{3,2,1,0:T(8,128)}, u32[]{:S(2)}, u32[]{:S(2)}) collective-permute-start(f32[1,4,8,1024]{3,2,1,0:T(8,128)} %collective-permute-done), channel_id=1, source_target_pairs={{0,16},{4,20},{8,24},{12,28},{16,0},{20,4},{24,8},{28,12},{1,17},{... | collective-permute-start | bytes 393224 | tf_op jit(solution)/shard_map/cond/branch_1_fun/ppermute | solution.py:341
  23.8 0.8 %collective-permute-done.1 = f32[1,4,8,1024]{3,2,1,0:T(8,128)} collective-permute-done((f32[1,4,8,1024]{3,2,1,0:T(8,128)}, f32[1,4,8,1024]{3,2,1,0:T(8,128)}, u32[]{:S(2)}, u32[]{:S(2)}) %collective-permute-start.1) | collective-permute-done | bytes 131104 | tf_op jit(solution)/shard_map/cond/branch_1_fun/ppermute | solution.py:341
  24.7 2.9 %collective-permute-done.2 = f32[1,4,8,1024]{3,2,1,0:T(8,128)} collective-permute-done((f32[1,4,8,1024]{3,2,1,0:T(8,128)}, f32[1,4,8,1024]{3,2,1,0:T(8,128)}, u32[]{:S(2)}, u32[]{:S(2)}) %collective-permute-start.2) | collective-permute-done | bytes 131104 | tf_op jit(solution)/shard_map/cond/branch_1_fun/ppermute | solution.py:341
  27.6 1.1 %pad_maximum_fusion = f32[4,4,8,1024]{3,2,1,0:T(8,128)S(1)} fusion(f32[1,4,8,1024]{3,2,1,0:T(8,128)} %collective-permute-done.2, f32[1,4,8,1024]{3,2,1,0:T(8,128)} %collective-permute-done.1, f32[1,4,8,1024]{3,2,1,0:T(8,128)} %collective-permute-done, f32[1,4,8,1024]{3,2,1,0:T(8,128)} %maximum_bitcast_fusion), kind=kLoop, calls=%fused_computation | loop fusion | flops 393216 | bytes 1048576 | tf_op jit(solution)/shard_map/cond/branch_1_fun/concatenate | solution.py:487
  28.7 0.1 collective-permute-start.3
  28.8 2.0 %collective-permute-done.3 = f32[4,4,8,1024]{3,2,1,0:T(8,128)} collective-permute-done((f32[4,4,8,1024]{3,2,1,0:T(8,128)S(1)}, f32[4,4,8,1024]{3,2,1,0:T(8,128)}, u32[]{:S(2)}, u32[]{:S(2)}) %collective-permute-start.3) | collective-permute-done | bytes 524320 | tf_op jit(solution)/shard_map/cond/branch_1_fun/ppermute | solution.py:341
  30.8 0.0 copy-start.3
  30.8 0.7 copy-done.3
  31.5 3.1 %shard_map.78 = (bf16[256,256]{1,0:T(8,128)(2,1)S(1)}, bf16[256,256]{1,0:T(8,128)(2,1)S(1)}, bf16[288,256]{1,0:T(8,128)(2,1)S(1)}, bf16[288,256]{1,0:T(8,128)(2,...) custom-call(f32[1,65]{1,0:T(1,128)S(1)} %bitcast.22), custom_call_target="tpu_custom_call" | custom-call | tf_op jit(solution)/shard_map/pallas_call | solution.py:498
  34.6 0.0 collective-permute-done.7.refs_1_
  34.6 1.1 %collective-permute-done.8.refs_2_ = f32[64,1024]{1,0:T(8,128)S(1)} collective-permute-done((f32[64,1024]{1,0:T(8,128)S(1)}, f32[64,1024]{1,0:T(8,128)S(1)}, u32[]{:S(2)}, u32[]{:S(2)}) %collective-permute-start.8) | collective-permute-done | bytes 262176 | tf_op jit(solution)/shard_map/ppermute | solution.py:341
  35.7 0.0 collective-permute-done.9.refs_3_
  35.7 5.9 %shard_map.79 = (f32[72,512]{1,0:T(8,128)S(1)}, f32[72,512]{1,0:T(8,128)S(1)}, f32[72,512]{1,0:T(8,128)S(1)}, f32[72,512]{1,0:T(8,128)S(1)}) custom-call(f32[64,1024]{1,0:T(8,128)S(1)} %get-tuple-element.75.refs_0_, f32[64,1024]{1,0:T(8,128)S(1)} %collective-permute-done.7.refs_1_, f32[64,1024]{1,0:T(8,128)S(1)} %collective-permute-done.8.refs_2_, ...), custom_call_target="tpu_custom_call" | custom-call | flops 8589934592 | bytes 8388608 | tf_op jit(solution)/shard_map/pallas_call | solution.py:365
  41.7 0.1 collective-permute-start.12
  41.7 2.7 %collective-permute-start.10 = (f32[72,512]{1,0:T(8,128)S(1)}, f32[72,512]{1,0:T(8,128)S(1)}, u32[]{:S(2)}, u32[]{:S(2)}) collective-permute-start(f32[72,512]{1,0:T(8,128)S(1)} %get-tuple-element.113), channel_id=1, source_target_pairs={{0,3},{1,2},{2,1},{3,0},{4,7},{5,6},{6,5},{7,4},{8,11},{9,10},{10,... | collective-permute-start | bytes 442376 | tf_op jit(solution)/shard_map/ppermute | solution.py:341
  44.4 0.8 collective-permute-start.11
  45.2 3.2 %collective-permute-done.12 = f32[72,512]{1,0:T(8,128)S(1)} collective-permute-done((f32[72,512]{1,0:T(8,128)S(1)}, f32[72,512]{1,0:T(8,128)S(1)}, u32[]{:S(2)}, u32[]{:S(2)}) %collective-permute-start.12) | collective-permute-done | bytes 147488 | tf_op jit(solution)/shard_map/ppermute | solution.py:341
  48.4 4.0 %collective-permute-done.10 = f32[72,512]{1,0:T(8,128)S(1)} collective-permute-done((f32[72,512]{1,0:T(8,128)S(1)}, f32[72,512]{1,0:T(8,128)S(1)}, u32[]{:S(2)}, u32[]{:S(2)}) %collective-permute-start.10) | collective-permute-done | bytes 147488 | tf_op jit(solution)/shard_map/ppermute | solution.py:341
  52.4 5.1 %collective-permute-done.11 = f32[72,512]{1,0:T(8,128)S(1)} collective-permute-done((f32[72,512]{1,0:T(8,128)S(1)}, f32[72,512]{1,0:T(8,128)S(1)}, u32[]{:S(2)}, u32[]{:S(2)}) %collective-permute-start.11) | collective-permute-done | bytes 147488 | tf_op jit(solution)/shard_map/ppermute | solution.py:341
  57.5 0.1 dynamic-slice_bitcast_fusion
  57.6 1.6 %collective-permute-start.13 = (f32[72,512]{1,0:T(8,128)S(1)}, f32[72,512]{1,0:T(8,128)S(1)}, u32[]{:S(2)}, u32[]{:S(2)}) collective-permute-start(f32[72,512]{1,0:T(8,128)S(1)} %get-tuple-element.122), channel_id=1, source_target_pairs={{0,8},{4,12},{8,0},{12,4},{16,24},{20,28},{24,16},{28,20},{1,9},{5... | collective-permute-start | bytes 442376 | tf_op jit(solution)/shard_map/ppermute | solution.py:341
  59.2 1.5 %collective-permute-start.14 = (f32[72,512]{1,0:T(8,128)S(1)}, f32[72,512]{1,0:T(8,128)S(1)}, u32[]{:S(2)}, u32[]{:S(2)}) collective-permute-start(f32[72,512]{1,0:T(8,128)S(1)} %get-tuple-element.121), channel_id=1, source_target_pairs={{0,16},{4,20},{8,24},{12,28},{16,0},{20,4},{24,8},{28,12},{1,17},{... | collective-permute-start | bytes 442376 | tf_op jit(solution)/shard_map/ppermute | solution.py:341
  60.7 0.0 copy-start
  60.7 0.0 copy-start.1
  60.7 0.5 collective-permute-start.15
  61.1 0.0 collective-permute-start.16
  61.2 3.2 %collective-permute-done.13.refs_1_ = f32[72,512]{1,0:T(8,128)S(1)} collective-permute-done((f32[72,512]{1,0:T(8,128)S(1)}, f32[72,512]{1,0:T(8,128)S(1)}, u32[]{:S(2)}, u32[]{:S(2)}) %collective-permute-start.13) | collective-permute-done | bytes 147488 | tf_op jit(solution)/shard_map/ppermute | solution.py:341
  64.3 0.0 collective-permute-start.17
  64.3 2.9 %collective-permute-done.14.refs_2_ = f32[72,512]{1,0:T(8,128)S(1)} collective-permute-done((f32[72,512]{1,0:T(8,128)S(1)}, f32[72,512]{1,0:T(8,128)S(1)}, u32[]{:S(2)}, u32[]{:S(2)}) %collective-permute-start.14) | collective-permute-done | bytes 147488 | tf_op jit(solution)/shard_map/ppermute | solution.py:341
  67.2 0.0 collective-permute-start.18
  67.2 0.0 collective-permute-done.15.refs_3_
  67.2 0.5 collective-permute-start.19
  67.7 0.0 collective-permute-done.16.refs_4_
  67.7 0.0 collective-permute-done.17.refs_5_
  67.7 0.9 %collective-permute-done.18.refs_6_ = f32[72,512]{1,0:T(8,128)S(1)} collective-permute-done((f32[72,512]{1,0:T(8,128)S(1)}, f32[72,512]{1,0:T(8,128)S(1)}, u32[]{:S(2)}, u32[]{:S(2)}) %collective-permute-start.18) | collective-permute-done | bytes 147488 | tf_op jit(solution)/shard_map/ppermute | solution.py:341
  68.6 0.2 collective-permute-done.19.refs_7_
  68.8 0.0 copy-done
  68.8 0.0 copy-done.1
  68.8 1.6 %shard_map.80 = (f32[64,512]{1,0:T(8,128)S(1)}, f32[64,512]{1,0:T(8,128)S(1)}, f32[64,512]{1,0:T(8,128)S(1)}, f32[64,512]{1,0:T(8,128)S(1)}) custom-call(s32[8]{0:T(128)S(1)} %copy-done, s32[8]{0:T(128)S(1)} %copy-done.1, f32[72,512]{1,0:T(8,128)S(1)} %get-tuple-element.123.refs_0_, f32[72,512]{1,0:T(8,128)S(1)} %collective-permute-done.13.refs_1_, ...), custom_call_target="tpu_custom_call" | custom-call | flops 16777216 | bytes 8388608 | tf_op jit(solution)/shard_map/pallas_call | solution.py:409
  70.4 0.3 collective-permute-start.20
  70.7 1.0 %collective-permute-start.21 = (f32[64,512]{1,0:T(8,128)S(1)}, f32[64,512]{1,0:T(8,128)S(1)}, u32[]{:S(2)}, u32[]{:S(2)}) collective-permute-start(f32[64,512]{1,0:T(8,128)S(1)} %get-tuple-element.118.refs_10_), channel_id=1, source_target_pairs={{0,16},{4,20},{8,24},{12,28},{16,0},{20,4},{24,8},{28,12},{1,17},{... | collective-permute-start | bytes 393224 | tf_op jit(solution)/shard_map/ppermute | solution.py:341
  71.8 0.0 copy-start.2
  71.8 2.2 %collective-permute-start.22 = (f32[64,512]{1,0:T(8,128)S(1)}, f32[64,512]{1,0:T(8,128)S(1)}, u32[]{:S(2)}, u32[]{:S(2)}) collective-permute-start(f32[64,512]{1,0:T(8,128)S(1)} %get-tuple-element.119.refs_11_), channel_id=1, source_target_pairs={{0,24},{4,28},{8,16},{12,20},{16,8},{20,12},{24,0},{28,4},{1,25},{... | collective-permute-start | bytes 393224 | tf_op jit(solution)/shard_map/ppermute | solution.py:341
  74.0 0.0 copy-done.2
  74.0 2.6 %shard_map.82 = f32[8,64,256]{2,1,0:T(8,128)} custom-call(s32[8]{0:T(128)S(1)} %copy-done, s32[8]{0:T(128)S(1)} %copy-done.1, s32[8]{0:T(128)S(1)} %copy-done.2, f32[72,512]{1,0:T(8,128)S(1)} %get-tuple-element.123.refs_0_, f32[72,512]{1,0:T(8,128)S(1)} %collective-permute-done.13.refs_1_, f32[72,512]{1,0:T(8,128)S(1)} %collective-permute-done.14.refs_2_, ...), custom_call_target="tpu_custom_call" | custom-call | flops 16777216 | bytes 8388608 | tf_op jit(solution)/shard_map/pallas_call | solution.py:419
  76.6 0.2 collective-permute-done.20.refs_1_
  76.8 0.0 collective-permute-done.21.refs_2_
  76.8 2.6 %collective-permute-done.22.refs_3_ = f32[64,512]{1,0:T(8,128)S(1)} collective-permute-done((f32[64,512]{1,0:T(8,128)S(1)}, f32[64,512]{1,0:T(8,128)S(1)}, u32[]{:S(2)}, u32[]{:S(2)}) %collective-permute-start.22) | collective-permute-done | bytes 131104 | tf_op jit(solution)/shard_map/ppermute | solution.py:341
  79.5 0.8 %shard_map.81 = f32[64,2048]{1,0:T(8,128)} custom-call(f32[64,512]{1,0:T(8,128)S(1)} %get-tuple-element.116.refs_0_.refs_8_, f32[64,512]{1,0:T(8,128)S(1)} %collective-permute-done.20.refs_1_, f32[64,512]{1,0:T(8,128)S(1)} %collective-permute-done.21.refs_2_, f32[64,512]{1,0:T(8,128)S(1)} %collective-permute-done.22.refs_3_), custom_call_target="tpu_custom_call" | custom-call | bytes 1048576 | tf_op jit(solution)/shard_map/pallas_call | solution.py:431
  (1 shorter events, 0.0 us)
Async XLA Ops:
  2.0 7.0 %collective-permute-start.4 = (f32[8,1024]{1,0:T(8,128)S(1)}, f32[8,1024]{1,0:T(8,128)S(1)}, u32[]{:S(2)}, u32[]{:S(2)}) collective-permute-start(f32[8,1024]{1,0:T(8,128)S(1)} %get-tuple-element.72), channel_id=1, source_target_pairs={{0,3},{1,2},{2,1},{3,0},{4,7},{5,6},{6,5},{7,4},{8,11},{9,10},{10,... | collective-permute-start | bytes 98312 | tf_op jit(solution)/shard_map/ppermute | solution.py:341
  7.1 4.8 %collective-permute-start.5 = (f32[8,1024]{1,0:T(8,128)S(1)}, f32[8,1024]{1,0:T(8,128)S(1)}, u32[]{:S(2)}, u32[]{:S(2)}) collective-permute-start(f32[8,1024]{1,0:T(8,128)S(1)} %get-tuple-element.73), channel_id=1, source_target_pairs={{0,2},{1,3},{2,0},{3,1},{4,6},{5,7},{6,4},{7,5},{8,10},{9,11},{10,... | collective-permute-start | bytes 98312 | tf_op jit(solution)/shard_map/ppermute | solution.py:341
  7.2 4.8 %collective-permute-start.6 = (f32[8,1024]{1,0:T(8,128)S(1)}, f32[8,1024]{1,0:T(8,128)S(1)}, u32[]{:S(2)}, u32[]{:S(2)}) collective-permute-start(f32[8,1024]{1,0:T(8,128)S(1)} %get-tuple-element.74), channel_id=1, source_target_pairs={{0,1},{1,0},{2,3},{3,2},{4,5},{5,4},{6,7},{7,6},{8,9},{9,8},{10,11... | collective-permute-start | bytes 98312 | tf_op jit(solution)/shard_map/ppermute | solution.py:341
  12.0 22.7 %collective-permute-start.7 = (f32[64,1024]{1,0:T(8,128)S(1)}, f32[64,1024]{1,0:T(8,128)S(1)}, u32[]{:S(2)}, u32[]{:S(2)}) collective-permute-start(f32[64,1024]{1,0:T(8,128)S(1)} %get-tuple-element.76), channel_id=1, source_target_pairs={{0,3},{1,2},{2,1},{3,0},{4,7},{5,6},{6,5},{7,4},{8,11},{9,10},{10,... | collective-permute-start | bytes 786440 | tf_op jit(solution)/shard_map/ppermute | solution.py:341
  13.4 22.3 %collective-permute-start.8 = (f32[64,1024]{1,0:T(8,128)S(1)}, f32[64,1024]{1,0:T(8,128)S(1)}, u32[]{:S(2)}, u32[]{:S(2)}) collective-permute-start(f32[64,1024]{1,0:T(8,128)S(1)} %get-tuple-element.77), channel_id=1, source_target_pairs={{0,2},{1,3},{2,0},{3,1},{4,6},{5,7},{6,4},{7,5},{8,10},{9,11},{10,... | collective-permute-start | bytes 786440 | tf_op jit(solution)/shard_map/ppermute | solution.py:341
  14.0 21.7 %collective-permute-start.9 = (f32[64,1024]{1,0:T(8,128)S(1)}, f32[64,1024]{1,0:T(8,128)S(1)}, u32[]{:S(2)}, u32[]{:S(2)}) collective-permute-start(f32[64,1024]{1,0:T(8,128)S(1)} %get-tuple-element.78), channel_id=1, source_target_pairs={{0,1},{1,0},{2,3},{3,2},{4,5},{5,4},{6,7},{7,6},{8,9},{9,8},{10,11... | collective-permute-start | bytes 786440 | tf_op jit(solution)/shard_map/ppermute | solution.py:341
  17.0 5.3 %collective-permute-start = (f32[1,4,8,1024]{3,2,1,0:T(8,128)}, f32[1,4,8,1024]{3,2,1,0:T(8,128)}, u32[]{:S(2)}, u32[]{:S(2)}) collective-permute-start(f32[1,4,8,1024]{3,2,1,0:T(8,128)} %maximum_bitcast_fusion), channel_id=1, source_target_pairs={{0,8},{4,12},{8,0},{12,4},{16,24},{20,28},{24,16},{28,20},{1,9},{5... | collective-permute-start | bytes 393224 | tf_op jit(solution)/shard_map/cond/branch_1_fun/ppermute | solution.py:341
  18.5 6.1 %collective-permute-start.1 = (f32[1,4,8,1024]{3,2,1,0:T(8,128)}, f32[1,4,8,1024]{3,2,1,0:T(8,128)}, u32[]{:S(2)}, u32[]{:S(2)}) collective-permute-start(f32[1,4,8,1024]{3,2,1,0:T(8,128)} %maximum_bitcast_fusion), channel_id=1, source_target_pairs={{0,16},{4,20},{8,24},{12,28},{16,0},{20,4},{24,8},{28,12},{1,17},{... | collective-permute-start | bytes 393224 | tf_op jit(solution)/shard_map/cond/branch_1_fun/ppermute | solution.py:341
  22.3 5.3 %collective-permute-start.2 = (f32[1,4,8,1024]{3,2,1,0:T(8,128)}, f32[1,4,8,1024]{3,2,1,0:T(8,128)}, u32[]{:S(2)}, u32[]{:S(2)}) collective-permute-start(f32[1,4,8,1024]{3,2,1,0:T(8,128)} %collective-permute-done), channel_id=1, source_target_pairs={{0,16},{4,20},{8,24},{12,28},{16,0},{20,4},{24,8},{28,12},{1,17},{... | collective-permute-start | bytes 393224 | tf_op jit(solution)/shard_map/cond/branch_1_fun/ppermute | solution.py:341
  28.7 2.1 %collective-permute-start.3 = (f32[4,4,8,1024]{3,2,1,0:T(8,128)S(1)}, f32[4,4,8,1024]{3,2,1,0:T(8,128)}, u32[]{:S(2)}, u32[]{:S(2)}) collective-permute-start(f32[4,4,8,1024]{3,2,1,0:T(8,128)S(1)} %pad_maximum_fusion), channel_id=1, source_target_pairs={{0,4},{4,0},{8,12},{12,8},{16,20},{20,16},{24,28},{28,24},{1,5},{5... | collective-permute-start | bytes 1572872 | tf_op jit(solution)/shard_map/cond/branch_1_fun/ppermute | solution.py:341
  30.8 0.7 copy-start.3
  41.7 6.7 %collective-permute-start.12 = (f32[72,512]{1,0:T(8,128)S(1)}, f32[72,512]{1,0:T(8,128)S(1)}, u32[]{:S(2)}, u32[]{:S(2)}) collective-permute-start(f32[72,512]{1,0:T(8,128)S(1)} %get-tuple-element.115), channel_id=1, source_target_pairs={{0,1},{1,0},{2,3},{3,2},{4,5},{5,4},{6,7},{7,6},{8,9},{9,8},{10,11... | collective-permute-start | bytes 442376 | tf_op jit(solution)/shard_map/ppermute | solution.py:341
  41.7 10.6 %collective-permute-start.10 = (f32[72,512]{1,0:T(8,128)S(1)}, f32[72,512]{1,0:T(8,128)S(1)}, u32[]{:S(2)}, u32[]{:S(2)}) collective-permute-start(f32[72,512]{1,0:T(8,128)S(1)} %get-tuple-element.113), channel_id=1, source_target_pairs={{0,3},{1,2},{2,1},{3,0},{4,7},{5,6},{6,5},{7,4},{8,11},{9,10},{10,... | collective-permute-start | bytes 442376 | tf_op jit(solution)/shard_map/ppermute | solution.py:341
  44.4 13.0 %collective-permute-start.11 = (f32[72,512]{1,0:T(8,128)S(1)}, f32[72,512]{1,0:T(8,128)S(1)}, u32[]{:S(2)}, u32[]{:S(2)}) collective-permute-start(f32[72,512]{1,0:T(8,128)S(1)} %get-tuple-element.114), channel_id=1, source_target_pairs={{0,2},{1,3},{2,0},{3,1},{4,6},{5,7},{6,4},{7,5},{8,10},{9,11},{10,... | collective-permute-start | bytes 442376 | tf_op jit(solution)/shard_map/ppermute | solution.py:341
  57.6 6.7 %collective-permute-start.13 = (f32[72,512]{1,0:T(8,128)S(1)}, f32[72,512]{1,0:T(8,128)S(1)}, u32[]{:S(2)}, u32[]{:S(2)}) collective-permute-start(f32[72,512]{1,0:T(8,128)S(1)} %get-tuple-element.122), channel_id=1, source_target_pairs={{0,8},{4,12},{8,0},{12,4},{16,24},{20,28},{24,16},{28,20},{1,9},{5... | collective-permute-start | bytes 442376 | tf_op jit(solution)/shard_map/ppermute | solution.py:341
  59.2 8.1 %collective-permute-start.14 = (f32[72,512]{1,0:T(8,128)S(1)}, f32[72,512]{1,0:T(8,128)S(1)}, u32[]{:S(2)}, u32[]{:S(2)}) collective-permute-start(f32[72,512]{1,0:T(8,128)S(1)} %get-tuple-element.121), channel_id=1, source_target_pairs={{0,16},{4,20},{8,24},{12,28},{16,0},{20,4},{24,8},{28,12},{1,17},{... | collective-permute-start | bytes 442376 | tf_op jit(solution)/shard_map/ppermute | solution.py:341
  60.7 8.1 %copy-start = (s32[8]{0:T(128)S(1)}, s32[8]{0:T(128)}, u32[]{:S(2)}) copy-start(s32[8]{0:T(128)} %pair_one.3) | copy-start | bytes 100
  60.7 8.1 %copy-start.1 = (s32[8]{0:T(128)S(1)}, s32[8]{0:T(128)}, u32[]{:S(2)}) copy-start(s32[8]{0:T(128)} %pair_two.3) | copy-start | bytes 100
  60.7 6.5 %collective-permute-start.15 = (f32[72,512]{1,0:T(8,128)S(1)}, f32[72,512]{1,0:T(8,128)S(1)}, u32[]{:S(2)}, u32[]{:S(2)}) collective-permute-start(f32[72,512]{1,0:T(8,128)S(1)} %get-tuple-element.120), channel_id=1, source_target_pairs={{0,24},{4,28},{8,16},{12,20},{16,8},{20,12},{24,0},{28,4},{1,25},{... | collective-permute-start | bytes 442376 | tf_op jit(solution)/shard_map/ppermute | solution.py:341
  61.1 6.6 %collective-permute-start.16 = (f32[72,512]{1,0:T(8,128)S(1)}, f32[72,512]{1,0:T(8,128)S(1)}, u32[]{:S(2)}, u32[]{:S(2)}) collective-permute-start(f32[72,512]{1,0:T(8,128)S(1)} %get-tuple-element.123.refs_0_), channel_id=1, source_target_pairs={{0,4},{4,0},{8,12},{12,8},{16,20},{20,16},{24,28},{28,24},{1,5},{5... | collective-permute-start | bytes 442376 | tf_op jit(solution)/shard_map/ppermute | solution.py:341
  64.3 3.4 %collective-permute-start.17 = (f32[72,512]{1,0:T(8,128)S(1)}, f32[72,512]{1,0:T(8,128)S(1)}, u32[]{:S(2)}, u32[]{:S(2)}) collective-permute-start(f32[72,512]{1,0:T(8,128)S(1)} %collective-permute-done.13.refs_1_), channel_id=1, source_target_pairs={{0,4},{4,0},{8,12},{12,8},{16,20},{20,16},{24,28},{28,24},{1,5},{5... | collective-permute-start | bytes 442376 | tf_op jit(solution)/shard_map/ppermute | solution.py:341
  67.2 1.4 %collective-permute-start.18 = (f32[72,512]{1,0:T(8,128)S(1)}, f32[72,512]{1,0:T(8,128)S(1)}, u32[]{:S(2)}, u32[]{:S(2)}) collective-permute-start(f32[72,512]{1,0:T(8,128)S(1)} %collective-permute-done.14.refs_2_), channel_id=1, source_target_pairs={{0,4},{4,0},{8,12},{12,8},{16,20},{20,16},{24,28},{28,24},{1,5},{5... | collective-permute-start | bytes 442376 | tf_op jit(solution)/shard_map/ppermute | solution.py:341
  67.2 1.6 %collective-permute-start.19 = (f32[72,512]{1,0:T(8,128)S(1)}, f32[72,512]{1,0:T(8,128)S(1)}, u32[]{:S(2)}, u32[]{:S(2)}) collective-permute-start(f32[72,512]{1,0:T(8,128)S(1)} %collective-permute-done.15.refs_3_), channel_id=1, source_target_pairs={{0,4},{4,0},{8,12},{12,8},{16,20},{20,16},{24,28},{28,24},{1,5},{5... | collective-permute-start | bytes 442376 | tf_op jit(solution)/shard_map/ppermute | solution.py:341
  70.4 6.4 %collective-permute-start.20 = (f32[64,512]{1,0:T(8,128)S(1)}, f32[64,512]{1,0:T(8,128)S(1)}, u32[]{:S(2)}, u32[]{:S(2)}) collective-permute-start(f32[64,512]{1,0:T(8,128)S(1)} %get-tuple-element.117.refs_9_), channel_id=1, source_target_pairs={{0,8},{4,12},{8,0},{12,4},{16,24},{20,28},{24,16},{28,20},{1,9},{5... | collective-permute-start | bytes 393224 | tf_op jit(solution)/shard_map/ppermute | solution.py:341
  70.7 6.1 %collective-permute-start.21 = (f32[64,512]{1,0:T(8,128)S(1)}, f32[64,512]{1,0:T(8,128)S(1)}, u32[]{:S(2)}, u32[]{:S(2)}) collective-permute-start(f32[64,512]{1,0:T(8,128)S(1)} %get-tuple-element.118.refs_10_), channel_id=1, source_target_pairs={{0,16},{4,20},{8,24},{12,28},{16,0},{20,4},{24,8},{28,12},{1,17},{... | collective-permute-start | bytes 393224 | tf_op jit(solution)/shard_map/ppermute | solution.py:341
  71.8 2.3 %copy-start.2 = (s32[8]{0:T(128)S(1)}, s32[8]{0:T(128)}, u32[]{:S(2)}) copy-start(s32[8]{0:T(128)} %owner.1) | copy-start | bytes 100
  71.8 7.7 %collective-permute-start.22 = (f32[64,512]{1,0:T(8,128)S(1)}, f32[64,512]{1,0:T(8,128)S(1)}, u32[]{:S(2)}, u32[]{:S(2)}) collective-permute-start(f32[64,512]{1,0:T(8,128)S(1)} %get-tuple-element.119.refs_11_), channel_id=1, source_target_pairs={{0,24},{4,28},{8,16},{12,20},{16,8},{20,12},{24,0},{28,4},{1,25},{... | collective-permute-start | bytes 393224 | tf_op jit(solution)/shard_map/ppermute | solution.py:341

commit v7 on v6

--- a/solution.py
+++ b/solution.py
@@ -45,6 +45,7 @@
         self.chips = sim_devices // 2
         self.sharers = min(sim_devices, row_local // 8)
         self.share_rows = row_local // self.sharers
+        self.head = row_local // 8
         self.length = max(2 * wide, -(-self.rows // lane) * lane)
         inner = range(lane, self.width - lane, wide)
         blocks = [(0, lane)] + [(a, min(a + wide, self.width - lane)) for a in inner]
@@ -66,7 +67,7 @@
 
 def piece_kernel(plan, maps, weight, *refs):
     count = plan.row_devices
-    pieces, parts = refs[:count], refs[count : 2 * count]
+    heads, tails = refs[:count], refs[count : 2 * count]
     padded, weights, given, sems = refs[2 * count :]
     rows_at, sims_at = lax.axis_index("rows"), lax.axis_index("sims")
     chunk = plan.row_local // loads
@@ -84,17 +85,17 @@
     for target in (padded, weights):
         target[:, : plan.halo] = zeros
         target[:, plan.halo + plan.columns :] = zeros
-    starts = [pl.multiple_of((rows_at ^ step) * plan.share, lane) for step in plan.steps]
     for number in range(loads):
         for copy in copies[number]:
             copy.wait()
         rows = slice(number * chunk, (number + 1) * chunk)
         padded[rows, inner] = weights[rows, inner] * given[rows]
-        for piece, column in zip(pieces, starts):
-            piece[rows] = padded[rows, pl.ds(column, plan.width)]
     row = pl.multiple_of(lax.rem(sims_at, plan.sharers) * plan.share_rows, plan.share_rows)
-    for part, column in zip(parts, starts):
-        part[...] = weights[pl.ds(row, plan.share_rows), pl.ds(column, plan.width)]
+    for index, step in enumerate(plan.steps):
+        span = pl.ds(pl.multiple_of((rows_at ^ step) * plan.share, lane), plan.width)
+        heads[index][: plan.share_rows] = weights[pl.ds(row, plan.share_rows), span]
+        heads[index][plan.share_rows :] = padded[: plan.head, span]
+        tails[index][...] = padded[plan.head :, span]
 
 
 def band(plan, taps, rows, columns, offset):
@@ -185,7 +186,7 @@
         del refs[:number]
         return taken
 
-    pieces = take(plan.row_devices)
+    heads, tails = take(plan.row_devices), take(plan.row_devices)
     parts = take(len(sharers))
     square, final = take(2), take(2)
     bands = [take(2) for _ in plan.blocks]
@@ -199,11 +200,13 @@
                 row = row + (lax.rem(lax.axis_index("sims"), plan.sharers) ^ offset) * plan.share_rows
                 rows = pl.ds(pl.multiple_of(row, plan.share_rows), plan.share_rows)
                 pltpu.make_async_copy(part.at[slot, index], weight.at[rows], sem).start()
-    for step, piece in zip(plan.steps, pieces):
-        rows = pl.ds(pl.multiple_of((lax.axis_index("rows") ^ step) * plan.row_local, plan.row_local), plan.row_local)
-        value = piece[...]
+    for index, step in enumerate(plan.steps):
+        row = pl.multiple_of((lax.axis_index("rows") ^ step) * plan.row_local, plan.row_local)
+        rows = pl.ds(row, plan.row_local)
+        value = jnp.concatenate([heads[index][plan.share_rows :], tails[index][...]], axis=0)
         seen[rows, :] = value
         high[rows, :], low[rows, :] = split(value)
+
     def rows_pass(table, start, stop, full=True):
         count = table[0].shape[0]
         for a in range(start, stop, wide):
@@ -357,7 +360,7 @@
     )
 
 
-def run_filter(plan, sharers, pieces, parts, tables):
+def run_filter(plan, sharers, heads, tails, parts, tables):
     vmem = pl.BlockSpec(memory_space=pltpu.VMEM)
     far = pl.BlockSpec(memory_space=pltpu.HBM)
     full = (plan.rows, plan.width)
@@ -365,7 +368,7 @@
     return call(
         functools.partial(filter_kernel, plan, sharers),
         [jax.ShapeDtypeStruct((plan.slab, plan.share), jnp.float32)] * plan.row_devices,
-        [vmem] * plan.row_devices + [far] * len(parts) + [vmem] * len(tables),
+        [vmem] * (2 * plan.row_devices) + [far] * len(parts) + [vmem] * len(tables),
         [pltpu.VMEM(full, jnp.float32)] * 5
         + [pltpu.VMEM((plan.row_devices * plan.slab, plan.share), jnp.float32)]
         + [pltpu.VMEM((-(-plan.row_devices * plan.slab // lane) * lane, lane), jnp.float32)]
@@ -374,7 +377,7 @@
         + [pltpu.SemaphoreType.DMA],
         1 << 33,
         1 << 23,
-    )(*pieces, *parts, *tables)
+    )(*heads, *tails, *parts, *tables)
 
 
 def order_of(plan, offset):
@@ -461,17 +464,19 @@
     cells = row_local * columns
     made = call(
         functools.partial(piece_kernel, plan),
-        [f32(row_local, plan.width)] * row_devices + [f32(plan.share_rows, plan.width)] * row_devices,
+        [f32(plan.share_rows + plan.head, plan.width)] * row_devices
+        + [f32(row_local - plan.head, plan.width)] * row_devices,
         [far, far],
         [pltpu.VMEM((row_local, columns + 2 * plan.halo), jnp.float32)] * 2
         + [pltpu.VMEM((row_local, columns), jnp.float32), pltpu.SemaphoreType.DMA((2, loads))],
         cells,
         16 * cells,
     )(pinned(maps.reshape(row_local, columns)), pinned(weight))
-    pieces, parts = made[:row_devices], made[row_devices:]
-    parts = exchange_all(plan, parts)
-    pieces, parts = lax.optimization_barrier((pieces, parts))
-    pieces = exchange_all(plan, pieces)
+    heads, tails = made[:row_devices], made[row_devices:]
+    heads = exchange_all(plan, heads)
+    tails, heads = lax.optimization_barrier((tails, heads))
+    tails = exchange_all(plan, tails)
+    parts = lax.optimization_barrier(jnp.stack([head[: plan.share_rows] for head in heads])[None])
     shapes = [(plan.rows, plan.rows), (row_devices * plan.slab, plan.rows)]
     for block in plan.blocks + plan.out_blocks[:1]:
         low, high = plan.window(block)
@@ -479,31 +484,32 @@
     shapes.append((2 * wide, lane))
 
 
-    def spread(parts):
-        found = {0: jnp.stack(parts)[None]}
+    def prepare(parts, beam):
+        tables = call(
+            functools.partial(table_kernel, plan),
+            [b16(*shape) for shape in shapes for _ in range(2)],
+            [vmem],
+            [pltpu.VMEM((8, lane), jnp.float32)],
+            1 << 32,
+            1 << 23,
+        )(beam[None])
+        found = {0: parts}
         for bit in [1 << i for i in range(1, plan.sharers.bit_length() - 1)]:
             found |= {offset | bit: exchange(value, "sims", bit) for offset, value in found.items()}
         sharers[:] = [[offset] for offset in found] + [[offset ^ 1 for offset in found]]
-        return [*found.values(), exchange(jnp.concatenate(list(found.values())), "sims", 1)]
+        whole, tables = lax.optimization_barrier((jnp.concatenate(list(found.values())), tables))
+        return [*found.values(), exchange(whole, "sims", 1)], tables
 
     sharers = []
-    made = jax.eval_shape(spread, parts)
-    parts = lax.cond(
+    made = jax.eval_shape(prepare, parts, beam)
+    parts, tables = lax.cond(
         lax.axis_index("rows") < row_devices,
-        spread,
-        lambda parts: jax.tree.map(lambda x: jnp.zeros(x.shape, x.dtype), made),
+        prepare,
+        lambda parts, beam: jax.tree.map(lambda x: jnp.zeros(x.shape, x.dtype), made),
         parts,
+        beam,
     )
-    beam, parts = lax.optimization_barrier((beam, parts))
-    tables = call(
-        functools.partial(table_kernel, plan),
-        [b16(*shape) for shape in shapes for _ in range(2)],
-        [vmem],
-        [pltpu.VMEM((8, lane), jnp.float32)],
-        0,
-        0,
-    )(beam[None])
-    filtered = run_filter(plan, sharers, pieces, parts, tables)
+    filtered = run_filter(plan, sharers, heads, tails, parts, tables)
     estimate, mean_field = run_estimates(plan, filtered, pair_one, pair_two, owner)
     return estimate.reshape(maps.shape), mean_field
 

time: 80.7 us -> 75.5 us (0.936)
  waiting for transfers between devices: 35.6 us -> 30.3 us
  other arithmetic: 1.83 us -> 0.99 us
    ppermute x23, waiting for transfers between devices: 35.6 us -> 30.3 us  [exchange(): return lax.ppermute(value, axis, [(i, i ^ offset) for i in range(count)])]
  transfers between devices with their start and end apart: 23 -> 23, of which waited for: 16 -> 14; matrix products, arithmetic and copies ran while one was open for 2% -> 1% of each run, Pallas kernels for 7% -> 8%
where the time goes in v7:
time: 75.5 us; the launch traced here: 75.2 us
  waiting for transfers between devices  30.3 us (40%)
  starting transfers between devices  26.3 us (35%)
  Pallas kernels  15.8 us (21%)
  other arithmetic  0.99 us (1%)
  between operations  0.89 us (1%)
    ppermute x23, waiting for transfers between devices, exchange(): return lax.ppermute(value, axis, [(i, i ^ offset) for i in range(count)])  30.3 us
    ppermute x23, starting transfers between devices, exchange(): return lax.ppermute(value, axis, [(i, i ^ offset) for i in range(count)])  26.3 us
    pallas_call x1, Pallas kernels, run_filter(): call(functools.partial(filter_kernel, plan, sharers), [jax.ShapeDtypeStru...  6.21 us
    pallas_call x1, Pallas kernels, prepare(): call(functools.partial(table_kernel, plan), [b16(*shape) for shape in sha...  3.14 us
    pallas_call x1, Pallas kernels, run_estimates(): call(functools.partial(mean_kernel, plan, kept), [f32(OWNERS, plan.row_lo...  2.59 us
    pallas_call x1, Pallas kernels, run_estimates(): call(functools.partial(estimate_kernel, plan), [f32(plan.row_local, plan....  1.64 us
  transfers between devices with their start and end apart: 23, of which 14 were waited for; matrix products, arithmetic and copies ran while one was open for 1% of the time, Pallas kernels for 8%

profile of v7, /device:TPU:0, one launch (start us, length us, event | category | flops | bytes accessed | tf_op | source)
XLA Modules:
  0.0 75.2 jit_solution(17597412089103316793)
XLA Ops:
  0.6 1.4 %shard_map.78 = (f32[16,1024]{1,0:T(8,128)S(1)}, f32[16,1024]{1,0:T(8,128)S(1)}, f32[16,1024]{1,0:T(8,128)S(1)}, f32[16,1024]{1,0:T(8,128)S(1)}, f32[56,1024]{1,...) custom-call(f32[64,2048]{1,0:T(8,128)} %bitcast.26, f32[64,2048]{1,0:T(8,128)} %weight.1), custom_call_target="tpu_custom_call" | custom-call | flops 131072 | bytes 2097152 | tf_op jit(solution)/shard_map/pallas_call | solution.py:465
  2.1 5.1 %collective-permute-start.4 = (f32[16,1024]{1,0:T(8,128)S(1)}, f32[16,1024]{1,0:T(8,128)S(1)}, u32[]{:S(2)}, u32[]{:S(2)}) collective-permute-start(f32[16,1024]{1,0:T(8,128)S(1)} %get-tuple-element.97), channel_id=1, source_target_pairs={{0,3},{1,2},{2,1},{3,0},{4,7},{5,6},{6,5},{7,4},{8,11},{9,10},{10,... | collective-permute-start | bytes 196616 | tf_op jit(solution)/shard_map/ppermute | solution.py:344
  7.2 0.0 collective-permute-start.5
  7.2 0.6 collective-permute-start.6
  7.8 1.9 %collective-permute-done.4.refs_1_ = f32[16,1024]{1,0:T(8,128)S(1)} collective-permute-done((f32[16,1024]{1,0:T(8,128)S(1)}, f32[16,1024]{1,0:T(8,128)S(1)}, u32[]{:S(2)}, u32[]{:S(2)}) %collective-permute-start.4) | collective-permute-done | bytes 65568 | tf_op jit(solution)/shard_map/ppermute | solution.py:344
  9.8 3.0 %collective-permute-done.5.refs_2_ = f32[16,1024]{1,0:T(8,128)S(1)} collective-permute-done((f32[16,1024]{1,0:T(8,128)S(1)}, f32[16,1024]{1,0:T(8,128)S(1)}, u32[]{:S(2)}, u32[]{:S(2)}) %collective-permute-start.5) | collective-permute-done | bytes 65568 | tf_op jit(solution)/shard_map/ppermute | solution.py:344
  12.8 0.0 collective-permute-done.6.refs_3_
  12.8 2.7 %collective-permute-start.7 = (f32[56,1024]{1,0:T(8,128)S(1)}, f32[56,1024]{1,0:T(8,128)S(1)}, u32[]{:S(2)}, u32[]{:S(2)}) collective-permute-start(f32[56,1024]{1,0:T(8,128)S(1)} %get-tuple-element.105), channel_id=1, source_target_pairs={{0,3},{1,2},{2,1},{3,0},{4,7},{5,6},{6,5},{7,4},{8,11},{9,10},{10,... | collective-permute-start | bytes 688136 | tf_op jit(solution)/shard_map/ppermute | solution.py:344
  15.5 0.0 collective-permute-start.8
  15.5 1.7 %collective-permute-start.9 = (f32[56,1024]{1,0:T(8,128)S(1)}, f32[56,1024]{1,0:T(8,128)S(1)}, u32[]{:S(2)}, u32[]{:S(2)}) collective-permute-start(f32[56,1024]{1,0:T(8,128)S(1)} %get-tuple-element.107), channel_id=1, source_target_pairs={{0,1},{1,0},{2,3},{3,2},{4,5},{5,4},{6,7},{7,6},{8,9},{9,8},{10,11... | collective-permute-start | bytes 688136 | tf_op jit(solution)/shard_map/ppermute | solution.py:344
  17.2 0.0 copy-start.7
  17.2 0.6 copy-done.7
  17.9 13.1 %conditional.1 = (f32[1,4,8,1024]{3,2,1,0:T(8,128)S(1)}, f32[1,4,8,1024]{3,2,1,0:T(8,128)S(1)}, f32[1,4,8,1024]{3,2,1,0:T(8,128)S(1)}, f32[1,4,8,1024]{3,2,1,0:T...) conditional(s32[]{:T(128)} %convert_element_type.3, () %tuple.19, ...), branch_computations={%region_0.0_spmd, %region_1.0_spmd} | conditional | flops 4295360512 | bytes 15466952 | solution.py:505
  17.9 1.5 %collective-permute-start = (f32[1,4,8,1024]{3,2,1,0:T(8,128)S(1)}, f32[1,4,8,1024]{3,2,1,0:T(8,128)S(1)}, u32[]{:S(2)}, u32[]{:S(2)}) collective-permute-start(f32[1,4,8,1024]{3,2,1,0:T(8,128)S(1)} %get-tuple-element.172), channel_id=1, source_target_pairs={{0,8},{4,12},{8,0},{12,4},{16,24},{20,28},{24,16},{28,20},{1,9},{5... | collective-permute-start | bytes 393224 | tf_op jit(solution)/shard_map/cond/branch_1_fun/ppermute | solution.py:344
  19.4 1.5 %collective-permute-start.1 = (f32[1,4,8,1024]{3,2,1,0:T(8,128)S(1)}, f32[1,4,8,1024]{3,2,1,0:T(8,128)S(1)}, u32[]{:S(2)}, u32[]{:S(2)}) collective-permute-start(f32[1,4,8,1024]{3,2,1,0:T(8,128)S(1)} %get-tuple-element.172), channel_id=1, source_target_pairs={{0,16},{4,20},{8,24},{12,28},{16,0},{20,4},{24,8},{28,12},{1,17},{... | collective-permute-start | bytes 393224 | tf_op jit(solution)/shard_map/cond/branch_1_fun/ppermute | solution.py:344
  20.9 2.0 %collective-permute-done = f32[1,4,8,1024]{3,2,1,0:T(8,128)S(1)} collective-permute-done((f32[1,4,8,1024]{3,2,1,0:T(8,128)S(1)}, f32[1,4,8,1024]{3,2,1,0:T(8,128)S(1)}, u32[]{:S(2)}, u32[]{:S(2)}) %collective-permute-start) | collective-permute-done | bytes 131104 | tf_op jit(solution)/shard_map/cond/branch_1_fun/ppermute | solution.py:344
  22.8 1.5 %collective-permute-start.2 = (f32[1,4,8,1024]{3,2,1,0:T(8,128)S(1)}, f32[1,4,8,1024]{3,2,1,0:T(8,128)}, u32[]{:S(2)}, u32[]{:S(2)}) collective-permute-start(f32[1,4,8,1024]{3,2,1,0:T(8,128)S(1)} %collective-permute-done), channel_id=1, source_target_pairs={{0,16},{4,20},{8,24},{12,28},{16,0},{20,4},{24,8},{28,12},{1,17},{... | collective-permute-start | bytes 393224 | tf_op jit(solution)/shard_map/cond/branch_1_fun/ppermute | solution.py:344
  24.4 3.1 %branch_1_fun.1 = (bf16[256,256]{1,0:T(8,128)(2,1)S(1)}, bf16[256,256]{1,0:T(8,128)(2,1)S(1)}, bf16[288,256]{1,0:T(8,128)(2,1)S(1)}, bf16[288,256]{1,0:T(8,128)(...) custom-call(f32[1,65]{1,0:T(1,128)S(1)} %bitcast.31), custom_call_target="tpu_custom_call" | custom-call | flops 4294967296 | bytes 8388608 | tf_op jit(solution)/shard_map/cond/branch_1_fun/pallas_call | solution.py:488
  27.5 0.0 collective-permute-done.1
  27.5 0.0 copy-start.5
  27.5 0.4 collective-permute-done.2
  27.9 0.0 copy-done.3
  27.9 0.9 %pad_maximum_fusion = f32[4,4,8,1024]{3,2,1,0:T(8,128)S(1)} fusion(f32[1,4,8,1024]{3,2,1,0:T(8,128)} %collective-permute-done.2, f32[1,4,8,1024]{3,2,1,0:T(8,128)S(1)} %collective-permute-done.1, f32[1,4,8,1024]{3,2,1,0:T(8,128)S(1)} %collective-permute-done, f32[1,4,8,1024]{3,2,1,0:T(8,128)S(1)} %get-tuple-element.172), kind=kLoop, calls=%fused_computation | loop fusion | flops 393216 | bytes 1048576 | tf_op jit(solution)/shard_map/cond/branch_1_fun/concatenate | solution.py:500
  28.9 0.0 copy-done.5
  28.9 0.0 copy-start.4
  28.9 0.0 copy-start.6
  28.9 0.1 collective-permute-start.3
  29.0 2.0 %collective-permute-done.3 = f32[4,4,8,1024]{3,2,1,0:T(8,128)} collective-permute-done((f32[4,4,8,1024]{3,2,1,0:T(8,128)S(1)}, f32[4,4,8,1024]{3,2,1,0:T(8,128)}, u32[]{:S(2)}, u32[]{:S(2)}) %collective-permute-start.3) | collective-permute-done | bytes 524320 | tf_op jit(solution)/shard_map/cond/branch_1_fun/ppermute | solution.py:344
  31.0 0.0 copy-done.4
  31.0 0.0 collective-permute-done.7.refs_5_
  31.0 3.3 %collective-permute-done.8.refs_6_ = f32[56,1024]{1,0:T(8,128)S(1)} collective-permute-done((f32[56,1024]{1,0:T(8,128)S(1)}, f32[56,1024]{1,0:T(8,128)S(1)}, u32[]{:S(2)}, u32[]{:S(2)}) %collective-permute-start.8) | collective-permute-done | bytes 229408 | tf_op jit(solution)/shard_map/ppermute | solution.py:344
  34.3 0.0 collective-permute-done.9.refs_7_
  34.3 6.2 %shard_map.79 = (f32[72,512]{1,0:T(8,128)S(1)}, f32[72,512]{1,0:T(8,128)S(1)}, f32[72,512]{1,0:T(8,128)S(1)}, f32[72,512]{1,0:T(8,128)S(1)}) custom-call(f32[16,1024]{1,0:T(8,128)S(1)} %get-tuple-element.100.refs_0_, f32[16,1024]{1,0:T(8,128)S(1)} %collective-permute-done.4.refs_1_, f32[16,1024]{1,0:T(8,128)S(1)} %collective-permute-done.5.refs_2_, ...), custom_call_target="tpu_custom_call" | custom-call | flops 8589934592 | bytes 8388608 | tf_op jit(solution)/shard_map/pallas_call | solution.py:368
  40.5 0.1 collective-permute-start.12
  40.6 2.2 %collective-permute-start.11 = (f32[72,512]{1,0:T(8,128)S(1)}, f32[72,512]{1,0:T(8,128)S(1)}, u32[]{:S(2)}, u32[]{:S(2)}) collective-permute-start(f32[72,512]{1,0:T(8,128)S(1)} %get-tuple-element.133), channel_id=1, source_target_pairs={{0,2},{1,3},{2,0},{3,1},{4,6},{5,7},{6,4},{7,5},{8,10},{9,11},{10,... | collective-permute-start | bytes 442376 | tf_op jit(solution)/shard_map/ppermute | solution.py:344
  42.8 2.1 %collective-permute-start.10 = (f32[72,512]{1,0:T(8,128)S(1)}, f32[72,512]{1,0:T(8,128)S(1)}, u32[]{:S(2)}, u32[]{:S(2)}) collective-permute-start(f32[72,512]{1,0:T(8,128)S(1)} %get-tuple-element.132), channel_id=1, source_target_pairs={{0,3},{1,2},{2,1},{3,0},{4,7},{5,6},{6,5},{7,4},{8,11},{9,10},{10,... | collective-permute-start | bytes 442376 | tf_op jit(solution)/shard_map/ppermute | solution.py:344
  45.0 2.5 %collective-permute-done.12 = f32[72,512]{1,0:T(8,128)S(1)} collective-permute-done((f32[72,512]{1,0:T(8,128)S(1)}, f32[72,512]{1,0:T(8,128)S(1)}, u32[]{:S(2)}, u32[]{:S(2)}) %collective-permute-start.12) | collective-permute-done | bytes 147488 | tf_op jit(solution)/shard_map/ppermute | solution.py:344
  47.5 5.6 %collective-permute-done.11 = f32[72,512]{1,0:T(8,128)S(1)} collective-permute-done((f32[72,512]{1,0:T(8,128)S(1)}, f32[72,512]{1,0:T(8,128)S(1)}, u32[]{:S(2)}, u32[]{:S(2)}) %collective-permute-start.11) | collective-permute-done | bytes 147488 | tf_op jit(solution)/shard_map/ppermute | solution.py:344
  53.0 0.0 collective-permute-done.10
  53.1 0.1 dynamic-slice_bitcast_fusion
  53.2 1.5 %collective-permute-start.13 = (f32[72,512]{1,0:T(8,128)S(1)}, f32[72,512]{1,0:T(8,128)S(1)}, u32[]{:S(2)}, u32[]{:S(2)}) collective-permute-start(f32[72,512]{1,0:T(8,128)S(1)} %get-tuple-element.143), channel_id=1, source_target_pairs={{0,8},{4,12},{8,0},{12,4},{16,24},{20,28},{24,16},{28,20},{1,9},{5... | collective-permute-start | bytes 442376 | tf_op jit(solution)/shard_map/ppermute | solution.py:344
  54.7 1.5 %collective-permute-start.14 = (f32[72,512]{1,0:T(8,128)S(1)}, f32[72,512]{1,0:T(8,128)S(1)}, u32[]{:S(2)}, u32[]{:S(2)}) collective-permute-start(f32[72,512]{1,0:T(8,128)S(1)} %get-tuple-element.142), channel_id=1, source_target_pairs={{0,16},{4,20},{8,24},{12,28},{16,0},{20,4},{24,8},{28,12},{1,17},{... | collective-permute-start | bytes 442376 | tf_op jit(solution)/shard_map/ppermute | solution.py:344
  56.2 0.5 collective-permute-start.15
  56.7 0.0 collective-permute-start.16
  56.7 1.6 %collective-permute-done.13.refs_1_ = f32[72,512]{1,0:T(8,128)S(1)} collective-permute-done((f32[72,512]{1,0:T(8,128)S(1)}, f32[72,512]{1,0:T(8,128)S(1)}, u32[]{:S(2)}, u32[]{:S(2)}) %collective-permute-start.13) | collective-permute-done | bytes 147488 | tf_op jit(solution)/shard_map/ppermute | solution.py:344
  58.4 0.0 collective-permute-start.17
  58.4 1.5 %collective-permute-done.14.refs_2_ = f32[72,512]{1,0:T(8,128)S(1)} collective-permute-done((f32[72,512]{1,0:T(8,128)S(1)}, f32[72,512]{1,0:T(8,128)S(1)}, u32[]{:S(2)}, u32[]{:S(2)}) %collective-permute-start.14) | collective-permute-done | bytes 147488 | tf_op jit(solution)/shard_map/ppermute | solution.py:344
  59.8 0.0 collective-permute-start.18
  59.8 2.4 %collective-permute-done.15.refs_3_ = f32[72,512]{1,0:T(8,128)S(1)} collective-permute-done((f32[72,512]{1,0:T(8,128)S(1)}, f32[72,512]{1,0:T(8,128)S(1)}, u32[]{:S(2)}, u32[]{:S(2)}) %collective-permute-start.15) | collective-permute-done | bytes 147488 | tf_op jit(solution)/shard_map/ppermute | solution.py:344
  62.3 0.0 collective-permute-start.19
  62.3 0.0 collective-permute-done.16.refs_4_
  62.3 0.0 collective-permute-done.17.refs_5_
  62.3 0.0 collective-permute-done.18.refs_6_
  62.3 1.3 %collective-permute-done.19.refs_7_ = f32[72,512]{1,0:T(8,128)S(1)} collective-permute-done((f32[72,512]{1,0:T(8,128)S(1)}, f32[72,512]{1,0:T(8,128)S(1)}, u32[]{:S(2)}, u32[]{:S(2)}) %collective-permute-start.19) | collective-permute-done | bytes 147488 | tf_op jit(solution)/shard_map/ppermute | solution.py:344
  63.6 0.0 copy-done
  63.7 1.6 %shard_map.80 = (f32[64,512]{1,0:T(8,128)S(1)}, f32[64,512]{1,0:T(8,128)S(1)}, f32[64,512]{1,0:T(8,128)S(1)}, f32[64,512]{1,0:T(8,128)S(1)}) custom-call(s32[8]{0:T(128)S(1)} %copy-done, s32[8]{0:T(128)S(1)} %copy-done.1, f32[72,512]{1,0:T(8,128)S(1)} %get-tuple-element.144.refs_0_, f32[72,512]{1,0:T(8,128)S(1)} %collective-permute-done.13.refs_1_, ...), custom_call_target="tpu_custom_call" | custom-call | flops 16777216 | bytes 8388608 | tf_op jit(solution)/shard_map/pallas_call | solution.py:412
  65.3 0.6 collective-permute-start.20
  65.9 0.9 %collective-permute-start.21 = (f32[64,512]{1,0:T(8,128)S(1)}, f32[64,512]{1,0:T(8,128)S(1)}, u32[]{:S(2)}, u32[]{:S(2)}) collective-permute-start(f32[64,512]{1,0:T(8,128)S(1)} %get-tuple-element.137.refs_10_), channel_id=1, source_target_pairs={{0,16},{4,20},{8,24},{12,28},{16,0},{20,4},{24,8},{28,12},{1,17},{... | collective-permute-start | bytes 393224 | tf_op jit(solution)/shard_map/ppermute | solution.py:344
  66.8 2.1 %collective-permute-start.22 = (f32[64,512]{1,0:T(8,128)S(1)}, f32[64,512]{1,0:T(8,128)S(1)}, u32[]{:S(2)}, u32[]{:S(2)}) collective-permute-start(f32[64,512]{1,0:T(8,128)S(1)} %get-tuple-element.138.refs_11_), channel_id=1, source_target_pairs={{0,24},{4,28},{8,16},{12,20},{16,8},{20,12},{24,0},{28,4},{1,25},{... | collective-permute-start | bytes 393224 | tf_op jit(solution)/shard_map/ppermute | solution.py:344
  68.9 2.6 %shard_map.82 = f32[8,64,256]{2,1,0:T(8,128)} custom-call(s32[8]{0:T(128)S(1)} %copy-done, s32[8]{0:T(128)S(1)} %copy-done.1, s32[8]{0:T(128)S(1)} %copy-done.2, f32[72,512]{1,0:T(8,128)S(1)} %get-tuple-element.144.refs_0_, f32[72,512]{1,0:T(8,128)S(1)} %collective-permute-done.13.refs_1_, f32[72,512]{1,0:T(8,128)S(1)} %collective-permute-done.14.refs_2_, ...), custom_call_target="tpu_custom_call" | custom-call | flops 16777216 | bytes 8388608 | tf_op jit(solution)/shard_map/pallas_call | solution.py:422
  71.5 0.3 collective-permute-done.20.refs_1_
  71.7 0.0 collective-permute-done.21.refs_2_
  71.7 2.5 %collective-permute-done.22.refs_3_ = f32[64,512]{1,0:T(8,128)S(1)} collective-permute-done((f32[64,512]{1,0:T(8,128)S(1)}, f32[64,512]{1,0:T(8,128)S(1)}, u32[]{:S(2)}, u32[]{:S(2)}) %collective-permute-start.22) | collective-permute-done | bytes 131104 | tf_op jit(solution)/shard_map/ppermute | solution.py:344
  74.2 0.8 %shard_map.81 = f32[64,2048]{1,0:T(8,128)} custom-call(f32[64,512]{1,0:T(8,128)S(1)} %get-tuple-element.135.refs_0_.refs_8_, f32[64,512]{1,0:T(8,128)S(1)} %collective-permute-done.20.refs_1_, f32[64,512]{1,0:T(8,128)S(1)} %collective-permute-done.21.refs_2_, f32[64,512]{1,0:T(8,128)S(1)} %collective-permute-done.22.refs_3_), custom_call_target="tpu_custom_call" | custom-call | bytes 1048576 | tf_op jit(solution)/shard_map/pallas_call | solution.py:434
  (12 shorter events, 0.1 us)
Async XLA Ops:
  2.1 7.7 %collective-permute-start.4 = (f32[16,1024]{1,0:T(8,128)S(1)}, f32[16,1024]{1,0:T(8,128)S(1)}, u32[]{:S(2)}, u32[]{:S(2)}) collective-permute-start(f32[16,1024]{1,0:T(8,128)S(1)} %get-tuple-element.97), channel_id=1, source_target_pairs={{0,3},{1,2},{2,1},{3,0},{4,7},{5,6},{6,5},{7,4},{8,11},{9,10},{10,... | collective-permute-start | bytes 196616 | tf_op jit(solution)/shard_map/ppermute | solution.py:344
  7.2 5.6 %collective-permute-start.5 = (f32[16,1024]{1,0:T(8,128)S(1)}, f32[16,1024]{1,0:T(8,128)S(1)}, u32[]{:S(2)}, u32[]{:S(2)}) collective-permute-start(f32[16,1024]{1,0:T(8,128)S(1)} %get-tuple-element.98), channel_id=1, source_target_pairs={{0,2},{1,3},{2,0},{3,1},{4,6},{5,7},{6,4},{7,5},{8,10},{9,11},{10,... | collective-permute-start | bytes 196616 | tf_op jit(solution)/shard_map/ppermute | solution.py:344
  7.2 5.6 %collective-permute-start.6 = (f32[16,1024]{1,0:T(8,128)S(1)}, f32[16,1024]{1,0:T(8,128)S(1)}, u32[]{:S(2)}, u32[]{:S(2)}) collective-permute-start(f32[16,1024]{1,0:T(8,128)S(1)} %get-tuple-element.99), channel_id=1, source_target_pairs={{0,1},{1,0},{2,3},{3,2},{4,5},{5,4},{6,7},{7,6},{8,9},{9,8},{10,11... | collective-permute-start | bytes 196616 | tf_op jit(solution)/shard_map/ppermute | solution.py:344
  12.8 18.2 %collective-permute-start.7 = (f32[56,1024]{1,0:T(8,128)S(1)}, f32[56,1024]{1,0:T(8,128)S(1)}, u32[]{:S(2)}, u32[]{:S(2)}) collective-permute-start(f32[56,1024]{1,0:T(8,128)S(1)} %get-tuple-element.105), channel_id=1, source_target_pairs={{0,3},{1,2},{2,1},{3,0},{4,7},{5,6},{6,5},{7,4},{8,11},{9,10},{10,... | collective-permute-start | bytes 688136 | tf_op jit(solution)/shard_map/ppermute | solution.py:344
  15.5 18.8 %collective-permute-start.8 = (f32[56,1024]{1,0:T(8,128)S(1)}, f32[56,1024]{1,0:T(8,128)S(1)}, u32[]{:S(2)}, u32[]{:S(2)}) collective-permute-start(f32[56,1024]{1,0:T(8,128)S(1)} %get-tuple-element.106), channel_id=1, source_target_pairs={{0,2},{1,3},{2,0},{3,1},{4,6},{5,7},{6,4},{7,5},{8,10},{9,11},{10,... | collective-permute-start | bytes 688136 | tf_op jit(solution)/shard_map/ppermute | solution.py:344
  15.5 18.8 %collective-permute-start.9 = (f32[56,1024]{1,0:T(8,128)S(1)}, f32[56,1024]{1,0:T(8,128)S(1)}, u32[]{:S(2)}, u32[]{:S(2)}) collective-permute-start(f32[56,1024]{1,0:T(8,128)S(1)} %get-tuple-element.107), channel_id=1, source_target_pairs={{0,1},{1,0},{2,3},{3,2},{4,5},{5,4},{6,7},{7,6},{8,9},{9,8},{10,11... | collective-permute-start | bytes 688136 | tf_op jit(solution)/shard_map/ppermute | solution.py:344
  17.2 0.7 copy-start.7
  17.9 5.0 %collective-permute-start = (f32[1,4,8,1024]{3,2,1,0:T(8,128)S(1)}, f32[1,4,8,1024]{3,2,1,0:T(8,128)S(1)}, u32[]{:S(2)}, u32[]{:S(2)}) collective-permute-start(f32[1,4,8,1024]{3,2,1,0:T(8,128)S(1)} %get-tuple-element.172), channel_id=1, source_target_pairs={{0,8},{4,12},{8,0},{12,4},{16,24},{20,28},{24,16},{28,20},{1,9},{5... | collective-permute-start | bytes 393224 | tf_op jit(solution)/shard_map/cond/branch_1_fun/ppermute | solution.py:344
  19.4 8.1 %collective-permute-start.1 = (f32[1,4,8,1024]{3,2,1,0:T(8,128)S(1)}, f32[1,4,8,1024]{3,2,1,0:T(8,128)S(1)}, u32[]{:S(2)}, u32[]{:S(2)}) collective-permute-start(f32[1,4,8,1024]{3,2,1,0:T(8,128)S(1)} %get-tuple-element.172), channel_id=1, source_target_pairs={{0,16},{4,20},{8,24},{12,28},{16,0},{20,4},{24,8},{28,12},{1,17},{... | collective-permute-start | bytes 393224 | tf_op jit(solution)/shard_map/cond/branch_1_fun/ppermute | solution.py:344
  22.8 5.1 %copy-start.3 = (f32[1,4,8,1024]{3,2,1,0:T(8,128)}, f32[1,4,8,1024]{3,2,1,0:T(8,128)S(1)}, u32[]{:S(2)}) copy-start(f32[1,4,8,1024]{3,2,1,0:T(8,128)S(1)} %collective-permute-done) | copy-start | bytes 393220 | tf_op jit(solution)/shard_map/cond
  22.8 5.1 %collective-permute-start.2 = (f32[1,4,8,1024]{3,2,1,0:T(8,128)S(1)}, f32[1,4,8,1024]{3,2,1,0:T(8,128)}, u32[]{:S(2)}, u32[]{:S(2)}) collective-permute-start(f32[1,4,8,1024]{3,2,1,0:T(8,128)S(1)} %collective-permute-done), channel_id=1, source_target_pairs={{0,16},{4,20},{8,24},{12,28},{16,0},{20,4},{24,8},{28,12},{1,17},{... | collective-permute-start | bytes 393224 | tf_op jit(solution)/shard_map/cond/branch_1_fun/ppermute | solution.py:344
  27.5 1.3 %copy-start.5 = (f32[1,4,8,1024]{3,2,1,0:T(8,128)}, f32[1,4,8,1024]{3,2,1,0:T(8,128)S(1)}, u32[]{:S(2)}) copy-start(f32[1,4,8,1024]{3,2,1,0:T(8,128)S(1)} %collective-permute-done.1) | copy-start | bytes 393220 | tf_op jit(solution)/shard_map/cond
  28.9 2.1 %copy-start.4 = (f32[1,4,8,1024]{3,2,1,0:T(8,128)S(1)}, f32[1,4,8,1024]{3,2,1,0:T(8,128)}, u32[]{:S(2)}) copy-start(f32[1,4,8,1024]{3,2,1,0:T(8,128)} %copy-done.3) | copy-start | bytes 393220 | tf_op jit(solution)/shard_map/cond
  28.9 2.1 %copy-start.6 = (f32[1,4,8,1024]{3,2,1,0:T(8,128)S(1)}, f32[1,4,8,1024]{3,2,1,0:T(8,128)}, u32[]{:S(2)}) copy-start(f32[1,4,8,1024]{3,2,1,0:T(8,128)} %copy-done.5) | copy-start | bytes 393220 | tf_op jit(solution)/shard_map/cond
  28.9 2.1 %collective-permute-start.3 = (f32[4,4,8,1024]{3,2,1,0:T(8,128)S(1)}, f32[4,4,8,1024]{3,2,1,0:T(8,128)}, u32[]{:S(2)}, u32[]{:S(2)}) collective-permute-start(f32[4,4,8,1024]{3,2,1,0:T(8,128)S(1)} %pad_maximum_fusion), channel_id=1, source_target_pairs={{0,4},{4,0},{8,12},{12,8},{16,20},{20,16},{24,28},{28,24},{1,5},{5... | collective-permute-start | bytes 1572872 | tf_op jit(solution)/shard_map/cond/branch_1_fun/ppermute | solution.py:344
  40.5 6.9 %collective-permute-start.12 = (f32[72,512]{1,0:T(8,128)S(1)}, f32[72,512]{1,0:T(8,128)S(1)}, u32[]{:S(2)}, u32[]{:S(2)}) collective-permute-start(f32[72,512]{1,0:T(8,128)S(1)} %get-tuple-element.134), channel_id=1, source_target_pairs={{0,1},{1,0},{2,3},{3,2},{4,5},{5,4},{6,7},{7,6},{8,9},{9,8},{10,11... | collective-permute-start | bytes 442376 | tf_op jit(solution)/shard_map/ppermute | solution.py:344
  40.6 12.5 %collective-permute-start.11 = (f32[72,512]{1,0:T(8,128)S(1)}, f32[72,512]{1,0:T(8,128)S(1)}, u32[]{:S(2)}, u32[]{:S(2)}) collective-permute-start(f32[72,512]{1,0:T(8,128)S(1)} %get-tuple-element.133), channel_id=1, source_target_pairs={{0,2},{1,3},{2,0},{3,1},{4,6},{5,7},{6,4},{7,5},{8,10},{9,11},{10,... | collective-permute-start | bytes 442376 | tf_op jit(solution)/shard_map/ppermute | solution.py:344
  42.8 10.2 %collective-permute-start.10 = (f32[72,512]{1,0:T(8,128)S(1)}, f32[72,512]{1,0:T(8,128)S(1)}, u32[]{:S(2)}, u32[]{:S(2)}) collective-permute-start(f32[72,512]{1,0:T(8,128)S(1)} %get-tuple-element.132), channel_id=1, source_target_pairs={{0,3},{1,2},{2,1},{3,0},{4,7},{5,6},{6,5},{7,4},{8,11},{9,10},{10,... | collective-permute-start | bytes 442376 | tf_op jit(solution)/shard_map/ppermute | solution.py:344
  53.2 5.2 %collective-permute-start.13 = (f32[72,512]{1,0:T(8,128)S(1)}, f32[72,512]{1,0:T(8,128)S(1)}, u32[]{:S(2)}, u32[]{:S(2)}) collective-permute-start(f32[72,512]{1,0:T(8,128)S(1)} %get-tuple-element.143), channel_id=1, source_target_pairs={{0,8},{4,12},{8,0},{12,4},{16,24},{20,28},{24,16},{28,20},{1,9},{5... | collective-permute-start | bytes 442376 | tf_op jit(solution)/shard_map/ppermute | solution.py:344
  54.7 5.1 %collective-permute-start.14 = (f32[72,512]{1,0:T(8,128)S(1)}, f32[72,512]{1,0:T(8,128)S(1)}, u32[]{:S(2)}, u32[]{:S(2)}) collective-permute-start(f32[72,512]{1,0:T(8,128)S(1)} %get-tuple-element.142), channel_id=1, source_target_pairs={{0,16},{4,20},{8,24},{12,28},{16,0},{20,4},{24,8},{28,12},{1,17},{... | collective-permute-start | bytes 442376 | tf_op jit(solution)/shard_map/ppermute | solution.py:344
  56.2 7.4 %copy-start = (s32[8]{0:T(128)S(1)}, s32[8]{0:T(128)}, u32[]{:S(2)}) copy-start(s32[8]{0:T(128)} %pair_one.3) | copy-start | bytes 100
  56.2 7.4 %copy-start.1 = (s32[8]{0:T(128)S(1)}, s32[8]{0:T(128)}, u32[]{:S(2)}) copy-start(s32[8]{0:T(128)} %pair_two.3) | copy-start | bytes 100
  56.2 6.0 %collective-permute-start.15 = (f32[72,512]{1,0:T(8,128)S(1)}, f32[72,512]{1,0:T(8,128)S(1)}, u32[]{:S(2)}, u32[]{:S(2)}) collective-permute-start(f32[72,512]{1,0:T(8,128)S(1)} %get-tuple-element.141), channel_id=1, source_target_pairs={{0,24},{4,28},{8,16},{12,20},{16,8},{20,12},{24,0},{28,4},{1,25},{... | collective-permute-start | bytes 442376 | tf_op jit(solution)/shard_map/ppermute | solution.py:344
  56.7 5.6 %collective-permute-start.16 = (f32[72,512]{1,0:T(8,128)S(1)}, f32[72,512]{1,0:T(8,128)S(1)}, u32[]{:S(2)}, u32[]{:S(2)}) collective-permute-start(f32[72,512]{1,0:T(8,128)S(1)} %get-tuple-element.144.refs_0_), channel_id=1, source_target_pairs={{0,4},{4,0},{8,12},{12,8},{16,20},{20,16},{24,28},{28,24},{1,5},{5... | collective-permute-start | bytes 442376 | tf_op jit(solution)/shard_map/ppermute | solution.py:344
  58.4 3.9 %collective-permute-start.17 = (f32[72,512]{1,0:T(8,128)S(1)}, f32[72,512]{1,0:T(8,128)S(1)}, u32[]{:S(2)}, u32[]{:S(2)}) collective-permute-start(f32[72,512]{1,0:T(8,128)S(1)} %collective-permute-done.13.refs_1_), channel_id=1, source_target_pairs={{0,4},{4,0},{8,12},{12,8},{16,20},{20,16},{24,28},{28,24},{1,5},{5... | collective-permute-start | bytes 442376 | tf_op jit(solution)/shard_map/ppermute | solution.py:344
  59.8 2.4 %collective-permute-start.18 = (f32[72,512]{1,0:T(8,128)S(1)}, f32[72,512]{1,0:T(8,128)S(1)}, u32[]{:S(2)}, u32[]{:S(2)}) collective-permute-start(f32[72,512]{1,0:T(8,128)S(1)} %collective-permute-done.14.refs_2_), channel_id=1, source_target_pairs={{0,4},{4,0},{8,12},{12,8},{16,20},{20,16},{24,28},{28,24},{1,5},{5... | collective-permute-start | bytes 442376 | tf_op jit(solution)/shard_map/ppermute | solution.py:344
  62.3 1.4 %collective-permute-start.19 = (f32[72,512]{1,0:T(8,128)S(1)}, f32[72,512]{1,0:T(8,128)S(1)}, u32[]{:S(2)}, u32[]{:S(2)}) collective-permute-start(f32[72,512]{1,0:T(8,128)S(1)} %collective-permute-done.15.refs_3_), channel_id=1, source_target_pairs={{0,4},{4,0},{8,12},{12,8},{16,20},{20,16},{24,28},{28,24},{1,5},{5... | collective-permute-start | bytes 442376 | tf_op jit(solution)/shard_map/ppermute | solution.py:344
  65.3 6.4 %collective-permute-start.20 = (f32[64,512]{1,0:T(8,128)S(1)}, f32[64,512]{1,0:T(8,128)S(1)}, u32[]{:S(2)}, u32[]{:S(2)}) collective-permute-start(f32[64,512]{1,0:T(8,128)S(1)} %get-tuple-element.136.refs_9_), channel_id=1, source_target_pairs={{0,8},{4,12},{8,0},{12,4},{16,24},{20,28},{24,16},{28,20},{1,9},{5... | collective-permute-start | bytes 393224 | tf_op jit(solution)/shard_map/ppermute | solution.py:344
  65.9 5.8 %collective-permute-start.21 = (f32[64,512]{1,0:T(8,128)S(1)}, f32[64,512]{1,0:T(8,128)S(1)}, u32[]{:S(2)}, u32[]{:S(2)}) collective-permute-start(f32[64,512]{1,0:T(8,128)S(1)} %get-tuple-element.137.refs_10_), channel_id=1, source_target_pairs={{0,16},{4,20},{8,24},{12,28},{16,0},{20,4},{24,8},{28,12},{1,17},{... | collective-permute-start | bytes 393224 | tf_op jit(solution)/shard_map/ppermute | solution.py:344
  66.8 2.1 %copy-start.2 = (s32[8]{0:T(128)S(1)}, s32[8]{0:T(128)}, u32[]{:S(2)}) copy-start(s32[8]{0:T(128)} %owner.1) | copy-start | bytes 100
  66.8 7.4 %collective-permute-start.22 = (f32[64,512]{1,0:T(8,128)S(1)}, f32[64,512]{1,0:T(8,128)S(1)}, u32[]{:S(2)}, u32[]{:S(2)}) collective-permute-start(f32[64,512]{1,0:T(8,128)S(1)} %get-tuple-element.138.refs_11_), channel_id=1, source_target_pairs={{0,24},{4,28},{8,16},{12,20},{16,8},{20,12},{24,0},{28,4},{1,25},{... | collective-permute-start | bytes 393224 | tf_op jit(solution)/shard_map/ppermute | solution.py:344

commit v8 on v7

--- a/solution.py
+++ b/solution.py
@@ -43,6 +43,7 @@
         self.width = self.share + 2 * self.halo
         self.slab = row_local + 4 * rim
         self.chips = sim_devices // 2
+        self.hops = [0, *sorted(range(1, self.chips), key=lambda offset: -offset.bit_count())]
         self.sharers = min(sim_devices, row_local // 8)
         self.share_rows = row_local // self.sharers
         self.head = row_local // 8
@@ -109,10 +110,13 @@
 
 
 def table_kernel(plan, beam, *refs):
-    refs, line = refs[:-1], refs[-1]
+    refs, given, line, sem = refs[:-3], *refs[-3:]
     count = beam.shape[1]
+    copy = pltpu.make_async_copy(beam, given, sem)
+    copy.start()
     line[...] = jnp.zeros(line.shape, jnp.float32)
-    line[:1, :count] = beam[...]
+    copy.wait()
+    line[:1, :count] = given[...]
     kernel = line[...]
     kernel = kernel / jnp.sum(kernel[:1], axis=1, keepdims=True)
     size = kernel.shape[1]
@@ -192,14 +196,11 @@
     bands = [take(2) for _ in plan.blocks]
     last, edges = take(2), take(2)
     outs = take(plan.row_devices)
-    seen, weight, image, base, total, field, side, high, low, mid_high, mid_low, sem = refs
-    for part, owners in zip(parts, sharers):
-        for slot, offset in enumerate(owners):
-            for index, step in enumerate(plan.steps):
-                row = (lax.axis_index("rows") ^ step) * plan.row_local
-                row = row + (lax.rem(lax.axis_index("sims"), plan.sharers) ^ offset) * plan.share_rows
-                rows = pl.ds(pl.multiple_of(row, plan.share_rows), plan.share_rows)
-                pltpu.make_async_copy(part.at[slot, index], weight.at[rows], sem).start()
+    seen, weight, image, base, total, field, side, high, low, mid_high, mid_low, shares, sem = refs
+    first = 0
+    for part in parts:
+        pltpu.make_async_copy(part, shares.at[pl.ds(first, part.shape[0])], sem).start()
+        first += part.shape[0]
     for index, step in enumerate(plan.steps):
         row = pl.multiple_of((lax.axis_index("rows") ^ step) * plan.row_local, plan.row_local)
         rows = pl.ds(row, plan.row_local)
@@ -231,7 +232,12 @@
         if iteration == 0:
             for i, window in zip(chosen, windows):
                 base[:, slice(*plan.blocks[i])] = columns_pass(bands[i], plan.rows, window)
-            pltpu.make_async_copy(weight, weight, sem).wait()
+            pltpu.make_async_copy(shares, shares, sem).wait()
+            for slot, offset in enumerate(offset for owners in sharers for offset in owners):
+                for index, step in enumerate(plan.steps):
+                    row = (lax.axis_index("rows") ^ step) * plan.row_local
+                    row = row + (lax.rem(lax.axis_index("sims"), plan.sharers) ^ offset) * plan.share_rows
+                    weight[pl.ds(pl.multiple_of(row, plan.share_rows), plan.share_rows), :] = shares[slot, index]
         for i, window in zip(chosen, windows):
             a, b = plan.blocks[i]
             value = base[:, a:b]
@@ -288,8 +294,8 @@
     here = lax.axis_index("sims") // 2
     corner[...] = jnp.zeros(corner.shape, jnp.float32)
     kept = plan.row_local + 2 * rim
-    for step in range(plan.chips):
-        for source, parity in ((near[step], core), (far[step], 1 - core)):
+    for index, step in enumerate(plan.hops):
+        for source, parity in ((near[index], core), (far[index], 1 - core)):
             at = 2 * (here ^ step) + parity
             every[at, :, : plan.share] = source[:kept]
             corner[lane - rim :] = source[kept : kept + rim, :lane]
@@ -306,7 +312,7 @@
     every, corner = refs[-2:]
     collect(plan, near, far, every, corner)
     chip, core = lax.axis_index("sims") // 2, lax.axis_index("sims") % 2
-    for step, out in enumerate(outs):
+    for step, out in zip(plan.hops, outs):
         out[...] = mixed(every, pair_one, pair_two, 2 * (chip ^ step) + core)
 
 
@@ -316,7 +322,7 @@
     collect(plan, near, far, every, corner)
     chip, core = lax.axis_index("sims") // 2, lax.axis_index("sims") % 2
     whole[...] = jnp.zeros(whole.shape, jnp.float32)
-    for step, estimate in enumerate(done):
+    for step, estimate in zip(plan.hops, done):
         sim = 2 * (chip ^ step)
         whole[owner[sim + core]] += estimate[...]
         whole[owner[sim + 1 - core]] += mixed(every, pair_one, pair_two, sim + 1 - core)
@@ -331,7 +337,7 @@
 def join_kernel(plan, *refs):
     pieces, estimate, sems = refs[: plan.chips], refs[plan.chips], refs[plan.chips + 1]
     copies = []
-    for step, piece in enumerate(pieces):
+    for step, piece in zip(plan.hops, pieces):
         column = pl.multiple_of(((lax.axis_index("sims") // 2) ^ step) * plan.share, lane)
         copies.append(pltpu.make_async_copy(piece, estimate.at[:, pl.ds(column, plan.share)], sems.at[step]))
         copies[-1].start()
@@ -374,6 +380,7 @@
         + [pltpu.VMEM((-(-plan.row_devices * plan.slab // lane) * lane, lane), jnp.float32)]
         + [pltpu.VMEM(full, jnp.bfloat16)] * 2
         + [pltpu.VMEM(tall, jnp.bfloat16)] * 2
+        + [pltpu.VMEM((plan.sharers, plan.row_devices, plan.share_rows, plan.width), jnp.float32)]
         + [pltpu.SemaphoreType.DMA],
         1 << 33,
         1 << 23,
@@ -401,7 +408,7 @@
     moved = jnp.stack(exchange_all(plan, pieces))
     here = (lax.axis_index("sims") // 2) ^ lax.axis_index("rows")
     near = []
-    for step in range(plan.chips):
+    for step in plan.hops:
         value = lax.dynamic_index_in_dim(moved, order_of(plan, here ^ step), keepdims=False)
         near.append(exchange(value, "sims", 2 * step) if step else value)
     far = [exchange(value, "sims", 1) for value in near]
@@ -430,7 +437,7 @@
     if kept != field_width:
         start = (lax.axis_index("sims") % 2) * field_width
         mean_field = lax.dynamic_slice_in_dim(mean_field, start, field_width, axis=2)
-    moved = [value if step == 0 else exchange(value, "sims", 2 * step) for step, value in enumerate(found)]
+    moved = [exchange(value, "sims", 2 * step) if step else value for step, value in zip(plan.hops, found)]
     [estimate] = call(
         functools.partial(join_kernel, plan),
         [f32(plan.row_local, plan.columns)],
@@ -488,11 +495,11 @@
         tables = call(
             functools.partial(table_kernel, plan),
             [b16(*shape) for shape in shapes for _ in range(2)],
-            [vmem],
-            [pltpu.VMEM((8, lane), jnp.float32)],
+            [far],
+            [pltpu.VMEM((1, taps), jnp.float32), pltpu.VMEM((8, lane), jnp.float32), pltpu.SemaphoreType.DMA],
             1 << 32,
             1 << 23,
-        )(beam[None])
+        )(pinned(beam))
         found = {0: parts}
         for bit in [1 << i for i in range(1, plan.sharers.bit_length() - 1)]:
             found |= {offset | bit: exchange(value, "sims", bit) for offset, value in found.items()}
@@ -501,13 +508,13 @@
         return [*found.values(), exchange(whole, "sims", 1)], tables
 
     sharers = []
-    made = jax.eval_shape(prepare, parts, beam)
+    made = jax.eval_shape(prepare, parts, beam[None])
     parts, tables = lax.cond(
         lax.axis_index("rows") < row_devices,
         prepare,
         lambda parts, beam: jax.tree.map(lambda x: jnp.zeros(x.shape, x.dtype), made),
         parts,
-        beam,
+        beam[None],
     )
     filtered = run_filter(plan, sharers, heads, tails, parts, tables)
     estimate, mean_field = run_estimates(plan, filtered, pair_one, pair_two, owner)

time: 75.5 us -> 74.3 us (0.984)
  transfers between devices with their start and end apart: 23 -> 23, of which waited for: 14 -> 15; matrix products, arithmetic and copies ran while one was open for 1% -> 1% of each run, Pallas kernels for 8% -> 9%
where the time goes in v8:
time: 74.3 us; the launch traced here: 74.1 us
  waiting for transfers between devices  29.6 us (40%)
  starting transfers between devices  26.4 us (36%)
  Pallas kernels  15.9 us (21%)
  other arithmetic  1.03 us (1%)
  between operations  0.87 us (1%)
    ppermute x23, waiting for transfers between devices, exchange(): return lax.ppermute(value, axis, [(i, i ^ offset) for i in range(count)])  29.6 us
    ppermute x23, starting transfers between devices, exchange(): return lax.ppermute(value, axis, [(i, i ^ offset) for i in range(count)])  26.4 us
    pallas_call x1, Pallas kernels, run_filter(): call(functools.partial(filter_kernel, plan, sharers), [jax.ShapeDtypeStru...  5.64 us
    pallas_call x1, Pallas kernels, prepare(): call(functools.partial(table_kernel, plan), [b16(*shape) for shape in sha...  3.8 us
    pallas_call x1, Pallas kernels, run_estimates(): call(functools.partial(mean_kernel, plan, kept), [f32(OWNERS, plan.row_lo...  2.6 us
    pallas_call x1, Pallas kernels, run_estimates(): call(functools.partial(estimate_kernel, plan), [f32(plan.row_local, plan....  1.64 us
  transfers between devices with their start and end apart: 23, of which 15 were waited for; matrix products, arithmetic and copies ran while one was open for 1% of the time, Pallas kernels for 9%

profile of v8, /device:TPU:0, one launch (start us, length us, event | category | flops | bytes accessed | tf_op | source)
XLA Modules:
  0.0 74.1 jit_solution(7194965277032661339)
XLA Ops:
  0.6 1.4 %shard_map.78 = (f32[16,1024]{1,0:T(8,128)S(1)}, f32[16,1024]{1,0:T(8,128)S(1)}, f32[16,1024]{1,0:T(8,128)S(1)}, f32[16,1024]{1,0:T(8,128)S(1)}, f32[56,1024]{1,...) custom-call(f32[64,2048]{1,0:T(8,128)} %bitcast.26, f32[64,2048]{1,0:T(8,128)} %weight.1), custom_call_target="tpu_custom_call" | custom-call | flops 131072 | bytes 2097152 | tf_op jit(solution)/shard_map/pallas_call | solution.py:472
  2.1 5.1 %collective-permute-start.4 = (f32[16,1024]{1,0:T(8,128)S(1)}, f32[16,1024]{1,0:T(8,128)S(1)}, u32[]{:S(2)}, u32[]{:S(2)}) collective-permute-start(f32[16,1024]{1,0:T(8,128)S(1)} %get-tuple-element.98), channel_id=1, source_target_pairs={{0,3},{1,2},{2,1},{3,0},{4,7},{5,6},{6,5},{7,4},{8,11},{9,10},{10,... | collective-permute-start | bytes 196616 | tf_op jit(solution)/shard_map/ppermute | solution.py:350
  7.2 0.0 collective-permute-start.5
  7.2 0.6 collective-permute-start.6
  7.8 1.9 %collective-permute-done.4.refs_1_ = f32[16,1024]{1,0:T(8,128)S(1)} collective-permute-done((f32[16,1024]{1,0:T(8,128)S(1)}, f32[16,1024]{1,0:T(8,128)S(1)}, u32[]{:S(2)}, u32[]{:S(2)}) %collective-permute-start.4) | collective-permute-done | bytes 65568 | tf_op jit(solution)/shard_map/ppermute | solution.py:350
  9.8 3.0 %collective-permute-done.5.refs_2_ = f32[16,1024]{1,0:T(8,128)S(1)} collective-permute-done((f32[16,1024]{1,0:T(8,128)S(1)}, f32[16,1024]{1,0:T(8,128)S(1)}, u32[]{:S(2)}, u32[]{:S(2)}) %collective-permute-start.5) | collective-permute-done | bytes 65568 | tf_op jit(solution)/shard_map/ppermute | solution.py:350
  12.8 0.0 collective-permute-done.6.refs_3_
  12.8 2.7 %collective-permute-start.7 = (f32[56,1024]{1,0:T(8,128)S(1)}, f32[56,1024]{1,0:T(8,128)S(1)}, u32[]{:S(2)}, u32[]{:S(2)}) collective-permute-start(f32[56,1024]{1,0:T(8,128)S(1)} %get-tuple-element.106), channel_id=1, source_target_pairs={{0,3},{1,2},{2,1},{3,0},{4,7},{5,6},{6,5},{7,4},{8,11},{9,10},{10,... | collective-permute-start | bytes 688136 | tf_op jit(solution)/shard_map/ppermute | solution.py:350
  15.5 0.0 collective-permute-start.8
  15.5 1.7 %collective-permute-start.9 = (f32[56,1024]{1,0:T(8,128)S(1)}, f32[56,1024]{1,0:T(8,128)S(1)}, u32[]{:S(2)}, u32[]{:S(2)}) collective-permute-start(f32[56,1024]{1,0:T(8,128)S(1)} %get-tuple-element.108), channel_id=1, source_target_pairs={{0,1},{1,0},{2,3},{3,2},{4,5},{5,4},{6,7},{7,6},{8,9},{9,8},{10,11... | collective-permute-start | bytes 688136 | tf_op jit(solution)/shard_map/ppermute | solution.py:350
  17.2 13.5 %conditional.1 = (f32[1,4,8,1024]{3,2,1,0:T(8,128)S(1)}, f32[1,4,8,1024]{3,2,1,0:T(8,128)S(1)}, f32[1,4,8,1024]{3,2,1,0:T(8,128)S(1)}, f32[1,4,8,1024]{3,2,1,0:T...) conditional(s32[]{:T(128)} %convert_element_type.3, () %tuple.19, ...), branch_computations={%region_0.0_spmd, %region_1.0_spmd} | conditional | flops 4295360512 | bytes 15466952 | solution.py:512
  17.2 1.6 %collective-permute-start = (f32[1,4,8,1024]{3,2,1,0:T(8,128)S(1)}, f32[1,4,8,1024]{3,2,1,0:T(8,128)S(1)}, u32[]{:S(2)}, u32[]{:S(2)}) collective-permute-start(f32[1,4,8,1024]{3,2,1,0:T(8,128)S(1)} %get-tuple-element.173), channel_id=1, source_target_pairs={{0,8},{4,12},{8,0},{12,4},{16,24},{20,28},{24,16},{28,20},{1,9},{5... | collective-permute-start | bytes 393224 | tf_op jit(solution)/shard_map/cond/branch_1_fun/ppermute | solution.py:350
  18.8 1.5 %collective-permute-start.1 = (f32[1,4,8,1024]{3,2,1,0:T(8,128)S(1)}, f32[1,4,8,1024]{3,2,1,0:T(8,128)S(1)}, u32[]{:S(2)}, u32[]{:S(2)}) collective-permute-start(f32[1,4,8,1024]{3,2,1,0:T(8,128)S(1)} %get-tuple-element.173), channel_id=1, source_target_pairs={{0,16},{4,20},{8,24},{12,28},{16,0},{20,4},{24,8},{28,12},{1,17},{... | collective-permute-start | bytes 393224 | tf_op jit(solution)/shard_map/cond/branch_1_fun/ppermute | solution.py:350
  20.3 2.0 %collective-permute-done = f32[1,4,8,1024]{3,2,1,0:T(8,128)S(1)} collective-permute-done((f32[1,4,8,1024]{3,2,1,0:T(8,128)S(1)}, f32[1,4,8,1024]{3,2,1,0:T(8,128)S(1)}, u32[]{:S(2)}, u32[]{:S(2)}) %collective-permute-start) | collective-permute-done | bytes 131104 | tf_op jit(solution)/shard_map/cond/branch_1_fun/ppermute | solution.py:350
  22.3 1.5 %collective-permute-start.2 = (f32[1,4,8,1024]{3,2,1,0:T(8,128)S(1)}, f32[1,4,8,1024]{3,2,1,0:T(8,128)}, u32[]{:S(2)}, u32[]{:S(2)}) collective-permute-start(f32[1,4,8,1024]{3,2,1,0:T(8,128)S(1)} %collective-permute-done), channel_id=1, source_target_pairs={{0,16},{4,20},{8,24},{12,28},{16,0},{20,4},{24,8},{28,12},{1,17},{... | collective-permute-start | bytes 393224 | tf_op jit(solution)/shard_map/cond/branch_1_fun/ppermute | solution.py:350
  23.8 3.8 %branch_1_fun.1 = (bf16[256,256]{1,0:T(8,128)(2,1)S(1)}, bf16[256,256]{1,0:T(8,128)(2,1)S(1)}, bf16[288,256]{1,0:T(8,128)(2,1)S(1)}, bf16[288,256]{1,0:T(8,128)(...) custom-call(f32[1,65]{1,0:T(1,128)} %bitcast.31), custom_call_target="tpu_custom_call" | custom-call | flops 4294967296 | bytes 8388608 | tf_op jit(solution)/shard_map/cond/branch_1_fun/pallas_call | solution.py:495
  27.6 0.0 collective-permute-done.1
  27.6 0.0 copy-start.5
  27.6 0.0 collective-permute-done.2
  27.6 0.0 copy-done.3
  27.6 1.0 %pad_maximum_fusion = f32[4,4,8,1024]{3,2,1,0:T(8,128)S(1)} fusion(f32[1,4,8,1024]{3,2,1,0:T(8,128)} %collective-permute-done.2, f32[1,4,8,1024]{3,2,1,0:T(8,128)S(1)} %collective-permute-done.1, f32[1,4,8,1024]{3,2,1,0:T(8,128)S(1)} %collective-permute-done, f32[1,4,8,1024]{3,2,1,0:T(8,128)S(1)} %get-tuple-element.173), kind=kLoop, calls=%fused_computation | loop fusion | flops 393216 | bytes 1048576 | tf_op jit(solution)/shard_map/cond/branch_1_fun/concatenate | solution.py:507
  28.6 0.0 copy-done.5
  28.6 0.0 copy-start.4
  28.6 0.0 copy-start.6
  28.7 0.1 collective-permute-start.3
  28.8 2.0 %collective-permute-done.3 = f32[4,4,8,1024]{3,2,1,0:T(8,128)} collective-permute-done((f32[4,4,8,1024]{3,2,1,0:T(8,128)S(1)}, f32[4,4,8,1024]{3,2,1,0:T(8,128)}, u32[]{:S(2)}, u32[]{:S(2)}) %collective-permute-start.3) | collective-permute-done | bytes 524320 | tf_op jit(solution)/shard_map/cond/branch_1_fun/ppermute | solution.py:350
  30.8 0.0 copy-done.4
  30.8 0.0 copy-done.6
  30.8 0.0 collective-permute-done.7.refs_5_
  30.8 3.5 %collective-permute-done.8.refs_6_ = f32[56,1024]{1,0:T(8,128)S(1)} collective-permute-done((f32[56,1024]{1,0:T(8,128)S(1)}, f32[56,1024]{1,0:T(8,128)S(1)}, u32[]{:S(2)}, u32[]{:S(2)}) %collective-permute-start.8) | collective-permute-done | bytes 229408 | tf_op jit(solution)/shard_map/ppermute | solution.py:350
  34.3 0.0 collective-permute-done.9.refs_7_
  34.3 5.6 %shard_map.79 = (f32[72,512]{1,0:T(8,128)S(1)}, f32[72,512]{1,0:T(8,128)S(1)}, f32[72,512]{1,0:T(8,128)S(1)}, f32[72,512]{1,0:T(8,128)S(1)}) custom-call(f32[16,1024]{1,0:T(8,128)S(1)} %get-tuple-element.101.refs_0_, f32[16,1024]{1,0:T(8,128)S(1)} %collective-permute-done.4.refs_1_, f32[16,1024]{1,0:T(8,128)S(1)} %collective-permute-done.5.refs_2_, ...), custom_call_target="tpu_custom_call" | custom-call | flops 8589934592 | bytes 8388608 | tf_op jit(solution)/shard_map/pallas_call | solution.py:374
  39.9 0.1 collective-permute-start.12
  40.0 2.2 %collective-permute-start.11 = (f32[72,512]{1,0:T(8,128)S(1)}, f32[72,512]{1,0:T(8,128)S(1)}, u32[]{:S(2)}, u32[]{:S(2)}) collective-permute-start(f32[72,512]{1,0:T(8,128)S(1)} %get-tuple-element.134), channel_id=1, source_target_pairs={{0,2},{1,3},{2,0},{3,1},{4,6},{5,7},{6,4},{7,5},{8,10},{9,11},{10,... | collective-permute-start | bytes 442376 | tf_op jit(solution)/shard_map/ppermute | solution.py:350
  42.3 2.1 %collective-permute-start.10 = (f32[72,512]{1,0:T(8,128)S(1)}, f32[72,512]{1,0:T(8,128)S(1)}, u32[]{:S(2)}, u32[]{:S(2)}) collective-permute-start(f32[72,512]{1,0:T(8,128)S(1)} %get-tuple-element.133), channel_id=1, source_target_pairs={{0,3},{1,2},{2,1},{3,0},{4,7},{5,6},{6,5},{7,4},{8,11},{9,10},{10,... | collective-permute-start | bytes 442376 | tf_op jit(solution)/shard_map/ppermute | solution.py:350
  44.4 2.5 %collective-permute-done.12 = f32[72,512]{1,0:T(8,128)S(1)} collective-permute-done((f32[72,512]{1,0:T(8,128)S(1)}, f32[72,512]{1,0:T(8,128)S(1)}, u32[]{:S(2)}, u32[]{:S(2)}) %collective-permute-start.12) | collective-permute-done | bytes 147488 | tf_op jit(solution)/shard_map/ppermute | solution.py:350
  46.9 5.6 %collective-permute-done.11 = f32[72,512]{1,0:T(8,128)S(1)} collective-permute-done((f32[72,512]{1,0:T(8,128)S(1)}, f32[72,512]{1,0:T(8,128)S(1)}, u32[]{:S(2)}, u32[]{:S(2)}) %collective-permute-start.11) | collective-permute-done | bytes 147488 | tf_op jit(solution)/shard_map/ppermute | solution.py:350
  52.5 0.0 collective-permute-done.10
  52.5 0.1 dynamic-slice_bitcast_fusion
  52.6 2.5 %collective-permute-start.13 = (f32[72,512]{1,0:T(8,128)S(1)}, f32[72,512]{1,0:T(8,128)S(1)}, u32[]{:S(2)}, u32[]{:S(2)}) collective-permute-start(f32[72,512]{1,0:T(8,128)S(1)} %get-tuple-element.144), channel_id=1, source_target_pairs={{0,24},{4,28},{8,16},{12,20},{16,8},{20,12},{24,0},{28,4},{1,25},{... | collective-permute-start | bytes 442376 | tf_op jit(solution)/shard_map/ppermute | solution.py:350
  55.1 0.5 collective-permute-start.14
  55.6 0.5 collective-permute-start.15
  56.2 0.0 collective-permute-start.16
  56.2 2.5 %collective-permute-done.13.refs_1_ = f32[72,512]{1,0:T(8,128)S(1)} collective-permute-done((f32[72,512]{1,0:T(8,128)S(1)}, f32[72,512]{1,0:T(8,128)S(1)}, u32[]{:S(2)}, u32[]{:S(2)}) %collective-permute-start.13) | collective-permute-done | bytes 147488 | tf_op jit(solution)/shard_map/ppermute | solution.py:350
  58.7 0.0 collective-permute-start.17
  58.7 1.6 %collective-permute-done.14.refs_2_ = f32[72,512]{1,0:T(8,128)S(1)} collective-permute-done((f32[72,512]{1,0:T(8,128)S(1)}, f32[72,512]{1,0:T(8,128)S(1)}, u32[]{:S(2)}, u32[]{:S(2)}) %collective-permute-start.14) | collective-permute-done | bytes 147488 | tf_op jit(solution)/shard_map/ppermute | solution.py:350
  60.3 0.0 collective-permute-start.18
  60.3 0.4 collective-permute-done.15.refs_3_
  60.8 0.1 collective-permute-start.19
  60.8 0.0 collective-permute-done.16.refs_4_
  60.8 0.0 collective-permute-done.17.refs_5_
  60.9 0.9 %collective-permute-done.18.refs_6_ = f32[72,512]{1,0:T(8,128)S(1)} collective-permute-done((f32[72,512]{1,0:T(8,128)S(1)}, f32[72,512]{1,0:T(8,128)S(1)}, u32[]{:S(2)}, u32[]{:S(2)}) %collective-permute-start.18) | collective-permute-done | bytes 147488 | tf_op jit(solution)/shard_map/ppermute | solution.py:350
  61.7 0.5 collective-permute-done.19.refs_7_
  62.2 0.0 copy-done
  62.2 0.0 copy-done.1
  62.2 1.6 %shard_map.80 = (f32[64,512]{1,0:T(8,128)S(1)}, f32[64,512]{1,0:T(8,128)S(1)}, f32[64,512]{1,0:T(8,128)S(1)}, f32[64,512]{1,0:T(8,128)S(1)}) custom-call(s32[8]{0:T(128)S(1)} %copy-done, s32[8]{0:T(128)S(1)} %copy-done.1, f32[72,512]{1,0:T(8,128)S(1)} %get-tuple-element.145.refs_0_, f32[72,512]{1,0:T(8,128)S(1)} %collective-permute-done.13.refs_1_, ...), custom_call_target="tpu_custom_call" | custom-call | flops 16777216 | bytes 8388608 | tf_op jit(solution)/shard_map/pallas_call | solution.py:419
  63.8 2.0 %collective-permute-start.20 = (f32[64,512]{1,0:T(8,128)S(1)}, f32[64,512]{1,0:T(8,128)S(1)}, u32[]{:S(2)}, u32[]{:S(2)}) collective-permute-start(f32[64,512]{1,0:T(8,128)S(1)} %get-tuple-element.137.refs_9_), channel_id=1, source_target_pairs={{0,24},{4,28},{8,16},{12,20},{16,8},{20,12},{24,0},{28,4},{1,25},{... | collective-permute-start | bytes 393224 | tf_op jit(solution)/shard_map/ppermute | solution.py:350
  65.8 0.5 collective-permute-start.21
  66.4 1.0 %collective-permute-start.22 = (f32[64,512]{1,0:T(8,128)S(1)}, f32[64,512]{1,0:T(8,128)S(1)}, u32[]{:S(2)}, u32[]{:S(2)}) collective-permute-start(f32[64,512]{1,0:T(8,128)S(1)} %get-tuple-element.139.refs_11_), channel_id=1, source_target_pairs={{0,16},{4,20},{8,24},{12,28},{16,0},{20,4},{24,8},{28,12},{1,17},{... | collective-permute-start | bytes 393224 | tf_op jit(solution)/shard_map/ppermute | solution.py:350
  67.4 2.6 %shard_map.82 = f32[8,64,256]{2,1,0:T(8,128)} custom-call(s32[8]{0:T(128)S(1)} %copy-done, s32[8]{0:T(128)S(1)} %copy-done.1, s32[8]{0:T(128)S(1)} %copy-done.2, f32[72,512]{1,0:T(8,128)S(1)} %get-tuple-element.145.refs_0_, f32[72,512]{1,0:T(8,128)S(1)} %collective-permute-done.13.refs_1_, f32[72,512]{1,0:T(8,128)S(1)} %collective-permute-done.14.refs_2_, ...), custom_call_target="tpu_custom_call" | custom-call | flops 16777216 | bytes 8388608 | tf_op jit(solution)/shard_map/pallas_call | solution.py:429
  70.0 1.2 %collective-permute-done.20.refs_1_ = f32[64,512]{1,0:T(8,128)S(1)} collective-permute-done((f32[64,512]{1,0:T(8,128)S(1)}, f32[64,512]{1,0:T(8,128)S(1)}, u32[]{:S(2)}, u32[]{:S(2)}) %collective-permute-start.20) | collective-permute-done | bytes 131104 | tf_op jit(solution)/shard_map/ppermute | solution.py:350
  71.1 1.6 %collective-permute-done.21.refs_2_ = f32[64,512]{1,0:T(8,128)S(1)} collective-permute-done((f32[64,512]{1,0:T(8,128)S(1)}, f32[64,512]{1,0:T(8,128)S(1)}, u32[]{:S(2)}, u32[]{:S(2)}) %collective-permute-start.21) | collective-permute-done | bytes 131104 | tf_op jit(solution)/shard_map/ppermute | solution.py:350
  72.7 0.5 collective-permute-done.22.refs_3_
  73.1 0.8 %shard_map.81 = f32[64,2048]{1,0:T(8,128)} custom-call(f32[64,512]{1,0:T(8,128)S(1)} %get-tuple-element.136.refs_0_.refs_8_, f32[64,512]{1,0:T(8,128)S(1)} %collective-permute-done.20.refs_1_, f32[64,512]{1,0:T(8,128)S(1)} %collective-permute-done.21.refs_2_, f32[64,512]{1,0:T(8,128)S(1)} %collective-permute-done.22.refs_3_), custom_call_target="tpu_custom_call" | custom-call | bytes 1048576 | tf_op jit(solution)/shard_map/pallas_call | solution.py:441
  (10 shorter events, 0.1 us)
Async XLA Ops:
  2.1 7.7 %collective-permute-start.4 = (f32[16,1024]{1,0:T(8,128)S(1)}, f32[16,1024]{1,0:T(8,128)S(1)}, u32[]{:S(2)}, u32[]{:S(2)}) collective-permute-start(f32[16,1024]{1,0:T(8,128)S(1)} %get-tuple-element.98), channel_id=1, source_target_pairs={{0,3},{1,2},{2,1},{3,0},{4,7},{5,6},{6,5},{7,4},{8,11},{9,10},{10,... | collective-permute-start | bytes 196616 | tf_op jit(solution)/shard_map/ppermute | solution.py:350
  7.2 5.6 %collective-permute-start.5 = (f32[16,1024]{1,0:T(8,128)S(1)}, f32[16,1024]{1,0:T(8,128)S(1)}, u32[]{:S(2)}, u32[]{:S(2)}) collective-permute-start(f32[16,1024]{1,0:T(8,128)S(1)} %get-tuple-element.99), channel_id=1, source_target_pairs={{0,2},{1,3},{2,0},{3,1},{4,6},{5,7},{6,4},{7,5},{8,10},{9,11},{10,... | collective-permute-start | bytes 196616 | tf_op jit(solution)/shard_map/ppermute | solution.py:350
  7.2 5.6 %collective-permute-start.6 = (f32[16,1024]{1,0:T(8,128)S(1)}, f32[16,1024]{1,0:T(8,128)S(1)}, u32[]{:S(2)}, u32[]{:S(2)}) collective-permute-start(f32[16,1024]{1,0:T(8,128)S(1)} %get-tuple-element.100), channel_id=1, source_target_pairs={{0,1},{1,0},{2,3},{3,2},{4,5},{5,4},{6,7},{7,6},{8,9},{9,8},{10,11... | collective-permute-start | bytes 196616 | tf_op jit(solution)/shard_map/ppermute | solution.py:350
  12.8 18.0 %collective-permute-start.7 = (f32[56,1024]{1,0:T(8,128)S(1)}, f32[56,1024]{1,0:T(8,128)S(1)}, u32[]{:S(2)}, u32[]{:S(2)}) collective-permute-start(f32[56,1024]{1,0:T(8,128)S(1)} %get-tuple-element.106), channel_id=1, source_target_pairs={{0,3},{1,2},{2,1},{3,0},{4,7},{5,6},{6,5},{7,4},{8,11},{9,10},{10,... | collective-permute-start | bytes 688136 | tf_op jit(solution)/shard_map/ppermute | solution.py:350
  15.5 18.8 %collective-permute-start.8 = (f32[56,1024]{1,0:T(8,128)S(1)}, f32[56,1024]{1,0:T(8,128)S(1)}, u32[]{:S(2)}, u32[]{:S(2)}) collective-permute-start(f32[56,1024]{1,0:T(8,128)S(1)} %get-tuple-element.107), channel_id=1, source_target_pairs={{0,2},{1,3},{2,0},{3,1},{4,6},{5,7},{6,4},{7,5},{8,10},{9,11},{10,... | collective-permute-start | bytes 688136 | tf_op jit(solution)/shard_map/ppermute | solution.py:350
  15.5 18.8 %collective-permute-start.9 = (f32[56,1024]{1,0:T(8,128)S(1)}, f32[56,1024]{1,0:T(8,128)S(1)}, u32[]{:S(2)}, u32[]{:S(2)}) collective-permute-start(f32[56,1024]{1,0:T(8,128)S(1)} %get-tuple-element.108), channel_id=1, source_target_pairs={{0,1},{1,0},{2,3},{3,2},{4,5},{5,4},{6,7},{7,6},{8,9},{9,8},{10,11... | collective-permute-start | bytes 688136 | tf_op jit(solution)/shard_map/ppermute | solution.py:350
  17.2 5.0 %collective-permute-start = (f32[1,4,8,1024]{3,2,1,0:T(8,128)S(1)}, f32[1,4,8,1024]{3,2,1,0:T(8,128)S(1)}, u32[]{:S(2)}, u32[]{:S(2)}) collective-permute-start(f32[1,4,8,1024]{3,2,1,0:T(8,128)S(1)} %get-tuple-element.173), channel_id=1, source_target_pairs={{0,8},{4,12},{8,0},{12,4},{16,24},{20,28},{24,16},{28,20},{1,9},{5... | collective-permute-start | bytes 393224 | tf_op jit(solution)/shard_map/cond/branch_1_fun/ppermute | solution.py:350
  18.8 8.8 %collective-permute-start.1 = (f32[1,4,8,1024]{3,2,1,0:T(8,128)S(1)}, f32[1,4,8,1024]{3,2,1,0:T(8,128)S(1)}, u32[]{:S(2)}, u32[]{:S(2)}) collective-permute-start(f32[1,4,8,1024]{3,2,1,0:T(8,128)S(1)} %get-tuple-element.173), channel_id=1, source_target_pairs={{0,16},{4,20},{8,24},{12,28},{16,0},{20,4},{24,8},{28,12},{1,17},{... | collective-permute-start | bytes 393224 | tf_op jit(solution)/shard_map/cond/branch_1_fun/ppermute | solution.py:350
  22.3 5.4 %copy-start.3 = (f32[1,4,8,1024]{3,2,1,0:T(8,128)}, f32[1,4,8,1024]{3,2,1,0:T(8,128)S(1)}, u32[]{:S(2)}) copy-start(f32[1,4,8,1024]{3,2,1,0:T(8,128)S(1)} %collective-permute-done) | copy-start | bytes 393220 | tf_op jit(solution)/shard_map/cond
  22.3 5.4 %collective-permute-start.2 = (f32[1,4,8,1024]{3,2,1,0:T(8,128)S(1)}, f32[1,4,8,1024]{3,2,1,0:T(8,128)}, u32[]{:S(2)}, u32[]{:S(2)}) collective-permute-start(f32[1,4,8,1024]{3,2,1,0:T(8,128)S(1)} %collective-permute-done), channel_id=1, source_target_pairs={{0,16},{4,20},{8,24},{12,28},{16,0},{20,4},{24,8},{28,12},{1,17},{... | collective-permute-start | bytes 393224 | tf_op jit(solution)/shard_map/cond/branch_1_fun/ppermute | solution.py:350
  27.6 1.0 %copy-start.5 = (f32[1,4,8,1024]{3,2,1,0:T(8,128)}, f32[1,4,8,1024]{3,2,1,0:T(8,128)S(1)}, u32[]{:S(2)}) copy-start(f32[1,4,8,1024]{3,2,1,0:T(8,128)S(1)} %collective-permute-done.1) | copy-start | bytes 393220 | tf_op jit(solution)/shard_map/cond
  28.6 2.1 %copy-start.4 = (f32[1,4,8,1024]{3,2,1,0:T(8,128)S(1)}, f32[1,4,8,1024]{3,2,1,0:T(8,128)}, u32[]{:S(2)}) copy-start(f32[1,4,8,1024]{3,2,1,0:T(8,128)} %copy-done.3) | copy-start | bytes 393220 | tf_op jit(solution)/shard_map/cond
  28.6 2.1 %copy-start.6 = (f32[1,4,8,1024]{3,2,1,0:T(8,128)S(1)}, f32[1,4,8,1024]{3,2,1,0:T(8,128)}, u32[]{:S(2)}) copy-start(f32[1,4,8,1024]{3,2,1,0:T(8,128)} %copy-done.5) | copy-start | bytes 393220 | tf_op jit(solution)/shard_map/cond
  28.7 2.1 %collective-permute-start.3 = (f32[4,4,8,1024]{3,2,1,0:T(8,128)S(1)}, f32[4,4,8,1024]{3,2,1,0:T(8,128)}, u32[]{:S(2)}, u32[]{:S(2)}) collective-permute-start(f32[4,4,8,1024]{3,2,1,0:T(8,128)S(1)} %pad_maximum_fusion), channel_id=1, source_target_pairs={{0,4},{4,0},{8,12},{12,8},{16,20},{20,16},{24,28},{28,24},{1,5},{5... | collective-permute-start | bytes 1572872 | tf_op jit(solution)/shard_map/cond/branch_1_fun/ppermute | solution.py:350
  39.9 6.9 %collective-permute-start.12 = (f32[72,512]{1,0:T(8,128)S(1)}, f32[72,512]{1,0:T(8,128)S(1)}, u32[]{:S(2)}, u32[]{:S(2)}) collective-permute-start(f32[72,512]{1,0:T(8,128)S(1)} %get-tuple-element.135), channel_id=1, source_target_pairs={{0,1},{1,0},{2,3},{3,2},{4,5},{5,4},{6,7},{7,6},{8,9},{9,8},{10,11... | collective-permute-start | bytes 442376 | tf_op jit(solution)/shard_map/ppermute | solution.py:350
  40.0 12.5 %collective-permute-start.11 = (f32[72,512]{1,0:T(8,128)S(1)}, f32[72,512]{1,0:T(8,128)S(1)}, u32[]{:S(2)}, u32[]{:S(2)}) collective-permute-start(f32[72,512]{1,0:T(8,128)S(1)} %get-tuple-element.134), channel_id=1, source_target_pairs={{0,2},{1,3},{2,0},{3,1},{4,6},{5,7},{6,4},{7,5},{8,10},{9,11},{10,... | collective-permute-start | bytes 442376 | tf_op jit(solution)/shard_map/ppermute | solution.py:350
  42.3 10.2 %collective-permute-start.10 = (f32[72,512]{1,0:T(8,128)S(1)}, f32[72,512]{1,0:T(8,128)S(1)}, u32[]{:S(2)}, u32[]{:S(2)}) collective-permute-start(f32[72,512]{1,0:T(8,128)S(1)} %get-tuple-element.133), channel_id=1, source_target_pairs={{0,3},{1,2},{2,1},{3,0},{4,7},{5,6},{6,5},{7,4},{8,11},{9,10},{10,... | collective-permute-start | bytes 442376 | tf_op jit(solution)/shard_map/ppermute | solution.py:350
  52.6 6.1 %collective-permute-start.13 = (f32[72,512]{1,0:T(8,128)S(1)}, f32[72,512]{1,0:T(8,128)S(1)}, u32[]{:S(2)}, u32[]{:S(2)}) collective-permute-start(f32[72,512]{1,0:T(8,128)S(1)} %get-tuple-element.144), channel_id=1, source_target_pairs={{0,24},{4,28},{8,16},{12,20},{16,8},{20,12},{24,0},{28,4},{1,25},{... | collective-permute-start | bytes 442376 | tf_op jit(solution)/shard_map/ppermute | solution.py:350
  55.1 5.2 %collective-permute-start.14 = (f32[72,512]{1,0:T(8,128)S(1)}, f32[72,512]{1,0:T(8,128)S(1)}, u32[]{:S(2)}, u32[]{:S(2)}) collective-permute-start(f32[72,512]{1,0:T(8,128)S(1)} %get-tuple-element.143), channel_id=1, source_target_pairs={{0,8},{4,12},{8,0},{12,4},{16,24},{20,28},{24,16},{28,20},{1,9},{5... | collective-permute-start | bytes 442376 | tf_op jit(solution)/shard_map/ppermute | solution.py:350
  55.6 6.5 %copy-start = (s32[8]{0:T(128)S(1)}, s32[8]{0:T(128)}, u32[]{:S(2)}) copy-start(s32[8]{0:T(128)} %pair_one.3) | copy-start | bytes 100
  55.6 6.5 %copy-start.1 = (s32[8]{0:T(128)S(1)}, s32[8]{0:T(128)}, u32[]{:S(2)}) copy-start(s32[8]{0:T(128)} %pair_two.3) | copy-start | bytes 100
  55.6 5.1 %collective-permute-start.15 = (f32[72,512]{1,0:T(8,128)S(1)}, f32[72,512]{1,0:T(8,128)S(1)}, u32[]{:S(2)}, u32[]{:S(2)}) collective-permute-start(f32[72,512]{1,0:T(8,128)S(1)} %get-tuple-element.142), channel_id=1, source_target_pairs={{0,16},{4,20},{8,24},{12,28},{16,0},{20,4},{24,8},{28,12},{1,17},{... | collective-permute-start | bytes 442376 | tf_op jit(solution)/shard_map/ppermute | solution.py:350
  56.2 4.7 %collective-permute-start.16 = (f32[72,512]{1,0:T(8,128)S(1)}, f32[72,512]{1,0:T(8,128)S(1)}, u32[]{:S(2)}, u32[]{:S(2)}) collective-permute-start(f32[72,512]{1,0:T(8,128)S(1)} %get-tuple-element.145.refs_0_), channel_id=1, source_target_pairs={{0,4},{4,0},{8,12},{12,8},{16,20},{20,16},{24,28},{28,24},{1,5},{5... | collective-permute-start | bytes 442376 | tf_op jit(solution)/shard_map/ppermute | solution.py:350
  58.7 2.1 %collective-permute-start.17 = (f32[72,512]{1,0:T(8,128)S(1)}, f32[72,512]{1,0:T(8,128)S(1)}, u32[]{:S(2)}, u32[]{:S(2)}) collective-permute-start(f32[72,512]{1,0:T(8,128)S(1)} %collective-permute-done.13.refs_1_), channel_id=1, source_target_pairs={{0,4},{4,0},{8,12},{12,8},{16,20},{20,16},{24,28},{28,24},{1,5},{5... | collective-permute-start | bytes 442376 | tf_op jit(solution)/shard_map/ppermute | solution.py:350
  60.3 1.4 %collective-permute-start.18 = (f32[72,512]{1,0:T(8,128)S(1)}, f32[72,512]{1,0:T(8,128)S(1)}, u32[]{:S(2)}, u32[]{:S(2)}) collective-permute-start(f32[72,512]{1,0:T(8,128)S(1)} %collective-permute-done.14.refs_2_), channel_id=1, source_target_pairs={{0,4},{4,0},{8,12},{12,8},{16,20},{20,16},{24,28},{28,24},{1,5},{5... | collective-permute-start | bytes 442376 | tf_op jit(solution)/shard_map/ppermute | solution.py:350
  60.8 1.4 %collective-permute-start.19 = (f32[72,512]{1,0:T(8,128)S(1)}, f32[72,512]{1,0:T(8,128)S(1)}, u32[]{:S(2)}, u32[]{:S(2)}) collective-permute-start(f32[72,512]{1,0:T(8,128)S(1)} %collective-permute-done.15.refs_3_), channel_id=1, source_target_pairs={{0,4},{4,0},{8,12},{12,8},{16,20},{20,16},{24,28},{28,24},{1,5},{5... | collective-permute-start | bytes 442376 | tf_op jit(solution)/shard_map/ppermute | solution.py:350
  63.8 7.3 %collective-permute-start.20 = (f32[64,512]{1,0:T(8,128)S(1)}, f32[64,512]{1,0:T(8,128)S(1)}, u32[]{:S(2)}, u32[]{:S(2)}) collective-permute-start(f32[64,512]{1,0:T(8,128)S(1)} %get-tuple-element.137.refs_9_), channel_id=1, source_target_pairs={{0,24},{4,28},{8,16},{12,20},{16,8},{20,12},{24,0},{28,4},{1,25},{... | collective-permute-start | bytes 393224 | tf_op jit(solution)/shard_map/ppermute | solution.py:350
  65.8 6.9 %collective-permute-start.21 = (f32[64,512]{1,0:T(8,128)S(1)}, f32[64,512]{1,0:T(8,128)S(1)}, u32[]{:S(2)}, u32[]{:S(2)}) collective-permute-start(f32[64,512]{1,0:T(8,128)S(1)} %get-tuple-element.138.refs_10_), channel_id=1, source_target_pairs={{0,8},{4,12},{8,0},{12,4},{16,24},{20,28},{24,16},{28,20},{1,9},{5... | collective-permute-start | bytes 393224 | tf_op jit(solution)/shard_map/ppermute | solution.py:350
  66.4 1.0 %copy-start.2 = (s32[8]{0:T(128)S(1)}, s32[8]{0:T(128)}, u32[]{:S(2)}) copy-start(s32[8]{0:T(128)} %owner.1) | copy-start | bytes 100
  66.4 6.8 %collective-permute-start.22 = (f32[64,512]{1,0:T(8,128)S(1)}, f32[64,512]{1,0:T(8,128)S(1)}, u32[]{:S(2)}, u32[]{:S(2)}) collective-permute-start(f32[64,512]{1,0:T(8,128)S(1)} %get-tuple-element.139.refs_11_), channel_id=1, source_target_pairs={{0,16},{4,20},{8,24},{12,28},{16,0},{20,4},{24,8},{28,12},{1,17},{... | collective-permute-start | bytes 393224 | tf_op jit(solution)/shard_map/ppermute | solution.py:350

commit v9 on v8

--- a/solution.py
+++ b/solution.py
@@ -17,7 +17,7 @@
 wide = 256
 stretch = 1024
 rim = 2
-loads = 4
+loads = 7
 vmem_bytes = 48 * 1024 * 1024
 
 
@@ -66,37 +66,60 @@
         return [i for i, (a, b) in enumerate(self.blocks) if b > low and a < self.width - low]
 
 
-def piece_kernel(plan, maps, weight, *refs):
-    count = plan.row_devices
-    heads, tails = refs[:count], refs[count : 2 * count]
-    padded, weights, given, sems = refs[2 * count :]
-    rows_at, sims_at = lax.axis_index("rows"), lax.axis_index("sims")
-    chunk = plan.row_local // loads
+def spread_out(plan, padded, outs, first, rows):
+    for step, out in zip(plan.steps, outs):
+        column = pl.multiple_of((lax.axis_index("rows") ^ step) * plan.share, lane)
+        out[first : first + rows.size] = padded[rows, pl.ds(column, plan.width)]
+
+
+def clear_sides(plan, padded):
+    zeros = jnp.zeros((padded.shape[0], plan.halo), jnp.float32)
+    padded[:, : plan.halo] = zeros
+    padded[:, plan.halo + plan.columns :] = zeros
+
+
+def head_kernel(plan, maps, weight, *refs):
+    heads = refs[: plan.row_devices]
+    share, padded, given, sems = refs[plan.row_devices :]
+    row = pl.multiple_of(lax.rem(lax.axis_index("sims"), plan.sharers) * plan.share_rows, plan.share_rows)
     inner = slice(plan.halo, plan.halo + plan.columns)
+    copies = [
+        pltpu.make_async_copy(weight.at[pl.ds(row, plan.share_rows)], share.at[:, inner], sems.at[0]),
+        pltpu.make_async_copy(weight.at[: plan.head], padded.at[:, inner], sems.at[1]),
+        pltpu.make_async_copy(maps.at[: plan.head], given, sems.at[2]),
+    ]
+    for copy in copies:
+        copy.start()
+    clear_sides(plan, share)
+    clear_sides(plan, padded)
+    for copy in copies:
+        copy.wait()
+    padded[:, inner] = padded[:, inner] * given[...]
+    spread_out(plan, share, heads, 0, pl.ds(0, plan.share_rows))
+    spread_out(plan, padded, heads, plan.share_rows, pl.ds(0, plan.head))
+
+
+def tail_kernel(plan, maps, weight, *refs):
+    tails = refs[: plan.row_devices]
+    padded, given, sems = refs[plan.row_devices :]
+    inner = slice(plan.halo, plan.halo + plan.columns)
+    chunk = (plan.row_local - plan.head) // loads
     copies = []
     for number in range(loads):
-        rows = pl.ds(number * chunk, chunk)
+        rows, source = pl.ds(number * chunk, chunk), pl.ds(plan.head + number * chunk, chunk)
         copies.append((
-            pltpu.make_async_copy(weight.at[rows], weights.at[rows, inner], sems.at[0, number]),
-            pltpu.make_async_copy(maps.at[rows], given.at[rows], sems.at[1, number]),
+            pltpu.make_async_copy(weight.at[source], padded.at[rows, inner], sems.at[0, number]),
+            pltpu.make_async_copy(maps.at[source], given.at[rows], sems.at[1, number]),
         ))
         for copy in copies[-1]:
             copy.start()
-    zeros = jnp.zeros((plan.row_local, plan.halo), jnp.float32)
-    for target in (padded, weights):
-        target[:, : plan.halo] = zeros
-        target[:, plan.halo + plan.columns :] = zeros
+    clear_sides(plan, padded)
     for number in range(loads):
         for copy in copies[number]:
             copy.wait()
-        rows = slice(number * chunk, (number + 1) * chunk)
-        padded[rows, inner] = weights[rows, inner] * given[rows]
-    row = pl.multiple_of(lax.rem(sims_at, plan.sharers) * plan.share_rows, plan.share_rows)
-    for index, step in enumerate(plan.steps):
-        span = pl.ds(pl.multiple_of((rows_at ^ step) * plan.share, lane), plan.width)
-        heads[index][: plan.share_rows] = weights[pl.ds(row, plan.share_rows), span]
-        heads[index][plan.share_rows :] = padded[: plan.head, span]
-        tails[index][...] = padded[plan.head :, span]
+        rows = pl.ds(number * chunk, chunk)
+        padded[rows, inner] = padded[rows, inner] * given[rows]
+        spread_out(plan, padded, tails, number * chunk, rows)
 
 
 def band(plan, taps, rows, columns, offset):
@@ -469,19 +492,29 @@
         return jax.ShapeDtypeStruct(shape, jnp.bfloat16)
 
     cells = row_local * columns
-    made = call(
-        functools.partial(piece_kernel, plan),
-        [f32(plan.share_rows + plan.head, plan.width)] * row_devices
-        + [f32(row_local - plan.head, plan.width)] * row_devices,
+    inputs = pinned(maps.reshape(row_local, columns)), pinned(weight)
+    padded = columns + 2 * plan.halo
+    heads = call(
+        functools.partial(head_kernel, plan),
+        [f32(plan.share_rows + plan.head, plan.width)] * row_devices,
         [far, far],
-        [pltpu.VMEM((row_local, columns + 2 * plan.halo), jnp.float32)] * 2
-        + [pltpu.VMEM((row_local, columns), jnp.float32), pltpu.SemaphoreType.DMA((2, loads))],
+        [pltpu.VMEM((rows, padded), jnp.float32) for rows in (plan.share_rows, plan.head)]
+        + [pltpu.VMEM((plan.head, columns), jnp.float32), pltpu.SemaphoreType.DMA((3,))],
+        cells // 8,
+        2 * cells,
+    )(*inputs)
+    rest = row_local - plan.head
+    tails = call(
+        functools.partial(tail_kernel, plan),
+        [f32(rest, plan.width)] * row_devices,
+        [far, far],
+        [pltpu.VMEM((rest, padded), jnp.float32), pltpu.VMEM((rest, columns), jnp.float32)]
+        + [pltpu.SemaphoreType.DMA((2, loads))],
         cells,
         16 * cells,
-    )(pinned(maps.reshape(row_local, columns)), pinned(weight))
-    heads, tails = made[:row_devices], made[row_devices:]
+    )(*inputs)
     heads = exchange_all(plan, heads)
-    tails, heads = lax.optimization_barrier((tails, heads))
+    tails, heads[1], heads[2] = lax.optimization_barrier((tails, heads[1], heads[2]))
     tails = exchange_all(plan, tails)
     parts = lax.optimization_barrier(jnp.stack([head[: plan.share_rows] for head in heads])[None])
     shapes = [(plan.rows, plan.rows), (row_devices * plan.slab, plan.rows)]

time: 74.3 us -> 73.9 us (level)
  waiting for transfers between devices: 29.6 us -> 28.1 us
  Pallas kernels: 15.9 us -> 16.8 us
    ppermute x23, waiting for transfers between devices: 29.6 us -> 28.1 us  [exchange(): return lax.ppermute(value, axis, [(i, i ^ offset) for i in range(count)])]
    pallas_call x1 -> x2, Pallas kernels: 1.45 us -> 2.32 us  [the longest x1 1.33 us: body(): call(functools.partial(tail_kernel, plan), [f32(rest, plan.width)] * row_...]
  transfers between devices with their start and end apart: 23 -> 23, of which waited for: 15 -> 15; matrix products, arithmetic and copies ran while one was open for 1% -> 1% of each run, Pallas kernels for 9% -> 11%
where the time goes in v9:
time: 73.9 us; the launch traced here: 73.5 us
  waiting for transfers between devices  28.1 us (38%)
  starting transfers between devices  26.4 us (36%)
  Pallas kernels  16.8 us (23%)
  other arithmetic  1.03 us (1%)
  between operations  0.89 us (1%)
    ppermute x23, waiting for transfers between devices, exchange(): return lax.ppermute(value, axis, [(i, i ^ offset) for i in range(count)])  28.1 us
    ppermute x23, starting transfers between devices, exchange(): return lax.ppermute(value, axis, [(i, i ^ offset) for i in range(count)])  26.4 us
    pallas_call x1, Pallas kernels, run_filter(): call(functools.partial(filter_kernel, plan, sharers), [jax.ShapeDtypeStru...  5.64 us
    pallas_call x1, Pallas kernels, prepare(): call(functools.partial(table_kernel, plan), [b16(*shape) for shape in sha...  3.8 us
    pallas_call x1, Pallas kernels, run_estimates(): call(functools.partial(mean_kernel, plan, kept), [f32(OWNERS, plan.row_lo...  2.59 us
    pallas_call x1, Pallas kernels, run_estimates(): call(functools.partial(estimate_kernel, plan), [f32(plan.row_local, plan....  1.65 us
  transfers between devices with their start and end apart: 23, of which 15 were waited for; matrix products, arithmetic and copies ran while one was open for 1% of the time, Pallas kernels for 11%

profile of v9, /device:TPU:0, one launch (start us, length us, event | category | flops | bytes accessed | tf_op | source)
XLA Modules:
  0.0 73.5 jit_solution(14368272703667623109)
XLA Ops:
  0.6 1.0 %shard_map.78 = (f32[16,1024]{1,0:T(8,128)S(1)}, f32[16,1024]{1,0:T(8,128)S(1)}, f32[16,1024]{1,0:T(8,128)S(1)}, f32[16,1024]{1,0:T(8,128)S(1)}) custom-call(f32[64,2048]{1,0:T(8,128)} %bitcast.26, f32[64,2048]{1,0:T(8,128)} %weight.3), custom_call_target="tpu_custom_call" | custom-call | flops 16384 | bytes 262144 | tf_op jit(solution)/shard_map/pallas_call | solution.py:497
  1.6 5.1 %collective-permute-start.4 = (f32[16,1024]{1,0:T(8,128)S(1)}, f32[16,1024]{1,0:T(8,128)S(1)}, u32[]{:S(2)}, u32[]{:S(2)}) collective-permute-start(f32[16,1024]{1,0:T(8,128)S(1)} %get-tuple-element.96), channel_id=1, source_target_pairs={{0,3},{1,2},{2,1},{3,0},{4,7},{5,6},{6,5},{7,4},{8,11},{9,10},{10,... | collective-permute-start | bytes 196616 | tf_op jit(solution)/shard_map/ppermute | solution.py:373
  6.7 0.0 collective-permute-start.5
  6.7 0.6 collective-permute-start.6
  7.4 1.3 %shard_map.79 = (f32[56,1024]{1,0:T(8,128)S(1)}, f32[56,1024]{1,0:T(8,128)S(1)}, f32[56,1024]{1,0:T(8,128)S(1)}, f32[56,1024]{1,0:T(8,128)S(1)}) custom-call(f32[64,2048]{1,0:T(8,128)} %bitcast.27, f32[64,2048]{1,0:T(8,128)} %weight.3), custom_call_target="tpu_custom_call" | custom-call | flops 131072 | bytes 2097152 | tf_op jit(solution)/shard_map/pallas_call | solution.py:507
  8.7 0.6 collective-permute-done.4.refs_1_
  9.3 3.0 %collective-permute-done.5.refs_2_ = f32[16,1024]{1,0:T(8,128)S(1)} collective-permute-done((f32[16,1024]{1,0:T(8,128)S(1)}, f32[16,1024]{1,0:T(8,128)S(1)}, u32[]{:S(2)}, u32[]{:S(2)}) %collective-permute-start.5) | collective-permute-done | bytes 65568 | tf_op jit(solution)/shard_map/ppermute | solution.py:373
  12.3 2.7 %collective-permute-start.7 = (f32[56,1024]{1,0:T(8,128)S(1)}, f32[56,1024]{1,0:T(8,128)S(1)}, u32[]{:S(2)}, u32[]{:S(2)}) collective-permute-start(f32[56,1024]{1,0:T(8,128)S(1)} %get-tuple-element.102), channel_id=1, source_target_pairs={{0,3},{1,2},{2,1},{3,0},{4,7},{5,6},{6,5},{7,4},{8,11},{9,10},{10,... | collective-permute-start | bytes 688136 | tf_op jit(solution)/shard_map/ppermute | solution.py:373
  15.0 0.0 collective-permute-start.8
  15.0 1.7 %collective-permute-start.9 = (f32[56,1024]{1,0:T(8,128)S(1)}, f32[56,1024]{1,0:T(8,128)S(1)}, u32[]{:S(2)}, u32[]{:S(2)}) collective-permute-start(f32[56,1024]{1,0:T(8,128)S(1)} %get-tuple-element.104), channel_id=1, source_target_pairs={{0,1},{1,0},{2,3},{3,2},{4,5},{5,4},{6,7},{7,6},{8,9},{9,8},{10,11... | collective-permute-start | bytes 688136 | tf_op jit(solution)/shard_map/ppermute | solution.py:373
  16.7 0.0 collective-permute-done.6.refs_3_
  16.8 13.5 %conditional.1 = (f32[1,4,8,1024]{3,2,1,0:T(8,128)S(1)}, f32[1,4,8,1024]{3,2,1,0:T(8,128)S(1)}, f32[1,4,8,1024]{3,2,1,0:T(8,128)S(1)}, f32[1,4,8,1024]{3,2,1,0:T...) conditional(s32[]{:T(128)} %convert_element_type.3, () %tuple.19, ...), branch_computations={%region_0.0_spmd, %region_1.0_spmd} | conditional | flops 4295360512 | bytes 15466952 | solution.py:545
  16.8 1.6 %collective-permute-start = (f32[1,4,8,1024]{3,2,1,0:T(8,128)S(1)}, f32[1,4,8,1024]{3,2,1,0:T(8,128)S(1)}, u32[]{:S(2)}, u32[]{:S(2)}) collective-permute-start(f32[1,4,8,1024]{3,2,1,0:T(8,128)S(1)} %get-tuple-element.167), channel_id=1, source_target_pairs={{0,8},{4,12},{8,0},{12,4},{16,24},{20,28},{24,16},{28,20},{1,9},{5... | collective-permute-start | bytes 393224 | tf_op jit(solution)/shard_map/cond/branch_1_fun/ppermute | solution.py:373
  18.3 1.5 %collective-permute-start.1 = (f32[1,4,8,1024]{3,2,1,0:T(8,128)S(1)}, f32[1,4,8,1024]{3,2,1,0:T(8,128)S(1)}, u32[]{:S(2)}, u32[]{:S(2)}) collective-permute-start(f32[1,4,8,1024]{3,2,1,0:T(8,128)S(1)} %get-tuple-element.167), channel_id=1, source_target_pairs={{0,16},{4,20},{8,24},{12,28},{16,0},{20,4},{24,8},{28,12},{1,17},{... | collective-permute-start | bytes 393224 | tf_op jit(solution)/shard_map/cond/branch_1_fun/ppermute | solution.py:373
  19.8 2.0 %collective-permute-done = f32[1,4,8,1024]{3,2,1,0:T(8,128)S(1)} collective-permute-done((f32[1,4,8,1024]{3,2,1,0:T(8,128)S(1)}, f32[1,4,8,1024]{3,2,1,0:T(8,128)S(1)}, u32[]{:S(2)}, u32[]{:S(2)}) %collective-permute-start) | collective-permute-done | bytes 131104 | tf_op jit(solution)/shard_map/cond/branch_1_fun/ppermute | solution.py:373
  21.8 1.5 %collective-permute-start.2 = (f32[1,4,8,1024]{3,2,1,0:T(8,128)S(1)}, f32[1,4,8,1024]{3,2,1,0:T(8,128)}, u32[]{:S(2)}, u32[]{:S(2)}) collective-permute-start(f32[1,4,8,1024]{3,2,1,0:T(8,128)S(1)} %collective-permute-done), channel_id=1, source_target_pairs={{0,16},{4,20},{8,24},{12,28},{16,0},{20,4},{24,8},{28,12},{1,17},{... | collective-permute-start | bytes 393224 | tf_op jit(solution)/shard_map/cond/branch_1_fun/ppermute | solution.py:373
  23.3 3.8 %branch_1_fun.1 = (bf16[256,256]{1,0:T(8,128)(2,1)S(1)}, bf16[256,256]{1,0:T(8,128)(2,1)S(1)}, bf16[288,256]{1,0:T(8,128)(2,1)S(1)}, bf16[288,256]{1,0:T(8,128)(...) custom-call(f32[1,65]{1,0:T(1,128)} %bitcast.32), custom_call_target="tpu_custom_call" | custom-call | flops 4294967296 | bytes 8388608 | tf_op jit(solution)/shard_map/cond/branch_1_fun/pallas_call | solution.py:528
  27.1 0.0 collective-permute-done.1
  27.1 0.0 copy-start.5
  27.1 0.0 collective-permute-done.2
  27.2 0.0 copy-done.3
  27.2 1.0 %pad_maximum_fusion = f32[4,4,8,1024]{3,2,1,0:T(8,128)S(1)} fusion(f32[1,4,8,1024]{3,2,1,0:T(8,128)} %collective-permute-done.2, f32[1,4,8,1024]{3,2,1,0:T(8,128)S(1)} %collective-permute-done.1, f32[1,4,8,1024]{3,2,1,0:T(8,128)S(1)} %collective-permute-done, f32[1,4,8,1024]{3,2,1,0:T(8,128)S(1)} %get-tuple-element.167), kind=kLoop, calls=%fused_computation | loop fusion | flops 393216 | bytes 1048576 | tf_op jit(solution)/shard_map/cond/branch_1_fun/concatenate | solution.py:540
  28.1 0.0 copy-done.5
  28.2 0.0 copy-start.4
  28.2 0.0 copy-start.6
  28.2 0.1 collective-permute-start.3
  28.3 2.0 %collective-permute-done.3 = f32[4,4,8,1024]{3,2,1,0:T(8,128)} collective-permute-done((f32[4,4,8,1024]{3,2,1,0:T(8,128)S(1)}, f32[4,4,8,1024]{3,2,1,0:T(8,128)}, u32[]{:S(2)}, u32[]{:S(2)}) %collective-permute-start.3) | collective-permute-done | bytes 524320 | tf_op jit(solution)/shard_map/cond/branch_1_fun/ppermute | solution.py:373
  30.3 0.0 copy-done.4
  30.3 0.0 copy-done.6
  30.3 0.0 collective-permute-done.7.refs_5_
  30.3 2.2 %collective-permute-done.8.refs_6_ = f32[56,1024]{1,0:T(8,128)S(1)} collective-permute-done((f32[56,1024]{1,0:T(8,128)S(1)}, f32[56,1024]{1,0:T(8,128)S(1)}, u32[]{:S(2)}, u32[]{:S(2)}) %collective-permute-start.8) | collective-permute-done | bytes 229408 | tf_op jit(solution)/shard_map/ppermute | solution.py:373
  32.5 0.0 collective-permute-done.9.refs_7_
  32.5 5.6 %shard_map.80 = (f32[72,512]{1,0:T(8,128)S(1)}, f32[72,512]{1,0:T(8,128)S(1)}, f32[72,512]{1,0:T(8,128)S(1)}, f32[72,512]{1,0:T(8,128)S(1)}) custom-call(f32[16,1024]{1,0:T(8,128)S(1)} %get-tuple-element.91.refs_0_, f32[16,1024]{1,0:T(8,128)S(1)} %collective-permute-done.4.refs_1_, f32[16,1024]{1,0:T(8,128)S(1)} %collective-permute-done.5.refs_2_, ...), custom_call_target="tpu_custom_call" | custom-call | flops 8589934592 | bytes 8388608 | tf_op jit(solution)/shard_map/pallas_call | solution.py:397
  38.1 0.1 collective-permute-start.12
  38.2 3.3 %collective-permute-start.11 = (f32[72,512]{1,0:T(8,128)S(1)}, f32[72,512]{1,0:T(8,128)S(1)}, u32[]{:S(2)}, u32[]{:S(2)}) collective-permute-start(f32[72,512]{1,0:T(8,128)S(1)} %get-tuple-element.130), channel_id=1, source_target_pairs={{0,2},{1,3},{2,0},{3,1},{4,6},{5,7},{6,4},{7,5},{8,10},{9,11},{10,... | collective-permute-start | bytes 442376 | tf_op jit(solution)/shard_map/ppermute | solution.py:373
  41.5 1.0 %collective-permute-start.10 = (f32[72,512]{1,0:T(8,128)S(1)}, f32[72,512]{1,0:T(8,128)S(1)}, u32[]{:S(2)}, u32[]{:S(2)}) collective-permute-start(f32[72,512]{1,0:T(8,128)S(1)} %get-tuple-element.129), channel_id=1, source_target_pairs={{0,3},{1,2},{2,1},{3,0},{4,7},{5,6},{6,5},{7,4},{8,11},{9,10},{10,... | collective-permute-start | bytes 442376 | tf_op jit(solution)/shard_map/ppermute | solution.py:373
  42.6 3.3 %collective-permute-done.12 = f32[72,512]{1,0:T(8,128)S(1)} collective-permute-done((f32[72,512]{1,0:T(8,128)S(1)}, f32[72,512]{1,0:T(8,128)S(1)}, u32[]{:S(2)}, u32[]{:S(2)}) %collective-permute-start.12) | collective-permute-done | bytes 147488 | tf_op jit(solution)/shard_map/ppermute | solution.py:373
  45.8 5.8 %collective-permute-done.11 = f32[72,512]{1,0:T(8,128)S(1)} collective-permute-done((f32[72,512]{1,0:T(8,128)S(1)}, f32[72,512]{1,0:T(8,128)S(1)}, u32[]{:S(2)}, u32[]{:S(2)}) %collective-permute-start.11) | collective-permute-done | bytes 147488 | tf_op jit(solution)/shard_map/ppermute | solution.py:373
  51.6 0.0 collective-permute-done.10
  51.7 0.1 dynamic-slice_bitcast_fusion
  51.7 2.7 %collective-permute-start.13 = (f32[72,512]{1,0:T(8,128)S(1)}, f32[72,512]{1,0:T(8,128)S(1)}, u32[]{:S(2)}, u32[]{:S(2)}) collective-permute-start(f32[72,512]{1,0:T(8,128)S(1)} %get-tuple-element.140), channel_id=1, source_target_pairs={{0,24},{4,28},{8,16},{12,20},{16,8},{20,12},{24,0},{28,4},{1,25},{... | collective-permute-start | bytes 442376 | tf_op jit(solution)/shard_map/ppermute | solution.py:373
  54.5 0.5 collective-permute-start.14
  55.0 0.3 collective-permute-start.15
  55.3 0.0 collective-permute-start.16
  55.3 2.5 %collective-permute-done.13.refs_1_ = f32[72,512]{1,0:T(8,128)S(1)} collective-permute-done((f32[72,512]{1,0:T(8,128)S(1)}, f32[72,512]{1,0:T(8,128)S(1)}, u32[]{:S(2)}, u32[]{:S(2)}) %collective-permute-start.13) | collective-permute-done | bytes 147488 | tf_op jit(solution)/shard_map/ppermute | solution.py:373
  57.9 0.0 collective-permute-start.17
  57.9 1.8 %collective-permute-done.14.refs_2_ = f32[72,512]{1,0:T(8,128)S(1)} collective-permute-done((f32[72,512]{1,0:T(8,128)S(1)}, f32[72,512]{1,0:T(8,128)S(1)}, u32[]{:S(2)}, u32[]{:S(2)}) %collective-permute-start.14) | collective-permute-done | bytes 147488 | tf_op jit(solution)/shard_map/ppermute | solution.py:373
  59.7 0.0 collective-permute-start.18
  59.7 0.4 collective-permute-done.15.refs_3_
  60.1 0.1 collective-permute-start.19
  60.2 0.0 collective-permute-done.16.refs_4_
  60.2 0.0 collective-permute-done.17.refs_5_
  60.2 0.9 %collective-permute-done.18.refs_6_ = f32[72,512]{1,0:T(8,128)S(1)} collective-permute-done((f32[72,512]{1,0:T(8,128)S(1)}, f32[72,512]{1,0:T(8,128)S(1)}, u32[]{:S(2)}, u32[]{:S(2)}) %collective-permute-start.18) | collective-permute-done | bytes 147488 | tf_op jit(solution)/shard_map/ppermute | solution.py:373
  61.1 0.5 collective-permute-done.19.refs_7_
  61.5 0.0 copy-done
  61.5 1.6 %shard_map.81 = (f32[64,512]{1,0:T(8,128)S(1)}, f32[64,512]{1,0:T(8,128)S(1)}, f32[64,512]{1,0:T(8,128)S(1)}, f32[64,512]{1,0:T(8,128)S(1)}) custom-call(s32[8]{0:T(128)S(1)} %copy-done, s32[8]{0:T(128)S(1)} %copy-done.1, f32[72,512]{1,0:T(8,128)S(1)} %get-tuple-element.141.refs_0_, f32[72,512]{1,0:T(8,128)S(1)} %collective-permute-done.13.refs_1_, ...), custom_call_target="tpu_custom_call" | custom-call | flops 16777216 | bytes 8388608 | tf_op jit(solution)/shard_map/pallas_call | solution.py:442
  63.2 2.0 %collective-permute-start.20 = (f32[64,512]{1,0:T(8,128)S(1)}, f32[64,512]{1,0:T(8,128)S(1)}, u32[]{:S(2)}, u32[]{:S(2)}) collective-permute-start(f32[64,512]{1,0:T(8,128)S(1)} %get-tuple-element.133.refs_9_), channel_id=1, source_target_pairs={{0,24},{4,28},{8,16},{12,20},{16,8},{20,12},{24,0},{28,4},{1,25},{... | collective-permute-start | bytes 393224 | tf_op jit(solution)/shard_map/ppermute | solution.py:373
  65.2 0.5 collective-permute-start.21
  65.7 1.0 %collective-permute-start.22 = (f32[64,512]{1,0:T(8,128)S(1)}, f32[64,512]{1,0:T(8,128)S(1)}, u32[]{:S(2)}, u32[]{:S(2)}) collective-permute-start(f32[64,512]{1,0:T(8,128)S(1)} %get-tuple-element.135.refs_11_), channel_id=1, source_target_pairs={{0,16},{4,20},{8,24},{12,28},{16,0},{20,4},{24,8},{28,12},{1,17},{... | collective-permute-start | bytes 393224 | tf_op jit(solution)/shard_map/ppermute | solution.py:373
  66.7 2.6 %shard_map.83 = f32[8,64,256]{2,1,0:T(8,128)} custom-call(s32[8]{0:T(128)S(1)} %copy-done, s32[8]{0:T(128)S(1)} %copy-done.1, s32[8]{0:T(128)S(1)} %copy-done.2, f32[72,512]{1,0:T(8,128)S(1)} %get-tuple-element.141.refs_0_, f32[72,512]{1,0:T(8,128)S(1)} %collective-permute-done.13.refs_1_, f32[72,512]{1,0:T(8,128)S(1)} %collective-permute-done.14.refs_2_, ...), custom_call_target="tpu_custom_call" | custom-call | flops 16777216 | bytes 8388608 | tf_op jit(solution)/shard_map/pallas_call | solution.py:452
  69.3 1.2 %collective-permute-done.20.refs_1_ = f32[64,512]{1,0:T(8,128)S(1)} collective-permute-done((f32[64,512]{1,0:T(8,128)S(1)}, f32[64,512]{1,0:T(8,128)S(1)}, u32[]{:S(2)}, u32[]{:S(2)}) %collective-permute-start.20) | collective-permute-done | bytes 131104 | tf_op jit(solution)/shard_map/ppermute | solution.py:373
  70.5 1.6 %collective-permute-done.21.refs_2_ = f32[64,512]{1,0:T(8,128)S(1)} collective-permute-done((f32[64,512]{1,0:T(8,128)S(1)}, f32[64,512]{1,0:T(8,128)S(1)}, u32[]{:S(2)}, u32[]{:S(2)}) %collective-permute-start.21) | collective-permute-done | bytes 131104 | tf_op jit(solution)/shard_map/ppermute | solution.py:373
  72.0 0.5 collective-permute-done.22.refs_3_
  72.5 0.8 %shard_map.82 = f32[64,2048]{1,0:T(8,128)} custom-call(f32[64,512]{1,0:T(8,128)S(1)} %get-tuple-element.132.refs_0_.refs_8_, f32[64,512]{1,0:T(8,128)S(1)} %collective-permute-done.20.refs_1_, f32[64,512]{1,0:T(8,128)S(1)} %collective-permute-done.21.refs_2_, f32[64,512]{1,0:T(8,128)S(1)} %collective-permute-done.22.refs_3_), custom_call_target="tpu_custom_call" | custom-call | bytes 1048576 | tf_op jit(solution)/shard_map/pallas_call | solution.py:464
  (12 shorter events, 0.1 us)
Async XLA Ops:
  1.6 7.7 %collective-permute-start.4 = (f32[16,1024]{1,0:T(8,128)S(1)}, f32[16,1024]{1,0:T(8,128)S(1)}, u32[]{:S(2)}, u32[]{:S(2)}) collective-permute-start(f32[16,1024]{1,0:T(8,128)S(1)} %get-tuple-element.96), channel_id=1, source_target_pairs={{0,3},{1,2},{2,1},{3,0},{4,7},{5,6},{6,5},{7,4},{8,11},{9,10},{10,... | collective-permute-start | bytes 196616 | tf_op jit(solution)/shard_map/ppermute | solution.py:373
  6.7 5.6 %collective-permute-start.5 = (f32[16,1024]{1,0:T(8,128)S(1)}, f32[16,1024]{1,0:T(8,128)S(1)}, u32[]{:S(2)}, u32[]{:S(2)}) collective-permute-start(f32[16,1024]{1,0:T(8,128)S(1)} %get-tuple-element.97), channel_id=1, source_target_pairs={{0,2},{1,3},{2,0},{3,1},{4,6},{5,7},{6,4},{7,5},{8,10},{9,11},{10,... | collective-permute-start | bytes 196616 | tf_op jit(solution)/shard_map/ppermute | solution.py:373
  6.7 10.0 %collective-permute-start.6 = (f32[16,1024]{1,0:T(8,128)S(1)}, f32[16,1024]{1,0:T(8,128)S(1)}, u32[]{:S(2)}, u32[]{:S(2)}) collective-permute-start(f32[16,1024]{1,0:T(8,128)S(1)} %get-tuple-element.100), channel_id=1, source_target_pairs={{0,1},{1,0},{2,3},{3,2},{4,5},{5,4},{6,7},{7,6},{8,9},{9,8},{10,11... | collective-permute-start | bytes 196616 | tf_op jit(solution)/shard_map/ppermute | solution.py:373
  12.3 18.0 %collective-permute-start.7 = (f32[56,1024]{1,0:T(8,128)S(1)}, f32[56,1024]{1,0:T(8,128)S(1)}, u32[]{:S(2)}, u32[]{:S(2)}) collective-permute-start(f32[56,1024]{1,0:T(8,128)S(1)} %get-tuple-element.102), channel_id=1, source_target_pairs={{0,3},{1,2},{2,1},{3,0},{4,7},{5,6},{6,5},{7,4},{8,11},{9,10},{10,... | collective-permute-start | bytes 688136 | tf_op jit(solution)/shard_map/ppermute | solution.py:373
  15.0 17.4 %collective-permute-start.8 = (f32[56,1024]{1,0:T(8,128)S(1)}, f32[56,1024]{1,0:T(8,128)S(1)}, u32[]{:S(2)}, u32[]{:S(2)}) collective-permute-start(f32[56,1024]{1,0:T(8,128)S(1)} %get-tuple-element.103), channel_id=1, source_target_pairs={{0,2},{1,3},{2,0},{3,1},{4,6},{5,7},{6,4},{7,5},{8,10},{9,11},{10,... | collective-permute-start | bytes 688136 | tf_op jit(solution)/shard_map/ppermute | solution.py:373
  15.0 17.4 %collective-permute-start.9 = (f32[56,1024]{1,0:T(8,128)S(1)}, f32[56,1024]{1,0:T(8,128)S(1)}, u32[]{:S(2)}, u32[]{:S(2)}) collective-permute-start(f32[56,1024]{1,0:T(8,128)S(1)} %get-tuple-element.104), channel_id=1, source_target_pairs={{0,1},{1,0},{2,3},{3,2},{4,5},{5,4},{6,7},{7,6},{8,9},{9,8},{10,11... | collective-permute-start | bytes 688136 | tf_op jit(solution)/shard_map/ppermute | solution.py:373
  16.8 5.0 %collective-permute-start = (f32[1,4,8,1024]{3,2,1,0:T(8,128)S(1)}, f32[1,4,8,1024]{3,2,1,0:T(8,128)S(1)}, u32[]{:S(2)}, u32[]{:S(2)}) collective-permute-start(f32[1,4,8,1024]{3,2,1,0:T(8,128)S(1)} %get-tuple-element.167), channel_id=1, source_target_pairs={{0,8},{4,12},{8,0},{12,4},{16,24},{20,28},{24,16},{28,20},{1,9},{5... | collective-permute-start | bytes 393224 | tf_op jit(solution)/shard_map/cond/branch_1_fun/ppermute | solution.py:373
  18.3 8.8 %collective-permute-start.1 = (f32[1,4,8,1024]{3,2,1,0:T(8,128)S(1)}, f32[1,4,8,1024]{3,2,1,0:T(8,128)S(1)}, u32[]{:S(2)}, u32[]{:S(2)}) collective-permute-start(f32[1,4,8,1024]{3,2,1,0:T(8,128)S(1)} %get-tuple-element.167), channel_id=1, source_target_pairs={{0,16},{4,20},{8,24},{12,28},{16,0},{20,4},{24,8},{28,12},{1,17},{... | collective-permute-start | bytes 393224 | tf_op jit(solution)/shard_map/cond/branch_1_fun/ppermute | solution.py:373
  21.8 5.4 %copy-start.3 = (f32[1,4,8,1024]{3,2,1,0:T(8,128)}, f32[1,4,8,1024]{3,2,1,0:T(8,128)S(1)}, u32[]{:S(2)}) copy-start(f32[1,4,8,1024]{3,2,1,0:T(8,128)S(1)} %collective-permute-done) | copy-start | bytes 393220 | tf_op jit(solution)/shard_map/cond
  21.8 5.3 %collective-permute-start.2 = (f32[1,4,8,1024]{3,2,1,0:T(8,128)S(1)}, f32[1,4,8,1024]{3,2,1,0:T(8,128)}, u32[]{:S(2)}, u32[]{:S(2)}) collective-permute-start(f32[1,4,8,1024]{3,2,1,0:T(8,128)S(1)} %collective-permute-done), channel_id=1, source_target_pairs={{0,16},{4,20},{8,24},{12,28},{16,0},{20,4},{24,8},{28,12},{1,17},{... | collective-permute-start | bytes 393224 | tf_op jit(solution)/shard_map/cond/branch_1_fun/ppermute | solution.py:373
  27.1 1.0 %copy-start.5 = (f32[1,4,8,1024]{3,2,1,0:T(8,128)}, f32[1,4,8,1024]{3,2,1,0:T(8,128)S(1)}, u32[]{:S(2)}) copy-start(f32[1,4,8,1024]{3,2,1,0:T(8,128)S(1)} %collective-permute-done.1) | copy-start | bytes 393220 | tf_op jit(solution)/shard_map/cond
  28.2 2.1 %copy-start.4 = (f32[1,4,8,1024]{3,2,1,0:T(8,128)S(1)}, f32[1,4,8,1024]{3,2,1,0:T(8,128)}, u32[]{:S(2)}) copy-start(f32[1,4,8,1024]{3,2,1,0:T(8,128)} %copy-done.3) | copy-start | bytes 393220 | tf_op jit(solution)/shard_map/cond
  28.2 2.1 %copy-start.6 = (f32[1,4,8,1024]{3,2,1,0:T(8,128)S(1)}, f32[1,4,8,1024]{3,2,1,0:T(8,128)}, u32[]{:S(2)}) copy-start(f32[1,4,8,1024]{3,2,1,0:T(8,128)} %copy-done.5) | copy-start | bytes 393220 | tf_op jit(solution)/shard_map/cond
  28.2 2.1 %collective-permute-start.3 = (f32[4,4,8,1024]{3,2,1,0:T(8,128)S(1)}, f32[4,4,8,1024]{3,2,1,0:T(8,128)}, u32[]{:S(2)}, u32[]{:S(2)}) collective-permute-start(f32[4,4,8,1024]{3,2,1,0:T(8,128)S(1)} %pad_maximum_fusion), channel_id=1, source_target_pairs={{0,4},{4,0},{8,12},{12,8},{16,20},{20,16},{24,28},{28,24},{1,5},{5... | collective-permute-start | bytes 1572872 | tf_op jit(solution)/shard_map/cond/branch_1_fun/ppermute | solution.py:373
  38.1 7.7 %collective-permute-start.12 = (f32[72,512]{1,0:T(8,128)S(1)}, f32[72,512]{1,0:T(8,128)S(1)}, u32[]{:S(2)}, u32[]{:S(2)}) collective-permute-start(f32[72,512]{1,0:T(8,128)S(1)} %get-tuple-element.131), channel_id=1, source_target_pairs={{0,1},{1,0},{2,3},{3,2},{4,5},{5,4},{6,7},{7,6},{8,9},{9,8},{10,11... | collective-permute-start | bytes 442376 | tf_op jit(solution)/shard_map/ppermute | solution.py:373
  38.2 13.4 %collective-permute-start.11 = (f32[72,512]{1,0:T(8,128)S(1)}, f32[72,512]{1,0:T(8,128)S(1)}, u32[]{:S(2)}, u32[]{:S(2)}) collective-permute-start(f32[72,512]{1,0:T(8,128)S(1)} %get-tuple-element.130), channel_id=1, source_target_pairs={{0,2},{1,3},{2,0},{3,1},{4,6},{5,7},{6,4},{7,5},{8,10},{9,11},{10,... | collective-permute-start | bytes 442376 | tf_op jit(solution)/shard_map/ppermute | solution.py:373
  41.5 10.1 %collective-permute-start.10 = (f32[72,512]{1,0:T(8,128)S(1)}, f32[72,512]{1,0:T(8,128)S(1)}, u32[]{:S(2)}, u32[]{:S(2)}) collective-permute-start(f32[72,512]{1,0:T(8,128)S(1)} %get-tuple-element.129), channel_id=1, source_target_pairs={{0,3},{1,2},{2,1},{3,0},{4,7},{5,6},{6,5},{7,4},{8,11},{9,10},{10,... | collective-permute-start | bytes 442376 | tf_op jit(solution)/shard_map/ppermute | solution.py:373
  51.7 6.1 %collective-permute-start.13 = (f32[72,512]{1,0:T(8,128)S(1)}, f32[72,512]{1,0:T(8,128)S(1)}, u32[]{:S(2)}, u32[]{:S(2)}) collective-permute-start(f32[72,512]{1,0:T(8,128)S(1)} %get-tuple-element.140), channel_id=1, source_target_pairs={{0,24},{4,28},{8,16},{12,20},{16,8},{20,12},{24,0},{28,4},{1,25},{... | collective-permute-start | bytes 442376 | tf_op jit(solution)/shard_map/ppermute | solution.py:373
  54.5 5.2 %collective-permute-start.14 = (f32[72,512]{1,0:T(8,128)S(1)}, f32[72,512]{1,0:T(8,128)S(1)}, u32[]{:S(2)}, u32[]{:S(2)}) collective-permute-start(f32[72,512]{1,0:T(8,128)S(1)} %get-tuple-element.139), channel_id=1, source_target_pairs={{0,8},{4,12},{8,0},{12,4},{16,24},{20,28},{24,16},{28,20},{1,9},{5... | collective-permute-start | bytes 442376 | tf_op jit(solution)/shard_map/ppermute | solution.py:373
  55.0 6.5 %copy-start = (s32[8]{0:T(128)S(1)}, s32[8]{0:T(128)}, u32[]{:S(2)}) copy-start(s32[8]{0:T(128)} %pair_one.3) | copy-start | bytes 100
  55.0 6.5 %copy-start.1 = (s32[8]{0:T(128)S(1)}, s32[8]{0:T(128)}, u32[]{:S(2)}) copy-start(s32[8]{0:T(128)} %pair_two.3) | copy-start | bytes 100
  55.0 5.1 %collective-permute-start.15 = (f32[72,512]{1,0:T(8,128)S(1)}, f32[72,512]{1,0:T(8,128)S(1)}, u32[]{:S(2)}, u32[]{:S(2)}) collective-permute-start(f32[72,512]{1,0:T(8,128)S(1)} %get-tuple-element.138), channel_id=1, source_target_pairs={{0,16},{4,20},{8,24},{12,28},{16,0},{20,4},{24,8},{28,12},{1,17},{... | collective-permute-start | bytes 442376 | tf_op jit(solution)/shard_map/ppermute | solution.py:373
  55.3 4.9 %collective-permute-start.16 = (f32[72,512]{1,0:T(8,128)S(1)}, f32[72,512]{1,0:T(8,128)S(1)}, u32[]{:S(2)}, u32[]{:S(2)}) collective-permute-start(f32[72,512]{1,0:T(8,128)S(1)} %get-tuple-element.141.refs_0_), channel_id=1, source_target_pairs={{0,4},{4,0},{8,12},{12,8},{16,20},{20,16},{24,28},{28,24},{1,5},{5... | collective-permute-start | bytes 442376 | tf_op jit(solution)/shard_map/ppermute | solution.py:373
  57.9 2.4 %collective-permute-start.17 = (f32[72,512]{1,0:T(8,128)S(1)}, f32[72,512]{1,0:T(8,128)S(1)}, u32[]{:S(2)}, u32[]{:S(2)}) collective-permute-start(f32[72,512]{1,0:T(8,128)S(1)} %collective-permute-done.13.refs_1_), channel_id=1, source_target_pairs={{0,4},{4,0},{8,12},{12,8},{16,20},{20,16},{24,28},{28,24},{1,5},{5... | collective-permute-start | bytes 442376 | tf_op jit(solution)/shard_map/ppermute | solution.py:373
  59.7 1.4 %collective-permute-start.18 = (f32[72,512]{1,0:T(8,128)S(1)}, f32[72,512]{1,0:T(8,128)S(1)}, u32[]{:S(2)}, u32[]{:S(2)}) collective-permute-start(f32[72,512]{1,0:T(8,128)S(1)} %collective-permute-done.14.refs_2_), channel_id=1, source_target_pairs={{0,4},{4,0},{8,12},{12,8},{16,20},{20,16},{24,28},{28,24},{1,5},{5... | collective-permute-start | bytes 442376 | tf_op jit(solution)/shard_map/ppermute | solution.py:373
  60.1 1.4 %collective-permute-start.19 = (f32[72,512]{1,0:T(8,128)S(1)}, f32[72,512]{1,0:T(8,128)S(1)}, u32[]{:S(2)}, u32[]{:S(2)}) collective-permute-start(f32[72,512]{1,0:T(8,128)S(1)} %collective-permute-done.15.refs_3_), channel_id=1, source_target_pairs={{0,4},{4,0},{8,12},{12,8},{16,20},{20,16},{24,28},{28,24},{1,5},{5... | collective-permute-start | bytes 442376 | tf_op jit(solution)/shard_map/ppermute | solution.py:373
  63.2 7.3 %collective-permute-start.20 = (f32[64,512]{1,0:T(8,128)S(1)}, f32[64,512]{1,0:T(8,128)S(1)}, u32[]{:S(2)}, u32[]{:S(2)}) collective-permute-start(f32[64,512]{1,0:T(8,128)S(1)} %get-tuple-element.133.refs_9_), channel_id=1, source_target_pairs={{0,24},{4,28},{8,16},{12,20},{16,8},{20,12},{24,0},{28,4},{1,25},{... | collective-permute-start | bytes 393224 | tf_op jit(solution)/shard_map/ppermute | solution.py:373
  65.2 6.9 %collective-permute-start.21 = (f32[64,512]{1,0:T(8,128)S(1)}, f32[64,512]{1,0:T(8,128)S(1)}, u32[]{:S(2)}, u32[]{:S(2)}) collective-permute-start(f32[64,512]{1,0:T(8,128)S(1)} %get-tuple-element.134.refs_10_), channel_id=1, source_target_pairs={{0,8},{4,12},{8,0},{12,4},{16,24},{20,28},{24,16},{28,20},{1,9},{5... | collective-permute-start | bytes 393224 | tf_op jit(solution)/shard_map/ppermute | solution.py:373
  65.7 1.0 %copy-start.2 = (s32[8]{0:T(128)S(1)}, s32[8]{0:T(128)}, u32[]{:S(2)}) copy-start(s32[8]{0:T(128)} %owner.1) | copy-start | bytes 100
  65.7 6.8 %collective-permute-start.22 = (f32[64,512]{1,0:T(8,128)S(1)}, f32[64,512]{1,0:T(8,128)S(1)}, u32[]{:S(2)}, u32[]{:S(2)}) collective-permute-start(f32[64,512]{1,0:T(8,128)S(1)} %get-tuple-element.135.refs_11_), channel_id=1, source_target_pairs={{0,16},{4,20},{8,24},{12,28},{16,0},{20,4},{24,8},{28,12},{1,17},{... | collective-permute-start | bytes 393224 | tf_op jit(solution)/shard_map/ppermute | solution.py:373

commit v10 on v9

--- a/solution.py
+++ b/solution.py
@@ -251,7 +251,8 @@
     for iteration in range(ITERS):
         chosen = plan.stage_blocks(iteration)
         windows = [plan.window(plan.blocks[i]) for i in chosen]
-        rows_pass(square, windows[0][0], windows[-1][1], iteration == 0)
+        trim = lane if iteration == ITERS - 1 and plan.halo - rim - 3 * plan.margin >= lane else 0
+        rows_pass(square, max(windows[0][0], trim), min(windows[-1][1], plan.width - trim), iteration == 0)
         if iteration == 0:
             for i, window in zip(chosen, windows):
                 base[:, slice(*plan.blocks[i])] = columns_pass(bands[i], plan.rows, window)
@@ -265,8 +266,10 @@
             a, b = plan.blocks[i]
             value = base[:, a:b]
             if iteration > 0:
-                value = keep * image[:, a:b] + value - columns_pass(bands[i], plan.rows, window, False)
-            image[:, a:b] = value
+                before = image if iteration > 1 else base
+                value = keep * before[:, a:b] + value - columns_pass(bands[i], plan.rows, window, False)
+            if 0 < iteration < ITERS - 1:
+                image[:, a:b] = value
             product = weight[:, a:b] * value
             given = seen[:, a:b]
             total[:, a:b] = given - product + keep * (total[:, a:b] if iteration > 0 else given)

time: 73.9 us -> 73.7 us (level)
  no operation moved by 1% of the time
where the time goes in v10:
time: 73.7 us; the launch traced here: 73.3 us
  waiting for transfers between devices  28.1 us (38%)
  starting transfers between devices  26.4 us (36%)
  Pallas kernels  16.6 us (23%)
  other arithmetic  1.03 us (1%)
  between operations  0.89 us (1%)
    ppermute x23, waiting for transfers between devices, exchange(): return lax.ppermute(value, axis, [(i, i ^ offset) for i in range(count)])  28.1 us
    ppermute x23, starting transfers between devices, exchange(): return lax.ppermute(value, axis, [(i, i ^ offset) for i in range(count)])  26.4 us
    pallas_call x1, Pallas kernels, run_filter(): call(functools.partial(filter_kernel, plan, sharers), [jax.ShapeDtypeStru...  5.45 us
    pallas_call x1, Pallas kernels, prepare(): call(functools.partial(table_kernel, plan), [b16(*shape) for shape in sha...  3.8 us
    pallas_call x1, Pallas kernels, run_estimates(): call(functools.partial(mean_kernel, plan, kept), [f32(OWNERS, plan.row_lo...  2.59 us
    pallas_call x1, Pallas kernels, run_estimates(): call(functools.partial(estimate_kernel, plan), [f32(plan.row_local, plan....  1.64 us
  transfers between devices with their start and end apart: 23, of which 15 were waited for; matrix products, arithmetic and copies ran while one was open for 1% of the time, Pallas kernels for 11%

profile of v10, /device:TPU:0, one launch (start us, length us, event | category | flops | bytes accessed | tf_op | source)
XLA Modules:
  0.0 73.3 jit_solution(15132984276806053965)
XLA Ops:
  0.6 1.0 %shard_map.78 = (f32[16,1024]{1,0:T(8,128)S(1)}, f32[16,1024]{1,0:T(8,128)S(1)}, f32[16,1024]{1,0:T(8,128)S(1)}, f32[16,1024]{1,0:T(8,128)S(1)}) custom-call(f32[64,2048]{1,0:T(8,128)} %bitcast.26, f32[64,2048]{1,0:T(8,128)} %weight.3), custom_call_target="tpu_custom_call" | custom-call | flops 16384 | bytes 262144 | tf_op jit(solution)/shard_map/pallas_call | solution.py:500
  1.6 5.1 %collective-permute-start.4 = (f32[16,1024]{1,0:T(8,128)S(1)}, f32[16,1024]{1,0:T(8,128)S(1)}, u32[]{:S(2)}, u32[]{:S(2)}) collective-permute-start(f32[16,1024]{1,0:T(8,128)S(1)} %get-tuple-element.96), channel_id=1, source_target_pairs={{0,3},{1,2},{2,1},{3,0},{4,7},{5,6},{6,5},{7,4},{8,11},{9,10},{10,... | collective-permute-start | bytes 196616 | tf_op jit(solution)/shard_map/ppermute | solution.py:376
  6.7 0.0 collective-permute-start.5
  6.7 0.6 collective-permute-start.6
  7.4 1.3 %shard_map.79 = (f32[56,1024]{1,0:T(8,128)S(1)}, f32[56,1024]{1,0:T(8,128)S(1)}, f32[56,1024]{1,0:T(8,128)S(1)}, f32[56,1024]{1,0:T(8,128)S(1)}) custom-call(f32[64,2048]{1,0:T(8,128)} %bitcast.27, f32[64,2048]{1,0:T(8,128)} %weight.3), custom_call_target="tpu_custom_call" | custom-call | flops 131072 | bytes 2097152 | tf_op jit(solution)/shard_map/pallas_call | solution.py:510
  8.7 0.6 collective-permute-done.4.refs_1_
  9.3 3.0 %collective-permute-done.5.refs_2_ = f32[16,1024]{1,0:T(8,128)S(1)} collective-permute-done((f32[16,1024]{1,0:T(8,128)S(1)}, f32[16,1024]{1,0:T(8,128)S(1)}, u32[]{:S(2)}, u32[]{:S(2)}) %collective-permute-start.5) | collective-permute-done | bytes 65568 | tf_op jit(solution)/shard_map/ppermute | solution.py:376
  12.3 2.7 %collective-permute-start.7 = (f32[56,1024]{1,0:T(8,128)S(1)}, f32[56,1024]{1,0:T(8,128)S(1)}, u32[]{:S(2)}, u32[]{:S(2)}) collective-permute-start(f32[56,1024]{1,0:T(8,128)S(1)} %get-tuple-element.102), channel_id=1, source_target_pairs={{0,3},{1,2},{2,1},{3,0},{4,7},{5,6},{6,5},{7,4},{8,11},{9,10},{10,... | collective-permute-start | bytes 688136 | tf_op jit(solution)/shard_map/ppermute | solution.py:376
  15.0 0.0 collective-permute-start.8
  15.0 1.7 %collective-permute-start.9 = (f32[56,1024]{1,0:T(8,128)S(1)}, f32[56,1024]{1,0:T(8,128)S(1)}, u32[]{:S(2)}, u32[]{:S(2)}) collective-permute-start(f32[56,1024]{1,0:T(8,128)S(1)} %get-tuple-element.104), channel_id=1, source_target_pairs={{0,1},{1,0},{2,3},{3,2},{4,5},{5,4},{6,7},{7,6},{8,9},{9,8},{10,11... | collective-permute-start | bytes 688136 | tf_op jit(solution)/shard_map/ppermute | solution.py:376
  16.7 0.0 collective-permute-done.6.refs_3_
  16.8 13.5 %conditional.1 = (f32[1,4,8,1024]{3,2,1,0:T(8,128)S(1)}, f32[1,4,8,1024]{3,2,1,0:T(8,128)S(1)}, f32[1,4,8,1024]{3,2,1,0:T(8,128)S(1)}, f32[1,4,8,1024]{3,2,1,0:T...) conditional(s32[]{:T(128)} %convert_element_type.3, () %tuple.19, ...), branch_computations={%region_0.0_spmd, %region_1.0_spmd} | conditional | flops 4295360512 | bytes 15466952 | solution.py:548
  16.8 1.6 %collective-permute-start = (f32[1,4,8,1024]{3,2,1,0:T(8,128)S(1)}, f32[1,4,8,1024]{3,2,1,0:T(8,128)S(1)}, u32[]{:S(2)}, u32[]{:S(2)}) collective-permute-start(f32[1,4,8,1024]{3,2,1,0:T(8,128)S(1)} %get-tuple-element.167), channel_id=1, source_target_pairs={{0,8},{4,12},{8,0},{12,4},{16,24},{20,28},{24,16},{28,20},{1,9},{5... | collective-permute-start | bytes 393224 | tf_op jit(solution)/shard_map/cond/branch_1_fun/ppermute | solution.py:376
  18.3 1.5 %collective-permute-start.1 = (f32[1,4,8,1024]{3,2,1,0:T(8,128)S(1)}, f32[1,4,8,1024]{3,2,1,0:T(8,128)S(1)}, u32[]{:S(2)}, u32[]{:S(2)}) collective-permute-start(f32[1,4,8,1024]{3,2,1,0:T(8,128)S(1)} %get-tuple-element.167), channel_id=1, source_target_pairs={{0,16},{4,20},{8,24},{12,28},{16,0},{20,4},{24,8},{28,12},{1,17},{... | collective-permute-start | bytes 393224 | tf_op jit(solution)/shard_map/cond/branch_1_fun/ppermute | solution.py:376
  19.8 2.0 %collective-permute-done = f32[1,4,8,1024]{3,2,1,0:T(8,128)S(1)} collective-permute-done((f32[1,4,8,1024]{3,2,1,0:T(8,128)S(1)}, f32[1,4,8,1024]{3,2,1,0:T(8,128)S(1)}, u32[]{:S(2)}, u32[]{:S(2)}) %collective-permute-start) | collective-permute-done | bytes 131104 | tf_op jit(solution)/shard_map/cond/branch_1_fun/ppermute | solution.py:376
  21.8 1.5 %collective-permute-start.2 = (f32[1,4,8,1024]{3,2,1,0:T(8,128)S(1)}, f32[1,4,8,1024]{3,2,1,0:T(8,128)}, u32[]{:S(2)}, u32[]{:S(2)}) collective-permute-start(f32[1,4,8,1024]{3,2,1,0:T(8,128)S(1)} %collective-permute-done), channel_id=1, source_target_pairs={{0,16},{4,20},{8,24},{12,28},{16,0},{20,4},{24,8},{28,12},{1,17},{... | collective-permute-start | bytes 393224 | tf_op jit(solution)/shard_map/cond/branch_1_fun/ppermute | solution.py:376
  23.3 3.8 %branch_1_fun.1 = (bf16[256,256]{1,0:T(8,128)(2,1)S(1)}, bf16[256,256]{1,0:T(8,128)(2,1)S(1)}, bf16[288,256]{1,0:T(8,128)(2,1)S(1)}, bf16[288,256]{1,0:T(8,128)(...) custom-call(f32[1,65]{1,0:T(1,128)} %bitcast.32), custom_call_target="tpu_custom_call" | custom-call | flops 4294967296 | bytes 8388608 | tf_op jit(solution)/shard_map/cond/branch_1_fun/pallas_call | solution.py:531
  27.1 0.0 collective-permute-done.1
  27.1 0.0 copy-start.5
  27.1 0.0 collective-permute-done.2
  27.2 0.0 copy-done.3
  27.2 1.0 %pad_maximum_fusion = f32[4,4,8,1024]{3,2,1,0:T(8,128)S(1)} fusion(f32[1,4,8,1024]{3,2,1,0:T(8,128)} %collective-permute-done.2, f32[1,4,8,1024]{3,2,1,0:T(8,128)S(1)} %collective-permute-done.1, f32[1,4,8,1024]{3,2,1,0:T(8,128)S(1)} %collective-permute-done, f32[1,4,8,1024]{3,2,1,0:T(8,128)S(1)} %get-tuple-element.167), kind=kLoop, calls=%fused_computation | loop fusion | flops 393216 | bytes 1048576 | tf_op jit(solution)/shard_map/cond/branch_1_fun/concatenate | solution.py:543
  28.1 0.0 copy-done.5
  28.2 0.0 copy-start.4
  28.2 0.0 copy-start.6
  28.2 0.1 collective-permute-start.3
  28.3 2.0 %collective-permute-done.3 = f32[4,4,8,1024]{3,2,1,0:T(8,128)} collective-permute-done((f32[4,4,8,1024]{3,2,1,0:T(8,128)S(1)}, f32[4,4,8,1024]{3,2,1,0:T(8,128)}, u32[]{:S(2)}, u32[]{:S(2)}) %collective-permute-start.3) | collective-permute-done | bytes 524320 | tf_op jit(solution)/shard_map/cond/branch_1_fun/ppermute | solution.py:376
  30.3 0.0 copy-done.4
  30.3 0.0 copy-done.6
  30.3 0.0 collective-permute-done.7.refs_5_
  30.3 2.2 %collective-permute-done.8.refs_6_ = f32[56,1024]{1,0:T(8,128)S(1)} collective-permute-done((f32[56,1024]{1,0:T(8,128)S(1)}, f32[56,1024]{1,0:T(8,128)S(1)}, u32[]{:S(2)}, u32[]{:S(2)}) %collective-permute-start.8) | collective-permute-done | bytes 229408 | tf_op jit(solution)/shard_map/ppermute | solution.py:376
  32.5 0.0 collective-permute-done.9.refs_7_
  32.5 5.4 %shard_map.80 = (f32[72,512]{1,0:T(8,128)S(1)}, f32[72,512]{1,0:T(8,128)S(1)}, f32[72,512]{1,0:T(8,128)S(1)}, f32[72,512]{1,0:T(8,128)S(1)}) custom-call(f32[16,1024]{1,0:T(8,128)S(1)} %get-tuple-element.91.refs_0_, f32[16,1024]{1,0:T(8,128)S(1)} %collective-permute-done.4.refs_1_, f32[16,1024]{1,0:T(8,128)S(1)} %collective-permute-done.5.refs_2_, ...), custom_call_target="tpu_custom_call" | custom-call | flops 8589934592 | bytes 8388608 | tf_op jit(solution)/shard_map/pallas_call | solution.py:400
  37.9 0.1 collective-permute-start.12
  38.0 3.3 %collective-permute-start.11 = (f32[72,512]{1,0:T(8,128)S(1)}, f32[72,512]{1,0:T(8,128)S(1)}, u32[]{:S(2)}, u32[]{:S(2)}) collective-permute-start(f32[72,512]{1,0:T(8,128)S(1)} %get-tuple-element.130), channel_id=1, source_target_pairs={{0,2},{1,3},{2,0},{3,1},{4,6},{5,7},{6,4},{7,5},{8,10},{9,11},{10,... | collective-permute-start | bytes 442376 | tf_op jit(solution)/shard_map/ppermute | solution.py:376
  41.3 1.1 %collective-permute-start.10 = (f32[72,512]{1,0:T(8,128)S(1)}, f32[72,512]{1,0:T(8,128)S(1)}, u32[]{:S(2)}, u32[]{:S(2)}) collective-permute-start(f32[72,512]{1,0:T(8,128)S(1)} %get-tuple-element.129), channel_id=1, source_target_pairs={{0,3},{1,2},{2,1},{3,0},{4,7},{5,6},{6,5},{7,4},{8,11},{9,10},{10,... | collective-permute-start | bytes 442376 | tf_op jit(solution)/shard_map/ppermute | solution.py:376
  42.4 3.2 %collective-permute-done.12 = f32[72,512]{1,0:T(8,128)S(1)} collective-permute-done((f32[72,512]{1,0:T(8,128)S(1)}, f32[72,512]{1,0:T(8,128)S(1)}, u32[]{:S(2)}, u32[]{:S(2)}) %collective-permute-start.12) | collective-permute-done | bytes 147488 | tf_op jit(solution)/shard_map/ppermute | solution.py:376
  45.6 5.8 %collective-permute-done.11 = f32[72,512]{1,0:T(8,128)S(1)} collective-permute-done((f32[72,512]{1,0:T(8,128)S(1)}, f32[72,512]{1,0:T(8,128)S(1)}, u32[]{:S(2)}, u32[]{:S(2)}) %collective-permute-start.11) | collective-permute-done | bytes 147488 | tf_op jit(solution)/shard_map/ppermute | solution.py:376
  51.5 0.0 collective-permute-done.10
  51.5 0.1 dynamic-slice_bitcast_fusion
  51.6 2.7 %collective-permute-start.13 = (f32[72,512]{1,0:T(8,128)S(1)}, f32[72,512]{1,0:T(8,128)S(1)}, u32[]{:S(2)}, u32[]{:S(2)}) collective-permute-start(f32[72,512]{1,0:T(8,128)S(1)} %get-tuple-element.140), channel_id=1, source_target_pairs={{0,24},{4,28},{8,16},{12,20},{16,8},{20,12},{24,0},{28,4},{1,25},{... | collective-permute-start | bytes 442376 | tf_op jit(solution)/shard_map/ppermute | solution.py:376
  54.3 0.5 collective-permute-start.14
  54.8 0.3 collective-permute-start.15
  55.1 0.0 collective-permute-start.16
  55.1 2.5 %collective-permute-done.13.refs_1_ = f32[72,512]{1,0:T(8,128)S(1)} collective-permute-done((f32[72,512]{1,0:T(8,128)S(1)}, f32[72,512]{1,0:T(8,128)S(1)}, u32[]{:S(2)}, u32[]{:S(2)}) %collective-permute-start.13) | collective-permute-done | bytes 147488 | tf_op jit(solution)/shard_map/ppermute | solution.py:376
  57.7 0.0 collective-permute-start.17
  57.7 1.8 %collective-permute-done.14.refs_2_ = f32[72,512]{1,0:T(8,128)S(1)} collective-permute-done((f32[72,512]{1,0:T(8,128)S(1)}, f32[72,512]{1,0:T(8,128)S(1)}, u32[]{:S(2)}, u32[]{:S(2)}) %collective-permute-start.14) | collective-permute-done | bytes 147488 | tf_op jit(solution)/shard_map/ppermute | solution.py:376
  59.5 0.0 collective-permute-start.18
  59.5 0.4 collective-permute-done.15.refs_3_
  60.0 0.1 collective-permute-start.19
  60.0 0.0 collective-permute-done.16.refs_4_
  60.0 0.0 collective-permute-done.17.refs_5_
  60.0 0.9 %collective-permute-done.18.refs_6_ = f32[72,512]{1,0:T(8,128)S(1)} collective-permute-done((f32[72,512]{1,0:T(8,128)S(1)}, f32[72,512]{1,0:T(8,128)S(1)}, u32[]{:S(2)}, u32[]{:S(2)}) %collective-permute-start.18) | collective-permute-done | bytes 147488 | tf_op jit(solution)/shard_map/ppermute | solution.py:376
  60.9 0.5 collective-permute-done.19.refs_7_
  61.3 0.0 copy-done.1
  61.3 1.6 %shard_map.81 = (f32[64,512]{1,0:T(8,128)S(1)}, f32[64,512]{1,0:T(8,128)S(1)}, f32[64,512]{1,0:T(8,128)S(1)}, f32[64,512]{1,0:T(8,128)S(1)}) custom-call(s32[8]{0:T(128)S(1)} %copy-done, s32[8]{0:T(128)S(1)} %copy-done.1, f32[72,512]{1,0:T(8,128)S(1)} %get-tuple-element.141.refs_0_, f32[72,512]{1,0:T(8,128)S(1)} %collective-permute-done.13.refs_1_, ...), custom_call_target="tpu_custom_call" | custom-call | flops 16777216 | bytes 8388608 | tf_op jit(solution)/shard_map/pallas_call | solution.py:445
  63.0 2.0 %collective-permute-start.20 = (f32[64,512]{1,0:T(8,128)S(1)}, f32[64,512]{1,0:T(8,128)S(1)}, u32[]{:S(2)}, u32[]{:S(2)}) collective-permute-start(f32[64,512]{1,0:T(8,128)S(1)} %get-tuple-element.133.refs_9_), channel_id=1, source_target_pairs={{0,24},{4,28},{8,16},{12,20},{16,8},{20,12},{24,0},{28,4},{1,25},{... | collective-permute-start | bytes 393224 | tf_op jit(solution)/shard_map/ppermute | solution.py:376
  65.0 0.5 collective-permute-start.21
  65.5 1.0 %collective-permute-start.22 = (f32[64,512]{1,0:T(8,128)S(1)}, f32[64,512]{1,0:T(8,128)S(1)}, u32[]{:S(2)}, u32[]{:S(2)}) collective-permute-start(f32[64,512]{1,0:T(8,128)S(1)} %get-tuple-element.135.refs_11_), channel_id=1, source_target_pairs={{0,16},{4,20},{8,24},{12,28},{16,0},{20,4},{24,8},{28,12},{1,17},{... | collective-permute-start | bytes 393224 | tf_op jit(solution)/shard_map/ppermute | solution.py:376
  66.5 2.6 %shard_map.83 = f32[8,64,256]{2,1,0:T(8,128)} custom-call(s32[8]{0:T(128)S(1)} %copy-done, s32[8]{0:T(128)S(1)} %copy-done.1, s32[8]{0:T(128)S(1)} %copy-done.2, f32[72,512]{1,0:T(8,128)S(1)} %get-tuple-element.141.refs_0_, f32[72,512]{1,0:T(8,128)S(1)} %collective-permute-done.13.refs_1_, f32[72,512]{1,0:T(8,128)S(1)} %collective-permute-done.14.refs_2_, ...), custom_call_target="tpu_custom_call" | custom-call | flops 16777216 | bytes 8388608 | tf_op jit(solution)/shard_map/pallas_call | solution.py:455
  69.1 1.2 %collective-permute-done.20.refs_1_ = f32[64,512]{1,0:T(8,128)S(1)} collective-permute-done((f32[64,512]{1,0:T(8,128)S(1)}, f32[64,512]{1,0:T(8,128)S(1)}, u32[]{:S(2)}, u32[]{:S(2)}) %collective-permute-start.20) | collective-permute-done | bytes 131104 | tf_op jit(solution)/shard_map/ppermute | solution.py:376
  70.3 1.6 %collective-permute-done.21.refs_2_ = f32[64,512]{1,0:T(8,128)S(1)} collective-permute-done((f32[64,512]{1,0:T(8,128)S(1)}, f32[64,512]{1,0:T(8,128)S(1)}, u32[]{:S(2)}, u32[]{:S(2)}) %collective-permute-start.21) | collective-permute-done | bytes 131104 | tf_op jit(solution)/shard_map/ppermute | solution.py:376
  71.9 0.4 collective-permute-done.22.refs_3_
  72.3 0.8 %shard_map.82 = f32[64,2048]{1,0:T(8,128)} custom-call(f32[64,512]{1,0:T(8,128)S(1)} %get-tuple-element.132.refs_0_.refs_8_, f32[64,512]{1,0:T(8,128)S(1)} %collective-permute-done.20.refs_1_, f32[64,512]{1,0:T(8,128)S(1)} %collective-permute-done.21.refs_2_, f32[64,512]{1,0:T(8,128)S(1)} %collective-permute-done.22.refs_3_), custom_call_target="tpu_custom_call" | custom-call | bytes 1048576 | tf_op jit(solution)/shard_map/pallas_call | solution.py:467
  (12 shorter events, 0.1 us)
Async XLA Ops:
  1.6 7.7 %collective-permute-start.4 = (f32[16,1024]{1,0:T(8,128)S(1)}, f32[16,1024]{1,0:T(8,128)S(1)}, u32[]{:S(2)}, u32[]{:S(2)}) collective-permute-start(f32[16,1024]{1,0:T(8,128)S(1)} %get-tuple-element.96), channel_id=1, source_target_pairs={{0,3},{1,2},{2,1},{3,0},{4,7},{5,6},{6,5},{7,4},{8,11},{9,10},{10,... | collective-permute-start | bytes 196616 | tf_op jit(solution)/shard_map/ppermute | solution.py:376
  6.7 5.6 %collective-permute-start.5 = (f32[16,1024]{1,0:T(8,128)S(1)}, f32[16,1024]{1,0:T(8,128)S(1)}, u32[]{:S(2)}, u32[]{:S(2)}) collective-permute-start(f32[16,1024]{1,0:T(8,128)S(1)} %get-tuple-element.97), channel_id=1, source_target_pairs={{0,2},{1,3},{2,0},{3,1},{4,6},{5,7},{6,4},{7,5},{8,10},{9,11},{10,... | collective-permute-start | bytes 196616 | tf_op jit(solution)/shard_map/ppermute | solution.py:376
  6.7 10.0 %collective-permute-start.6 = (f32[16,1024]{1,0:T(8,128)S(1)}, f32[16,1024]{1,0:T(8,128)S(1)}, u32[]{:S(2)}, u32[]{:S(2)}) collective-permute-start(f32[16,1024]{1,0:T(8,128)S(1)} %get-tuple-element.100), channel_id=1, source_target_pairs={{0,1},{1,0},{2,3},{3,2},{4,5},{5,4},{6,7},{7,6},{8,9},{9,8},{10,11... | collective-permute-start | bytes 196616 | tf_op jit(solution)/shard_map/ppermute | solution.py:376
  12.3 18.0 %collective-permute-start.7 = (f32[56,1024]{1,0:T(8,128)S(1)}, f32[56,1024]{1,0:T(8,128)S(1)}, u32[]{:S(2)}, u32[]{:S(2)}) collective-permute-start(f32[56,1024]{1,0:T(8,128)S(1)} %get-tuple-element.102), channel_id=1, source_target_pairs={{0,3},{1,2},{2,1},{3,0},{4,7},{5,6},{6,5},{7,4},{8,11},{9,10},{10,... | collective-permute-start | bytes 688136 | tf_op jit(solution)/shard_map/ppermute | solution.py:376
  15.0 17.4 %collective-permute-start.8 = (f32[56,1024]{1,0:T(8,128)S(1)}, f32[56,1024]{1,0:T(8,128)S(1)}, u32[]{:S(2)}, u32[]{:S(2)}) collective-permute-start(f32[56,1024]{1,0:T(8,128)S(1)} %get-tuple-element.103), channel_id=1, source_target_pairs={{0,2},{1,3},{2,0},{3,1},{4,6},{5,7},{6,4},{7,5},{8,10},{9,11},{10,... | collective-permute-start | bytes 688136 | tf_op jit(solution)/shard_map/ppermute | solution.py:376
  15.0 17.4 %collective-permute-start.9 = (f32[56,1024]{1,0:T(8,128)S(1)}, f32[56,1024]{1,0:T(8,128)S(1)}, u32[]{:S(2)}, u32[]{:S(2)}) collective-permute-start(f32[56,1024]{1,0:T(8,128)S(1)} %get-tuple-element.104), channel_id=1, source_target_pairs={{0,1},{1,0},{2,3},{3,2},{4,5},{5,4},{6,7},{7,6},{8,9},{9,8},{10,11... | collective-permute-start | bytes 688136 | tf_op jit(solution)/shard_map/ppermute | solution.py:376
  16.8 5.0 %collective-permute-start = (f32[1,4,8,1024]{3,2,1,0:T(8,128)S(1)}, f32[1,4,8,1024]{3,2,1,0:T(8,128)S(1)}, u32[]{:S(2)}, u32[]{:S(2)}) collective-permute-start(f32[1,4,8,1024]{3,2,1,0:T(8,128)S(1)} %get-tuple-element.167), channel_id=1, source_target_pairs={{0,8},{4,12},{8,0},{12,4},{16,24},{20,28},{24,16},{28,20},{1,9},{5... | collective-permute-start | bytes 393224 | tf_op jit(solution)/shard_map/cond/branch_1_fun/ppermute | solution.py:376
  18.3 8.8 %collective-permute-start.1 = (f32[1,4,8,1024]{3,2,1,0:T(8,128)S(1)}, f32[1,4,8,1024]{3,2,1,0:T(8,128)S(1)}, u32[]{:S(2)}, u32[]{:S(2)}) collective-permute-start(f32[1,4,8,1024]{3,2,1,0:T(8,128)S(1)} %get-tuple-element.167), channel_id=1, source_target_pairs={{0,16},{4,20},{8,24},{12,28},{16,0},{20,4},{24,8},{28,12},{1,17},{... | collective-permute-start | bytes 393224 | tf_op jit(solution)/shard_map/cond/branch_1_fun/ppermute | solution.py:376
  21.8 5.4 %copy-start.3 = (f32[1,4,8,1024]{3,2,1,0:T(8,128)}, f32[1,4,8,1024]{3,2,1,0:T(8,128)S(1)}, u32[]{:S(2)}) copy-start(f32[1,4,8,1024]{3,2,1,0:T(8,128)S(1)} %collective-permute-done) | copy-start | bytes 393220 | tf_op jit(solution)/shard_map/cond
  21.8 5.3 %collective-permute-start.2 = (f32[1,4,8,1024]{3,2,1,0:T(8,128)S(1)}, f32[1,4,8,1024]{3,2,1,0:T(8,128)}, u32[]{:S(2)}, u32[]{:S(2)}) collective-permute-start(f32[1,4,8,1024]{3,2,1,0:T(8,128)S(1)} %collective-permute-done), channel_id=1, source_target_pairs={{0,16},{4,20},{8,24},{12,28},{16,0},{20,4},{24,8},{28,12},{1,17},{... | collective-permute-start | bytes 393224 | tf_op jit(solution)/shard_map/cond/branch_1_fun/ppermute | solution.py:376
  27.1 1.0 %copy-start.5 = (f32[1,4,8,1024]{3,2,1,0:T(8,128)}, f32[1,4,8,1024]{3,2,1,0:T(8,128)S(1)}, u32[]{:S(2)}) copy-start(f32[1,4,8,1024]{3,2,1,0:T(8,128)S(1)} %collective-permute-done.1) | copy-start | bytes 393220 | tf_op jit(solution)/shard_map/cond
  28.2 2.1 %copy-start.4 = (f32[1,4,8,1024]{3,2,1,0:T(8,128)S(1)}, f32[1,4,8,1024]{3,2,1,0:T(8,128)}, u32[]{:S(2)}) copy-start(f32[1,4,8,1024]{3,2,1,0:T(8,128)} %copy-done.3) | copy-start | bytes 393220 | tf_op jit(solution)/shard_map/cond
  28.2 2.1 %copy-start.6 = (f32[1,4,8,1024]{3,2,1,0:T(8,128)S(1)}, f32[1,4,8,1024]{3,2,1,0:T(8,128)}, u32[]{:S(2)}) copy-start(f32[1,4,8,1024]{3,2,1,0:T(8,128)} %copy-done.5) | copy-start | bytes 393220 | tf_op jit(solution)/shard_map/cond
  28.2 2.1 %collective-permute-start.3 = (f32[4,4,8,1024]{3,2,1,0:T(8,128)S(1)}, f32[4,4,8,1024]{3,2,1,0:T(8,128)}, u32[]{:S(2)}, u32[]{:S(2)}) collective-permute-start(f32[4,4,8,1024]{3,2,1,0:T(8,128)S(1)} %pad_maximum_fusion), channel_id=1, source_target_pairs={{0,4},{4,0},{8,12},{12,8},{16,20},{20,16},{24,28},{28,24},{1,5},{5... | collective-permute-start | bytes 1572872 | tf_op jit(solution)/shard_map/cond/branch_1_fun/ppermute | solution.py:376
  37.9 7.7 %collective-permute-start.12 = (f32[72,512]{1,0:T(8,128)S(1)}, f32[72,512]{1,0:T(8,128)S(1)}, u32[]{:S(2)}, u32[]{:S(2)}) collective-permute-start(f32[72,512]{1,0:T(8,128)S(1)} %get-tuple-element.131), channel_id=1, source_target_pairs={{0,1},{1,0},{2,3},{3,2},{4,5},{5,4},{6,7},{7,6},{8,9},{9,8},{10,11... | collective-permute-start | bytes 442376 | tf_op jit(solution)/shard_map/ppermute | solution.py:376
  38.0 13.4 %collective-permute-start.11 = (f32[72,512]{1,0:T(8,128)S(1)}, f32[72,512]{1,0:T(8,128)S(1)}, u32[]{:S(2)}, u32[]{:S(2)}) collective-permute-start(f32[72,512]{1,0:T(8,128)S(1)} %get-tuple-element.130), channel_id=1, source_target_pairs={{0,2},{1,3},{2,0},{3,1},{4,6},{5,7},{6,4},{7,5},{8,10},{9,11},{10,... | collective-permute-start | bytes 442376 | tf_op jit(solution)/shard_map/ppermute | solution.py:376
  41.3 10.1 %collective-permute-start.10 = (f32[72,512]{1,0:T(8,128)S(1)}, f32[72,512]{1,0:T(8,128)S(1)}, u32[]{:S(2)}, u32[]{:S(2)}) collective-permute-start(f32[72,512]{1,0:T(8,128)S(1)} %get-tuple-element.129), channel_id=1, source_target_pairs={{0,3},{1,2},{2,1},{3,0},{4,7},{5,6},{6,5},{7,4},{8,11},{9,10},{10,... | collective-permute-start | bytes 442376 | tf_op jit(solution)/shard_map/ppermute | solution.py:376
  51.6 6.1 %collective-permute-start.13 = (f32[72,512]{1,0:T(8,128)S(1)}, f32[72,512]{1,0:T(8,128)S(1)}, u32[]{:S(2)}, u32[]{:S(2)}) collective-permute-start(f32[72,512]{1,0:T(8,128)S(1)} %get-tuple-element.140), channel_id=1, source_target_pairs={{0,24},{4,28},{8,16},{12,20},{16,8},{20,12},{24,0},{28,4},{1,25},{... | collective-permute-start | bytes 442376 | tf_op jit(solution)/shard_map/ppermute | solution.py:376
  54.3 5.2 %collective-permute-start.14 = (f32[72,512]{1,0:T(8,128)S(1)}, f32[72,512]{1,0:T(8,128)S(1)}, u32[]{:S(2)}, u32[]{:S(2)}) collective-permute-start(f32[72,512]{1,0:T(8,128)S(1)} %get-tuple-element.139), channel_id=1, source_target_pairs={{0,8},{4,12},{8,0},{12,4},{16,24},{20,28},{24,16},{28,20},{1,9},{5... | collective-permute-start | bytes 442376 | tf_op jit(solution)/shard_map/ppermute | solution.py:376
  54.8 6.5 %copy-start = (s32[8]{0:T(128)S(1)}, s32[8]{0:T(128)}, u32[]{:S(2)}) copy-start(s32[8]{0:T(128)} %pair_one.3) | copy-start | bytes 100
  54.8 6.5 %copy-start.1 = (s32[8]{0:T(128)S(1)}, s32[8]{0:T(128)}, u32[]{:S(2)}) copy-start(s32[8]{0:T(128)} %pair_two.3) | copy-start | bytes 100
  54.8 5.1 %collective-permute-start.15 = (f32[72,512]{1,0:T(8,128)S(1)}, f32[72,512]{1,0:T(8,128)S(1)}, u32[]{:S(2)}, u32[]{:S(2)}) collective-permute-start(f32[72,512]{1,0:T(8,128)S(1)} %get-tuple-element.138), channel_id=1, source_target_pairs={{0,16},{4,20},{8,24},{12,28},{16,0},{20,4},{24,8},{28,12},{1,17},{... | collective-permute-start | bytes 442376 | tf_op jit(solution)/shard_map/ppermute | solution.py:376
  55.1 4.9 %collective-permute-start.16 = (f32[72,512]{1,0:T(8,128)S(1)}, f32[72,512]{1,0:T(8,128)S(1)}, u32[]{:S(2)}, u32[]{:S(2)}) collective-permute-start(f32[72,512]{1,0:T(8,128)S(1)} %get-tuple-element.141.refs_0_), channel_id=1, source_target_pairs={{0,4},{4,0},{8,12},{12,8},{16,20},{20,16},{24,28},{28,24},{1,5},{5... | collective-permute-start | bytes 442376 | tf_op jit(solution)/shard_map/ppermute | solution.py:376
  57.7 2.4 %collective-permute-start.17 = (f32[72,512]{1,0:T(8,128)S(1)}, f32[72,512]{1,0:T(8,128)S(1)}, u32[]{:S(2)}, u32[]{:S(2)}) collective-permute-start(f32[72,512]{1,0:T(8,128)S(1)} %collective-permute-done.13.refs_1_), channel_id=1, source_target_pairs={{0,4},{4,0},{8,12},{12,8},{16,20},{20,16},{24,28},{28,24},{1,5},{5... | collective-permute-start | bytes 442376 | tf_op jit(solution)/shard_map/ppermute | solution.py:376
  59.5 1.4 %collective-permute-start.18 = (f32[72,512]{1,0:T(8,128)S(1)}, f32[72,512]{1,0:T(8,128)S(1)}, u32[]{:S(2)}, u32[]{:S(2)}) collective-permute-start(f32[72,512]{1,0:T(8,128)S(1)} %collective-permute-done.14.refs_2_), channel_id=1, source_target_pairs={{0,4},{4,0},{8,12},{12,8},{16,20},{20,16},{24,28},{28,24},{1,5},{5... | collective-permute-start | bytes 442376 | tf_op jit(solution)/shard_map/ppermute | solution.py:376
  60.0 1.4 %collective-permute-start.19 = (f32[72,512]{1,0:T(8,128)S(1)}, f32[72,512]{1,0:T(8,128)S(1)}, u32[]{:S(2)}, u32[]{:S(2)}) collective-permute-start(f32[72,512]{1,0:T(8,128)S(1)} %collective-permute-done.15.refs_3_), channel_id=1, source_target_pairs={{0,4},{4,0},{8,12},{12,8},{16,20},{20,16},{24,28},{28,24},{1,5},{5... | collective-permute-start | bytes 442376 | tf_op jit(solution)/shard_map/ppermute | solution.py:376
  63.0 7.3 %collective-permute-start.20 = (f32[64,512]{1,0:T(8,128)S(1)}, f32[64,512]{1,0:T(8,128)S(1)}, u32[]{:S(2)}, u32[]{:S(2)}) collective-permute-start(f32[64,512]{1,0:T(8,128)S(1)} %get-tuple-element.133.refs_9_), channel_id=1, source_target_pairs={{0,24},{4,28},{8,16},{12,20},{16,8},{20,12},{24,0},{28,4},{1,25},{... | collective-permute-start | bytes 393224 | tf_op jit(solution)/shard_map/ppermute | solution.py:376
  65.0 6.9 %collective-permute-start.21 = (f32[64,512]{1,0:T(8,128)S(1)}, f32[64,512]{1,0:T(8,128)S(1)}, u32[]{:S(2)}, u32[]{:S(2)}) collective-permute-start(f32[64,512]{1,0:T(8,128)S(1)} %get-tuple-element.134.refs_10_), channel_id=1, source_target_pairs={{0,8},{4,12},{8,0},{12,4},{16,24},{20,28},{24,16},{28,20},{1,9},{5... | collective-permute-start | bytes 393224 | tf_op jit(solution)/shard_map/ppermute | solution.py:376
  65.5 1.0 %copy-start.2 = (s32[8]{0:T(128)S(1)}, s32[8]{0:T(128)}, u32[]{:S(2)}) copy-start(s32[8]{0:T(128)} %owner.1) | copy-start | bytes 100
  65.5 6.8 %collective-permute-start.22 = (f32[64,512]{1,0:T(8,128)S(1)}, f32[64,512]{1,0:T(8,128)S(1)}, u32[]{:S(2)}, u32[]{:S(2)}) collective-permute-start(f32[64,512]{1,0:T(8,128)S(1)} %get-tuple-element.135.refs_11_), channel_id=1, source_target_pairs={{0,16},{4,20},{8,24},{12,28},{16,0},{20,4},{24,8},{28,12},{1,17},{... | collective-permute-start | bytes 393224 | tf_op jit(solution)/shard_map/ppermute | solution.py:376
